TPU v7x, 32 devices: a whole 2x2x4 slice. The times are simulated.
32 devices in a mesh: section: 4 (over y, x), dom: 8 (over z, core).
Axes of the slice: x: 2, y: 2, z: 4, core: 2. Of those that a mesh axis runs over, the one named last changes fastest.
Arguments:
- layer_inputs: bfloat16 [4, 1, 3072, 512], P('section', None, 'dom'), may hold values from -6 to 6
- top_grad: bfloat16 [1, 3072, 512], P(None, 'dom'), may hold values from -6 to 6
- w_qkv: bfloat16 [4, 512, 1536], P('section')
- w_out: bfloat16 [4, 512, 512], P('section'), may hold values from -0.25 to 0.25
- neighbours: int32 [24, 3], P('dom'), may hold values from -1 to 23, as said below
Outputs:
- input_grads: bfloat16 [4, 1, 3072, 512], P('section', None, 'dom')
- qkv_grad: float32 [4, 512, 1536], P('section', 'dom')
- out_grad: float32 [4, 512, 512], P('section', 'dom')
Inputs may be any that keep to these rules, and one draw needn't show every extreme that they name: `neighbours`: entry 0 of block b is b; the other entries name distinct blocks (b + o) mod 24 with 0 < |o| <= 1, then -1 to the end of the row. The first block of every index of dom lists 3 blocks.
All inputs are finite; a program needn't handle non-finite values.
Results may differ from a plain program's by a relative error of at most 0.017.
Values may be sent and summed in bfloat16 or wider, within the bound.
No kernel may reach another device: no remote copies, remote signals or barrier semaphores. Data moves between devices by JAX's collectives and lax.ppermute only.
A program may use at most 128 MiB of HBM per device.

v0:
```python
import jax
import jax.numpy as jnp
from jax import lax
from jax.sharding import PartitionSpec as P

HEADS = 8
KMAX = 3
HALO = 1


def extended_2(block, sides, width):
    for axis, dim in sides:
        count = lax.axis_size(axis)
        forward = [(i, i + 1) for i in range(count - 1)]
        forward.append((count - 1, 0))
        backward = [(target, source) for source, target in forward]
        low = lax.ppermute(
            lax.slice_in_dim(block, block.shape[dim] - width, None, axis=dim), axis, forward
        )
        high = lax.ppermute(lax.slice_in_dim(block, 0, width, axis=dim), axis, backward)
        block = jnp.concatenate([low, block, high], axis=dim)
    return block


def shifted(block, axis, distance):
    devices = range(lax.axis_size(axis))
    route = [((i - distance) % len(devices), i) for i in devices]
    return lax.ppermute(block, axis, route)


def shifted_2(block, axis, distance):
    devices = range(lax.axis_size(axis))
    route = [(i - distance, i) for i in devices if i - distance in devices]
    return lax.ppermute(block, axis, route)


def fetch_rims(keyval):
    extended = extended_2(keyval, (("dom", 0),), HALO)
    return extended


def layer_back(x, g, w_qkv, w_out, neighbours):
    blk, tile, width = x.shape
    hdim = width // HEADS
    scale = 1.0 / hdim**0.5
    xf = x.astype(jnp.float32)
    mean_value = jnp.mean(xf, axis=-1, keepdims=True)
    centered_input = xf - mean_value
    inverse_deviation = lax.rsqrt(
        jnp.mean(centered_input * centered_input, axis=-1, keepdims=True) + 1e-05
    )
    normalized_input = centered_input * inverse_deviation
    normed_rows = normalized_input.astype(jnp.bfloat16)
    flat = normed_rows.reshape(blk * tile, width)
    qkv = jnp.dot(flat, w_qkv, preferred_element_type=jnp.float32).astype(jnp.bfloat16)
    qkv = qkv.reshape(blk, tile, 3 * width)
    query = qkv[..., :width].reshape(blk, tile, HEADS, hdim)
    extended = fetch_rims(qkv[..., width:])
    parts = lax.axis_size("dom")
    where_me = lax.axis_index("dom")
    valid = neighbours >= 0
    where_at = jnp.where(valid, (neighbours - where_me * blk + HALO) % (blk * parts), 0)
    tiles = extended[where_at]
    keys = tiles[..., :width].reshape(blk, KMAX * tile, HEADS, hdim)
    values = tiles[..., width:].reshape(blk, KMAX * tile, HEADS, hdim)
    mask = jnp.repeat(valid, tile, axis=1)[:, None, None, :]
    scores = jnp.einsum("bqhd,bkhd->bhqk", query, keys, preferred_element_type=jnp.float32) * scale
    scores = jnp.where(mask, scores, -1e30)
    top = jnp.max(scores, axis=-1, keepdims=True)
    expo = jnp.exp(scores - top)
    probs = expo / jnp.sum(expo, axis=-1, keepdims=True)
    probs_b = probs.astype(jnp.bfloat16)
    attn = jnp.einsum(
        "bhqk,bkhd->bqhd", probs_b, values, preferred_element_type=jnp.float32
    ).astype(jnp.bfloat16)
    attn = attn.reshape(blk * tile, width)
    grad_rows = g.reshape(blk * tile, width)
    d_attn = jnp.dot(grad_rows, w_out.T, preferred_element_type=jnp.float32).astype(jnp.bfloat16)
    d_attn = d_attn.reshape(blk, tile, HEADS, hdim)
    d_prob = jnp.einsum("bqhd,bkhd->bhqk", d_attn, values, preferred_element_type=jnp.float32)
    d_score = (probs * (d_prob - jnp.sum(d_prob * probs, axis=-1, keepdims=True)) * scale).astype(
        jnp.bfloat16
    )
    d_query = jnp.einsum("bhqk,bkhd->bqhd", d_score, keys, preferred_element_type=jnp.float32)
    d_keys = jnp.einsum("bhqk,bqhd->bkhd", d_score, query, preferred_element_type=jnp.float32)
    d_values = jnp.einsum("bhqk,bqhd->bkhd", probs_b, d_attn, preferred_element_type=jnp.float32)
    d_tiles = jnp.concatenate(
        [d_keys.reshape(blk, KMAX, tile, width), d_values.reshape(blk, KMAX, tile, width)], axis=-1
    )
    slots = blk + 2 * HALO
    weighted = d_tiles * valid[:, :, None, None].astype(jnp.float32)
    d_extended = jnp.zeros((slots, tile, 2 * width), jnp.float32)
    d_extended = d_extended.at[where_at.reshape(-1)].add(
        weighted.reshape(blk * KMAX, tile, 2 * width)
    )
    lower_rim = d_extended[:HALO].astype(jnp.bfloat16)
    upper_rim = d_extended[HALO + blk :].astype(jnp.bfloat16)
    from_next = shifted(lower_rim, "dom", -1)
    from_prev = shifted(upper_rim, "dom", 1)
    d_keyval = d_extended[HALO : HALO + blk]
    d_keyval = d_keyval.at[blk - HALO :].add(from_next.astype(jnp.float32))
    d_keyval = d_keyval.at[:HALO].add(from_prev.astype(jnp.float32))
    d_qkv = jnp.concatenate([d_query.reshape(blk, tile, width), d_keyval], axis=-1).astype(
        jnp.bfloat16
    )
    d_qkv = d_qkv.reshape(blk * tile, 3 * width)
    normed_gradient = jnp.dot(d_qkv, w_qkv.T, preferred_element_type=jnp.float32).reshape(
        blk, tile, width
    )
    layernorm_gradient = inverse_deviation * (
        normed_gradient
        - jnp.mean(normed_gradient, axis=-1, keepdims=True)
        - normalized_input * jnp.mean(normed_gradient * normalized_input, axis=-1, keepdims=True)
    )
    d_input = (g.astype(jnp.float32) + layernorm_gradient).astype(jnp.bfloat16)
    return (d_input, flat, d_qkv, attn, grad_rows)


def local(layer_inputs, top_grad, w_qkv, w_out, neighbours):
    sections = lax.axis_size("section")
    section_me = lax.axis_index("section")
    micro = top_grad.shape[0]
    rows = top_grad.shape[1]
    width = top_grad.shape[2]
    blk = neighbours.shape[0]
    tile = rows // blk
    weight_in = w_qkv[0]
    weight_out = w_out[0]
    saved = layer_inputs[0]
    ticks = micro + sections - 1
    extra = (jnp.zeros((width, 3 * width), jnp.float32), jnp.zeros((width, width), jnp.float32))
    start_carry = (
        jnp.zeros((rows, width), jnp.bfloat16),
        jnp.zeros((micro, rows, width), jnp.bfloat16),
        extra,
    )

    def advance(tick, carry):
        received, results, extra = carry
        micro_idx = tick - (sections - 1 - section_me)
        active = (micro_idx >= 0) & (micro_idx < micro)
        safe = jnp.clip(micro_idx, 0, micro - 1)
        x_now = lax.dynamic_index_in_dim(saved, safe, 0, keepdims=False).reshape(blk, tile, width)
        top_now = lax.dynamic_index_in_dim(top_grad, safe, 0, keepdims=False)
        g_now = jnp.where(section_me == sections - 1, top_now, received).reshape(blk, tile, width)
        d_input, flat, d_qkv, attn, grad_rows = layer_back(
            x_now, g_now, weight_in, weight_out, neighbours
        )
        d_rows = d_input.reshape(rows, width)
        results = jnp.where(
            active, lax.dynamic_update_index_in_dim(results, d_rows, safe, 0), results
        )
        qkv_term = jnp.einsum("rd,re->de", flat, d_qkv, preferred_element_type=jnp.float32)
        out_term = jnp.einsum("rd,re->de", attn, grad_rows, preferred_element_type=jnp.float32)
        extra = (
            extra[0] + jnp.where(active, qkv_term, 0.0),
            extra[1] + jnp.where(active, out_term, 0.0),
        )
        received = shifted_2(d_rows, "section", -1)
        return (received, results, extra)

    received, results, extra = lax.fori_loop(0, ticks, advance, start_carry)
    first_part = extra[0]
    second_part = extra[1]
    summed = lax.psum_scatter(
        jnp.concatenate([first_part, second_part], axis=-1), "dom", scatter_dimension=0, tiled=True
    )
    return (results[None], summed[None, :, : 3 * width], summed[None, :, 3 * width :])


def solution(mesh):
    placed = (
        P("section", None, "dom", None),
        P(None, "dom", None),
        P("section", None, None),
        P("section", None, None),
        P("dom", None),
    )
    return jax.shard_map(
        local,
        mesh=mesh,
        in_specs=placed,
        out_specs=(
            P("section", None, "dom", None),
            P("section", "dom", None),
            P("section", "dom", None),
        ),
        check_vma=False,
    )
```

profile of v0, /device:TPU:0, one launch (start us, length us, event | category | flops | bytes accessed | tf_op | source)
XLA Modules:
  0.0 663.6 jit_solution(10143709784711705376)
XLA Ops:
  12.6 4.1 collective-permute-start.4
  18.0 2.9 collective-permute-done.3
  24.7 3.6 copy.25
  30.5 2.6 select_reduce_fusion
  33.2 565.4 %while.25 = (s32[]{:T(128)}, bf16[384,512]{1,0:T(8,128)(2,1)S(1)}, bf16[1,384,512]{2,1,0:T(8,128)(2,1)}, f32[512,1536]{1,0:T(8,128)}, f32[512,512]{1,0:T(8,128)}...) while((s32[]{:T(128)}, bf16[384,512]{1,0:T(8,128)(2,1)S(1)}, ...), condition=%wide.region_11.12_spmd.clone, body=%wide.region_3.11_spmd.clone.sunk | while | flops 3188003072 | bytes 227787952 | solution.py:162
  41.1 4.1 fusion.145
  45.2 4.1 reshape.605
  50.4 4.4 fusion.147
  60.8 25.4 %fusion.148 = f32[3,384,8,64]{1,3,2,0:T(8,128)} fusion(bf16[3,128,8,64]{1,3,2,0:T(8,128)(2,1)} %bitcast.180, f32[3,8,128,384]{3,2,1,0:T(8,128)} %fusion.147, f32[3,8,128,384]{3,2,1,0:T(8,128)} %copy-done.23, f32[3,8,128]{2,1,0:T(8,128)} %copy-done.24, f32[3,8,128]{2,1,0:T(8,128)} %get-tuple-element.662, pred[3,384]{1,0:T(4,128)(4,1)} %bitcast.189), kind=kOutput, calls=%fused_computation.19.clone.1 | convolution fusion | flops 166333824 | bytes 12215424 | tf_op jit(solution)/shard_map/while/body/eval_jaxpr/bhqk,bqhd->bkhd/dot_general | solution.py:85
  86.2 3.4 copy.52
  89.7 3.6 concatenate.71
  93.3 5.0 copy.53
  98.3 4.9 concatenate.72
  103.2 4.7 maximum_multiply_fusion.2
  108.2 7.7 %scatter_fusion = f32[5,128,1024]{2,1,0:T(8,128)S(1)} fusion(f32[5,128,1024]{2,1,0:T(8,128)S(1)} %broadcast.703, s32[9]{0:T(128)S(1)} %fusion.144, f32[9,128,1024]{2,1,0:T(8,128)} %maximum_multiply_fusion.2), kind=kCustom, calls=%fused_computation.1.clone.clone.1 | custom fusion | flops 1179648 | bytes 14155812 | tf_op jit(solution)/shard_map/while/body/eval_jaxpr/scatter-add | solution.py:93
  117.0 3.8 collective-permute-start
  120.9 4.6 fusion.156
  127.6 2.5 fusion.157
  130.2 22.5 %fusion.152 = bf16[3,8,128,64]{2,3,1,0:T(8,128)(2,1)} fusion(bf16[3,384,8,64]{1,3,2,0:T(8,128)(2,1)} %reshape.605, f32[3,8,128,384]{3,2,1,0:T(8,128)} %fusion.147, f32[3,8,128,384]{3,2,1,0:T(8,128)} %copy-done.23, f32[3,8,128]{2,1,0:T(8,128)S(1)} %copy-done.25, f32[3,8,128]{2,1,0:T(8,128)S(1)} %copy-done.21, pred[3,384]{1,0:T(4,128)(4,1)S(1)} %bitcast.193), kind=kOutput, calls=%fused_computation.24.clone.1 | convolution fusion | flops 166530432 | bytes 11035776 | tf_op jit(solution)/shard_map/while/body/eval_jaxpr/bhqk,bkhd->bqhd/dot_general | solution.py:84
  165.9 10.0 %collective-permute-done.2 = bf16[384,512]{1,0:T(8,128)(2,1)S(1)} collective-permute-done((bf16[384,512]{1,0:T(8,128)(2,1)S(1)}, bf16[384,512]{1,0:T(8,128)(2,1)S(1)}, u32[]{:S(2)}, u32[]{:S(2)}) %collective-permute-start.2) | collective-permute-done | bytes 393248 | tf_op jit(solution)/shard_map/while/body/eval_jaxpr/ppermute | solution.py:34
  183.6 4.1 fusion.145
  187.7 4.1 reshape.605
  193.0 4.4 fusion.147
  203.4 25.4 %fusion.148 = f32[3,384,8,64]{1,3,2,0:T(8,128)} fusion(bf16[3,128,8,64]{1,3,2,0:T(8,128)(2,1)} %bitcast.180, f32[3,8,128,384]{3,2,1,0:T(8,128)} %fusion.147, f32[3,8,128,384]{3,2,1,0:T(8,128)} %copy-done.23, f32[3,8,128]{2,1,0:T(8,128)} %copy-done.24, f32[3,8,128]{2,1,0:T(8,128)} %get-tuple-element.662, pred[3,384]{1,0:T(4,128)(4,1)} %bitcast.189), kind=kOutput, calls=%fused_computation.19.clone.1 | convolution fusion | flops 166333824 | bytes 12215424 | tf_op jit(solution)/shard_map/while/body/eval_jaxpr/bhqk,bqhd->bkhd/dot_general | solution.py:85
  228.7 3.4 copy.52
  232.2 3.6 concatenate.71
  235.8 5.0 copy.53
  240.8 4.9 concatenate.72
  245.7 4.7 maximum_multiply_fusion.2
  250.8 7.7 %scatter_fusion = f32[5,128,1024]{2,1,0:T(8,128)S(1)} fusion(f32[5,128,1024]{2,1,0:T(8,128)S(1)} %broadcast.703, s32[9]{0:T(128)S(1)} %fusion.144, f32[9,128,1024]{2,1,0:T(8,128)} %maximum_multiply_fusion.2), kind=kCustom, calls=%fused_computation.1.clone.clone.1 | custom fusion | flops 1179648 | bytes 14155812 | tf_op jit(solution)/shard_map/while/body/eval_jaxpr/scatter-add | solution.py:93
  260.9 4.6 fusion.156
  267.7 2.9 fusion.157
  270.6 22.5 %fusion.152 = bf16[3,8,128,64]{2,3,1,0:T(8,128)(2,1)} fusion(bf16[3,384,8,64]{1,3,2,0:T(8,128)(2,1)} %reshape.605, f32[3,8,128,384]{3,2,1,0:T(8,128)} %fusion.147, f32[3,8,128,384]{3,2,1,0:T(8,128)} %copy-done.23, f32[3,8,128]{2,1,0:T(8,128)S(1)} %copy-done.25, f32[3,8,128]{2,1,0:T(8,128)S(1)} %copy-done.21, pred[3,384]{1,0:T(4,128)(4,1)S(1)} %bitcast.193), kind=kOutput, calls=%fused_computation.24.clone.1 | convolution fusion | flops 166530432 | bytes 11035776 | tf_op jit(solution)/shard_map/while/body/eval_jaxpr/bhqk,bkhd->bqhd/dot_general | solution.py:84
  306.3 10.7 %collective-permute-done.2 = bf16[384,512]{1,0:T(8,128)(2,1)S(1)} collective-permute-done((bf16[384,512]{1,0:T(8,128)(2,1)S(1)}, bf16[384,512]{1,0:T(8,128)(2,1)S(1)}, u32[]{:S(2)}, u32[]{:S(2)}) %collective-permute-start.2) | collective-permute-done | bytes 393248 | tf_op jit(solution)/shard_map/while/body/eval_jaxpr/ppermute | solution.py:34
  324.7 4.1 fusion.145
  328.8 4.1 reshape.605
  334.0 4.4 fusion.147
  344.5 25.4 %fusion.148 = f32[3,384,8,64]{1,3,2,0:T(8,128)} fusion(bf16[3,128,8,64]{1,3,2,0:T(8,128)(2,1)} %bitcast.180, f32[3,8,128,384]{3,2,1,0:T(8,128)} %fusion.147, f32[3,8,128,384]{3,2,1,0:T(8,128)} %copy-done.23, f32[3,8,128]{2,1,0:T(8,128)} %copy-done.24, f32[3,8,128]{2,1,0:T(8,128)} %get-tuple-element.662, pred[3,384]{1,0:T(4,128)(4,1)} %bitcast.189), kind=kOutput, calls=%fused_computation.19.clone.1 | convolution fusion | flops 166333824 | bytes 12215424 | tf_op jit(solution)/shard_map/while/body/eval_jaxpr/bhqk,bqhd->bkhd/dot_general | solution.py:85
  369.8 3.4 copy.52
  373.3 3.6 concatenate.71
  376.9 5.0 copy.53
  381.9 4.9 concatenate.72
  386.8 4.7 maximum_multiply_fusion.2
  391.8 7.7 %scatter_fusion = f32[5,128,1024]{2,1,0:T(8,128)S(1)} fusion(f32[5,128,1024]{2,1,0:T(8,128)S(1)} %broadcast.703, s32[9]{0:T(128)S(1)} %fusion.144, f32[9,128,1024]{2,1,0:T(8,128)} %maximum_multiply_fusion.2), kind=kCustom, calls=%fused_computation.1.clone.clone.1 | custom fusion | flops 1179648 | bytes 14155812 | tf_op jit(solution)/shard_map/while/body/eval_jaxpr/scatter-add | solution.py:93
  401.4 4.6 fusion.156
  408.2 2.9 fusion.157
  411.1 22.5 %fusion.152 = bf16[3,8,128,64]{2,3,1,0:T(8,128)(2,1)} fusion(bf16[3,384,8,64]{1,3,2,0:T(8,128)(2,1)} %reshape.605, f32[3,8,128,384]{3,2,1,0:T(8,128)} %fusion.147, f32[3,8,128,384]{3,2,1,0:T(8,128)} %copy-done.23, f32[3,8,128]{2,1,0:T(8,128)S(1)} %copy-done.25, f32[3,8,128]{2,1,0:T(8,128)S(1)} %copy-done.21, pred[3,384]{1,0:T(4,128)(4,1)S(1)} %bitcast.193), kind=kOutput, calls=%fused_computation.24.clone.1 | convolution fusion | flops 166530432 | bytes 11035776 | tf_op jit(solution)/shard_map/while/body/eval_jaxpr/bhqk,bkhd->bqhd/dot_general | solution.py:84
  446.7 11.1 %collective-permute-done.2 = bf16[384,512]{1,0:T(8,128)(2,1)S(1)} collective-permute-done((bf16[384,512]{1,0:T(8,128)(2,1)S(1)}, bf16[384,512]{1,0:T(8,128)(2,1)S(1)}, u32[]{:S(2)}, u32[]{:S(2)}) %collective-permute-start.2) | collective-permute-done | bytes 393248 | tf_op jit(solution)/shard_map/while/body/eval_jaxpr/ppermute | solution.py:34
  465.6 4.1 fusion.145
  469.7 4.1 reshape.605
  474.9 4.4 fusion.147
  485.3 25.4 %fusion.148 = f32[3,384,8,64]{1,3,2,0:T(8,128)} fusion(bf16[3,128,8,64]{1,3,2,0:T(8,128)(2,1)} %bitcast.180, f32[3,8,128,384]{3,2,1,0:T(8,128)} %fusion.147, f32[3,8,128,384]{3,2,1,0:T(8,128)} %copy-done.23, f32[3,8,128]{2,1,0:T(8,128)} %copy-done.24, f32[3,8,128]{2,1,0:T(8,128)} %get-tuple-element.662, pred[3,384]{1,0:T(4,128)(4,1)} %bitcast.189), kind=kOutput, calls=%fused_computation.19.clone.1 | convolution fusion | flops 166333824 | bytes 12215424 | tf_op jit(solution)/shard_map/while/body/eval_jaxpr/bhqk,bqhd->bkhd/dot_general | solution.py:85
  510.7 3.4 copy.52
  514.1 3.6 concatenate.71
  517.8 5.0 copy.53
  522.7 4.9 concatenate.72
  527.7 4.7 maximum_multiply_fusion.2
  532.7 7.7 %scatter_fusion = f32[5,128,1024]{2,1,0:T(8,128)S(1)} fusion(f32[5,128,1024]{2,1,0:T(8,128)S(1)} %broadcast.703, s32[9]{0:T(128)S(1)} %fusion.144, f32[9,128,1024]{2,1,0:T(8,128)} %maximum_multiply_fusion.2), kind=kCustom, calls=%fused_computation.1.clone.clone.1 | custom fusion | flops 1179648 | bytes 14155812 | tf_op jit(solution)/shard_map/while/body/eval_jaxpr/scatter-add | solution.py:93
  542.7 4.6 fusion.156
  549.4 2.9 fusion.157
  552.3 22.5 %fusion.152 = bf16[3,8,128,64]{2,3,1,0:T(8,128)(2,1)} fusion(bf16[3,384,8,64]{1,3,2,0:T(8,128)(2,1)} %reshape.605, f32[3,8,128,384]{3,2,1,0:T(8,128)} %fusion.147, f32[3,8,128,384]{3,2,1,0:T(8,128)} %copy-done.23, f32[3,8,128]{2,1,0:T(8,128)S(1)} %copy-done.25, f32[3,8,128]{2,1,0:T(8,128)S(1)} %copy-done.21, pred[3,384]{1,0:T(4,128)(4,1)S(1)} %bitcast.193), kind=kOutput, calls=%fused_computation.24.clone.1 | convolution fusion | flops 166530432 | bytes 11035776 | tf_op jit(solution)/shard_map/while/body/eval_jaxpr/bhqk,bkhd->bqhd/dot_general | solution.py:84
  588.0 10.6 %collective-permute-done.2 = bf16[384,512]{1,0:T(8,128)(2,1)S(1)} collective-permute-done((bf16[384,512]{1,0:T(8,128)(2,1)S(1)}, bf16[384,512]{1,0:T(8,128)(2,1)S(1)}, u32[]{:S(2)}, u32[]{:S(2)}) %collective-permute-start.2) | collective-permute-done | bytes 393248 | tf_op jit(solution)/shard_map/while/body/eval_jaxpr/ppermute | solution.py:34
  598.6 4.6 pad_maximum_fusion.3
  603.2 50.3 %reduce-scatter.2.cloned.1.call-done = f32[64,2048]{1,0:T(8,128)} async-done(((f32[512,2048]{1,0:T(8,128)}), f32[64,2048]{1,0:T(8,128)}) %reduce-scatter.2.cloned.1.call-update) | async-done | bytes 524304 | tf_op jit(solution)/shard_map/reduce_scatter | solution.py:165
  (377 shorter events, 143.9 us)
Async XLA Ops:
  7.2 646.3 %reduce-scatter.2.cloned.1.call-start = ((), (), s32[]{:S(2)}) async-start(), calls=%async_computation.1 | async-start | bytes 4718592 | tf_op jit(solution)/shard_map/reduce_scatter | solution.py:165
  9.6 7.2 %copy-start.15 = (s32[3,3]{1,0:T(4,128)S(1)}, s32[3,3]{1,0:T(4,128)}, u32[]{:S(2)}) copy-start(s32[3,3]{1,0:T(4,128)} %param.15) | copy-start | bytes 112
  12.1 8.8 %collective-permute-start.3 = (bf16[1,128,1024]{2,1,0:T(8,128)(2,1)S(1)}, bf16[1,128,1024]{2,1,0:T(8,128)(2,1)S(1)}, u32[]{:S(2)}, u32[]{:S(2)}) collective-permute-start(bf16[1,128,1024]{2,1,0:T(8,128)(2,1)S(1)} %get-tuple-element.490), channel_id=1, source_target_pairs={{0,1},{1,2},{2,3},{3,4},{4,5},{5,6},{6,7},{7,0},{8,9},{9,10},{10,1... | collective-permute-start | bytes 786440 | tf_op jit(solution)/shard_map/while/body/eval_jaxpr/ppermute | solution.py:17
  12.6 8.7 %collective-permute-start.4 = (bf16[1,128,1024]{2,1,0:T(8,128)(2,1)S(1)}, bf16[1,128,1024]{2,1,0:T(8,128)(2,1)S(1)}, u32[]{:S(2)}, u32[]{:S(2)}) collective-permute-start(bf16[1,128,1024]{2,1,0:T(8,128)(2,1)S(1)} %get-tuple-element.491), channel_id=1, source_target_pairs={{1,0},{2,1},{3,2},{4,3},{5,4},{6,5},{7,6},{0,7},{9,8},{10,9},{11,1... | collective-permute-start | bytes 786440 | tf_op jit(solution)/shard_map/while/body/eval_jaxpr/ppermute | solution.py:20
  50.4 4.5 copy-start
  50.4 4.5 copy-start.7
  50.4 4.4 copy-start.10
  50.4 4.4 copy-start.16
  50.4 4.4 copy-start.20
  98.3 4.9 copy-start.18
  98.3 4.9 copy-start.22
  116.0 4.9 copy-start.1
  116.0 4.9 copy-start.17
  116.0 4.9 copy-start.21
  116.0 4.9 copy-start.25
  117.0 38.9 %collective-permute-start = (bf16[1,128,1024]{2,1,0:T(8,128)(2,1)}, bf16[1,128,1024]{2,1,0:T(8,128)(2,1)}, u32[]{:S(2)}, u32[]{:S(2)}) collective-permute-start(bf16[1,128,1024]{2,1,0:T(8,128)(2,1)} %get-tuple-element.605), channel_id=1, source_target_pairs={{1,0},{2,1},{3,2},{4,3},{5,4},{6,5},{7,6},{0,7},{9,8},{10,9},{11,1... | collective-permute-start | bytes 786440 | tf_op jit(solution)/shard_map/while/body/eval_jaxpr/ppermute | solution.py:28
  120.8 37.0 %collective-permute-start.1 = (bf16[1,128,1024]{2,1,0:T(8,128)(2,1)}, bf16[1,128,1024]{2,1,0:T(8,128)(2,1)}, u32[]{:S(2)}, u32[]{:S(2)}) collective-permute-start(bf16[1,128,1024]{2,1,0:T(8,128)(2,1)} %get-tuple-element.606), channel_id=1, source_target_pairs={{7,0},{0,1},{1,2},{2,3},{3,4},{4,5},{5,6},{6,7},{15,8},{8,9},{9,10... | collective-permute-start | bytes 786440 | tf_op jit(solution)/shard_map/while/body/eval_jaxpr/ppermute | solution.py:28
  155.9 5.5 copy-start.6
  155.9 5.5 copy-start.19
  162.7 13.2 %collective-permute-start.2 = (bf16[384,512]{1,0:T(8,128)(2,1)S(1)}, bf16[384,512]{1,0:T(8,128)(2,1)S(1)}, u32[]{:S(2)}, u32[]{:S(2)}) collective-permute-start(bf16[384,512]{1,0:T(8,128)(2,1)S(1)} %bitcast.174), channel_id=1, source_target_pairs={{8,0},{16,8},{24,16},{9,1},{17,9},{25,17},{10,2},{18,10},{26,18},{... | collective-permute-start | bytes 1179656 | tf_op jit(solution)/shard_map/while/body/eval_jaxpr/ppermute | solution.py:34
  164.3 11.6 %copy-start.9 = (bf16[1,512,512]{2,1,0:T(8,128)(2,1)S(1)}, bf16[1,512,512]{2,1,0:T(8,128)(2,1)}, u32[]{:S(2)}) copy-start(bf16[1,512,512]{2,1,0:T(8,128)(2,1)} %get-tuple-element.694) | copy-start | bytes 1572868 | tf_op jit(solution)/shard_map/while
  164.3 11.6 %copy-start.12 = (bf16[1,384,512]{2,1,0:T(8,128)(2,1)S(1)}, bf16[1,384,512]{2,1,0:T(8,128)(2,1)}, u32[]{:S(2)}) copy-start(bf16[1,384,512]{2,1,0:T(8,128)(2,1)} %get-tuple-element.715) | copy-start | bytes 1179652 | tf_op jit(solution)/shard_map/while
  165.9 10.0 %copy-start.3 = (f32[512,1536]{1,0:T(8,128)}, f32[512,1536]{1,0:T(8,128)S(1)}, u32[]{:S(2)}) copy-start(f32[512,1536]{1,0:T(8,128)S(1)} %fusion.155) | copy-start | bytes 9437188 | tf_op jit(solution)/shard_map/while
  192.9 4.5 copy-start
  192.9 4.5 copy-start.7
  192.9 4.4 copy-start.10
  192.9 4.4 copy-start.16
  192.9 4.4 copy-start.20
  240.8 4.9 copy-start.18
  240.8 4.9 copy-start.22
  259.6 36.8 %collective-permute-start = (bf16[1,128,1024]{2,1,0:T(8,128)(2,1)}, bf16[1,128,1024]{2,1,0:T(8,128)(2,1)}, u32[]{:S(2)}, u32[]{:S(2)}) collective-permute-start(bf16[1,128,1024]{2,1,0:T(8,128)(2,1)} %get-tuple-element.605), channel_id=1, source_target_pairs={{1,0},{2,1},{3,2},{4,3},{5,4},{6,5},{7,6},{0,7},{9,8},{10,9},{11,1... | collective-permute-start | bytes 786440 | tf_op jit(solution)/shard_map/while/body/eval_jaxpr/ppermute | solution.py:28
  260.9 37.4 %collective-permute-start.1 = (bf16[1,128,1024]{2,1,0:T(8,128)(2,1)}, bf16[1,128,1024]{2,1,0:T(8,128)(2,1)}, u32[]{:S(2)}, u32[]{:S(2)}) collective-permute-start(bf16[1,128,1024]{2,1,0:T(8,128)(2,1)} %get-tuple-element.606), channel_id=1, source_target_pairs={{7,0},{0,1},{1,2},{2,3},{3,4},{4,5},{5,6},{6,7},{15,8},{8,9},{9,10... | collective-permute-start | bytes 786440 | tf_op jit(solution)/shard_map/while/body/eval_jaxpr/ppermute | solution.py:28
  296.3 5.5 copy-start.6
  296.3 5.5 copy-start.19
  303.1 13.9 %collective-permute-start.2 = (bf16[384,512]{1,0:T(8,128)(2,1)S(1)}, bf16[384,512]{1,0:T(8,128)(2,1)S(1)}, u32[]{:S(2)}, u32[]{:S(2)}) collective-permute-start(bf16[384,512]{1,0:T(8,128)(2,1)S(1)} %bitcast.174), channel_id=1, source_target_pairs={{8,0},{16,8},{24,16},{9,1},{17,9},{25,17},{10,2},{18,10},{26,18},{... | collective-permute-start | bytes 1179656 | tf_op jit(solution)/shard_map/while/body/eval_jaxpr/ppermute | solution.py:34
  304.7 12.3 %copy-start.9 = (bf16[1,512,512]{2,1,0:T(8,128)(2,1)S(1)}, bf16[1,512,512]{2,1,0:T(8,128)(2,1)}, u32[]{:S(2)}) copy-start(bf16[1,512,512]{2,1,0:T(8,128)(2,1)} %get-tuple-element.694) | copy-start | bytes 1572868 | tf_op jit(solution)/shard_map/while
  304.7 12.3 %copy-start.12 = (bf16[1,384,512]{2,1,0:T(8,128)(2,1)S(1)}, bf16[1,384,512]{2,1,0:T(8,128)(2,1)}, u32[]{:S(2)}) copy-start(bf16[1,384,512]{2,1,0:T(8,128)(2,1)} %get-tuple-element.715) | copy-start | bytes 1179652 | tf_op jit(solution)/shard_map/while
  306.3 10.7 %copy-start.3 = (f32[512,1536]{1,0:T(8,128)}, f32[512,1536]{1,0:T(8,128)S(1)}, u32[]{:S(2)}) copy-start(f32[512,1536]{1,0:T(8,128)S(1)} %fusion.155) | copy-start | bytes 9437188 | tf_op jit(solution)/shard_map/while
  334.0 4.5 copy-start
  334.0 4.5 copy-start.7
  334.0 4.4 copy-start.10
  381.9 4.9 copy-start.18
  381.9 4.9 copy-start.22
  400.6 36.1 %collective-permute-start = (bf16[1,128,1024]{2,1,0:T(8,128)(2,1)}, bf16[1,128,1024]{2,1,0:T(8,128)(2,1)}, u32[]{:S(2)}, u32[]{:S(2)}) collective-permute-start(bf16[1,128,1024]{2,1,0:T(8,128)(2,1)} %get-tuple-element.605), channel_id=1, source_target_pairs={{1,0},{2,1},{3,2},{4,3},{5,4},{6,5},{7,6},{0,7},{9,8},{10,9},{11,1... | collective-permute-start | bytes 786440 | tf_op jit(solution)/shard_map/while/body/eval_jaxpr/ppermute | solution.py:28
  401.4 37.4 %collective-permute-start.1 = (bf16[1,128,1024]{2,1,0:T(8,128)(2,1)}, bf16[1,128,1024]{2,1,0:T(8,128)(2,1)}, u32[]{:S(2)}, u32[]{:S(2)}) collective-permute-start(bf16[1,128,1024]{2,1,0:T(8,128)(2,1)} %get-tuple-element.606), channel_id=1, source_target_pairs={{7,0},{0,1},{1,2},{2,3},{3,4},{4,5},{5,6},{6,7},{15,8},{8,9},{9,10... | collective-permute-start | bytes 786440 | tf_op jit(solution)/shard_map/while/body/eval_jaxpr/ppermute | solution.py:28
  436.8 5.5 copy-start.6
  436.8 5.5 copy-start.19
  443.5 14.3 %collective-permute-start.2 = (bf16[384,512]{1,0:T(8,128)(2,1)S(1)}, bf16[384,512]{1,0:T(8,128)(2,1)S(1)}, u32[]{:S(2)}, u32[]{:S(2)}) collective-permute-start(bf16[384,512]{1,0:T(8,128)(2,1)S(1)} %bitcast.174), channel_id=1, source_target_pairs={{8,0},{16,8},{24,16},{9,1},{17,9},{25,17},{10,2},{18,10},{26,18},{... | collective-permute-start | bytes 1179656 | tf_op jit(solution)/shard_map/while/body/eval_jaxpr/ppermute | solution.py:34
  445.2 12.7 %copy-start.9 = (bf16[1,512,512]{2,1,0:T(8,128)(2,1)S(1)}, bf16[1,512,512]{2,1,0:T(8,128)(2,1)}, u32[]{:S(2)}) copy-start(bf16[1,512,512]{2,1,0:T(8,128)(2,1)} %get-tuple-element.694) | copy-start | bytes 1572868 | tf_op jit(solution)/shard_map/while
  445.2 12.7 %copy-start.12 = (bf16[1,384,512]{2,1,0:T(8,128)(2,1)S(1)}, bf16[1,384,512]{2,1,0:T(8,128)(2,1)}, u32[]{:S(2)}) copy-start(bf16[1,384,512]{2,1,0:T(8,128)(2,1)} %get-tuple-element.715) | copy-start | bytes 1179652 | tf_op jit(solution)/shard_map/while
  446.7 11.1 %copy-start.3 = (f32[512,1536]{1,0:T(8,128)}, f32[512,1536]{1,0:T(8,128)S(1)}, u32[]{:S(2)}) copy-start(f32[512,1536]{1,0:T(8,128)S(1)} %fusion.155) | copy-start | bytes 9437188 | tf_op jit(solution)/shard_map/while
  474.9 4.5 copy-start
  474.9 4.5 copy-start.7
  474.9 4.4 copy-start.10
  522.7 4.9 copy-start.18
  522.7 4.9 copy-start.22
  541.5 36.5 %collective-permute-start = (bf16[1,128,1024]{2,1,0:T(8,128)(2,1)}, bf16[1,128,1024]{2,1,0:T(8,128)(2,1)}, u32[]{:S(2)}, u32[]{:S(2)}) collective-permute-start(bf16[1,128,1024]{2,1,0:T(8,128)(2,1)} %get-tuple-element.605), channel_id=1, source_target_pairs={{1,0},{2,1},{3,2},{4,3},{5,4},{6,5},{7,6},{0,7},{9,8},{10,9},{11,1... | collective-permute-start | bytes 786440 | tf_op jit(solution)/shard_map/while/body/eval_jaxpr/ppermute | solution.py:28
  542.6 37.4 %collective-permute-start.1 = (bf16[1,128,1024]{2,1,0:T(8,128)(2,1)}, bf16[1,128,1024]{2,1,0:T(8,128)(2,1)}, u32[]{:S(2)}, u32[]{:S(2)}) collective-permute-start(bf16[1,128,1024]{2,1,0:T(8,128)(2,1)} %get-tuple-element.606), channel_id=1, source_target_pairs={{7,0},{0,1},{1,2},{2,3},{3,4},{4,5},{5,6},{6,7},{15,8},{8,9},{9,10... | collective-permute-start | bytes 786440 | tf_op jit(solution)/shard_map/while/body/eval_jaxpr/ppermute | solution.py:28
  578.0 5.5 copy-start.6
  578.0 5.5 copy-start.19
  584.8 13.8 %collective-permute-start.2 = (bf16[384,512]{1,0:T(8,128)(2,1)S(1)}, bf16[384,512]{1,0:T(8,128)(2,1)S(1)}, u32[]{:S(2)}, u32[]{:S(2)}) collective-permute-start(bf16[384,512]{1,0:T(8,128)(2,1)S(1)} %bitcast.174), channel_id=1, source_target_pairs={{8,0},{16,8},{24,16},{9,1},{17,9},{25,17},{10,2},{18,10},{26,18},{... | collective-permute-start | bytes 1179656 | tf_op jit(solution)/shard_map/while/body/eval_jaxpr/ppermute | solution.py:34
  586.4 12.2 %copy-start.9 = (bf16[1,512,512]{2,1,0:T(8,128)(2,1)S(1)}, bf16[1,512,512]{2,1,0:T(8,128)(2,1)}, u32[]{:S(2)}) copy-start(bf16[1,512,512]{2,1,0:T(8,128)(2,1)} %get-tuple-element.694) | copy-start | bytes 1572868 | tf_op jit(solution)/shard_map/while
  586.4 12.1 %copy-start.12 = (bf16[1,384,512]{2,1,0:T(8,128)(2,1)S(1)}, bf16[1,384,512]{2,1,0:T(8,128)(2,1)}, u32[]{:S(2)}) copy-start(bf16[1,384,512]{2,1,0:T(8,128)(2,1)} %get-tuple-element.715) | copy-start | bytes 1179652 | tf_op jit(solution)/shard_map/while
  588.0 10.6 %copy-start.3 = (f32[512,1536]{1,0:T(8,128)}, f32[512,1536]{1,0:T(8,128)S(1)}, u32[]{:S(2)}) copy-start(f32[512,1536]{1,0:T(8,128)S(1)} %fusion.155) | copy-start | bytes 9437188 | tf_op jit(solution)/shard_map/while
  (43 other events, 110.3 us)
Sparse Core Ops, SparseCore 0:
  603.3 50.0 reduce-scatter.1
where the time goes:
time: 667 us; the launch traced here: 664 us
  matrix products  279 us (42%)
  local copies, waits for them, and re-layouts  170 us (25%)
  waiting for transfers between devices  96 us (14%)
  other arithmetic  84.4 us (13%)
  starting transfers between devices  17.3 us (3%)
  between operations  14.2 us (2%)
    dot_general x4, matrix products, layer_back(): jnp.einsum('bhqk,bqhd->bkhd', d_score, query, preferred_element_type=jnp....  102 us
    dot_general x4, matrix products, layer_back(): jnp.einsum('bhqk,bkhd->bqhd', d_score, keys, preferred_element_type=jnp.f...  90.1 us
    reduce_scatter x1, waiting for transfers between devices, local(): lax.psum_scatter(jnp.concatenate([first_part, second_part], axis=-1), 'do...  50.3 us
    ppermute x4, waiting for transfers between devices, shifted_2(): return lax.ppermute(block, axis, route)  42.4 us
    concatenate x8, local copies, waits for them, and re-layouts, layer_back(): jnp.concatenate([d_keys.reshape(blk, KMAX, tile, width), d_values.reshape...  34.1 us
    scatter-add x4, other arithmetic, layer_back(): d_extended.at[where_at.reshape(-1)]  30.9 us
    transpose x4, local copies, waits for them, and re-layouts, layer_back(): jnp.einsum('bhqk,bqhd->bkhd', d_score, query, preferred_element_type=jnp....  20 us
    mul x4, other arithmetic, layer_back(): weighted = d_tiles * valid[:, :, None, None].astype(jnp.float32)  18.8 us
  transfers between devices with their start and end apart: 15, of which 7 were waited for; matrix products, arithmetic and copies ran while one was open for 24% of the time, Pallas kernels for 0%

commit v1 on v0

v1 whole, which is shorter than its diff:
```python
import functools

import jax
import jax.numpy as jnp
from jax import lax
from jax.experimental import pallas as pl
from jax.experimental.pallas import tpu as pltpu
from jax.sharding import PartitionSpec as P

HEADS = 8
EPS = 1e-05
F32 = jnp.float32
BF16 = jnp.bfloat16
NN = (((1,), (0,)), ((), ()))
NT = (((1,), (1,)), ((), ()))
VMEM_LIMIT = 40 * 1024 * 1024


def mm(a, b, dims=NN):
    return lax.dot_general(a, b, dims, preferred_element_type=F32)


def prelude_kernel(
    blk, tile, flags, x_lo, x, x_hi, top, w_qkv,
    xn_t, inv, v_nat, k_t, q_t, probs, attn_t, g_t, k_nat, v_t,
):
    width = x.shape[1]
    hdim = width // HEADS
    scale = 1.0 / hdim**0.5
    for t in range(blk + 2):
        if t == 0:
            rows = x_lo[...]
        elif t == blk + 1:
            rows = x_hi[...]
        else:
            rows = x[(t - 1) * tile : t * tile, :]
        here = slice(t * tile, (t + 1) * tile)
        xf = rows.astype(F32)
        cent = xf - jnp.mean(xf, axis=-1, keepdims=True)
        rstd = lax.rsqrt(jnp.mean(cent * cent, axis=-1, keepdims=True) + EPS)
        xhat = cent * rstd
        xn = xhat.astype(BF16)
        xn_t[:, here] = xhat.T.astype(BF16)
        inv[:, here] = jnp.broadcast_to(rstd, (tile, 128)).T[0:8, :]
        keyval = mm(xn, w_qkv[:, width:])
        k_t[:, here] = (keyval[:, :width].T * scale).astype(BF16)
        v_t[:, here] = keyval[:, width:].T.astype(BF16)
        keyval = keyval.astype(BF16)
        for h in range(HEADS):
            k_nat[h, here, :] = keyval[:, h * hdim : (h + 1) * hdim]
            v_nat[h, here, :] = keyval[:, width + h * hdim : width + (h + 1) * hdim]
        if 0 < t <= blk:
            own = slice((t - 1) * tile, t * tile)
            query = mm(xn, w_qkv[:, :width])
            q_t[:, own] = (query.T * scale).astype(BF16)
            g_t[:, own] = jnp.where(
                flags[2 * blk] > 0, top[own, :].astype(F32).T, 0.0
            ).astype(BF16)
    for b in range(blk):
        own = slice(b * tile, (b + 1) * tile)
        near = slice(b * tile, (b + 3) * tile)
        for h in range(HEADS):
            head = slice(h * hdim, (h + 1) * hdim)
            s = mm(k_nat[h, near, :], q_t[head, own])
            s = jnp.concatenate(
                [
                    jnp.where(flags[b] > 0, s[:tile], -1e30),
                    s[tile : 2 * tile],
                    jnp.where(flags[blk + b] > 0, s[2 * tile :], -1e30),
                ],
                axis=0,
            )
            e = jnp.exp(s - jnp.max(s, axis=0, keepdims=True))
            p = (e * (1.0 / jnp.sum(e, axis=0, keepdims=True))).astype(BF16)
            probs[h, b] = p
            attn_t[head, own] = mm(v_t[head, near], p).astype(BF16)


def prelude(flags, x_lo, x, x_hi, top, w_qkv, blk):
    rows, width = x.shape
    tile = rows // blk
    hdim = width // HEADS
    ext = rows + 2 * tile
    vmem = pl.BlockSpec(memory_space=pltpu.VMEM)
    return pl.pallas_call(
        functools.partial(prelude_kernel, blk, tile),
        in_specs=[pl.BlockSpec(memory_space=pltpu.SMEM)] + [vmem] * 5,
        out_specs=[vmem] * 8,
        out_shape=[
            jax.ShapeDtypeStruct((width, ext), BF16),
            jax.ShapeDtypeStruct((8, ext), F32),
            jax.ShapeDtypeStruct((HEADS, ext, hdim), BF16),
            jax.ShapeDtypeStruct((width, ext), BF16),
            jax.ShapeDtypeStruct((width, rows), BF16),
            jax.ShapeDtypeStruct((HEADS, blk, 3 * tile, tile), BF16),
            jax.ShapeDtypeStruct((width, rows), BF16),
            jax.ShapeDtypeStruct((width, rows), BF16),
        ],
        scratch_shapes=[
            pltpu.VMEM((HEADS, ext, hdim), BF16),
            pltpu.VMEM((width, ext), BF16),
        ],
        compiler_params=pltpu.CompilerParams(vmem_limit_bytes=VMEM_LIMIT),
        name="prelude",
    )(flags, x_lo, x, x_hi, top, w_qkv)


def stage_kernel(
    blk, tile, g_prev, arrived, w_qkv, w_out, xn_t, inv, v_nat, k_t, q_t, probs, attn_t,
    g_t, y, c, d_qkv, da_t, d_own,
):
    width = g_prev.shape[0]
    rows = blk * tile
    hdim = width // HEADS
    g = (g_prev[...].astype(F32) + arrived[...].astype(F32)).astype(BF16)
    g_t[...] = g
    da_t[...] = mm(w_out[...], g).astype(BF16)
    for h in range(HEADS):
        head = slice(h * hdim, (h + 1) * hdim)
        dk = [None] * (blk + 2)
        dv = [None] * (blk + 2)
        for b in range(blk):
            own = slice(b * tile, (b + 1) * tile)
            near = slice(b * tile, (b + 3) * tile)
            da = da_t[head, own]
            total = jnp.sum(da.astype(F32) * attn_t[head, own].astype(F32), axis=0, keepdims=True)
            p = probs[h, b]
            dp = mm(v_nat[h, near, :], da)
            ds = (p.astype(F32) * (dp - total)).astype(BF16)
            d_own[head, own] = mm(k_t[head, near], ds).astype(BF16)
            key_part = mm(q_t[head, own], ds, NT)
            value_part = mm(da, p, NT)
            for j in range(3):
                cols = slice(j * tile, (j + 1) * tile)
                t = b + j
                dk[t] = key_part[:, cols] if dk[t] is None else dk[t] + key_part[:, cols]
                dv[t] = value_part[:, cols] if dv[t] is None else dv[t] + value_part[:, cols]
        for t in range(blk + 2):
            here = slice(t * tile, (t + 1) * tile)
            d_qkv[width + h * hdim : width + (h + 1) * hdim, here] = dk[t].astype(BF16)
            d_qkv[2 * width + h * hdim : 2 * width + (h + 1) * hdim, here] = dv[t].astype(BF16)
    for t in (0, blk + 1):
        here = slice(t * tile, (t + 1) * tile)
        d_qkv[:width, here] = jnp.zeros((width, tile), BF16)
    d_qkv[:width, tile : tile + rows] = d_own[...]
    for t in range(blk + 2):
        here = slice(t * tile, (t + 1) * tile)
        dn = mm(w_qkv[...], d_qkv[:, here])
        xhat = xn_t[:, here].astype(F32)
        first = jnp.mean(dn, axis=0, keepdims=True)
        second = jnp.mean(dn * xhat, axis=0, keepdims=True)
        out = inv[0:1, here] * (dn - first - xhat * second)
        if t == 0:
            c[0] = out.astype(BF16)
        elif t == blk + 1:
            c[1] = out.astype(BF16)
        else:
            own = slice((t - 1) * tile, t * tile)
            y[:, own] = (g[:, own].astype(F32) + out).astype(BF16)


def stage(g_prev, arrived, w_qkv, w_out, saved, blk):
    xn_t, inv, v_nat, k_t, q_t, probs, attn_t = saved
    width, rows = g_prev.shape
    tile = rows // blk
    ext = rows + 2 * tile
    vmem = pl.BlockSpec(memory_space=pltpu.VMEM)
    return pl.pallas_call(
        functools.partial(stage_kernel, blk, tile),
        in_specs=[vmem] * 11,
        out_specs=[vmem] * 4,
        out_shape=[
            jax.ShapeDtypeStruct((width, rows), BF16),
            jax.ShapeDtypeStruct((width, rows), BF16),
            jax.ShapeDtypeStruct((2, width, tile), BF16),
            jax.ShapeDtypeStruct((3 * width, ext), BF16),
        ],
        scratch_shapes=[pltpu.VMEM((width, rows), BF16), pltpu.VMEM((width, rows), BF16)],
        compiler_params=pltpu.CompilerParams(vmem_limit_bytes=VMEM_LIMIT),
        name="stage",
    )(g_prev, arrived, w_qkv, w_out, xn_t, inv, v_nat, k_t, q_t, probs, attn_t)


def weights_kernel(xn_t, d_qkv, attn_t, g_t, out):
    wide = d_qkv.shape[0]
    out[:, :wide] = mm(xn_t[...], d_qkv[...], NT).astype(BF16)
    out[:, wide:] = mm(attn_t[...], g_t[...], NT).astype(BF16)


def weights(xn_t, d_qkv, attn_t, g_t):
    width = g_t.shape[0]
    wide = d_qkv.shape[0]
    vmem = pl.BlockSpec(memory_space=pltpu.VMEM)
    return pl.pallas_call(
        weights_kernel,
        in_specs=[vmem] * 4,
        out_specs=vmem,
        out_shape=jax.ShapeDtypeStruct((width, wide + width), BF16),
        compiler_params=pltpu.CompilerParams(vmem_limit_bytes=VMEM_LIMIT),
        name="weights",
    )(xn_t, d_qkv, attn_t, g_t)


def ring(parts, distance):
    return [(i, (i + distance) % parts) for i in range(parts)]


def sum_scatter(term):
    parts = lax.axis_size("dom")
    if parts != 8:
        return lax.psum_scatter(term.astype(F32), "dom", scatter_dimension=0, tiled=True)
    me = lax.axis_index("dom")
    core, chip = me % 2, me // 2
    split = term.reshape(parts // 2, 2, term.shape[0] // parts, term.shape[1])
    keep = lax.dynamic_index_in_dim(split, core, 1, keepdims=False)
    give = lax.dynamic_index_in_dim(split, 1 - core, 1, keepdims=False)
    got = lax.ppermute(give, "dom", [(i, i ^ 1) for i in range(parts)])
    both = keep.astype(F32) + got.astype(F32)
    rounded = both.astype(BF16)
    total = lax.dynamic_index_in_dim(both, chip, 0, keepdims=False)
    pieces = []
    for k in range(1, parts // 2):
        give = lax.dynamic_index_in_dim(rounded, chip ^ k, 0, keepdims=False)
        pieces.append(lax.ppermute(give, "dom", [(i, i ^ (2 * k)) for i in range(parts)]))
    for piece in pieces:
        total = total + piece.astype(F32)
    return total


def local(layer_inputs, top_grad, w_qkv, w_out, neighbours):
    sections = lax.axis_size("section")
    section_me = lax.axis_index("section")
    parts = lax.axis_size("dom")
    me = lax.axis_index("dom")
    blk = neighbours.shape[0]
    rows, width = top_grad.shape[1:]
    tile = rows // blk
    x = layer_inputs[0, 0]
    w_in, w_back = w_qkv[0], w_out[0]
    x_lo = lax.ppermute(x[rows - tile :], "dom", ring(parts, 1))
    x_hi = lax.ppermute(x[:tile], "dom", ring(parts, -1))
    blocks = blk * parts
    mine = (me * blk + jnp.arange(blk))[:, None]
    others = neighbours[:, 1:]
    has_lo = jnp.any(others == (mine - 1) % blocks, axis=1)
    has_hi = jnp.any(others == (mine + 1) % blocks, axis=1)
    is_last = (section_me == sections - 1)[None]
    flags = jnp.concatenate([has_lo, has_hi, is_last]).astype(jnp.int32)
    *saved, g = prelude(flags, x_lo, x, x_hi, top_grad[0], w_in, blk)
    arrived = jnp.zeros_like(g)
    for k in range(sections):
        g, y, c, d_qkv = stage(g, arrived, w_in, w_back, saved, blk)
        if k == sections - 1:
            term = weights(saved[0], d_qkv, saved[6], g)
            summed = sum_scatter(term)
        from_prev = lax.ppermute(c[1], "dom", ring(parts, 1))
        from_next = lax.ppermute(c[0], "dom", ring(parts, -1))
        rims = jnp.concatenate(
            [from_prev, jnp.zeros((width, rows - 2 * tile), BF16), from_next], axis=1
        )
        y = (y.astype(F32) + rims.astype(F32)).astype(BF16)
        if k < sections - 1:
            arrived = lax.ppermute(y, "section", [(sections - 1 - k, sections - 2 - k)])
    return (y.T[None, None], summed[None, :, : 3 * width], summed[None, :, 3 * width :])


def solution(mesh):
    placed = (
        P("section", None, "dom", None),
        P(None, "dom", None),
        P("section", None, None),
        P("section", None, None),
        P("dom", None),
    )
    return jax.shard_map(
        local,
        mesh=mesh,
        in_specs=placed,
        out_specs=(
            P("section", None, "dom", None),
            P("section", "dom", None),
            P("section", "dom", None),
        ),
        check_vma=False,
    )
```

time: 667 us -> 163 us (0.24)
  matrix products: 279 us -> 0 us
  local copies, waits for them, and re-layouts: 170 us -> 19.1 us
  other arithmetic: 84.4 us -> 7.32 us
  Pallas kernels: 0 us -> 51 us
  waiting for transfers between devices: 96 us -> 57 us
  between operations: 14.2 us -> 1.06 us
  starting transfers between devices: 17.3 us -> 26.3 us
    dot_general x46 -> x0, matrix products: 279 us -> none  [the longest x4 102 us: layer_back(): jnp.einsum('bhqk,bqhd->bkhd', d_score, query, preferred_element_type=jnp....]
    pallas_call x0 -> x6, Pallas kernels: none -> 51 us  [the longest x4 40.1 us: stage(): pl.pallas_call(functools.partial(stage_kernel, blk, tile), in_specs=[vmem...]
    reduce_scatter x1 -> x0, waiting for transfers between devices: 50.3 us -> none  [local(): lax.psum_scatter(jnp.concatenate([first_part, second_part], axis=-1), 'do...]
    scatter-add x12 -> x0, other arithmetic: 46.6 us -> none  [the longest x4 30.9 us: layer_back(): d_extended.at[where_at.reshape(-1)]]
    concatenate x12 -> x1, local copies, waits for them, and re-layouts: 41.8 us -> 0.01 us  [local(): jnp.concatenate([from_prev, jnp.zeros((width, rows - 2 * tile), BF16), fr...]
    transpose x8 -> x0, local copies, waits for them, and re-layouts: 33.7 us -> none  [the longest x4 20 us: layer_back(): jnp.einsum('bhqk,bqhd->bkhd', d_score, query, preferred_element_type=jnp....]
    slice x26 -> x1, local copies, waits for them, and re-layouts: 30.8 us -> 0.99 us  [local(): x_hi = lax.ppermute(x[:tile], 'dom', ring(parts, -1))]
    reshape x17 -> x0, local copies, waits for them, and re-layouts: 28.1 us -> none  [the longest x5 17.6 us: layer_back(): keys = tiles[..., :width].reshape(blk, KMAX * tile, HEADS, hdim)]
  transfers between devices with their start and end apart: 15 -> 17, of which waited for: 7 -> 7; matrix products, arithmetic and copies ran while one was open for 24% -> 4% of each run, Pallas kernels for 0% -> 0%
where the time goes in v1:
time: 163 us; the launch traced here: 162 us
  waiting for transfers between devices  57 us (35%)
  Pallas kernels  51 us (31%)
  starting transfers between devices  26.3 us (16%)
  local copies, waits for them, and re-layouts  19.1 us (12%)
  other arithmetic  7.32 us (4%)
    pallas_call x4, Pallas kernels, stage(): pl.pallas_call(functools.partial(stage_kernel, blk, tile), in_specs=[vmem...  40.1 us
    ppermute x3, waiting for transfers between devices, local(): arrived = lax.ppermute(y, 'section', [(sections - 1 - k, sections - 2 - k)])  29.7 us
    unnamed x53, local copies, waits for them, and re-layouts  15.7 us
    ppermute x3, waiting for transfers between devices, sum_scatter(): lax.ppermute(give, 'dom', [(i, i ^ 2 * k) for i in range(parts)])  14.9 us
    ppermute x4, starting transfers between devices, local(): from_next = lax.ppermute(c[0], 'dom', ring(parts, -1))  13.7 us
    ppermute x4, waiting for transfers between devices, local(): from_prev = lax.ppermute(c[1], 'dom', ring(parts, 1))  10.8 us
    pallas_call x1, Pallas kernels, prelude(): pl.pallas_call(functools.partial(prelude_kernel, blk, tile), in_specs=[pl...  9.16 us
    ppermute x3, starting transfers between devices, sum_scatter(): lax.ppermute(give, 'dom', [(i, i ^ 2 * k) for i in range(parts)])  4.44 us
  transfers between devices with their start and end apart: 17, of which 7 were waited for; matrix products, arithmetic and copies ran while one was open for 4% of the time, Pallas kernels for 0%

profile of v1, /device:TPU:0, one launch (start us, length us, event | category | flops | bytes accessed | tf_op | source)
XLA Modules:
  0.0 161.8 jit_solution(12756543525038004418)
XLA Ops:
  0.6 1.0 slice_bitcast_fusion.10
  1.6 0.5 collective-permute-start
  2.1 4.1 %collective-permute-start.1 = (bf16[128,512]{1,0:T(8,128)(2,1)S(1)}, bf16[128,512]{1,0:T(8,128)(2,1)S(1)}, u32[]{:S(2)}, u32[]{:S(2)}) collective-permute-start(bf16[128,512]{1,0:T(8,128)(2,1)S(1)} %get-tuple-element.55), channel_id=1, source_target_pairs={{0,7},{1,0},{2,1},{3,2},{4,3},{5,4},{6,5},{7,6},{8,15},{9,8},{10,9... | collective-permute-start | bytes 393224 | tf_op jit(solution)/shard_map/ppermute | solution.py:241
  6.2 0.9 compare_reduce_fusion.1
  7.1 0.1 add_convert_fusion.4.flags
  7.2 1.7 %collective-permute-done.x_lo = bf16[128,512]{1,0:T(8,128)(2,1)S(1)} collective-permute-done((bf16[128,512]{1,0:T(8,128)(2,1)S(1)}, bf16[128,512]{1,0:T(8,128)(2,1)S(1)}, u32[]{:S(2)}, u32[]{:S(2)}) %collective-permute-start) | collective-permute-done | bytes 131104 | tf_op jit(solution)/shard_map/ppermute | solution.py:240
  8.9 0.7 copy-done.22
  9.6 0.7 copy-done.24
  10.2 1.4 copy-done
  11.6 1.0 copy-done.12
  12.6 1.0 copy-done.15
  13.6 0.9 copy-done.23
  14.5 0.9 copy-done.25
  15.4 9.2 %prelude.1 = (bf16[512,640]{1,0:T(8,128)(2,1)S(1)}, f32[8,640]{1,0:T(8,128)S(1)}, bf16[8,640,64]{2,1,0:T(8,128)(2,1)S(1)}, bf16[512,640]{1,0:T(8,128)(2,1)S(1)},...) custom-call(s32[7]{0:T(128)S(1)} %add_convert_fusion.4.flags, ...), custom_call_target="tpu_custom_call" | custom-call | tf_op jit(solution)/shard_map/prelude/pallas_call | solution.py:85
  24.6 0.0 copy-start.18
  24.7 9.9 %stage.4 = (bf16[512,384]{1,0:T(8,128)(2,1)S(1)}, bf16[512,384]{1,0:T(8,128)(2,1)S(1)}, bf16[2,512,128]{2,1,0:T(8,128)(2,1)S(1)}, bf16[1536,640]{1,0:T(8,128)(2,1)}) custom-call(bf16[512,384]{1,0:T(8,128)(2,1)S(1)} %get-tuple-element.24.g_prev, bf16[512,384]{1,0:T(8,128)(2,1)S(1)} %broadcast_in_dim.17.arrived, bf16[512,1536]{1,0:T(8,128)(2,1)S(1)} %bitcast.53, ...), custom_call_target="tpu_custom_call" | custom-call | tf_op jit(solution)/shard_map/stage/pallas_call | solution.py:168
  34.7 0.5 collective-permute-start.2
  35.2 3.1 %collective-permute-start.3 = (bf16[512,128]{1,0:T(8,128)(2,1)S(1)}, bf16[512,128]{1,0:T(8,128)(2,1)S(1)}, u32[]{:S(2)}, u32[]{:S(2)}) collective-permute-start(bf16[512,128]{1,0:T(8,128)(2,1)S(1)} %get-tuple-element.64), channel_id=1, source_target_pairs={{0,7},{1,0},{2,1},{3,2},{4,3},{5,4},{6,5},{7,6},{8,15},{9,8},{10,9... | collective-permute-start | bytes 393224 | tf_op jit(solution)/shard_map/ppermute | solution.py:257
  38.3 3.4 %collective-permute-done.2 = bf16[512,128]{1,0:T(8,128)(2,1)S(1)} collective-permute-done((bf16[512,128]{1,0:T(8,128)(2,1)S(1)}, bf16[512,128]{1,0:T(8,128)(2,1)S(1)}, u32[]{:S(2)}, u32[]{:S(2)}) %collective-permute-start.2) | collective-permute-done | bytes 131104 | tf_op jit(solution)/shard_map/ppermute | solution.py:256
  41.6 0.1 add_convert_fusion.3
  41.8 0.7 collective-permute-start.4
  42.5 9.7 %stage.5 = (bf16[512,384]{1,0:T(8,128)(2,1)S(1)}, bf16[512,384]{1,0:T(8,128)(2,1)S(1)}, bf16[2,512,128]{2,1,0:T(8,128)(2,1)S(1)}, bf16[1536,640]{1,0:T(8,128)(2,1)}) custom-call(bf16[512,384]{1,0:T(8,128)(2,1)S(1)} %get-tuple-element.32.g_prev, bf16[512,384]{1,0:T(8,128)(2,1)S(1)} %collective-permute-done.4.arrived, bf16[512,1536]{1,0:T(8,128)(2,1)S(1)} %bitcast.54, ...), custom_call_target="tpu_custom_call" | custom-call | tf_op jit(solution)/shard_map/stage/pallas_call | solution.py:168
  52.2 0.1 collective-permute-start.5
  52.3 3.5 %collective-permute-start.6 = (bf16[512,128]{1,0:T(8,128)(2,1)S(1)}, bf16[512,128]{1,0:T(8,128)(2,1)S(1)}, u32[]{:S(2)}, u32[]{:S(2)}) collective-permute-start(bf16[512,128]{1,0:T(8,128)(2,1)S(1)} %get-tuple-element.62), channel_id=1, source_target_pairs={{0,7},{1,0},{2,1},{3,2},{4,3},{5,4},{6,5},{7,6},{8,15},{9,8},{10,9... | collective-permute-start | bytes 393224 | tf_op jit(solution)/shard_map/ppermute | solution.py:257
  55.8 4.0 %collective-permute-done.5 = bf16[512,128]{1,0:T(8,128)(2,1)S(1)} collective-permute-done((bf16[512,128]{1,0:T(8,128)(2,1)S(1)}, bf16[512,128]{1,0:T(8,128)(2,1)S(1)}, u32[]{:S(2)}, u32[]{:S(2)}) %collective-permute-start.5) | collective-permute-done | bytes 131104 | tf_op jit(solution)/shard_map/ppermute | solution.py:256
  59.8 0.1 add_convert_fusion.2
  60.0 0.7 collective-permute-start.7
  60.7 9.7 %stage.6 = (bf16[512,384]{1,0:T(8,128)(2,1)S(1)}, bf16[512,384]{1,0:T(8,128)(2,1)S(1)}, bf16[2,512,128]{2,1,0:T(8,128)(2,1)S(1)}, bf16[1536,640]{1,0:T(8,128)(2,1)}) custom-call(bf16[512,384]{1,0:T(8,128)(2,1)S(1)} %get-tuple-element.35.g_prev, bf16[512,384]{1,0:T(8,128)(2,1)S(1)} %collective-permute-done.7.arrived, bf16[512,1536]{1,0:T(8,128)(2,1)S(1)} %bitcast.55, ...), custom_call_target="tpu_custom_call" | custom-call | tf_op jit(solution)/shard_map/stage/pallas_call | solution.py:168
  70.4 0.0 copy-start.16
  70.5 0.1 collective-permute-start.8
  70.6 3.5 %collective-permute-start.9 = (bf16[512,128]{1,0:T(8,128)(2,1)S(1)}, bf16[512,128]{1,0:T(8,128)(2,1)S(1)}, u32[]{:S(2)}, u32[]{:S(2)}) collective-permute-start(bf16[512,128]{1,0:T(8,128)(2,1)S(1)} %get-tuple-element.60), channel_id=1, source_target_pairs={{0,7},{1,0},{2,1},{3,2},{4,3},{5,4},{6,5},{7,6},{8,15},{9,8},{10,9... | collective-permute-start | bytes 393224 | tf_op jit(solution)/shard_map/ppermute | solution.py:257
  74.1 3.4 %collective-permute-done.8 = bf16[512,128]{1,0:T(8,128)(2,1)S(1)} collective-permute-done((bf16[512,128]{1,0:T(8,128)(2,1)S(1)}, bf16[512,128]{1,0:T(8,128)(2,1)S(1)}, u32[]{:S(2)}, u32[]{:S(2)}) %collective-permute-start.8) | collective-permute-done | bytes 131104 | tf_op jit(solution)/shard_map/ppermute | solution.py:256
  77.5 0.9 add_convert_fusion.1
  78.3 1.5 collective-permute-start.10
  79.9 29.7 %collective-permute-done.10.arrived = bf16[512,384]{1,0:T(8,128)(2,1)} collective-permute-done((bf16[512,384]{1,0:T(8,128)(2,1)}, bf16[512,384]{1,0:T(8,128)(2,1)}, u32[]{:S(2)}, u32[]{:S(2)}) %collective-permute-start.10) | collective-permute-done | bytes 393248 | tf_op jit(solution)/shard_map/ppermute | solution.py:263
  109.5 1.7 %copy-done.3 = bf16[8,3,384,128]{3,2,1,0:T(8,128)(2,1)S(1)} copy-done((bf16[8,3,384,128]{3,2,1,0:T(8,128)(2,1)S(1)}, bf16[8,3,384,128]{3,2,1,0:T(8,128)(2,1)}, u32[]{:S(2)}) %copy-start.3) | copy-done | bytes 2359320
  111.2 1.1 copy-done.5
  112.3 1.0 copy-done.7
  113.3 1.0 copy-done.9
  114.3 1.0 copy-done.11
  115.3 1.0 copy-done.17
  116.3 0.7 copy-done.19
  117.0 10.7 %stage.7 = (bf16[512,384]{1,0:T(8,128)(2,1)S(1)}, bf16[512,384]{1,0:T(8,128)(2,1)S(1)}, bf16[2,512,128]{2,1,0:T(8,128)(2,1)S(1)}, bf16[1536,640]{1,0:T(8,128)(2,1)S(1)}) custom-call(bf16[512,384]{1,0:T(8,128)(2,1)S(1)} %copy-done.17, bf16[512,384]{1,0:T(8,128)(2,1)} %collective-permute-done.10.arrived, bf16[512,1536]{1,0:T(8,128)(2,1)S(1)} %bitcast.56, ...), custom_call_target="tpu_custom_call" | custom-call | tf_op jit(solution)/shard_map/stage/pallas_call | solution.py:168
  127.8 0.0 copy-start.13
  127.8 0.0 copy-start.20
  127.8 1.7 %weights.1 = bf16[512,2048]{1,0:T(8,128)(2,1)S(1)} custom-call(bf16[512,640]{1,0:T(8,128)(2,1)S(1)} %get-tuple-element.25.xn_t, bf16[1536,640]{1,0:T(8,128)(2,1)S(1)} %get-tuple-element.43.d_qkv, bf16[512,384]{1,0:T(8,128)(2,1)S(1)} %copy-done.7, bf16[512,384]{1,0:T(8,128)(2,1)S(1)} %get-tuple-element.44.g_t), custom_call_target="tpu_custom_call" | custom-call | tf_op jit(solution)/shard_map/weights/pallas_call | solution.py:194
  129.5 0.0 copy-start.21
  129.6 0.1 dynamic-slice_bitcast_fusion
  129.7 0.1 collective-permute-start.13
  129.8 0.7 copy-done.21
  130.5 0.7 slice_bitcast_fusion.3
  131.2 3.5 %collective-permute-start.12 = (bf16[512,128]{1,0:T(8,128)(2,1)}, bf16[512,128]{1,0:T(8,128)(2,1)}, u32[]{:S(2)}, u32[]{:S(2)}) collective-permute-start(bf16[512,128]{1,0:T(8,128)(2,1)} %get-tuple-element.58), channel_id=1, source_target_pairs={{0,7},{1,0},{2,1},{3,2},{4,3},{5,4},{6,5},{7,6},{8,15},{9,8},{10,9... | collective-permute-start | bytes 393224 | tf_op jit(solution)/shard_map/ppermute | solution.py:257
  134.8 3.0 %fusion.3 = (bf16[4,64,2048]{2,1,0:T(8,128)(2,1)S(1)}, f32[4,64,2048]{2,1,0:T(8,128)}) fusion(bf16[4,64,2048]{2,1,0:T(8,128)(2,1)} %collective-permute-done.13, bf16[4,2,64,2048]{3,2,1,0:T(8,128)(2,1)S(1)} %bitcast.58, s32[]{:T(128)S(6)} %select_n.55), kind=kLoop, calls=%fused_computation.31 | loop fusion | flops 2097152 | bytes 5242884 | tf_op jit(solution)/shard_map/convert_element_type | solution.py:219
  137.8 0.1 dynamic-slice_bitcast_fusion.3
  137.8 0.1 collective-permute-start.14
  137.9 0.1 collective-permute-start.15
  138.0 4.3 %collective-permute-start.16 = (bf16[64,2048]{1,0:T(8,128)(2,1)S(1)}, bf16[64,2048]{1,0:T(8,128)(2,1)S(1)}, u32[]{:S(2)}, u32[]{:S(2)}) collective-permute-start(bf16[64,2048]{1,0:T(8,128)(2,1)S(1)} %get-tuple-element.53), channel_id=1, source_target_pairs={{0,6},{1,7},{2,4},{3,5},{4,2},{5,3},{6,0},{7,1},{8,14},{9,15},{10,... | collective-permute-start | bytes 786440 | tf_op jit(solution)/shard_map/ppermute | solution.py:224
  142.3 1.1 fusion.2
  143.4 0.9 copy.8
  144.3 2.9 %collective-permute-done.14 = bf16[64,2048]{1,0:T(8,128)(2,1)S(1)} collective-permute-done((bf16[64,2048]{1,0:T(8,128)(2,1)S(1)}, bf16[64,2048]{1,0:T(8,128)(2,1)S(1)}, u32[]{:S(2)}, u32[]{:S(2)}) %collective-permute-start.14) | collective-permute-done | bytes 262176 | tf_op jit(solution)/shard_map/ppermute | solution.py:224
  147.2 12.0 %collective-permute-done.15 = bf16[64,2048]{1,0:T(8,128)(2,1)S(1)} collective-permute-done((bf16[64,2048]{1,0:T(8,128)(2,1)S(1)}, bf16[64,2048]{1,0:T(8,128)(2,1)S(1)}, u32[]{:S(2)}, u32[]{:S(2)}) %collective-permute-start.15) | collective-permute-done | bytes 262176 | tf_op jit(solution)/shard_map/ppermute | solution.py:224
  159.2 1.2 fusion.1
  160.3 0.8 slice_bitcast_fusion
  161.1 0.7 slice_bitcast_fusion.1
  (50 shorter events, 0.2 us)
Async XLA Ops:
  1.6 7.3 %collective-permute-start = (bf16[128,512]{1,0:T(8,128)(2,1)S(1)}, bf16[128,512]{1,0:T(8,128)(2,1)S(1)}, u32[]{:S(2)}, u32[]{:S(2)}) collective-permute-start(bf16[128,512]{1,0:T(8,128)(2,1)S(1)} %get-tuple-element.56), channel_id=1, source_target_pairs={{0,1},{1,2},{2,3},{3,4},{4,5},{5,6},{6,7},{7,0},{8,9},{9,10},{10,1... | collective-permute-start | bytes 393224 | tf_op jit(solution)/shard_map/ppermute | solution.py:240
  2.1 7.4 %collective-permute-start.1 = (bf16[128,512]{1,0:T(8,128)(2,1)S(1)}, bf16[128,512]{1,0:T(8,128)(2,1)S(1)}, u32[]{:S(2)}, u32[]{:S(2)}) collective-permute-start(bf16[128,512]{1,0:T(8,128)(2,1)S(1)} %get-tuple-element.55), channel_id=1, source_target_pairs={{0,7},{1,0},{2,1},{3,2},{4,3},{5,4},{6,5},{7,6},{8,15},{9,8},{10,9... | collective-permute-start | bytes 393224 | tf_op jit(solution)/shard_map/ppermute | solution.py:241
  8.9 0.7 copy-start.22
  9.6 0.7 copy-start.24
  10.2 1.4 copy-start
  11.6 1.0 copy-start.12
  12.6 1.0 copy-start.15
  13.6 0.9 copy-start.23
  14.5 0.9 copy-start.25
  15.4 9.3 %copy-start.1 = (bf16[1,512,1536]{2,1,0:T(8,128)(2,1)S(1)}, bf16[1,512,1536]{2,1,0:T(8,128)(2,1)}, u32[]{:S(2)}) copy-start(bf16[1,512,1536]{2,1,0:T(8,128)(2,1)} %param.7) | copy-start | bytes 4718596
  15.4 9.3 %copy-start.8 = (bf16[1,512,512]{2,1,0:T(8,128)(2,1)S(1)}, bf16[1,512,512]{2,1,0:T(8,128)(2,1)}, u32[]{:S(2)}) copy-start(bf16[1,512,512]{2,1,0:T(8,128)(2,1)} %param.8) | copy-start | bytes 1572868
  24.6 36.1 %copy-start.2 = (bf16[8,3,384,128]{3,2,1,0:T(8,128)(2,1)}, bf16[8,3,384,128]{3,2,1,0:T(8,128)(2,1)S(1)}, u32[]{:S(2)}) copy-start(bf16[8,3,384,128]{3,2,1,0:T(8,128)(2,1)S(1)} %get-tuple-element.30.probs) | copy-start | bytes 7077892
  24.6 36.1 %copy-start.4 = (bf16[512,640]{1,0:T(8,128)(2,1)}, bf16[512,640]{1,0:T(8,128)(2,1)S(1)}, u32[]{:S(2)}) copy-start(bf16[512,640]{1,0:T(8,128)(2,1)S(1)} %get-tuple-element.28.k_t) | copy-start | bytes 1966084
  24.6 36.1 %copy-start.6 = (bf16[512,384]{1,0:T(8,128)(2,1)}, bf16[512,384]{1,0:T(8,128)(2,1)S(1)}, u32[]{:S(2)}) copy-start(bf16[512,384]{1,0:T(8,128)(2,1)S(1)} %get-tuple-element.31.attn_t) | copy-start | bytes 1179652
  24.6 36.1 %copy-start.10 = (bf16[512,384]{1,0:T(8,128)(2,1)}, bf16[512,384]{1,0:T(8,128)(2,1)S(1)}, u32[]{:S(2)}) copy-start(bf16[512,384]{1,0:T(8,128)(2,1)S(1)} %get-tuple-element.29.q_t) | copy-start | bytes 1179652
  24.6 36.1 %copy-start.18 = (f32[8,640]{1,0:T(8,128)}, f32[8,640]{1,0:T(8,128)S(1)}, u32[]{:S(2)}) copy-start(f32[8,640]{1,0:T(8,128)S(1)} %get-tuple-element.26.inv) | copy-start | bytes 61444
  34.7 7.0 %collective-permute-start.2 = (bf16[512,128]{1,0:T(8,128)(2,1)S(1)}, bf16[512,128]{1,0:T(8,128)(2,1)S(1)}, u32[]{:S(2)}, u32[]{:S(2)}) collective-permute-start(bf16[512,128]{1,0:T(8,128)(2,1)S(1)} %get-tuple-element.63), channel_id=1, source_target_pairs={{0,1},{1,2},{2,3},{3,4},{4,5},{5,6},{6,7},{7,0},{8,9},{9,10},{10,1... | collective-permute-start | bytes 393224 | tf_op jit(solution)/shard_map/ppermute | solution.py:256
  35.2 6.5 %collective-permute-start.3 = (bf16[512,128]{1,0:T(8,128)(2,1)S(1)}, bf16[512,128]{1,0:T(8,128)(2,1)S(1)}, u32[]{:S(2)}, u32[]{:S(2)}) collective-permute-start(bf16[512,128]{1,0:T(8,128)(2,1)S(1)} %get-tuple-element.64), channel_id=1, source_target_pairs={{0,7},{1,0},{2,1},{3,2},{4,3},{5,4},{6,5},{7,6},{8,15},{9,8},{10,9... | collective-permute-start | bytes 393224 | tf_op jit(solution)/shard_map/ppermute | solution.py:257
  41.8 0.7 collective-permute-start.4
  52.2 7.6 %collective-permute-start.5 = (bf16[512,128]{1,0:T(8,128)(2,1)S(1)}, bf16[512,128]{1,0:T(8,128)(2,1)S(1)}, u32[]{:S(2)}, u32[]{:S(2)}) collective-permute-start(bf16[512,128]{1,0:T(8,128)(2,1)S(1)} %get-tuple-element.61), channel_id=1, source_target_pairs={{0,1},{1,2},{2,3},{3,4},{4,5},{5,6},{6,7},{7,0},{8,9},{9,10},{10,1... | collective-permute-start | bytes 393224 | tf_op jit(solution)/shard_map/ppermute | solution.py:256
  52.3 7.5 %collective-permute-start.6 = (bf16[512,128]{1,0:T(8,128)(2,1)S(1)}, bf16[512,128]{1,0:T(8,128)(2,1)S(1)}, u32[]{:S(2)}, u32[]{:S(2)}) collective-permute-start(bf16[512,128]{1,0:T(8,128)(2,1)S(1)} %get-tuple-element.62), channel_id=1, source_target_pairs={{0,7},{1,0},{2,1},{3,2},{4,3},{5,4},{6,5},{7,6},{8,15},{9,8},{10,9... | collective-permute-start | bytes 393224 | tf_op jit(solution)/shard_map/ppermute | solution.py:257
  60.0 0.7 collective-permute-start.7
  70.4 7.9 %copy-start.16 = (bf16[512,384]{1,0:T(8,128)(2,1)}, bf16[512,384]{1,0:T(8,128)(2,1)S(1)}, u32[]{:S(2)}) copy-start(bf16[512,384]{1,0:T(8,128)(2,1)S(1)} %get-tuple-element.38.g_prev) | copy-start | bytes 1179652
  70.5 7.0 %collective-permute-start.8 = (bf16[512,128]{1,0:T(8,128)(2,1)S(1)}, bf16[512,128]{1,0:T(8,128)(2,1)S(1)}, u32[]{:S(2)}, u32[]{:S(2)}) collective-permute-start(bf16[512,128]{1,0:T(8,128)(2,1)S(1)} %get-tuple-element.59), channel_id=1, source_target_pairs={{0,1},{1,2},{2,3},{3,4},{4,5},{5,6},{6,7},{7,0},{8,9},{9,10},{10,1... | collective-permute-start | bytes 393224 | tf_op jit(solution)/shard_map/ppermute | solution.py:256
  70.6 6.9 %collective-permute-start.9 = (bf16[512,128]{1,0:T(8,128)(2,1)S(1)}, bf16[512,128]{1,0:T(8,128)(2,1)S(1)}, u32[]{:S(2)}, u32[]{:S(2)}) collective-permute-start(bf16[512,128]{1,0:T(8,128)(2,1)S(1)} %get-tuple-element.60), channel_id=1, source_target_pairs={{0,7},{1,0},{2,1},{3,2},{4,3},{5,4},{6,5},{7,6},{8,15},{9,8},{10,9... | collective-permute-start | bytes 393224 | tf_op jit(solution)/shard_map/ppermute | solution.py:257
  78.3 31.2 %collective-permute-start.10 = (bf16[512,384]{1,0:T(8,128)(2,1)}, bf16[512,384]{1,0:T(8,128)(2,1)}, u32[]{:S(2)}, u32[]{:S(2)}) collective-permute-start(bf16[512,384]{1,0:T(8,128)(2,1)} %add_convert_fusion.1), channel_id=1, source_target_pairs={{8,0},{9,1},{10,2},{11,3},{12,4},{13,5},{14,6},{15,7}} | collective-permute-start | bytes 1179656 | tf_op jit(solution)/shard_map/ppermute | solution.py:263
  109.5 1.7 %copy-start.3 = (bf16[8,3,384,128]{3,2,1,0:T(8,128)(2,1)S(1)}, bf16[8,3,384,128]{3,2,1,0:T(8,128)(2,1)}, u32[]{:S(2)}) copy-start(bf16[8,3,384,128]{3,2,1,0:T(8,128)(2,1)} %copy-done.2) | copy-start | bytes 7077892
  111.2 1.1 copy-start.5
  112.3 1.0 copy-start.7
  113.3 1.0 copy-start.9
  114.3 1.0 copy-start.11
  115.3 1.0 copy-start.17
  116.3 0.7 copy-start.19
  127.8 1.7 %copy-start.13 = (bf16[512,384]{1,0:T(8,128)(2,1)}, bf16[512,384]{1,0:T(8,128)(2,1)S(1)}, u32[]{:S(2)}) copy-start(bf16[512,384]{1,0:T(8,128)(2,1)S(1)} %get-tuple-element.41) | copy-start | bytes 1179652
  127.8 1.7 %copy-start.20 = (bf16[2,512,128]{2,1,0:T(8,128)(2,1)}, bf16[2,512,128]{2,1,0:T(8,128)(2,1)S(1)}, u32[]{:S(2)}) copy-start(bf16[2,512,128]{2,1,0:T(8,128)(2,1)S(1)} %get-tuple-element.42) | copy-start | bytes 786436
  129.5 1.0 copy-start.21
  129.7 5.1 %collective-permute-start.13 = (bf16[4,64,2048]{2,1,0:T(8,128)(2,1)S(1)}, bf16[4,64,2048]{2,1,0:T(8,128)(2,1)}, u32[]{:S(2)}, u32[]{:S(2)}) collective-permute-start(bf16[4,64,2048]{2,1,0:T(8,128)(2,1)S(1)} %dynamic-slice_bitcast_fusion), channel_id=1, source_target_pairs={{0,1},{1,0},{2,3},{3,2},{4,5},{5,4},{6,7},{7,6},{8,9},{9,8},{10,11... | collective-permute-start | bytes 3145736 | tf_op jit(solution)/shard_map/ppermute | solution.py:217
  131.2 11.1 %collective-permute-start.11 = (bf16[512,128]{1,0:T(8,128)(2,1)}, bf16[512,128]{1,0:T(8,128)(2,1)}, u32[]{:S(2)}, u32[]{:S(2)}) collective-permute-start(bf16[512,128]{1,0:T(8,128)(2,1)} %get-tuple-element.57), channel_id=1, source_target_pairs={{0,1},{1,2},{2,3},{3,4},{4,5},{5,6},{6,7},{7,0},{8,9},{9,10},{10,1... | collective-permute-start | bytes 393224 | tf_op jit(solution)/shard_map/ppermute | solution.py:256
  131.2 11.1 %copy-start.14 = (bf16[512,384]{1,0:T(8,128)(2,1)S(1)}, bf16[512,384]{1,0:T(8,128)(2,1)}, u32[]{:S(2)}) copy-start(bf16[512,384]{1,0:T(8,128)(2,1)} %copy-done.13) | copy-start | bytes 1179652
  131.2 11.1 %collective-permute-start.12 = (bf16[512,128]{1,0:T(8,128)(2,1)}, bf16[512,128]{1,0:T(8,128)(2,1)}, u32[]{:S(2)}, u32[]{:S(2)}) collective-permute-start(bf16[512,128]{1,0:T(8,128)(2,1)} %get-tuple-element.58), channel_id=1, source_target_pairs={{0,7},{1,0},{2,1},{3,2},{4,3},{5,4},{6,5},{7,6},{8,15},{9,8},{10,9... | collective-permute-start | bytes 393224 | tf_op jit(solution)/shard_map/ppermute | solution.py:257
  137.8 9.4 %collective-permute-start.14 = (bf16[64,2048]{1,0:T(8,128)(2,1)S(1)}, bf16[64,2048]{1,0:T(8,128)(2,1)S(1)}, u32[]{:S(2)}, u32[]{:S(2)}) collective-permute-start(bf16[64,2048]{1,0:T(8,128)(2,1)S(1)} %get-tuple-element.52), channel_id=1, source_target_pairs={{0,2},{1,3},{2,0},{3,1},{4,6},{5,7},{6,4},{7,5},{8,10},{9,11},{10,... | collective-permute-start | bytes 786440 | tf_op jit(solution)/shard_map/ppermute | solution.py:224
  137.9 21.3 %collective-permute-start.15 = (bf16[64,2048]{1,0:T(8,128)(2,1)S(1)}, bf16[64,2048]{1,0:T(8,128)(2,1)S(1)}, u32[]{:S(2)}, u32[]{:S(2)}) collective-permute-start(bf16[64,2048]{1,0:T(8,128)(2,1)S(1)} %get-tuple-element.54), channel_id=1, source_target_pairs={{0,4},{1,5},{2,6},{3,7},{4,0},{5,1},{6,2},{7,3},{8,12},{9,13},{10,... | collective-permute-start | bytes 786440 | tf_op jit(solution)/shard_map/ppermute | solution.py:224
  138.0 21.2 %collective-permute-start.16 = (bf16[64,2048]{1,0:T(8,128)(2,1)S(1)}, bf16[64,2048]{1,0:T(8,128)(2,1)S(1)}, u32[]{:S(2)}, u32[]{:S(2)}) collective-permute-start(bf16[64,2048]{1,0:T(8,128)(2,1)S(1)} %get-tuple-element.53), channel_id=1, source_target_pairs={{0,6},{1,7},{2,4},{3,5},{4,2},{5,3},{6,0},{7,1},{8,14},{9,15},{10,... | collective-permute-start | bytes 786440 | tf_op jit(solution)/shard_map/ppermute | solution.py:224

commit v2 on v0

v2 whole, which is shorter than its diff:
```python
import functools

import jax
import jax.numpy as jnp
from jax import lax
from jax.experimental import pallas as pl
from jax.experimental.pallas import tpu as pltpu
from jax.sharding import PartitionSpec as P

HEADS = 8
EPS = 1e-05
F32 = jnp.float32
BF16 = jnp.bfloat16
NN = (((1,), (0,)), ((), ()))
NT = (((1,), (1,)), ((), ()))
VMEM_LIMIT = 20 * 1024 * 1024


def mm(a, b, dims=NN):
    return lax.dot_general(a, b, dims, preferred_element_type=F32)


def cols(start, count=1, tile=128):
    return slice(start * tile, (start + count) * tile)


def call(kernel, name, outs, args, scratch=(), smem=0):
    vmem = pl.BlockSpec(memory_space=pltpu.VMEM)
    scalars = pl.BlockSpec(memory_space=pltpu.SMEM)
    return pl.pallas_call(
        kernel,
        in_specs=[scalars] * smem + [vmem] * (len(args) - smem),
        out_specs=[vmem] * len(outs),
        out_shape=[jax.ShapeDtypeStruct(shape, dtype) for shape, dtype in outs],
        scratch_shapes=[pltpu.VMEM(shape, dtype) for shape, dtype in scratch],
        compiler_params=pltpu.CompilerParams(vmem_limit_bytes=VMEM_LIMIT),
        name=name,
    )(*args)


def halves(pair, hdim):
    zero = jnp.zeros((hdim, pair.shape[1]), pair.dtype)
    return jnp.concatenate(
        [
            jnp.concatenate([pair[:hdim], zero], axis=0),
            jnp.concatenate([zero, pair[hdim:]], axis=0),
        ],
        axis=1,
    )


def normalize(rows):
    xf = rows.astype(F32)
    cent = xf - jnp.mean(xf, axis=-1, keepdims=True)
    rstd = lax.rsqrt(jnp.mean(cent * cent, axis=-1, keepdims=True) + EPS)
    return cent * rstd, rstd


def project_tile(t, tile, scale, rows, w_qkv, xn_t, inv, k_nat, v_nat, k_t, v_t):
    width = rows.shape[1]
    here = cols(t, tile=tile)
    xhat, rstd = normalize(rows)
    xn = xhat.astype(BF16)
    xn_t[:, here] = xhat.T.astype(BF16)
    inv[:, here] = jnp.broadcast_to(rstd, (tile, 128)).T[0:8, :]
    keyval = mm(xn, w_qkv[:, width:])
    k_t[:, here] = (keyval[:, :width].T * scale).astype(BF16)
    v_t[:, here] = keyval[:, width:].T.astype(BF16)
    k_nat[here, :] = keyval[:, :width].astype(BF16)
    v_nat[here, :] = keyval[:, width:].astype(BF16)
    return xn


def prelude_own_kernel(
    blk, tile, scale, x, top, w_qkv, xn_t, inv, k_nat, v_nat, k_t, v_t, q_t, g_t
):
    width = x.shape[1]
    is_last = lax.axis_index("section") == lax.axis_size("section") - 1
    for b in range(blk):
        own = cols(b, tile=tile)
        xn = project_tile(
            b, tile, scale, x[own, :], w_qkv, xn_t, inv, k_nat, v_nat, k_t, v_t
        )
        q_t[:, own] = (mm(xn, w_qkv[:, :width]).T * scale).astype(BF16)
        g_t[:, own] = jnp.where(is_last, top[own, :].astype(F32).T, 0.0).astype(BF16)


def prelude_kernel(
    blk, tile, scale, neighbours, x_lo, x_hi, w_qkv, xn_own, inv_own, k_own, v_own, kt_own, vt_own, q_t,
    xn_t, inv, v_nat, k_t, probs, attn_t, k_nat, v_t, scores,
):
    width = x_lo.shape[1]
    hdim = width // HEADS
    ours = cols(1, blk, tile)
    xn_t[:, ours] = xn_own[...]
    inv[:, ours] = inv_own[...]
    k_nat[ours, :] = k_own[...]
    v_nat[ours, :] = v_own[...]
    k_t[:, ours] = kt_own[...]
    v_t[:, ours] = vt_own[...]
    for t, rows in ((0, x_lo), (blk + 1, x_hi)):
        project_tile(t, tile, scale, rows[...], w_qkv, xn_t, inv, k_nat, v_nat, k_t, v_t)
    blocks = blk * lax.axis_size("dom")
    for b in range(blk):
        mine = lax.axis_index("dom") * blk + b
        below, above = lax.rem(mine + blocks - 1, blocks), lax.rem(mine + 1, blocks)
        has_lo = has_hi = False
        for j in range(1, neighbours.shape[1]):
            has_lo |= neighbours[b, j] == below
            has_hi |= neighbours[b, j] == above
        for i in range(HEADS // 2):
            lanes = cols(i, tile=2 * hdim)
            q = halves(q_t[lanes, cols(b, tile=tile)], hdim)
            s = mm(k_nat[cols(b, 3, tile), lanes], q)
            scores[i, b] = jnp.concatenate(
                [
                    jnp.where(has_lo, s[:tile], -1e30),
                    s[tile : 2 * tile],
                    jnp.where(has_hi, s[2 * tile :], -1e30),
                ],
                axis=0,
            )
    for b in range(blk):
        for i in range(HEADS // 2):
            s = scores[i, b]
            e = jnp.exp(s - jnp.max(s, axis=0, keepdims=True))
            probs[i, b] = (e * (1.0 / jnp.sum(e, axis=0, keepdims=True))).astype(BF16)
    for b in range(blk):
        for h in range(HEADS):
            head = cols(h, tile=hdim)
            p = probs[h // 2, b, :, cols(h % 2, tile=tile)]
            attn_t[head, cols(b, tile=tile)] = mm(v_t[head, cols(b, 3, tile)], p).astype(BF16)


def score_grads(blk, tile, hdim, g, w_out, v_nat, probs, attn_t, da_t, ds):
    da_t[...] = mm(w_out[...], g).astype(BF16)
    for b in range(blk):
        own = cols(b, tile=tile)
        for i in range(HEADS // 2):
            lanes = cols(i, tile=2 * hdim)
            da = da_t[lanes, own]
            prod = da.astype(F32) * attn_t[lanes, own].astype(F32)
            total = jnp.concatenate(
                [
                    jnp.sum(prod[:hdim], axis=0, keepdims=True),
                    jnp.sum(prod[hdim:], axis=0, keepdims=True),
                ],
                axis=1,
            )
            dp = mm(v_nat[cols(b, 3, tile), lanes], halves(da, hdim))
            ds[i, b] = (probs[i, b].astype(F32) * (dp - total)).astype(BF16)


def rim_terms(blk, tile, hdim, q_t, da_t, probs, ds, d_qkv):
    width = q_t.shape[0]
    for side, b, j in ((0, 0, 0), (1, blk - 1, 2)):
        own, near, here = cols(b, tile=tile), cols(j, tile=tile), cols(side, tile=tile)
        for i in range(HEADS // 2):
            lanes = cols(i, tile=2 * hdim)
            after = slice(width + i * 2 * hdim, width + (i + 1) * 2 * hdim)
            d_qkv[lanes, here] = mm(halves(q_t[lanes, own], hdim), ds[i, b, near, :], NT).astype(BF16)
            d_qkv[after, here] = mm(
                halves(da_t[lanes, own], hdim), probs[i, b, near, :], NT
            ).astype(BF16)


def own_terms(blk, tile, hdim, first, last, q_t, k_t, da_t, probs, ds, d_qkv):
    width = q_t.shape[0]
    for i in range(HEADS // 2):
        lanes = cols(i, tile=2 * hdim)
        dk = [None] * (blk + 2)
        dv = [None] * (blk + 2)
        for b in range(blk):
            own = cols(b, tile=tile)
            low, high = max(b, first), min(b + 3, last + 1)
            near = slice((low - b) * tile, (high - b) * tile)
            key_part = mm(halves(q_t[lanes, own], hdim), ds[i, b, near, :], NT)
            value_part = mm(halves(da_t[lanes, own], hdim), probs[i, b, near, :], NT)
            for t in range(low, high):
                part = cols(t - low, tile=tile)
                dk[t] = key_part[:, part] if dk[t] is None else dk[t] + key_part[:, part]
                dv[t] = value_part[:, part] if dv[t] is None else dv[t] + value_part[:, part]
            for h in (2 * i, 2 * i + 1):
                head = cols(h, tile=hdim)
                d_qkv[head, cols(b + 1 - first, tile=tile)] = mm(
                    k_t[head, cols(b, 3, tile)], ds[i, b, :, cols(h % 2, tile=tile)]
                ).astype(BF16)
        for t in range(first, last + 1):
            here = cols(t - first, tile=tile)
            d_qkv[width + i * 2 * hdim : width + (i + 1) * 2 * hdim, here] = dk[t].astype(BF16)
            d_qkv[2 * width + i * 2 * hdim : 2 * width + (i + 1) * 2 * hdim, here] = dv[t].astype(
                BF16
            )


def norm_grad(dn, xn, rstd):
    xhat = xn.astype(F32)
    first = jnp.mean(dn, axis=0, keepdims=True)
    second = jnp.mean(dn * xhat, axis=0, keepdims=True)
    return rstd * (dn - first - xhat * second)


def stage_first_kernel(
    blk, tile, g_prev, arrived, w_qkv, w_out, xn_t, inv, v_nat, q_t, probs, attn_t,
    g_t, da_t, ds, c_lo, c_hi, d_rim,
):
    width = g_prev.shape[0]
    hdim = width // HEADS
    g = (g_prev[...].astype(F32) + arrived[...].astype(F32)).astype(BF16)
    g_t[...] = g
    score_grads(blk, tile, hdim, g, w_out, v_nat, probs, attn_t, da_t, ds)
    rim_terms(blk, tile, hdim, q_t, da_t, probs, ds, d_rim)
    dn = mm(w_qkv[:, width:], d_rim[...])
    for side, t, c in ((0, 0, c_lo), (1, blk + 1, c_hi)):
        here = cols(t, tile=tile)
        c[...] = norm_grad(
            dn[:, cols(side, tile=tile)], xn_t[:, here], inv[0:1, here]
        ).astype(BF16)


def stage_second_kernel(
    blk, tile, g_t, da_t, ds, w_qkv, xn_t, inv, k_t, q_t, probs, y, d_qkv
):
    width = g_t.shape[0]
    hdim = width // HEADS
    own_terms(blk, tile, hdim, 1, blk, q_t, k_t, da_t, probs, ds, d_qkv)
    dn = mm(w_qkv[...], d_qkv[...])
    for b in range(blk):
        own, here = cols(b, tile=tile), cols(b + 1, tile=tile)
        out = norm_grad(dn[:, own], xn_t[:, here], inv[0:1, here])
        y[:, own] = (g_t[:, own].astype(F32) + out).astype(BF16)


def last_terms_kernel(
    blk, tile, g_prev, arrived, w_out, v_nat, k_t, q_t, probs, attn_t, g_t, d_qkv, da_t, ds
):
    width = g_prev.shape[0]
    hdim = width // HEADS
    g = (g_prev[...].astype(F32) + arrived[...].astype(F32)).astype(BF16)
    g_t[...] = g
    score_grads(blk, tile, hdim, g, w_out, v_nat, probs, attn_t, da_t, ds)
    for t in (0, blk + 1):
        d_qkv[:width, cols(t, tile=tile)] = jnp.zeros((width, tile), BF16)
    own_terms(blk, tile, hdim, 0, blk + 1, q_t, k_t, da_t, probs, ds, d_qkv)


def last_input_kernel(blk, tile, after, g_t, d_qkv, w_qkv, xn_t, inv, y, c_lo, c_hi):
    dn = mm(w_qkv[...], d_qkv[...])
    for t in range(blk + 2):
        here = cols(t, tile=tile)
        out = norm_grad(dn[:, here], xn_t[:, here], inv[0:1, here])
        if t == 0:
            c_lo[...] = out.astype(BF16)
        elif t == blk + 1:
            c_hi[...] = out.astype(BF16)
        else:
            own = cols(t - 1, tile=tile)
            y[:, own] = (g_t[:, own].astype(F32) + out).astype(BF16)


def finish_input_kernel(blk, tile, y_t, from_prev, from_next, out):
    for b in range(blk):
        own = cols(b, tile=tile)
        part = y_t[:, own].astype(F32)
        if b == 0:
            part = part + from_prev[...].astype(F32)
        if b == blk - 1:
            part = part + from_next[...].astype(F32)
        out[own, :] = part.T.astype(BF16)


def add_rims(blk, tile, y, from_prev, from_next, out):
    own = cols(0, tile=tile)
    out[...] = y[...]
    out[:, own] = (y[:, own].astype(F32) + from_prev[...].astype(F32)).astype(BF16)
    own = cols(blk - 1, tile=tile)
    out[:, own] = (out[:, own].astype(F32) + from_next[...].astype(F32)).astype(BF16)


def weight_rows(core, chips, rows, xn_t, d_qkv, attn_t, g_t):
    def picked(ref):
        starts = [pl.multiple_of((2 * z + core) * rows, rows) for z in range(chips)]
        return jnp.concatenate([ref[pl.ds(s, rows), :] for s in starts], axis=0)

    return mm(picked(xn_t), d_qkv[...], NT), mm(picked(attn_t), g_t[...], NT)


def give_kernel(chips, core, xn_t, d_qkv, attn_t, g_t, out):
    rows = xn_t.shape[0] // (2 * chips)
    wide = d_qkv.shape[0]
    if core is None:
        core = 1 - lax.rem(lax.axis_index("dom"), 2)
    a, b = weight_rows(core, chips, rows, xn_t, d_qkv, attn_t, g_t)
    for z in range(chips):
        out[z, :, :wide] = a[z * rows : (z + 1) * rows].astype(BF16)
        out[z, :, wide:] = b[z * rows : (z + 1) * rows].astype(BF16)


def keep_kernel(chips, xn_t, d_qkv, attn_t, g_t, got, *outs):
    *pieces, own, both = outs
    rows = xn_t.shape[0] // (2 * chips)
    wide = d_qkv.shape[0]
    me = lax.axis_index("dom")
    chip = me // 2
    a, b = weight_rows(lax.rem(me, 2), chips, rows, xn_t, d_qkv, attn_t, g_t)
    for z in range(chips):
        here = slice(z * rows, (z + 1) * rows)
        both[z, :, :wide] = a[here] + got[z, :, :wide].astype(F32)
        both[z, :, wide:] = b[here] + got[z, :, wide:].astype(F32)
    own[...] = both[chip]
    for k in range(1, chips):
        pieces[k - 1][...] = both[lax.bitwise_xor(chip, k)].astype(BF16)


def total_kernel(own, *refs):
    *pieces, first, second = refs
    total = own[...]
    for piece in pieces:
        total = total + piece[...].astype(F32)
    wide = first.shape[1]
    first[...] = total[:, :wide]
    second[...] = total[:, wide:]


def ring(parts, distance):
    return [(i, (i + distance) % parts) for i in range(parts)]


def weight_grads(xn_t, d_qkv, attn_t, g_t):
    parts = lax.axis_size("dom")
    width, wide = g_t.shape[0], d_qkv.shape[0]
    every = wide + width
    if parts != 8:
        rows = width // 2
        halves_of = []
        for core in (0, 1):
            out = call(
                functools.partial(give_kernel, 1, core), "weight_rows", [((1, rows, every), BF16)],
                [xn_t, d_qkv, attn_t, g_t],
            )[0]
            halves_of.append(out[0])
        term = jnp.concatenate(halves_of, axis=0).astype(F32)
        total = lax.psum_scatter(term, "dom", scatter_dimension=0, tiled=True)
        return total[:, :wide], total[:, wide:], g_t
    chips = parts // 2
    rows = width // parts
    give = call(
        functools.partial(give_kernel, chips, None), "give", [((chips, rows, every), BF16)],
        [xn_t, d_qkv, attn_t, g_t],
    )[0]
    got = lax.ppermute(give, "dom", [(i, i ^ 1) for i in range(parts)])
    *pieces, own = call(
        functools.partial(keep_kernel, chips), "keep",
        [((rows, every), BF16)] * (chips - 1) + [((rows, every), F32)],
        [xn_t, d_qkv, attn_t, g_t, got],
        scratch=[((chips, rows, every), F32)],
    )
    pieces = [
        lax.ppermute(piece, "dom", [(i, i ^ (2 * k)) for i in range(parts)])
        for k, piece in enumerate(pieces, 1)
    ]
    first, second = call(
        total_kernel, "total", [((rows, wide), F32), ((rows, width), F32)], [own, *pieces]
    )
    return first, second, own


def local(layer_inputs, top_grad, w_qkv, w_out, neighbours):
    sections = lax.axis_size("section")
    parts = lax.axis_size("dom")
    blk = neighbours.shape[0]
    rows, width = top_grad.shape[1:]
    tile = rows // blk
    ext = rows + 2 * tile
    hdim = width // HEADS
    scale = 1.0 / hdim**0.5
    x = layer_inputs[0, 0]
    w_in, w_back = w_qkv[0], w_out[0]
    x_lo = lax.ppermute(x[rows - tile :], "dom", ring(parts, 1))
    x_hi = lax.ppermute(x[:tile], "dom", ring(parts, -1))
    *kept, q_t, g_t = call(
        functools.partial(prelude_own_kernel, blk, tile, scale), "prelude_own",
        [
            ((width, rows), BF16), ((8, rows), F32), ((rows, width), BF16), ((rows, width), BF16),
            ((width, rows), BF16), ((width, rows), BF16), ((width, rows), BF16), ((width, rows), BF16),
        ],
        [x, top_grad[0], w_in],
    )
    pair_shape = (HEADS // 2, blk, 3 * tile, 2 * tile)
    xn_t, inv, v_nat, k_t, probs, attn_t = call(
        functools.partial(prelude_kernel, blk, tile, scale), "prelude",
        [
            ((width, ext), BF16), ((8, ext), F32), ((ext, width), BF16), ((width, ext), BF16),
            (pair_shape, BF16), ((width, rows), BF16),
        ],
        [neighbours, x_lo, x_hi, w_in, *kept, q_t],
        scratch=[((ext, width), BF16), ((width, ext), BF16), (pair_shape, F32)], smem=1,
    )
    arrived = jnp.zeros_like(g_t)
    for k in range(sections - 1):
        g_t, da_t, ds, c_lo, c_hi = call(
            functools.partial(stage_first_kernel, blk, tile), "stage_first",
            [((width, rows), BF16), ((width, rows), BF16), (pair_shape, BF16), ((width, tile), BF16), ((width, tile), BF16)],
            [g_t, arrived, w_in, w_back, xn_t, inv, v_nat, q_t, probs, attn_t],
            scratch=[((2 * width, 2 * tile), BF16)],
        )
        from_prev = lax.ppermute(c_hi, "dom", ring(parts, 1))
        from_next = lax.ppermute(c_lo, "dom", ring(parts, -1))
        y = call(
            functools.partial(stage_second_kernel, blk, tile), "stage_second",
            [((width, rows), BF16)],
            [g_t, da_t, ds, w_in, xn_t, inv, k_t, q_t, probs],
            scratch=[((3 * width, rows), BF16)],
        )[0]
        y = call(
            functools.partial(add_rims, blk, tile), "add_rims", [((width, rows), BF16)],
            [y, from_prev, from_next],
        )[0]
        arrived = lax.ppermute(y, "section", [(sections - 1 - k, sections - 2 - k)])
    g_t, d_qkv = call(
        functools.partial(last_terms_kernel, blk, tile), "last_terms",
        [((width, rows), BF16), ((3 * width, ext), BF16)],
        [g_t, arrived, w_back, v_nat, k_t, q_t, probs, attn_t],
        scratch=[((width, rows), BF16), (pair_shape, BF16)],
    )
    qkv_grad, out_grad, after = weight_grads(xn_t, d_qkv, attn_t, g_t)
    y, c_lo, c_hi = call(
        functools.partial(last_input_kernel, blk, tile), "last_input",
        [((width, rows), BF16), ((width, tile), BF16), ((width, tile), BF16)],
        [after, g_t, d_qkv, w_in, xn_t, inv],
    )
    from_prev = lax.ppermute(c_hi, "dom", ring(parts, 1))
    from_next = lax.ppermute(c_lo, "dom", ring(parts, -1))
    y = call(
        functools.partial(finish_input_kernel, blk, tile), "finish_input", [((rows, width), BF16)],
        [y, from_prev, from_next],
    )[0]
    return (y[None, None], qkv_grad[None], out_grad[None])


def solution(mesh):
    placed = (
        P("section", None, "dom", None),
        P(None, "dom", None),
        P("section", None, None),
        P("section", None, None),
        P("dom", None),
    )
    return jax.shard_map(
        local,
        mesh=mesh,
        in_specs=placed,
        out_specs=(
            P("section", None, "dom", None),
            P("section", "dom", None),
            P("section", "dom", None),
        ),
        check_vma=False,
    )
```

time: 667 us -> 110 us (0.16)
  the two profiles are of different devices: /device:TPU:0 before, /device:TPU:9 now
where the time goes in v2:
time: 110 us
  waiting for transfers between devices  60.5 us (55%)
  Pallas kernels  30.6 us (28%)
  starting transfers between devices  13.6 us (12%)
  local copies, waits for them, and re-layouts  4.53 us (4%)
    pallas_call x17, Pallas kernels, call(): pl.pallas_call(kernel, in_specs=[scalars] * smem + [vmem] * (len(args) -...  30.6 us
    ppermute x3, waiting for transfers between devices, local(): arrived = lax.ppermute(y, 'section', [(sections - 1 - k, sections - 2 - k)])  26.6 us
    ppermute x4, waiting for transfers between devices, local(): from_prev = lax.ppermute(c_hi, 'dom', ring(parts, 1))  21.9 us
    ppermute x4, waiting for transfers between devices, local(): from_next = lax.ppermute(c_lo, 'dom', ring(parts, -1))  9.77 us
    ppermute x3, starting transfers between devices, weight_grads(): lax.ppermute(piece, 'dom', [(i, i ^ 2 * k) for i in range(parts)])  3.92 us
    unnamed x12, local copies, waits for them, and re-layouts  3.5 us
    ppermute x3, starting transfers between devices, local(): arrived = lax.ppermute(y, 'section', [(sections - 1 - k, sections - 2 - k)])  2.88 us
    ppermute x4, starting transfers between devices, local(): from_prev = lax.ppermute(c_hi, 'dom', ring(parts, 1))  2.72 us
  transfers between devices with their start and end apart: 17, of which 7 were waited for; matrix products, arithmetic and copies ran while one was open for 0% of the time, Pallas kernels for 12%

profile of v2, /device:TPU:9, one launch (start us, length us, event | category | flops | bytes accessed | tf_op | source)
XLA Modules:
  0.0 110.2 jit_solution(8679200834645719224)
XLA Ops:
  0.6 0.0 copy-start.5
  0.6 1.0 slice_bitcast_fusion
  1.6 0.7 collective-permute-start.1
  2.4 1.2 %collective-permute-start = (bf16[128,512]{1,0:T(8,128)(2,1)S(1)}, bf16[128,512]{1,0:T(8,128)(2,1)S(1)}, u32[]{:S(2)}, u32[]{:S(2)}) collective-permute-start(bf16[128,512]{1,0:T(8,128)(2,1)S(1)} %get-tuple-element.84), channel_id=1, source_target_pairs={{0,1},{1,2},{2,3},{3,4},{4,5},{5,6},{6,7},{7,0},{8,9},{9,10},{10,1... | collective-permute-start | bytes 393224 | tf_op jit(solution)/shard_map/ppermute | solution.py:379
  3.6 0.0 copy-start
  3.6 1.4 %copy-done = bf16[1,512,1536]{2,1,0:T(8,128)(2,1)S(1)} copy-done((bf16[1,512,1536]{2,1,0:T(8,128)(2,1)S(1)}, bf16[1,512,1536]{2,1,0:T(8,128)(2,1)}, u32[]{:S(2)}) %copy-start) | copy-done | bytes 1572888
  5.0 0.0 copy-start.3
  5.0 1.0 copy-done.3
  6.0 0.0 copy-start.4
  6.0 1.0 copy-done.4
  7.0 0.0 copy-start.1
  7.0 1.3 %prelude_own.1 = (bf16[512,384]{1,0:T(8,128)(2,1)S(1)}, f32[8,384]{1,0:T(8,128)S(1)}, bf16[384,512]{1,0:T(8,128)(2,1)S(1)}, bf16[384,512]{1,0:T(8,128)(2,1)S(1)}...) custom-call(bf16[384,512]{1,0:T(8,128)(2,1)S(1)} %bitcast.24, ...), custom_call_target="tpu_custom_call" | custom-call | tf_op jit(solution)/shard_map/prelude_own/pallas_call | solution.py:30
  8.3 0.0 copy-start.2
  8.3 0.0 collective-permute-done.1.x_hi
  8.3 0.0 collective-permute-done.x_lo
  8.3 0.0 copy-done.5
  8.3 0.1 copy-done.1
  8.4 3.5 %prelude.1 = (bf16[512,640]{1,0:T(8,128)(2,1)S(1)}, f32[8,640]{1,0:T(8,128)S(1)}, bf16[640,512]{1,0:T(8,128)(2,1)S(1)}, bf16[512,640]{1,0:T(8,128)(2,1)S(1)}, bf...) custom-call(s32[3,3]{1,0:T(4,128)S(1)} %copy-done.5, bf16[128,512]{1,0:T(8,128)(2,1)S(1)} %collective-permute-done.x_lo, ...), custom_call_target="tpu_custom_call" | custom-call | tf_op jit(solution)/shard_map/prelude/pallas_call | solution.py:30
  12.0 0.0 copy-done.2
  12.0 2.4 %stage_first.3 = (bf16[512,384]{1,0:T(8,128)(2,1)S(1)}, bf16[512,384]{1,0:T(8,128)(2,1)S(1)}, bf16[4,3,384,256]{3,2,1,0:T(8,128)(2,1)S(1)}, bf16[512,128]{1,0:T(8,128)(2,1)S(1)}, bf16[512,128]{1,0:T(8,128)(2,1)S(1)}) custom-call(bf16[512,384]{1,0:T(8,128)(2,1)S(1)} %get-tuple-element.51.g_prev, bf16[512,384]{1,0:T(8,128)(2,1)S(1)} %broadcast_in_dim.12.arrived, ...), custom_call_target="tpu_custom_call" | custom-call | tf_op jit(solution)/shard_map/stage_first/pallas_call | solution.py:30
  14.4 0.5 collective-permute-start.2
  14.9 0.1 collective-permute-start.3
  14.9 3.1 %stage_second.3.y = bf16[512,384]{1,0:T(8,128)(2,1)S(1)} custom-call(bf16[512,384]{1,0:T(8,128)(2,1)S(1)} %get-tuple-element.56.g_t.g_prev, bf16[512,384]{1,0:T(8,128)(2,1)S(1)} %get-tuple-element.57.da_t, bf16[4,3,384,256]{3,2,1,0:T(8,128)(2,1)S(1)} %get-tuple-element.58.ds, bf16[512,1536]{1,0:T(8,128)(2,1)S(1)} %bitcast.14, ...), custom_call_target="tpu_custom_call" | custom-call | tf_op jit(solution)/shard_map/stage_second/pallas_call | solution.py:30
  18.0 0.0 collective-permute-done.2.from_prev
  18.1 1.2 %collective-permute-done.3.from_next = bf16[512,128]{1,0:T(8,128)(2,1)S(1)} collective-permute-done((bf16[512,128]{1,0:T(8,128)(2,1)S(1)}, bf16[512,128]{1,0:T(8,128)(2,1)S(1)}, u32[]{:S(2)}, u32[]{:S(2)}) %collective-permute-start.3) | collective-permute-done | bytes 131104 | tf_op jit(solution)/shard_map/ppermute | solution.py:408
  19.3 0.1 add_rims.3
  19.4 0.7 collective-permute-start.4
  20.1 0.0 collective-permute-done.4.arrived
  20.1 2.4 %stage_first.4 = (bf16[512,384]{1,0:T(8,128)(2,1)S(1)}, bf16[512,384]{1,0:T(8,128)(2,1)S(1)}, bf16[4,3,384,256]{3,2,1,0:T(8,128)(2,1)S(1)}, bf16[512,128]{1,0:T(8,128)(2,1)S(1)}, bf16[512,128]{1,0:T(8,128)(2,1)S(1)}) custom-call(bf16[512,384]{1,0:T(8,128)(2,1)S(1)} %get-tuple-element.56.g_t.g_prev, bf16[512,384]{1,0:T(8,128)(2,1)S(1)} %collective-permute-done.4.arrived, ...), custom_call_target="tpu_custom_call" | custom-call | tf_op jit(solution)/shard_map/stage_first/pallas_call | solution.py:30
  22.5 0.5 collective-permute-start.5
  23.0 0.0 collective-permute-start.6
  23.1 3.1 %stage_second.4.y = bf16[512,384]{1,0:T(8,128)(2,1)S(1)} custom-call(bf16[512,384]{1,0:T(8,128)(2,1)S(1)} %get-tuple-element.62.g_t.g_prev, bf16[512,384]{1,0:T(8,128)(2,1)S(1)} %get-tuple-element.63.da_t, bf16[4,3,384,256]{3,2,1,0:T(8,128)(2,1)S(1)} %get-tuple-element.64.ds, bf16[512,1536]{1,0:T(8,128)(2,1)S(1)} %bitcast.16, ...), custom_call_target="tpu_custom_call" | custom-call | tf_op jit(solution)/shard_map/stage_second/pallas_call | solution.py:30
  26.2 0.0 collective-permute-done.5.from_prev
  26.2 2.6 %collective-permute-done.6.from_next = bf16[512,128]{1,0:T(8,128)(2,1)S(1)} collective-permute-done((bf16[512,128]{1,0:T(8,128)(2,1)S(1)}, bf16[512,128]{1,0:T(8,128)(2,1)S(1)}, u32[]{:S(2)}, u32[]{:S(2)}) %collective-permute-start.6) | collective-permute-done | bytes 131104 | tf_op jit(solution)/shard_map/ppermute | solution.py:408
  28.8 0.1 add_rims.4
  28.9 0.7 collective-permute-start.7
  29.6 0.0 collective-permute-done.7.arrived
  29.6 2.4 %stage_first.5 = (bf16[512,384]{1,0:T(8,128)(2,1)S(1)}, bf16[512,384]{1,0:T(8,128)(2,1)S(1)}, bf16[4,3,384,256]{3,2,1,0:T(8,128)(2,1)S(1)}, bf16[512,128]{1,0:T(8,128)(2,1)S(1)}, bf16[512,128]{1,0:T(8,128)(2,1)S(1)}) custom-call(bf16[512,384]{1,0:T(8,128)(2,1)S(1)} %get-tuple-element.62.g_t.g_prev, bf16[512,384]{1,0:T(8,128)(2,1)S(1)} %collective-permute-done.7.arrived, ...), custom_call_target="tpu_custom_call" | custom-call | tf_op jit(solution)/shard_map/stage_first/pallas_call | solution.py:30
  32.0 0.5 collective-permute-start.8
  32.5 0.0 collective-permute-start.9
  32.5 3.1 %stage_second.5.y = bf16[512,384]{1,0:T(8,128)(2,1)S(1)} custom-call(bf16[512,384]{1,0:T(8,128)(2,1)S(1)} %get-tuple-element.67.g_t.g_prev, bf16[512,384]{1,0:T(8,128)(2,1)S(1)} %get-tuple-element.68.da_t, bf16[4,3,384,256]{3,2,1,0:T(8,128)(2,1)S(1)} %get-tuple-element.69.ds, bf16[512,1536]{1,0:T(8,128)(2,1)S(1)} %bitcast.18, ...), custom_call_target="tpu_custom_call" | custom-call | tf_op jit(solution)/shard_map/stage_second/pallas_call | solution.py:30
  35.7 0.0 collective-permute-done.8.from_prev
  35.7 4.6 %collective-permute-done.9.from_next = bf16[512,128]{1,0:T(8,128)(2,1)S(1)} collective-permute-done((bf16[512,128]{1,0:T(8,128)(2,1)S(1)}, bf16[512,128]{1,0:T(8,128)(2,1)S(1)}, u32[]{:S(2)}, u32[]{:S(2)}) %collective-permute-start.9) | collective-permute-done | bytes 131104 | tf_op jit(solution)/shard_map/ppermute | solution.py:408
  40.2 0.1 add_rims.5
  40.4 1.5 %collective-permute-start.10 = (bf16[512,384]{1,0:T(8,128)(2,1)S(1)}, bf16[512,384]{1,0:T(8,128)(2,1)S(1)}, u32[]{:S(2)}, u32[]{:S(2)}) collective-permute-start(bf16[512,384]{1,0:T(8,128)(2,1)S(1)} %add_rims.5), channel_id=1, source_target_pairs={{8,0},{9,1},{10,2},{11,3},{12,4},{13,5},{14,6},{15,7}} | collective-permute-start | bytes 1179656 | tf_op jit(solution)/shard_map/ppermute | solution.py:419
  41.9 26.6 %collective-permute-done.10.arrived = bf16[512,384]{1,0:T(8,128)(2,1)S(1)} collective-permute-done((bf16[512,384]{1,0:T(8,128)(2,1)S(1)}, bf16[512,384]{1,0:T(8,128)(2,1)S(1)}, u32[]{:S(2)}, u32[]{:S(2)}) %collective-permute-start.10) | collective-permute-done | bytes 393248 | tf_op jit(solution)/shard_map/ppermute | solution.py:419
  68.5 3.3 %last_terms.1 = (bf16[512,384]{1,0:T(8,128)(2,1)S(1)}, bf16[1536,640]{1,0:T(8,128)(2,1)S(1)}) custom-call(bf16[512,384]{1,0:T(8,128)(2,1)S(1)} %get-tuple-element.67.g_t.g_prev, bf16[512,384]{1,0:T(8,128)(2,1)S(1)} %collective-permute-done.10.arrived, bf16[512,512]{1,0:T(8,128)(2,1)S(1)} %bitcast.23, bf16[640,512]{1,0:T(8,128)(2,1)S(1)} %get-tuple-element.53.v_nat, ...), custom_call_target="tpu_custom_call" | custom-call | tf_op jit(solution)/shard_map/last_terms/pallas_call | solution.py:30
  71.8 1.0 give.1
  72.7 2.0 %collective-permute-start.11 = (bf16[4,64,2048]{2,1,0:T(8,128)(2,1)S(1)}, bf16[4,64,2048]{2,1,0:T(8,128)(2,1)S(1)}, u32[]{:S(2)}, u32[]{:S(2)}) collective-permute-start(bf16[4,64,2048]{2,1,0:T(8,128)(2,1)S(1)} %give.1), channel_id=1, source_target_pairs={{0,1},{1,0},{2,3},{3,2},{4,5},{5,4},{6,7},{7,6},{8,9},{9,8},{10,11... | collective-permute-start | bytes 3145736 | tf_op jit(solution)/shard_map/ppermute | solution.py:351
  74.7 2.3 %collective-permute-done.11.got = bf16[4,64,2048]{2,1,0:T(8,128)(2,1)S(1)} collective-permute-done((bf16[4,64,2048]{2,1,0:T(8,128)(2,1)S(1)}, bf16[4,64,2048]{2,1,0:T(8,128)(2,1)S(1)}, u32[]{:S(2)}, u32[]{:S(2)}) %collective-permute-start.11) | collective-permute-done | bytes 1048608 | tf_op jit(solution)/shard_map/ppermute | solution.py:351
  77.0 1.1 keep.1
  78.1 2.7 %collective-permute-start.14 = (bf16[64,2048]{1,0:T(8,128)(2,1)S(1)}, bf16[64,2048]{1,0:T(8,128)(2,1)S(1)}, u32[]{:S(2)}, u32[]{:S(2)}) collective-permute-start(bf16[64,2048]{1,0:T(8,128)(2,1)S(1)} %get-tuple-element.78), channel_id=1, source_target_pairs={{0,2},{1,3},{2,0},{3,1},{4,6},{5,7},{6,4},{7,5},{8,10},{9,11},{10,... | collective-permute-start | bytes 786440 | tf_op jit(solution)/shard_map/ppermute | solution.py:359
  80.8 0.3 collective-permute-start.15
  81.1 0.9 collective-permute-start.16
  82.0 1.9 %last_input.1 = (bf16[512,384]{1,0:T(8,128)(2,1)S(1)}, bf16[512,128]{1,0:T(8,128)(2,1)S(1)}, bf16[512,128]{1,0:T(8,128)(2,1)S(1)}) custom-call(f32[64,2048]{1,0:T(8,128)S(1)} %get-tuple-element.74.after.own, bf16[512,384]{1,0:T(8,128)(2,1)S(1)} %get-tuple-element.73.g_t, bf16[1536,640]{1,0:T(8,128)(2,1)S(1)} %get-tuple-element.72.d_qkv, ...), custom_call_target="tpu_custom_call" | custom-call | tf_op jit(solution)/shard_map/last_input/pallas_call | solution.py:30
  83.9 1.2 %collective-permute-start.12 = (bf16[512,128]{1,0:T(8,128)(2,1)S(1)}, bf16[512,128]{1,0:T(8,128)(2,1)S(1)}, u32[]{:S(2)}, u32[]{:S(2)}) collective-permute-start(bf16[512,128]{1,0:T(8,128)(2,1)S(1)} %get-tuple-element.76), channel_id=1, source_target_pairs={{0,1},{1,2},{2,3},{3,4},{4,5},{5,6},{6,7},{7,0},{8,9},{9,10},{10,1... | collective-permute-start | bytes 393224 | tf_op jit(solution)/shard_map/ppermute | solution.py:432
  85.1 0.0 collective-permute-start.13
  85.1 21.9 %collective-permute-done.12.from_prev = bf16[512,128]{1,0:T(8,128)(2,1)S(1)} collective-permute-done((bf16[512,128]{1,0:T(8,128)(2,1)S(1)}, bf16[512,128]{1,0:T(8,128)(2,1)S(1)}, u32[]{:S(2)}, u32[]{:S(2)}) %collective-permute-start.12) | collective-permute-done | bytes 131104 | tf_op jit(solution)/shard_map/ppermute | solution.py:432
  107.0 1.4 %collective-permute-done.13.from_next = bf16[512,128]{1,0:T(8,128)(2,1)S(1)} collective-permute-done((bf16[512,128]{1,0:T(8,128)(2,1)S(1)}, bf16[512,128]{1,0:T(8,128)(2,1)S(1)}, u32[]{:S(2)}, u32[]{:S(2)}) %collective-permute-start.13) | collective-permute-done | bytes 131104 | tf_op jit(solution)/shard_map/ppermute | solution.py:433
  108.4 0.9 finish_input.1
  109.3 0.0 collective-permute-done.14.refs_0_
  109.3 0.0 collective-permute-done.15.refs_1_
  109.3 0.0 collective-permute-done.16.refs_2_
  109.3 0.9 total.1
  (1 shorter events, 0.0 us)
Async XLA Ops:
  0.6 7.7 %copy-start.5 = (s32[3,3]{1,0:T(4,128)S(1)}, s32[3,3]{1,0:T(4,128)}, u32[]{:S(2)}) copy-start(s32[3,3]{1,0:T(4,128)} %neighbours.1) | copy-start | bytes 112
  1.6 6.7 %collective-permute-start.1 = (bf16[128,512]{1,0:T(8,128)(2,1)S(1)}, bf16[128,512]{1,0:T(8,128)(2,1)S(1)}, u32[]{:S(2)}, u32[]{:S(2)}) collective-permute-start(bf16[128,512]{1,0:T(8,128)(2,1)S(1)} %get-tuple-element.83), channel_id=1, source_target_pairs={{0,7},{1,0},{2,1},{3,2},{4,3},{5,4},{6,5},{7,6},{8,15},{9,8},{10,9... | collective-permute-start | bytes 393224 | tf_op jit(solution)/shard_map/ppermute | solution.py:380
  2.4 5.9 %collective-permute-start = (bf16[128,512]{1,0:T(8,128)(2,1)S(1)}, bf16[128,512]{1,0:T(8,128)(2,1)S(1)}, u32[]{:S(2)}, u32[]{:S(2)}) collective-permute-start(bf16[128,512]{1,0:T(8,128)(2,1)S(1)} %get-tuple-element.84), channel_id=1, source_target_pairs={{0,1},{1,2},{2,3},{3,4},{4,5},{5,6},{6,7},{7,0},{8,9},{9,10},{10,1... | collective-permute-start | bytes 393224 | tf_op jit(solution)/shard_map/ppermute | solution.py:379
  3.6 1.4 %copy-start = (bf16[1,512,1536]{2,1,0:T(8,128)(2,1)S(1)}, bf16[1,512,1536]{2,1,0:T(8,128)(2,1)}, u32[]{:S(2)}) copy-start(bf16[1,512,1536]{2,1,0:T(8,128)(2,1)} %param.7) | copy-start | bytes 4718596
  5.0 1.0 copy-start.3
  6.0 1.0 copy-start.4
  7.0 1.4 %copy-start.1 = (bf16[1,512,1536]{2,1,0:T(8,128)(2,1)S(1)}, bf16[1,512,1536]{2,1,0:T(8,128)(2,1)}, u32[]{:S(2)}) copy-start(bf16[1,512,1536]{2,1,0:T(8,128)(2,1)} %param.7) | copy-start | bytes 4718596
  8.3 3.7 %copy-start.2 = (bf16[1,512,512]{2,1,0:T(8,128)(2,1)S(1)}, bf16[1,512,512]{2,1,0:T(8,128)(2,1)}, u32[]{:S(2)}) copy-start(bf16[1,512,512]{2,1,0:T(8,128)(2,1)} %param.8) | copy-start | bytes 1572868
  14.4 3.7 %collective-permute-start.2 = (bf16[512,128]{1,0:T(8,128)(2,1)S(1)}, bf16[512,128]{1,0:T(8,128)(2,1)S(1)}, u32[]{:S(2)}, u32[]{:S(2)}) collective-permute-start(bf16[512,128]{1,0:T(8,128)(2,1)S(1)} %get-tuple-element.60), channel_id=1, source_target_pairs={{0,1},{1,2},{2,3},{3,4},{4,5},{5,6},{6,7},{7,0},{8,9},{9,10},{10,1... | collective-permute-start | bytes 393224 | tf_op jit(solution)/shard_map/ppermute | solution.py:407
  14.9 4.4 %collective-permute-start.3 = (bf16[512,128]{1,0:T(8,128)(2,1)S(1)}, bf16[512,128]{1,0:T(8,128)(2,1)S(1)}, u32[]{:S(2)}, u32[]{:S(2)}) collective-permute-start(bf16[512,128]{1,0:T(8,128)(2,1)S(1)} %get-tuple-element.61), channel_id=1, source_target_pairs={{0,7},{1,0},{2,1},{3,2},{4,3},{5,4},{6,5},{7,6},{8,15},{9,8},{10,9... | collective-permute-start | bytes 393224 | tf_op jit(solution)/shard_map/ppermute | solution.py:408
  19.4 0.7 collective-permute-start.4
  22.5 3.7 %collective-permute-start.5 = (bf16[512,128]{1,0:T(8,128)(2,1)S(1)}, bf16[512,128]{1,0:T(8,128)(2,1)S(1)}, u32[]{:S(2)}, u32[]{:S(2)}) collective-permute-start(bf16[512,128]{1,0:T(8,128)(2,1)S(1)} %get-tuple-element.65), channel_id=1, source_target_pairs={{0,1},{1,2},{2,3},{3,4},{4,5},{5,6},{6,7},{7,0},{8,9},{9,10},{10,1... | collective-permute-start | bytes 393224 | tf_op jit(solution)/shard_map/ppermute | solution.py:407
  23.0 5.8 %collective-permute-start.6 = (bf16[512,128]{1,0:T(8,128)(2,1)S(1)}, bf16[512,128]{1,0:T(8,128)(2,1)S(1)}, u32[]{:S(2)}, u32[]{:S(2)}) collective-permute-start(bf16[512,128]{1,0:T(8,128)(2,1)S(1)} %get-tuple-element.66), channel_id=1, source_target_pairs={{0,7},{1,0},{2,1},{3,2},{4,3},{5,4},{6,5},{7,6},{8,15},{9,8},{10,9... | collective-permute-start | bytes 393224 | tf_op jit(solution)/shard_map/ppermute | solution.py:408
  28.9 0.7 collective-permute-start.7
  32.0 3.7 %collective-permute-start.8 = (bf16[512,128]{1,0:T(8,128)(2,1)S(1)}, bf16[512,128]{1,0:T(8,128)(2,1)S(1)}, u32[]{:S(2)}, u32[]{:S(2)}) collective-permute-start(bf16[512,128]{1,0:T(8,128)(2,1)S(1)} %get-tuple-element.70), channel_id=1, source_target_pairs={{0,1},{1,2},{2,3},{3,4},{4,5},{5,6},{6,7},{7,0},{8,9},{9,10},{10,1... | collective-permute-start | bytes 393224 | tf_op jit(solution)/shard_map/ppermute | solution.py:407
  32.5 7.7 %collective-permute-start.9 = (bf16[512,128]{1,0:T(8,128)(2,1)S(1)}, bf16[512,128]{1,0:T(8,128)(2,1)S(1)}, u32[]{:S(2)}, u32[]{:S(2)}) collective-permute-start(bf16[512,128]{1,0:T(8,128)(2,1)S(1)} %get-tuple-element.71), channel_id=1, source_target_pairs={{0,7},{1,0},{2,1},{3,2},{4,3},{5,4},{6,5},{7,6},{8,15},{9,8},{10,9... | collective-permute-start | bytes 393224 | tf_op jit(solution)/shard_map/ppermute | solution.py:408
  40.4 28.1 %collective-permute-start.10 = (bf16[512,384]{1,0:T(8,128)(2,1)S(1)}, bf16[512,384]{1,0:T(8,128)(2,1)S(1)}, u32[]{:S(2)}, u32[]{:S(2)}) collective-permute-start(bf16[512,384]{1,0:T(8,128)(2,1)S(1)} %add_rims.5), channel_id=1, source_target_pairs={{8,0},{9,1},{10,2},{11,3},{12,4},{13,5},{14,6},{15,7}} | collective-permute-start | bytes 1179656 | tf_op jit(solution)/shard_map/ppermute | solution.py:419
  72.7 4.3 %collective-permute-start.11 = (bf16[4,64,2048]{2,1,0:T(8,128)(2,1)S(1)}, bf16[4,64,2048]{2,1,0:T(8,128)(2,1)S(1)}, u32[]{:S(2)}, u32[]{:S(2)}) collective-permute-start(bf16[4,64,2048]{2,1,0:T(8,128)(2,1)S(1)} %give.1), channel_id=1, source_target_pairs={{0,1},{1,0},{2,3},{3,2},{4,5},{5,4},{6,7},{7,6},{8,9},{9,8},{10,11... | collective-permute-start | bytes 3145736 | tf_op jit(solution)/shard_map/ppermute | solution.py:351
  78.1 31.2 %collective-permute-start.14 = (bf16[64,2048]{1,0:T(8,128)(2,1)S(1)}, bf16[64,2048]{1,0:T(8,128)(2,1)S(1)}, u32[]{:S(2)}, u32[]{:S(2)}) collective-permute-start(bf16[64,2048]{1,0:T(8,128)(2,1)S(1)} %get-tuple-element.78), channel_id=1, source_target_pairs={{0,2},{1,3},{2,0},{3,1},{4,6},{5,7},{6,4},{7,5},{8,10},{9,11},{10,... | collective-permute-start | bytes 786440 | tf_op jit(solution)/shard_map/ppermute | solution.py:359
  80.8 28.5 %collective-permute-start.15 = (bf16[64,2048]{1,0:T(8,128)(2,1)S(1)}, bf16[64,2048]{1,0:T(8,128)(2,1)S(1)}, u32[]{:S(2)}, u32[]{:S(2)}) collective-permute-start(bf16[64,2048]{1,0:T(8,128)(2,1)S(1)} %get-tuple-element.79), channel_id=1, source_target_pairs={{0,4},{1,5},{2,6},{3,7},{4,0},{5,1},{6,2},{7,3},{8,12},{9,13},{10,... | collective-permute-start | bytes 786440 | tf_op jit(solution)/shard_map/ppermute | solution.py:359
  81.1 28.2 %collective-permute-start.16 = (bf16[64,2048]{1,0:T(8,128)(2,1)S(1)}, bf16[64,2048]{1,0:T(8,128)(2,1)S(1)}, u32[]{:S(2)}, u32[]{:S(2)}) collective-permute-start(bf16[64,2048]{1,0:T(8,128)(2,1)S(1)} %get-tuple-element.80), channel_id=1, source_target_pairs={{0,6},{1,7},{2,4},{3,5},{4,2},{5,3},{6,0},{7,1},{8,14},{9,15},{10,... | collective-permute-start | bytes 786440 | tf_op jit(solution)/shard_map/ppermute | solution.py:359
  83.9 23.1 %collective-permute-start.12 = (bf16[512,128]{1,0:T(8,128)(2,1)S(1)}, bf16[512,128]{1,0:T(8,128)(2,1)S(1)}, u32[]{:S(2)}, u32[]{:S(2)}) collective-permute-start(bf16[512,128]{1,0:T(8,128)(2,1)S(1)} %get-tuple-element.76), channel_id=1, source_target_pairs={{0,1},{1,2},{2,3},{3,4},{4,5},{5,6},{6,7},{7,0},{8,9},{9,10},{10,1... | collective-permute-start | bytes 393224 | tf_op jit(solution)/shard_map/ppermute | solution.py:432
  85.1 23.3 %collective-permute-start.13 = (bf16[512,128]{1,0:T(8,128)(2,1)S(1)}, bf16[512,128]{1,0:T(8,128)(2,1)S(1)}, u32[]{:S(2)}, u32[]{:S(2)}) collective-permute-start(bf16[512,128]{1,0:T(8,128)(2,1)S(1)} %get-tuple-element.77), channel_id=1, source_target_pairs={{0,7},{1,0},{2,1},{3,2},{4,3},{5,4},{6,5},{7,6},{8,15},{9,8},{10,9... | collective-permute-start | bytes 393224 | tf_op jit(solution)/shard_map/ppermute | solution.py:433

commit v3 on v2

v3 whole, which is shorter than its diff:
```python
import functools

import jax
import jax.numpy as jnp
from jax import lax
from jax.experimental import pallas as pl
from jax.experimental.pallas import tpu as pltpu
from jax.sharding import PartitionSpec as P

HEADS = 8
EPS = 1e-05
F32 = jnp.float32
BF16 = jnp.bfloat16
NN = (((1,), (0,)), ((), ()))
NT = (((1,), (1,)), ((), ()))
VMEM_LIMIT = 20 * 1024 * 1024


def mm(a, b, dims=NN):
    return lax.dot_general(a, b, dims, preferred_element_type=F32)


def cols(start, count=1, tile=128):
    return slice(start * tile, (start + count) * tile)


def call(kernel, name, outs, args, scratch=(), smem=0):
    vmem = pl.BlockSpec(memory_space=pltpu.VMEM)
    scalars = pl.BlockSpec(memory_space=pltpu.SMEM)
    return pl.pallas_call(
        kernel,
        in_specs=[scalars] * smem + [vmem] * (len(args) - smem),
        out_specs=[vmem] * len(outs),
        out_shape=[jax.ShapeDtypeStruct(shape, dtype) for shape, dtype in outs],
        scratch_shapes=[pltpu.VMEM(shape, dtype) for shape, dtype in scratch],
        compiler_params=pltpu.CompilerParams(vmem_limit_bytes=VMEM_LIMIT),
        cost_estimate=pl.CostEstimate(flops=1, bytes_accessed=1, transcendentals=0),
        name=name,
    )(*args)


def odd_device():
    return lax.rem(lax.axis_index("dom"), 2) == 1


def halves(pair, hdim):
    zero = jnp.zeros((hdim, pair.shape[1]), pair.dtype)
    return jnp.concatenate(
        [
            jnp.concatenate([pair[:hdim], zero], axis=0),
            jnp.concatenate([zero, pair[hdim:]], axis=0),
        ],
        axis=1,
    )


def normalize(rows):
    xf = rows.astype(F32)
    cent = xf - jnp.mean(xf, axis=-1, keepdims=True)
    rstd = lax.rsqrt(jnp.mean(cent * cent, axis=-1, keepdims=True) + EPS)
    return cent * rstd, rstd


def project_tile(t, tile, scale, rows, w_qkv, xn_t, inv, k_nat, v_nat, k_t, v_t):
    width = rows.shape[1]
    here = cols(t, tile=tile)
    xhat, rstd = normalize(rows)
    xn = xhat.astype(BF16)
    xn_t[:, here] = xhat.T.astype(BF16)
    inv[:, here] = jnp.broadcast_to(rstd, (tile, 128)).T[0:8, :]
    keyval = mm(xn, w_qkv[:, width:])
    k_t[:, here] = (keyval[:, :width].T * scale).astype(BF16)
    v_t[:, here] = keyval[:, width:].T.astype(BF16)
    k_nat[here, :] = keyval[:, :width].astype(BF16)
    v_nat[here, :] = keyval[:, width:].astype(BF16)
    return xn


def pick_kernel(tile, x, x_on, x_off):
    odd = odd_device()
    low, high = x[:tile, :].astype(F32), x[x.shape[0] - tile :, :].astype(F32)
    x_on[...] = jnp.where(odd, low, high).astype(BF16)
    x_off[...] = jnp.where(odd, high, low).astype(BF16)


def prelude_own_kernel(blk, tile, scale, x, w_qkv, xn_t, inv, k_nat, v_nat, k_t, v_t, q_t):
    width = x.shape[1]
    for b in range(blk):
        own = cols(b, tile=tile)
        xn = project_tile(
            b, tile, scale, x[own, :], w_qkv, xn_t, inv, k_nat, v_nat, k_t, v_t
        )
        q_t[:, own] = (mm(xn, w_qkv[:, :width]).T * scale).astype(BF16)


def prelude_kernel(
    blk, tile, scale, neighbours, x_on, x_off, w_qkv, xn_own, inv_own, k_own, v_own, kt_own, vt_own, q_t,
    top, xn_t, inv, v_nat, k_t, probs, attn_t, g_t, k_nat, v_t, scores,
):
    width = x_on.shape[1]
    hdim = width // HEADS
    ours = cols(1, blk, tile)
    xn_t[:, ours] = xn_own[...]
    inv[:, ours] = inv_own[...]
    k_nat[ours, :] = k_own[...]
    v_nat[ours, :] = v_own[...]
    k_t[:, ours] = kt_own[...]
    v_t[:, ours] = vt_own[...]
    is_last = lax.axis_index("section") == lax.axis_size("section") - 1
    for b in range(blk):
        own = cols(b, tile=tile)
        g_t[:, own] = jnp.where(is_last, top[own, :].astype(F32).T, 0.0).astype(BF16)
    odd = odd_device()
    x_lo = jnp.where(odd, x_on[...], x_off[...])
    x_hi = jnp.where(odd, x_off[...], x_on[...])
    for t, rows in ((0, x_lo), (blk + 1, x_hi)):
        project_tile(t, tile, scale, rows, w_qkv, xn_t, inv, k_nat, v_nat, k_t, v_t)
    blocks = blk * lax.axis_size("dom")
    for b in range(blk):
        mine = lax.axis_index("dom") * blk + b
        below, above = lax.rem(mine + blocks - 1, blocks), lax.rem(mine + 1, blocks)
        has_lo = has_hi = False
        for j in range(1, neighbours.shape[1]):
            has_lo |= neighbours[b, j] == below
            has_hi |= neighbours[b, j] == above
        for i in range(HEADS // 2):
            lanes = cols(i, tile=2 * hdim)
            q = halves(q_t[lanes, cols(b, tile=tile)], hdim)
            s = mm(k_nat[cols(b, 3, tile), lanes], q)
            scores[i, b] = jnp.concatenate(
                [
                    jnp.where(has_lo, s[:tile], -1e30),
                    s[tile : 2 * tile],
                    jnp.where(has_hi, s[2 * tile :], -1e30),
                ],
                axis=0,
            )
    for b in range(blk):
        for i in range(HEADS // 2):
            s = scores[i, b]
            e = jnp.exp(s - jnp.max(s, axis=0, keepdims=True))
            probs[i, b] = (e * (1.0 / jnp.sum(e, axis=0, keepdims=True))).astype(BF16)
    for b in range(blk):
        for h in range(HEADS):
            head = cols(h, tile=hdim)
            p = probs[h // 2, b, :, cols(h % 2, tile=tile)]
            attn_t[head, cols(b, tile=tile)] = mm(v_t[head, cols(b, 3, tile)], p).astype(BF16)


def arrive(blk, tile, g_prev, rest, one, g_t):
    odd = odd_device()
    for b in range(blk):
        own = cols(b, tile=tile)
        if b == 0:
            part = jnp.where(odd, rest[:, :tile], one[...])
        elif b == blk - 1:
            part = jnp.where(odd, one[...], rest[:, cols(b - 1, tile=tile)])
        else:
            part = jnp.where(odd, rest[:, own], rest[:, cols(b - 1, tile=tile)])
        g_t[:, own] = (g_prev[:, own].astype(F32) + part.astype(F32)).astype(BF16)


def score_grad(i, b, first, count, tile, hdim, v_nat, probs, attn_t, da_t):
    lanes, own = cols(i, tile=2 * hdim), cols(b, tile=tile)
    da = da_t[lanes, own]
    prod = da.astype(F32) * attn_t[lanes, own].astype(F32)
    total = jnp.concatenate(
        [
            jnp.sum(prod[:hdim], axis=0, keepdims=True),
            jnp.sum(prod[hdim:], axis=0, keepdims=True),
        ],
        axis=1,
    )
    dp = mm(v_nat[cols(b + first, count, tile), lanes], halves(da, hdim))
    return (probs[i, b, cols(first, count, tile), :].astype(F32) * (dp - total)).astype(BF16)


def score_grads(blk, tile, hdim, v_nat, probs, attn_t, da_t, ds):
    for b in range(blk):
        for i in range(HEADS // 2):
            ds[i, b] = score_grad(i, b, 0, 3, tile, hdim, v_nat, probs, attn_t, da_t)


def rim_terms(blk, tile, hdim, v_nat, probs, attn_t, q_t, da_t, d_kv):
    width = q_t.shape[0]
    sides = ((0, 0, 0), (1, blk - 1, 2))
    ds = {
        (side, i): score_grad(i, b, j, 1, tile, hdim, v_nat, probs, attn_t, da_t)
        for side, b, j in sides
        for i in range(HEADS // 2)
    }
    for side, b, j in sides:
        own, near, here = cols(b, tile=tile), cols(j, tile=tile), cols(side, tile=tile)
        for i in range(HEADS // 2):
            lanes = cols(i, tile=2 * hdim)
            after = slice(width + i * 2 * hdim, width + (i + 1) * 2 * hdim)
            d_kv[lanes, here] = mm(halves(q_t[lanes, own], hdim), ds[side, i], NT).astype(BF16)
            d_kv[after, here] = mm(
                halves(da_t[lanes, own], hdim), probs[i, b, near, :], NT
            ).astype(BF16)


def value_terms(blk, tile, hdim, first, last, da_t, probs, d_v):
    for i in range(HEADS // 2):
        lanes = cols(i, tile=2 * hdim)
        dv = [None] * (blk + 2)
        for b in range(blk):
            low, high = max(b, first), min(b + 3, last + 1)
            near = slice((low - b) * tile, (high - b) * tile)
            part = mm(halves(da_t[lanes, cols(b, tile=tile)], hdim), probs[i, b, near, :], NT)
            for t in range(low, high):
                more = part[:, cols(t - low, tile=tile)]
                dv[t] = more if dv[t] is None else dv[t] + more
        for t in range(first, last + 1):
            d_v[lanes, cols(t - first, tile=tile)] = dv[t].astype(BF16)


def query_key_terms(blk, tile, hdim, first, last, q_t, k_t, ds, d_qk):
    width = q_t.shape[0]
    for i in range(HEADS // 2):
        lanes = cols(i, tile=2 * hdim)
        dk = [None] * (blk + 2)
        for b in range(blk):
            low, high = max(b, first), min(b + 3, last + 1)
            near = slice((low - b) * tile, (high - b) * tile)
            part = mm(halves(q_t[lanes, cols(b, tile=tile)], hdim), ds[i, b, near, :], NT)
            for t in range(low, high):
                more = part[:, cols(t - low, tile=tile)]
                dk[t] = more if dk[t] is None else dk[t] + more
            for h in (2 * i, 2 * i + 1):
                head = cols(h, tile=hdim)
                d_qk[head, cols(b + 1 - first, tile=tile)] = mm(
                    k_t[head, cols(b, 3, tile)], ds[i, b, :, cols(h % 2, tile=tile)]
                ).astype(BF16)
        for t in range(first, last + 1):
            d_qk[width + i * 2 * hdim : width + (i + 1) * 2 * hdim, cols(t - first, tile=tile)] = dk[
                t
            ].astype(BF16)


def norm_grad(dn, xn, rstd):
    xhat = xn.astype(F32)
    first = jnp.mean(dn, axis=0, keepdims=True)
    second = jnp.mean(dn * xhat, axis=0, keepdims=True)
    return rstd * (dn - first - xhat * second)


def stage_rim_kernel(blk, tile, moved, *refs):
    if moved:
        g_prev, rest, one, *refs = refs
        *refs, g, da_t, c_on, c_off, d_rim = refs
        arrive(blk, tile, g_prev, rest, one, g)
    else:
        g, *refs = refs
        *refs, da_t, c_on, c_off, d_rim = refs
    w_qkv, w_out, xn_t, inv, v_nat, q_t, probs, attn_t = refs
    width = g.shape[0]
    hdim = width // HEADS
    da_t[...] = mm(w_out[...], g[...]).astype(BF16)
    rim_terms(blk, tile, hdim, v_nat, probs, attn_t, q_t, da_t, d_rim)
    dn = mm(w_qkv[:, width:], d_rim[...])
    c_lo, c_hi = (
        norm_grad(dn[:, cols(side, tile=tile)], xn_t[:, cols(t, tile=tile)], inv[0:1, cols(t, tile=tile)])
        for side, t in ((0, 0), (1, blk + 1))
    )
    odd = odd_device()
    c_on[...] = jnp.where(odd, c_lo, c_hi).astype(BF16)
    c_off[...] = jnp.where(odd, c_hi, c_lo).astype(BF16)


def stage_main_kernel(
    blk, tile, g_t, da_t, w_qkv, xn_t, inv, v_nat, k_t, q_t, probs, attn_t, rest, one, ds, d_qkv
):
    width = g_t.shape[0]
    hdim = width // HEADS
    score_grads(blk, tile, hdim, v_nat, probs, attn_t, da_t, ds)
    query_key_terms(blk, tile, hdim, 1, blk, q_t, k_t, ds, d_qkv)
    value_terms(blk, tile, hdim, 1, blk, da_t, probs, d_qkv.at[2 * width :])
    dn = mm(w_qkv[...], d_qkv[...])
    y = []
    for b in range(blk):
        own, here = cols(b, tile=tile), cols(b + 1, tile=tile)
        out = norm_grad(dn[:, own], xn_t[:, here], inv[0:1, here])
        y.append(g_t[:, own].astype(F32) + out)
    odd = odd_device()
    one[...] = jnp.where(odd, y[-1], y[0]).astype(BF16)
    for b in range(blk - 1):
        rest[:, cols(b, tile=tile)] = jnp.where(odd, y[b], y[b + 1]).astype(BF16)


def add_on_kernel(tile, rest, on, out):
    odd = odd_device()
    tiles = rest.shape[1] // tile
    out[...] = rest[...]
    for b, here in ((0, odd), (tiles - 1, jnp.logical_not(odd))):
        own = cols(b, tile=tile)
        more = jnp.where(here, on[...].astype(F32), 0.0)
        out[:, own] = (out[:, own].astype(F32) + more).astype(BF16)


def add_off_kernel(one, off, out):
    out[...] = (one[...].astype(F32) + off[...].astype(F32)).astype(BF16)


def last_terms_kernel(
    blk, tile, chips, g_prev, rest, one, w_out, v_nat, k_t, q_t, probs, attn_t, xn_t,
    g_t, d_qkv, *refs
):
    *give, da_t, ds = refs
    width = g_prev.shape[0]
    hdim = width // HEADS
    arrive(blk, tile, g_prev, rest, one, g_t)
    da_t[...] = mm(w_out[...], g_t[...]).astype(BF16)
    score_grads(blk, tile, hdim, v_nat, probs, attn_t, da_t, ds)
    value_terms(blk, tile, hdim, 0, blk + 1, da_t, probs, d_qkv.at[2 * width :])
    for t in (0, blk + 1):
        d_qkv[:width, cols(t, tile=tile)] = jnp.zeros((width, tile), BF16)
    query_key_terms(blk, tile, hdim, 0, blk + 1, q_t, k_t, ds, d_qkv)
    if give:
        give_rows(chips, [(xn_t, d_qkv), (attn_t, g_t)], *give)


def last_input_kernel(blk, tile, after, g_t, d_qkv, w_qkv, xn_t, inv, y, c_on, c_off):
    dn = mm(w_qkv[...], d_qkv[...])
    outs = [
        norm_grad(dn[:, cols(t, tile=tile)], xn_t[:, cols(t, tile=tile)], inv[0:1, cols(t, tile=tile)])
        for t in range(blk + 2)
    ]
    odd = odd_device()
    c_on[...] = jnp.where(odd, outs[0], outs[-1]).astype(BF16)
    c_off[...] = jnp.where(odd, outs[-1], outs[0]).astype(BF16)
    for b in range(blk):
        own = cols(b, tile=tile)
        y[:, own] = (g_t[:, own].astype(F32) + outs[b + 1]).astype(BF16)


def finish_input_kernel(blk, tile, y_t, on, off, out):
    odd = odd_device()
    from_prev, from_next = jnp.where(odd, on[...], off[...]), jnp.where(odd, off[...], on[...])
    for b in range(blk):
        own = cols(b, tile=tile)
        part = y_t[:, own].astype(F32)
        if b == 0:
            part = part + from_prev.astype(F32)
        if b == blk - 1:
            part = part + from_next.astype(F32)
        out[own, :] = part.T.astype(BF16)


def weight_rows(core, chips, terms):
    def picked(ref):
        rows = ref.shape[0] // (2 * chips)
        starts = [pl.multiple_of((2 * z + core) * rows, rows) for z in range(chips)]
        return jnp.concatenate([ref[pl.ds(s, rows), :] for s in starts], axis=0)

    return [mm(picked(left), right[...], NT) for left, right in terms]


def give_rows(chips, terms, out):
    core = 1 - lax.rem(lax.axis_index("dom"), 2)
    rows, start = out.shape[1], 0
    for part in weight_rows(core, chips, terms):
        across = slice(start, start + part.shape[1])
        for z in range(chips):
            out[z, :, across] = part[z * rows : (z + 1) * rows].astype(BF16)
        start += part.shape[1]


def keep_kernel(chips, steps, got, xn_t, d_qkv, attn_t, g_t, *refs):
    *outs, both = refs
    me = lax.axis_index("dom")
    chip = me // 2
    rows, start = got.shape[1], 0
    for part in weight_rows(lax.rem(me, 2), chips, [(xn_t, d_qkv), (attn_t, g_t)]):
        across = slice(start, start + part.shape[1])
        for z in range(chips):
            both[z, :, across] = part[z * rows : (z + 1) * rows] + got[z, :, across].astype(F32)
        start += part.shape[1]
    half = got.shape[2] // 2
    for n, (first, second) in enumerate(steps):
        give, own = outs[2 * n : 2 * n + 2]
        across = slice(n * half, (n + 1) * half)
        give[0] = both[lax.bitwise_xor(chip, first), :, across].astype(BF16)
        give[1] = both[lax.bitwise_xor(chip, first ^ second), :, across].astype(BF16)
        own[0] = both[chip, :, across]
        own[1] = both[lax.bitwise_xor(chip, second), :, across]


def middle_kernel(own_a, got_a, own_b, got_b, *refs):
    give_a, rest_a, give_b, rest_b = refs[-4:]
    for own, got, give, rest in ((own_b, got_b, give_b, rest_b), (own_a, got_a, give_a, rest_a)):
        rest[...] = own[0] + got[0].astype(F32)
        give[...] = (own[1] + got[1].astype(F32)).astype(BF16)


def total_kernel(rest_a, got_a, rest_b, got_b, qkv_grad, out_grad):
    width = out_grad.shape[1]
    qkv_grad[:, : 2 * width] = rest_a[...] + got_a[...].astype(F32)
    total = rest_b[...] + got_b[...].astype(F32)
    qkv_grad[:, 2 * width :] = total[:, :width]
    out_grad[...] = total[:, width:]


def ring(parts, distance):
    return [(i, (i + distance) % parts) for i in range(parts)]


def other_core(parts):
    return [(i, i ^ 1) for i in range(parts)]


def next_chip(parts):
    return [(i, (i + 1 if i % 2 else i - 1) % parts) for i in range(parts)]


def chips_apart(parts, step):
    return [(i, i ^ (2 * step)) for i in range(parts)]


def local(layer_inputs, top_grad, w_qkv, w_out, neighbours):
    sections = lax.axis_size("section")
    parts = lax.axis_size("dom")
    blk = neighbours.shape[0]
    rows, width = top_grad.shape[1:]
    tile = rows // blk
    ext = rows + 2 * tile
    hdim = width // HEADS
    scale = 1.0 / hdim**0.5
    x = layer_inputs[0, 0]
    w_in, w_back = w_qkv[0], w_out[0]
    x_on, x_off = call(
        functools.partial(pick_kernel, tile), "pick", [((tile, width), BF16)] * 2, [x]
    )
    x_on = lax.ppermute(x_on, "dom", other_core(parts))
    x_off = lax.ppermute(x_off, "dom", next_chip(parts))
    *kept, q_t = call(
        functools.partial(prelude_own_kernel, blk, tile, scale), "prelude_own",
        [
            ((width, rows), BF16), ((8, rows), F32), ((rows, width), BF16), ((rows, width), BF16),
            ((width, rows), BF16), ((width, rows), BF16), ((width, rows), BF16),
        ],
        [x, w_in],
    )
    pair_shape = (HEADS // 2, blk, 3 * tile, 2 * tile)
    xn_t, inv, v_nat, k_t, probs, attn_t, g_t = call(
        functools.partial(prelude_kernel, blk, tile, scale), "prelude",
        [
            ((width, ext), BF16), ((8, ext), F32), ((ext, width), BF16), ((width, ext), BF16),
            (pair_shape, BF16), ((width, rows), BF16), ((width, rows), BF16),
        ],
        [neighbours, x_on, x_off, w_in, *kept, q_t, top_grad[0]],
        scratch=[((ext, width), BF16), ((width, ext), BF16), (pair_shape, F32)], smem=1,
    )
    received = []
    for k in range(sections - 1):
        here = sections - 1 - k
        *new, da_t, c_on, c_off = call(
            functools.partial(stage_rim_kernel, blk, tile, k > 0), "stage_rim",
            [((width, rows), BF16)] * (1 + (k > 0)) + [((width, tile), BF16)] * 2,
            [g_t, *received, w_in, w_back, xn_t, inv, v_nat, q_t, probs, attn_t],
            scratch=[((2 * width, 2 * tile), BF16)],
        )
        if new:
            g_t = new[0]
        off = lax.ppermute(c_off, "dom", next_chip(parts))
        on = lax.ppermute(c_on, "dom", other_core(parts))
        rest, one = call(
            functools.partial(stage_main_kernel, blk, tile), "stage_main",
            [((width, rows - tile), BF16), ((width, tile), BF16)],
            [g_t, da_t, w_in, xn_t, inv, v_nat, k_t, q_t, probs, attn_t],
            scratch=[(pair_shape, BF16), ((3 * width, rows), BF16)],
        )
        rest = call(
            functools.partial(add_on_kernel, tile), "add_on", [((width, rows - tile), BF16)], [rest, on]
        )[0]
        one = call(add_off_kernel, "add_off", [((width, tile), BF16)], [one, off])[0]
        received = [lax.ppermute(part, "section", [(here, here - 1)]) for part in (rest, one)]
    direct = parts == 8
    chips = parts // 2
    every = 4 * width
    row = width // parts
    g_t, d_qkv, *give = call(
        functools.partial(last_terms_kernel, blk, tile, chips), "last_terms",
        [((width, rows), BF16), ((3 * width, ext), BF16)] + [((chips, row, every), BF16)] * direct,
        [g_t, *received, w_back, v_nat, k_t, q_t, probs, attn_t, xn_t],
        scratch=[((width, rows), BF16), (pair_shape, BF16)],
    )
    after = d_qkv
    if direct:
        got = lax.ppermute(give[0], "dom", other_core(parts))
        steps = ((1, 2), (2, 1))
        give_a, own_a, give_b, own_b = call(
            functools.partial(keep_kernel, chips, steps), "keep",
            [((2, row, every // 2), BF16), ((2, row, every // 2), F32)] * 2,
            [got, xn_t, d_qkv, attn_t, g_t], scratch=[((chips, row, every), F32)],
        )
        got_b = lax.ppermute(give_b, "dom", chips_apart(parts, steps[1][0]))
        got_a = lax.ppermute(give_a, "dom", chips_apart(parts, steps[0][0]))
        after = own_a
    y, c_on, c_off = call(
        functools.partial(last_input_kernel, blk, tile), "last_input",
        [((width, rows), BF16), ((width, tile), BF16), ((width, tile), BF16)],
        [after, g_t, d_qkv, w_in, xn_t, inv],
    )
    off = lax.ppermute(c_off, "dom", next_chip(parts))
    on = lax.ppermute(c_on, "dom", other_core(parts))
    if direct:
        give_a, rest_a, give_b, rest_b = call(
            middle_kernel, "middle", [((row, every // 2), BF16), ((row, every // 2), F32)] * 2,
            [own_a, got_a, own_b, got_b, on, off],
        )
        got_b = lax.ppermute(give_b, "dom", chips_apart(parts, steps[1][1]))
        got_a = lax.ppermute(give_a, "dom", chips_apart(parts, steps[0][1]))
    y = call(
        functools.partial(finish_input_kernel, blk, tile), "finish_input", [((rows, width), BF16)],
        [y, on, off],
    )[0]
    if direct:
        qkv_grad, out_grad = call(
            total_kernel, "total", [((row, 3 * width), F32), ((row, width), F32)],
            [rest_a, got_a, rest_b, got_b],
        )
    else:
        term = jnp.concatenate([mm(xn_t, d_qkv, NT), mm(attn_t, g_t, NT)], axis=1)
        total = lax.psum_scatter(term, "dom", scatter_dimension=0, tiled=True)
        qkv_grad, out_grad = total[:, : 3 * width], total[:, 3 * width :]
    return (y[None, None], qkv_grad[None], out_grad[None])


def solution(mesh):
    placed = (
        P("section", None, "dom", None),
        P(None, "dom", None),
        P("section", None, None),
        P("section", None, None),
        P("dom", None),
    )
    return jax.shard_map(
        local,
        mesh=mesh,
        in_specs=placed,
        out_specs=(
            P("section", None, "dom", None),
            P("section", "dom", None),
            P("section", "dom", None),
        ),
        check_vma=False,
    )
```

time: 110 us -> 107 us (0.973)
  the two profiles are of different devices: /device:TPU:9 before, /device:TPU:0 now
where the time goes in v3:
time: 107 us
  waiting for transfers between devices  46.9 us (44%)
  Pallas kernels  30.9 us (29%)
  starting transfers between devices  25.7 us (24%)
  local copies, waits for them, and re-layouts  2.41 us (2%)
    pallas_call x21, Pallas kernels, call(): pl.pallas_call(kernel, in_specs=[scalars] * smem + [vmem] * (len(args) -...  30.9 us
    ppermute x6, waiting for transfers between devices, local(): lax.ppermute(part, 'section', [(here, here - 1)])  27.8 us
    ppermute x4, waiting for transfers between devices, local(): off = lax.ppermute(c_off, 'dom', next_chip(parts))  11.6 us
    ppermute x4, starting transfers between devices, local(): off = lax.ppermute(c_off, 'dom', next_chip(parts))  8.34 us
    ppermute x6, starting transfers between devices, local(): lax.ppermute(part, 'section', [(here, here - 1)])  5.68 us
    ppermute x1, starting transfers between devices, local(): x_off = lax.ppermute(x_off, 'dom', next_chip(parts))  4.71 us
    ppermute x1, waiting for transfers between devices, local(): got_a = lax.ppermute(give_a, 'dom', chips_apart(parts, steps[0][1]))  4.1 us
    ppermute x1, waiting for transfers between devices, local(): got = lax.ppermute(give[0], 'dom', other_core(parts))  2.65 us
  transfers between devices with their start and end apart: 21, of which 8 were waited for; matrix products, arithmetic and copies ran while one was open for 0% of the time, Pallas kernels for 14%

profile of v3, /device:TPU:0, one launch (start us, length us, event | category | flops | bytes accessed | tf_op | source)
XLA Modules:
  0.0 106.9 jit_solution(8211497447224328037)
XLA Ops:
  0.6 0.0 copy-start.3
  0.6 1.0 copy-done.3
  1.6 0.1 pick.1
  1.7 0.5 collective-permute-start
  2.2 4.7 %collective-permute-start.1 = (bf16[128,512]{1,0:T(8,128)(2,1)S(1)}, bf16[128,512]{1,0:T(8,128)(2,1)S(1)}, u32[]{:S(2)}, u32[]{:S(2)}) collective-permute-start(bf16[128,512]{1,0:T(8,128)(2,1)S(1)} %get-tuple-element.53), channel_id=1, source_target_pairs={{0,7},{1,2},{2,1},{3,4},{4,3},{5,6},{6,5},{7,0},{8,15},{9,10},{10,... | collective-permute-start | bytes 393224 | tf_op jit(solution)/shard_map/ppermute | solution.py:435
  6.9 1.4 %copy-done = bf16[1,512,1536]{2,1,0:T(8,128)(2,1)S(1)} copy-done((bf16[1,512,1536]{2,1,0:T(8,128)(2,1)S(1)}, bf16[1,512,1536]{2,1,0:T(8,128)(2,1)}, u32[]{:S(2)}) %copy-start) | copy-done | bytes 1572888
  8.3 1.2 %prelude_own.1 = (bf16[512,384]{1,0:T(8,128)(2,1)S(1)}, f32[8,384]{1,0:T(8,128)S(1)}, bf16[384,512]{1,0:T(8,128)(2,1)S(1)}, bf16[384,512]{1,0:T(8,128)(2,1)S(1)}...) custom-call(bf16[384,512]{1,0:T(8,128)(2,1)S(1)} %bitcast.21, ...), custom_call_target="tpu_custom_call" | custom-call | flops 1 | bytes 1 | tf_op jit(solution)/shard_map/prelude_own/pallas_call | solution.py:30
  9.6 0.0 collective-permute-done.x_on
  9.6 0.7 collective-permute-done.1.x_off
  10.3 0.0 copy-start.2
  10.3 3.4 %prelude.1 = (bf16[512,640]{1,0:T(8,128)(2,1)S(1)}, f32[8,640]{1,0:T(8,128)S(1)}, bf16[640,512]{1,0:T(8,128)(2,1)S(1)}, bf16[512,640]{1,0:T(8,128)(2,1)S(1)}, bf...) custom-call(s32[3,3]{1,0:T(4,128)S(1)} %copy-done.5, ...), custom_call_target="tpu_custom_call" | custom-call | flops 1 | bytes 1 | tf_op jit(solution)/shard_map/prelude/pallas_call | solution.py:30
  13.8 2.0 %stage_rim.3 = (bf16[512,384]{1,0:T(8,128)(2,1)S(1)}, bf16[512,128]{1,0:T(8,128)(2,1)S(1)}, bf16[512,128]{1,0:T(8,128)(2,1)S(1)}) custom-call(bf16[512,384]{1,0:T(8,128)(2,1)S(1)} %get-tuple-element.61.refs_0_.g_t, bf16[512,1536]{1,0:T(8,128)(2,1)S(1)} %bitcast.9, bf16[512,512]{1,0:T(8,128)(2,1)S(1)} %bitcast.16, ...), custom_call_target="tpu_custom_call" | custom-call | flops 1 | bytes 1 | tf_op jit(solution)/shard_map/stage_rim/pallas_call | solution.py:30
  15.8 0.1 collective-permute-start.2
  15.9 2.9 %collective-permute-start.4 = (bf16[512,128]{1,0:T(8,128)(2,1)S(1)}, bf16[512,128]{1,0:T(8,128)(2,1)S(1)}, u32[]{:S(2)}, u32[]{:S(2)}) collective-permute-start(bf16[512,128]{1,0:T(8,128)(2,1)S(1)} %get-tuple-element.72), channel_id=1, source_target_pairs={{0,7},{1,2},{2,1},{3,4},{4,3},{5,6},{6,5},{7,0},{8,15},{9,10},{10,... | collective-permute-start | bytes 393224 | tf_op jit(solution)/shard_map/ppermute | solution.py:465
  18.8 3.5 %stage_main.3 = (bf16[512,256]{1,0:T(8,128)(2,1)S(1)}, bf16[512,128]{1,0:T(8,128)(2,1)S(1)}) custom-call(bf16[512,384]{1,0:T(8,128)(2,1)S(1)} %get-tuple-element.61.refs_0_.g_t, bf16[512,384]{1,0:T(8,128)(2,1)S(1)} %get-tuple-element.67.da_t, bf16[512,1536]{1,0:T(8,128)(2,1)S(1)} %bitcast.10, bf16[512,640]{1,0:T(8,128)(2,1)S(1)} %get-tuple-element.62.refs_3_.xn_t.refs_5_, ...), custom_call_target="tpu_custom_call" | custom-call | flops 1 | bytes 1 | tf_op jit(solution)/shard_map/stage_main/pallas_call | solution.py:30
  22.3 0.0 collective-permute-done.2.on
  22.3 0.1 add_on.3
  22.5 0.7 collective-permute-start.3
  23.2 0.3 collective-permute-done.4.off
  23.5 0.8 collective-permute-start.5
  24.4 0.0 collective-permute-done.5.refs_2_
  24.4 0.0 collective-permute-done.3.refs_1_
  24.4 2.1 %stage_rim.4 = (bf16[512,384]{1,0:T(8,128)(2,1)S(1)}, bf16[512,384]{1,0:T(8,128)(2,1)S(1)}, bf16[512,128]{1,0:T(8,128)(2,1)S(1)}, bf16[512,128]{1,0:T(8,128)(2,1)S(1)}) custom-call(bf16[512,384]{1,0:T(8,128)(2,1)S(1)} %get-tuple-element.61.refs_0_.g_t, bf16[512,256]{1,0:T(8,128)(2,1)S(1)} %collective-permute-done.3.refs_1_, ...), custom_call_target="tpu_custom_call" | custom-call | flops 1 | bytes 1 | tf_op jit(solution)/shard_map/stage_rim/pallas_call | solution.py:30
  26.5 0.1 collective-permute-start.6
  26.6 1.6 %collective-permute-start.8 = (bf16[512,128]{1,0:T(8,128)(2,1)S(1)}, bf16[512,128]{1,0:T(8,128)(2,1)S(1)}, u32[]{:S(2)}, u32[]{:S(2)}) collective-permute-start(bf16[512,128]{1,0:T(8,128)(2,1)S(1)} %get-tuple-element.78), channel_id=1, source_target_pairs={{0,7},{1,2},{2,1},{3,4},{4,3},{5,6},{6,5},{7,0},{8,15},{9,10},{10,... | collective-permute-start | bytes 393224 | tf_op jit(solution)/shard_map/ppermute | solution.py:465
  28.2 3.5 %stage_main.4 = (bf16[512,256]{1,0:T(8,128)(2,1)S(1)}, bf16[512,128]{1,0:T(8,128)(2,1)S(1)}) custom-call(bf16[512,384]{1,0:T(8,128)(2,1)S(1)} %get-tuple-element.73.g_t.refs_0_, bf16[512,384]{1,0:T(8,128)(2,1)S(1)} %get-tuple-element.74.da_t, bf16[512,1536]{1,0:T(8,128)(2,1)S(1)} %bitcast.12, bf16[512,640]{1,0:T(8,128)(2,1)S(1)} %get-tuple-element.62.refs_3_.xn_t.refs_5_, ...), custom_call_target="tpu_custom_call" | custom-call | flops 1 | bytes 1 | tf_op jit(solution)/shard_map/stage_main/pallas_call | solution.py:30
  31.7 0.0 collective-permute-done.6.on
  31.7 0.1 add_on.4
  31.9 0.7 collective-permute-start.7
  32.5 0.4 collective-permute-done.8.off
  33.0 0.7 collective-permute-start.9
  33.7 0.0 collective-permute-done.9.refs_2_
  33.7 0.0 collective-permute-done.7.refs_1_
  33.7 2.1 %stage_rim.5 = (bf16[512,384]{1,0:T(8,128)(2,1)S(1)}, bf16[512,384]{1,0:T(8,128)(2,1)S(1)}, bf16[512,128]{1,0:T(8,128)(2,1)S(1)}, bf16[512,128]{1,0:T(8,128)(2,1)S(1)}) custom-call(bf16[512,384]{1,0:T(8,128)(2,1)S(1)} %get-tuple-element.73.g_t.refs_0_, bf16[512,256]{1,0:T(8,128)(2,1)S(1)} %collective-permute-done.7.refs_1_, ...), custom_call_target="tpu_custom_call" | custom-call | flops 1 | bytes 1 | tf_op jit(solution)/shard_map/stage_rim/pallas_call | solution.py:30
  35.8 0.1 collective-permute-start.10
  35.9 1.7 %collective-permute-start.12 = (bf16[512,128]{1,0:T(8,128)(2,1)S(1)}, bf16[512,128]{1,0:T(8,128)(2,1)S(1)}, u32[]{:S(2)}, u32[]{:S(2)}) collective-permute-start(bf16[512,128]{1,0:T(8,128)(2,1)S(1)} %get-tuple-element.84), channel_id=1, source_target_pairs={{0,7},{1,2},{2,1},{3,4},{4,3},{5,6},{6,5},{7,0},{8,15},{9,10},{10,... | collective-permute-start | bytes 393224 | tf_op jit(solution)/shard_map/ppermute | solution.py:465
  37.6 3.5 %stage_main.5 = (bf16[512,256]{1,0:T(8,128)(2,1)S(1)}, bf16[512,128]{1,0:T(8,128)(2,1)S(1)}) custom-call(bf16[512,384]{1,0:T(8,128)(2,1)S(1)} %get-tuple-element.79.g_t.g_prev, bf16[512,384]{1,0:T(8,128)(2,1)S(1)} %get-tuple-element.80.da_t, bf16[512,1536]{1,0:T(8,128)(2,1)S(1)} %bitcast.14, bf16[512,640]{1,0:T(8,128)(2,1)S(1)} %get-tuple-element.62.refs_3_.xn_t.refs_5_, ...), custom_call_target="tpu_custom_call" | custom-call | flops 1 | bytes 1 | tf_op jit(solution)/shard_map/stage_main/pallas_call | solution.py:30
  41.1 0.0 collective-permute-done.10.on
  41.1 0.1 add_on.5
  41.2 1.3 %collective-permute-start.11 = (bf16[512,256]{1,0:T(8,128)(2,1)S(1)}, bf16[512,256]{1,0:T(8,128)(2,1)S(1)}, u32[]{:S(2)}, u32[]{:S(2)}) collective-permute-start(bf16[512,256]{1,0:T(8,128)(2,1)S(1)} %add_on.5), channel_id=1, source_target_pairs={{8,0},{9,1},{10,2},{11,3},{12,4},{13,5},{14,6},{15,7}} | collective-permute-start | bytes 786440 | tf_op jit(solution)/shard_map/ppermute | solution.py:477
  42.5 0.0 collective-permute-done.12.off
  42.6 1.5 %collective-permute-start.13 = (bf16[512,128]{1,0:T(8,128)(2,1)S(1)}, bf16[512,128]{1,0:T(8,128)(2,1)S(1)}, u32[]{:S(2)}, u32[]{:S(2)}) collective-permute-start(bf16[512,128]{1,0:T(8,128)(2,1)S(1)} %add_off.5), channel_id=1, source_target_pairs={{8,0},{9,1},{10,2},{11,3},{12,4},{13,5},{14,6},{15,7}} | collective-permute-start | bytes 393224 | tf_op jit(solution)/shard_map/ppermute | solution.py:477
  44.1 27.8 %collective-permute-done.13.one = bf16[512,128]{1,0:T(8,128)(2,1)S(1)} collective-permute-done((bf16[512,128]{1,0:T(8,128)(2,1)S(1)}, bf16[512,128]{1,0:T(8,128)(2,1)S(1)}, u32[]{:S(2)}, u32[]{:S(2)}) %collective-permute-start.13) | collective-permute-done | bytes 131104 | tf_op jit(solution)/shard_map/ppermute | solution.py:477
  71.9 0.0 collective-permute-done.11.rest
  71.9 4.0 %last_terms.1 = (bf16[512,384]{1,0:T(8,128)(2,1)S(1)}, bf16[1536,640]{1,0:T(8,128)(2,1)S(1)}, bf16[4,64,2048]{2,1,0:T(8,128)(2,1)S(1)}) custom-call(bf16[512,384]{1,0:T(8,128)(2,1)S(1)} %get-tuple-element.79.g_t.g_prev, bf16[512,256]{1,0:T(8,128)(2,1)S(1)} %collective-permute-done.11.rest, bf16[512,128]{1,0:T(8,128)(2,1)S(1)} %collective-permute-done.13.one, ...), custom_call_target="tpu_custom_call" | custom-call | flops 1 | bytes 1 | tf_op jit(solution)/shard_map/last_terms/pallas_call | solution.py:30
  76.0 0.1 collective-permute-start.14
  76.0 2.6 %collective-permute-done.14.got = bf16[4,64,2048]{2,1,0:T(8,128)(2,1)S(1)} collective-permute-done((bf16[4,64,2048]{2,1,0:T(8,128)(2,1)S(1)}, bf16[4,64,2048]{2,1,0:T(8,128)(2,1)S(1)}, u32[]{:S(2)}, u32[]{:S(2)}) %collective-permute-start.14) | collective-permute-done | bytes 1048608 | tf_op jit(solution)/shard_map/ppermute | solution.py:490
  78.7 1.1 keep.1
  79.8 1.0 collective-permute-start.17
  80.7 1.4 %collective-permute-start.18 = (bf16[2,64,1024]{2,1,0:T(8,128)(2,1)S(1)}, bf16[2,64,1024]{2,1,0:T(8,128)(2,1)S(1)}, u32[]{:S(2)}, u32[]{:S(2)}) collective-permute-start(bf16[2,64,1024]{2,1,0:T(8,128)(2,1)S(1)} %get-tuple-element.94), channel_id=1, source_target_pairs={{0,4},{1,5},{2,6},{3,7},{4,0},{5,1},{6,2},{7,3},{8,12},{9,13},{10,... | collective-permute-start | bytes 786440 | tf_op jit(solution)/shard_map/ppermute | solution.py:497
  82.2 1.8 %last_input.1 = (bf16[512,384]{1,0:T(8,128)(2,1)S(1)}, bf16[512,128]{1,0:T(8,128)(2,1)S(1)}, bf16[512,128]{1,0:T(8,128)(2,1)S(1)}) custom-call(f32[2,64,1024]{2,1,0:T(8,128)S(1)} %get-tuple-element.88.after.own_a, bf16[512,384]{1,0:T(8,128)(2,1)S(1)} %get-tuple-element.87.g_t, bf16[1536,640]{1,0:T(8,128)(2,1)S(1)} %get-tuple-element.86.d_qkv, ...), custom_call_target="tpu_custom_call" | custom-call | flops 1 | bytes 1 | tf_op jit(solution)/shard_map/last_input/pallas_call | solution.py:30
  84.0 0.1 collective-permute-start.15
  84.1 2.2 %collective-permute-start.16 = (bf16[512,128]{1,0:T(8,128)(2,1)S(1)}, bf16[512,128]{1,0:T(8,128)(2,1)S(1)}, u32[]{:S(2)}, u32[]{:S(2)}) collective-permute-start(bf16[512,128]{1,0:T(8,128)(2,1)S(1)} %get-tuple-element.91), channel_id=1, source_target_pairs={{0,7},{1,2},{2,1},{3,4},{4,3},{5,6},{6,5},{7,0},{8,15},{9,10},{10,... | collective-permute-start | bytes 393224 | tf_op jit(solution)/shard_map/ppermute | solution.py:505
  86.2 0.0 collective-permute-done.15.on.refs_0_
  86.2 10.9 %collective-permute-done.16.off.refs_1_ = bf16[512,128]{1,0:T(8,128)(2,1)S(1)} collective-permute-done((bf16[512,128]{1,0:T(8,128)(2,1)S(1)}, bf16[512,128]{1,0:T(8,128)(2,1)S(1)}, u32[]{:S(2)}, u32[]{:S(2)}) %collective-permute-start.16) | collective-permute-done | bytes 131104 | tf_op jit(solution)/shard_map/ppermute | solution.py:505
  97.1 0.0 collective-permute-done.17.got_a
  97.1 0.0 collective-permute-done.18.got_b
  97.1 0.1 middle.1
  97.2 2.6 %collective-permute-start.19 = (bf16[64,1024]{1,0:T(8,128)(2,1)S(1)}, bf16[64,1024]{1,0:T(8,128)(2,1)S(1)}, u32[]{:S(2)}, u32[]{:S(2)}) collective-permute-start(bf16[64,1024]{1,0:T(8,128)(2,1)S(1)} %get-tuple-element.96), channel_id=1, source_target_pairs={{0,4},{1,5},{2,6},{3,7},{4,0},{5,1},{6,2},{7,3},{8,12},{9,13},{10,... | collective-permute-start | bytes 393224 | tf_op jit(solution)/shard_map/ppermute | solution.py:513
  99.8 1.1 %collective-permute-start.20 = (bf16[64,1024]{1,0:T(8,128)(2,1)S(1)}, bf16[64,1024]{1,0:T(8,128)(2,1)S(1)}, u32[]{:S(2)}, u32[]{:S(2)}) collective-permute-start(bf16[64,1024]{1,0:T(8,128)(2,1)S(1)} %get-tuple-element.98), channel_id=1, source_target_pairs={{0,2},{1,3},{2,0},{3,1},{4,6},{5,7},{6,4},{7,5},{8,10},{9,11},{10,... | collective-permute-start | bytes 393224 | tf_op jit(solution)/shard_map/ppermute | solution.py:512
  101.0 0.9 finish_input.1
  101.9 4.1 %collective-permute-done.19.got_a = bf16[64,1024]{1,0:T(8,128)(2,1)S(1)} collective-permute-done((bf16[64,1024]{1,0:T(8,128)(2,1)S(1)}, bf16[64,1024]{1,0:T(8,128)(2,1)S(1)}, u32[]{:S(2)}, u32[]{:S(2)}) %collective-permute-start.19) | collective-permute-done | bytes 131104 | tf_op jit(solution)/shard_map/ppermute | solution.py:513
  106.0 0.1 collective-permute-done.20.got_b
  106.1 0.8 total.1
  (11 shorter events, 0.1 us)
Async XLA Ops:
  0.6 1.0 copy-start.3
  1.6 8.7 %copy-start.4 = (bf16[1,384,512]{2,1,0:T(8,128)(2,1)S(1)}, bf16[1,384,512]{2,1,0:T(8,128)(2,1)}, u32[]{:S(2)}) copy-start(bf16[1,384,512]{2,1,0:T(8,128)(2,1)} %param.6) | copy-start | bytes 1179652
  1.6 8.7 %copy-start.5 = (s32[3,3]{1,0:T(4,128)S(1)}, s32[3,3]{1,0:T(4,128)}, u32[]{:S(2)}) copy-start(s32[3,3]{1,0:T(4,128)} %neighbours.1) | copy-start | bytes 112
  1.7 7.9 %collective-permute-start = (bf16[128,512]{1,0:T(8,128)(2,1)S(1)}, bf16[128,512]{1,0:T(8,128)(2,1)S(1)}, u32[]{:S(2)}, u32[]{:S(2)}) collective-permute-start(bf16[128,512]{1,0:T(8,128)(2,1)S(1)} %get-tuple-element.52), channel_id=1, source_target_pairs={{0,1},{1,0},{2,3},{3,2},{4,5},{5,4},{6,7},{7,6},{8,9},{9,8},{10,11... | collective-permute-start | bytes 393224 | tf_op jit(solution)/shard_map/ppermute | solution.py:434
  2.2 8.1 %collective-permute-start.1 = (bf16[128,512]{1,0:T(8,128)(2,1)S(1)}, bf16[128,512]{1,0:T(8,128)(2,1)S(1)}, u32[]{:S(2)}, u32[]{:S(2)}) collective-permute-start(bf16[128,512]{1,0:T(8,128)(2,1)S(1)} %get-tuple-element.53), channel_id=1, source_target_pairs={{0,7},{1,2},{2,1},{3,4},{4,3},{5,6},{6,5},{7,0},{8,15},{9,10},{10,... | collective-permute-start | bytes 393224 | tf_op jit(solution)/shard_map/ppermute | solution.py:435
  6.9 1.4 %copy-start = (bf16[1,512,1536]{2,1,0:T(8,128)(2,1)S(1)}, bf16[1,512,1536]{2,1,0:T(8,128)(2,1)}, u32[]{:S(2)}) copy-start(bf16[1,512,1536]{2,1,0:T(8,128)(2,1)} %param.7) | copy-start | bytes 4718596
  8.3 1.9 %copy-start.1 = (bf16[1,512,1536]{2,1,0:T(8,128)(2,1)S(1)}, bf16[1,512,1536]{2,1,0:T(8,128)(2,1)}, u32[]{:S(2)}) copy-start(bf16[1,512,1536]{2,1,0:T(8,128)(2,1)} %param.7) | copy-start | bytes 4718596
  10.3 3.5 %copy-start.2 = (bf16[1,512,512]{2,1,0:T(8,128)(2,1)S(1)}, bf16[1,512,512]{2,1,0:T(8,128)(2,1)}, u32[]{:S(2)}) copy-start(bf16[1,512,512]{2,1,0:T(8,128)(2,1)} %param.8) | copy-start | bytes 1572868
  15.8 6.5 %collective-permute-start.2 = (bf16[512,128]{1,0:T(8,128)(2,1)S(1)}, bf16[512,128]{1,0:T(8,128)(2,1)S(1)}, u32[]{:S(2)}, u32[]{:S(2)}) collective-permute-start(bf16[512,128]{1,0:T(8,128)(2,1)S(1)} %get-tuple-element.70), channel_id=1, source_target_pairs={{0,1},{1,0},{2,3},{3,2},{4,5},{5,4},{6,7},{7,6},{8,9},{9,8},{10,11... | collective-permute-start | bytes 393224 | tf_op jit(solution)/shard_map/ppermute | solution.py:466
  15.9 7.6 %collective-permute-start.4 = (bf16[512,128]{1,0:T(8,128)(2,1)S(1)}, bf16[512,128]{1,0:T(8,128)(2,1)S(1)}, u32[]{:S(2)}, u32[]{:S(2)}) collective-permute-start(bf16[512,128]{1,0:T(8,128)(2,1)S(1)} %get-tuple-element.72), channel_id=1, source_target_pairs={{0,7},{1,2},{2,1},{3,4},{4,3},{5,6},{6,5},{7,0},{8,15},{9,10},{10,... | collective-permute-start | bytes 393224 | tf_op jit(solution)/shard_map/ppermute | solution.py:465
  22.5 1.9 %collective-permute-start.3 = (bf16[512,256]{1,0:T(8,128)(2,1)S(1)}, bf16[512,256]{1,0:T(8,128)(2,1)S(1)}, u32[]{:S(2)}, u32[]{:S(2)}) collective-permute-start(bf16[512,256]{1,0:T(8,128)(2,1)S(1)} %add_on.3), channel_id=1, source_target_pairs={{24,16},{25,17},{26,18},{27,19},{28,20},{29,21},{30,22},{31,23}} | collective-permute-start | bytes 786440 | tf_op jit(solution)/shard_map/ppermute | solution.py:477
  23.5 0.9 collective-permute-start.5
  26.5 5.2 %collective-permute-start.6 = (bf16[512,128]{1,0:T(8,128)(2,1)S(1)}, bf16[512,128]{1,0:T(8,128)(2,1)S(1)}, u32[]{:S(2)}, u32[]{:S(2)}) collective-permute-start(bf16[512,128]{1,0:T(8,128)(2,1)S(1)} %get-tuple-element.76), channel_id=1, source_target_pairs={{0,1},{1,0},{2,3},{3,2},{4,5},{5,4},{6,7},{7,6},{8,9},{9,8},{10,11... | collective-permute-start | bytes 393224 | tf_op jit(solution)/shard_map/ppermute | solution.py:466
  26.6 6.4 %collective-permute-start.8 = (bf16[512,128]{1,0:T(8,128)(2,1)S(1)}, bf16[512,128]{1,0:T(8,128)(2,1)S(1)}, u32[]{:S(2)}, u32[]{:S(2)}) collective-permute-start(bf16[512,128]{1,0:T(8,128)(2,1)S(1)} %get-tuple-element.78), channel_id=1, source_target_pairs={{0,7},{1,2},{2,1},{3,4},{4,3},{5,6},{6,5},{7,0},{8,15},{9,10},{10,... | collective-permute-start | bytes 393224 | tf_op jit(solution)/shard_map/ppermute | solution.py:465
  31.9 1.8 %collective-permute-start.7 = (bf16[512,256]{1,0:T(8,128)(2,1)S(1)}, bf16[512,256]{1,0:T(8,128)(2,1)S(1)}, u32[]{:S(2)}, u32[]{:S(2)}) collective-permute-start(bf16[512,256]{1,0:T(8,128)(2,1)S(1)} %add_on.4), channel_id=1, source_target_pairs={{16,8},{17,9},{18,10},{19,11},{20,12},{21,13},{22,14},{23,15}} | collective-permute-start | bytes 786440 | tf_op jit(solution)/shard_map/ppermute | solution.py:477
  33.0 0.7 collective-permute-start.9
  35.8 5.3 %collective-permute-start.10 = (bf16[512,128]{1,0:T(8,128)(2,1)S(1)}, bf16[512,128]{1,0:T(8,128)(2,1)S(1)}, u32[]{:S(2)}, u32[]{:S(2)}) collective-permute-start(bf16[512,128]{1,0:T(8,128)(2,1)S(1)} %get-tuple-element.82), channel_id=1, source_target_pairs={{0,1},{1,0},{2,3},{3,2},{4,5},{5,4},{6,7},{7,6},{8,9},{9,8},{10,11... | collective-permute-start | bytes 393224 | tf_op jit(solution)/shard_map/ppermute | solution.py:466
  35.9 6.7 %collective-permute-start.12 = (bf16[512,128]{1,0:T(8,128)(2,1)S(1)}, bf16[512,128]{1,0:T(8,128)(2,1)S(1)}, u32[]{:S(2)}, u32[]{:S(2)}) collective-permute-start(bf16[512,128]{1,0:T(8,128)(2,1)S(1)} %get-tuple-element.84), channel_id=1, source_target_pairs={{0,7},{1,2},{2,1},{3,4},{4,3},{5,6},{6,5},{7,0},{8,15},{9,10},{10,... | collective-permute-start | bytes 393224 | tf_op jit(solution)/shard_map/ppermute | solution.py:465
  41.2 30.7 %collective-permute-start.11 = (bf16[512,256]{1,0:T(8,128)(2,1)S(1)}, bf16[512,256]{1,0:T(8,128)(2,1)S(1)}, u32[]{:S(2)}, u32[]{:S(2)}) collective-permute-start(bf16[512,256]{1,0:T(8,128)(2,1)S(1)} %add_on.5), channel_id=1, source_target_pairs={{8,0},{9,1},{10,2},{11,3},{12,4},{13,5},{14,6},{15,7}} | collective-permute-start | bytes 786440 | tf_op jit(solution)/shard_map/ppermute | solution.py:477
  42.6 29.3 %collective-permute-start.13 = (bf16[512,128]{1,0:T(8,128)(2,1)S(1)}, bf16[512,128]{1,0:T(8,128)(2,1)S(1)}, u32[]{:S(2)}, u32[]{:S(2)}) collective-permute-start(bf16[512,128]{1,0:T(8,128)(2,1)S(1)} %add_off.5), channel_id=1, source_target_pairs={{8,0},{9,1},{10,2},{11,3},{12,4},{13,5},{14,6},{15,7}} | collective-permute-start | bytes 393224 | tf_op jit(solution)/shard_map/ppermute | solution.py:477
  76.0 2.7 %collective-permute-start.14 = (bf16[4,64,2048]{2,1,0:T(8,128)(2,1)S(1)}, bf16[4,64,2048]{2,1,0:T(8,128)(2,1)S(1)}, u32[]{:S(2)}, u32[]{:S(2)}) collective-permute-start(bf16[4,64,2048]{2,1,0:T(8,128)(2,1)S(1)} %get-tuple-element.85), channel_id=1, source_target_pairs={{0,1},{1,0},{2,3},{3,2},{4,5},{5,4},{6,7},{7,6},{8,9},{9,8},{10,11... | collective-permute-start | bytes 3145736 | tf_op jit(solution)/shard_map/ppermute | solution.py:490
  79.8 17.3 %collective-permute-start.17 = (bf16[2,64,1024]{2,1,0:T(8,128)(2,1)S(1)}, bf16[2,64,1024]{2,1,0:T(8,128)(2,1)S(1)}, u32[]{:S(2)}, u32[]{:S(2)}) collective-permute-start(bf16[2,64,1024]{2,1,0:T(8,128)(2,1)S(1)} %get-tuple-element.92), channel_id=1, source_target_pairs={{0,2},{1,3},{2,0},{3,1},{4,6},{5,7},{6,4},{7,5},{8,10},{9,11},{10,... | collective-permute-start | bytes 786440 | tf_op jit(solution)/shard_map/ppermute | solution.py:498
  80.7 16.4 %collective-permute-start.18 = (bf16[2,64,1024]{2,1,0:T(8,128)(2,1)S(1)}, bf16[2,64,1024]{2,1,0:T(8,128)(2,1)S(1)}, u32[]{:S(2)}, u32[]{:S(2)}) collective-permute-start(bf16[2,64,1024]{2,1,0:T(8,128)(2,1)S(1)} %get-tuple-element.94), channel_id=1, source_target_pairs={{0,4},{1,5},{2,6},{3,7},{4,0},{5,1},{6,2},{7,3},{8,12},{9,13},{10,... | collective-permute-start | bytes 786440 | tf_op jit(solution)/shard_map/ppermute | solution.py:497
  84.0 2.2 %collective-permute-start.15 = (bf16[512,128]{1,0:T(8,128)(2,1)S(1)}, bf16[512,128]{1,0:T(8,128)(2,1)S(1)}, u32[]{:S(2)}, u32[]{:S(2)}) collective-permute-start(bf16[512,128]{1,0:T(8,128)(2,1)S(1)} %get-tuple-element.90), channel_id=1, source_target_pairs={{0,1},{1,0},{2,3},{3,2},{4,5},{5,4},{6,7},{7,6},{8,9},{9,8},{10,11... | collective-permute-start | bytes 393224 | tf_op jit(solution)/shard_map/ppermute | solution.py:506
  84.1 13.0 %collective-permute-start.16 = (bf16[512,128]{1,0:T(8,128)(2,1)S(1)}, bf16[512,128]{1,0:T(8,128)(2,1)S(1)}, u32[]{:S(2)}, u32[]{:S(2)}) collective-permute-start(bf16[512,128]{1,0:T(8,128)(2,1)S(1)} %get-tuple-element.91), channel_id=1, source_target_pairs={{0,7},{1,2},{2,1},{3,4},{4,3},{5,6},{6,5},{7,0},{8,15},{9,10},{10,... | collective-permute-start | bytes 393224 | tf_op jit(solution)/shard_map/ppermute | solution.py:505
  97.2 8.8 %collective-permute-start.19 = (bf16[64,1024]{1,0:T(8,128)(2,1)S(1)}, bf16[64,1024]{1,0:T(8,128)(2,1)S(1)}, u32[]{:S(2)}, u32[]{:S(2)}) collective-permute-start(bf16[64,1024]{1,0:T(8,128)(2,1)S(1)} %get-tuple-element.96), channel_id=1, source_target_pairs={{0,4},{1,5},{2,6},{3,7},{4,0},{5,1},{6,2},{7,3},{8,12},{9,13},{10,... | collective-permute-start | bytes 393224 | tf_op jit(solution)/shard_map/ppermute | solution.py:513
  99.8 6.3 %collective-permute-start.20 = (bf16[64,1024]{1,0:T(8,128)(2,1)S(1)}, bf16[64,1024]{1,0:T(8,128)(2,1)S(1)}, u32[]{:S(2)}, u32[]{:S(2)}) collective-permute-start(bf16[64,1024]{1,0:T(8,128)(2,1)S(1)} %get-tuple-element.98), channel_id=1, source_target_pairs={{0,2},{1,3},{2,0},{3,1},{4,6},{5,7},{6,4},{7,5},{8,10},{9,11},{10,... | collective-permute-start | bytes 393224 | tf_op jit(solution)/shard_map/ppermute | solution.py:512

commit v4 on v3

v4 whole, which is shorter than its diff:
```python
import functools

import jax
import jax.numpy as jnp
from jax import lax
from jax.experimental import pallas as pl
from jax.experimental.pallas import tpu as pltpu
from jax.sharding import PartitionSpec as P

HEADS = 8
EPS = 1e-05
F32 = jnp.float32
BF16 = jnp.bfloat16
NN = (((1,), (0,)), ((), ()))
NT = (((1,), (1,)), ((), ()))
VMEM_LIMIT = 20 * 1024 * 1024


def mm(a, b, dims=NN):
    return lax.dot_general(a, b, dims, preferred_element_type=F32)


def cols(start, count=1, tile=128):
    return slice(start * tile, (start + count) * tile)


def call(kernel, name, outs, args, scratch=(), smem=0):
    vmem = pl.BlockSpec(memory_space=pltpu.VMEM)
    scalars = pl.BlockSpec(memory_space=pltpu.SMEM)
    return pl.pallas_call(
        kernel,
        in_specs=[scalars] * smem + [vmem] * (len(args) - smem),
        out_specs=[vmem] * len(outs),
        out_shape=[jax.ShapeDtypeStruct(shape, dtype) for shape, dtype in outs],
        scratch_shapes=[pltpu.VMEM(shape, dtype) for shape, dtype in scratch],
        compiler_params=pltpu.CompilerParams(vmem_limit_bytes=VMEM_LIMIT),
        cost_estimate=pl.CostEstimate(flops=1, bytes_accessed=1, transcendentals=0),
        name=name,
    )(*args)


def second_core():
    return lax.rem(lax.axis_index("dom"), 2) == 1


def block_of(b, blk):
    return jnp.where(second_core(), b, blk - 1 - b)


def rows_of(b, blk, tile):
    return pl.ds(pl.multiple_of(block_of(b, blk) * tile, tile), tile)


def halves(pair, hdim):
    zero = jnp.zeros((hdim, pair.shape[1]), pair.dtype)
    return jnp.concatenate(
        [
            jnp.concatenate([pair[:hdim], zero], axis=0),
            jnp.concatenate([zero, pair[hdim:]], axis=0),
        ],
        axis=1,
    )


def normalize(rows):
    xf = rows.astype(F32)
    cent = xf - jnp.mean(xf, axis=-1, keepdims=True)
    rstd = lax.rsqrt(jnp.mean(cent * cent, axis=-1, keepdims=True) + EPS)
    return cent * rstd, rstd


def project_tile(t, tile, scale, rows, w_qkv, xn_t, inv, k_nat, v_nat, k_t, v_t):
    width = rows.shape[1]
    here = cols(t, tile=tile)
    xhat, rstd = normalize(rows)
    xn = xhat.astype(BF16)
    xn_t[:, here] = xhat.T.astype(BF16)
    inv[:, here] = jnp.broadcast_to(rstd, (tile, 128)).T[0:8, :]
    keyval = mm(xn, w_qkv[:, width:])
    k_t[:, here] = (keyval[:, :width].T * scale).astype(BF16)
    v_t[:, here] = keyval[:, width:].T.astype(BF16)
    k_nat[here, :] = keyval[:, :width].astype(BF16)
    v_nat[here, :] = keyval[:, width:].astype(BF16)
    return xn


def pick_kernel(blk, tile, x, x_on, x_off):
    x_on[...] = x[rows_of(0, blk, tile), :]
    x_off[...] = x[rows_of(blk - 1, blk, tile), :]


def prelude_own_kernel(blk, tile, scale, x, w_qkv, xn_t, inv, k_nat, v_nat, k_t, v_t, q_t):
    width = x.shape[1]
    for b in range(blk):
        xn = project_tile(
            b, tile, scale, x[rows_of(b, blk, tile), :], w_qkv, xn_t, inv, k_nat, v_nat, k_t, v_t
        )
        q_t[:, cols(b, tile=tile)] = (mm(xn, w_qkv[:, :width]).T * scale).astype(BF16)


def prelude_kernel(
    blk, tile, scale, neighbours, x_on, x_off, w_qkv,
    xn_own, inv_own, k_own, v_own, kt_own, vt_own, q_t, top,
    xn_t, inv, v_nat, k_t, probs, attn_t, g_rest, g_one, k_nat, v_t, scores,
):
    width = x_on.shape[1]
    hdim = width // HEADS
    ours = cols(1, blk, tile)
    xn_t[:, ours] = xn_own[...]
    inv[:, ours] = inv_own[...]
    k_nat[ours, :] = k_own[...]
    v_nat[ours, :] = v_own[...]
    k_t[:, ours] = kt_own[...]
    v_t[:, ours] = vt_own[...]
    is_last = lax.axis_index("section") == lax.axis_size("section") - 1
    for b in range(blk):
        g = jnp.where(is_last, top[rows_of(b, blk, tile), :].astype(F32).T, 0.0).astype(BF16)
        if b < blk - 1:
            g_rest[:, cols(b, tile=tile)] = g
        else:
            g_one[...] = g
    for t, rows in ((0, x_on), (blk + 1, x_off)):
        project_tile(t, tile, scale, rows[...], w_qkv, xn_t, inv, k_nat, v_nat, k_t, v_t)
    blocks = blk * lax.axis_size("dom")
    second = second_core()
    for b in range(blk):
        place = block_of(b, blk)
        mine = lax.axis_index("dom") * blk + place
        below, above = lax.rem(mine + blocks - 1, blocks), lax.rem(mine + 1, blocks)
        before, after = jnp.where(second, below, above), jnp.where(second, above, below)
        has_before = has_after = False
        for j in range(1, neighbours.shape[1]):
            has_before |= neighbours[place, j] == before
            has_after |= neighbours[place, j] == after
        for i in range(HEADS // 2):
            lanes = cols(i, tile=2 * hdim)
            q = halves(q_t[lanes, cols(b, tile=tile)], hdim)
            s = mm(k_nat[cols(b, 3, tile), lanes], q)
            scores[i, b] = jnp.concatenate(
                [
                    jnp.where(has_before, s[:tile], -1e30),
                    s[tile : 2 * tile],
                    jnp.where(has_after, s[2 * tile :], -1e30),
                ],
                axis=0,
            )
    for b in range(blk):
        for i in range(HEADS // 2):
            s = scores[i, b]
            e = jnp.exp(s - jnp.max(s, axis=0, keepdims=True))
            probs[i, b] = (e * (1.0 / jnp.sum(e, axis=0, keepdims=True))).astype(BF16)
    for b in range(blk):
        for h in range(HEADS):
            head = cols(h, tile=hdim)
            p = probs[h // 2, b, :, cols(h % 2, tile=tile)]
            attn_t[head, cols(b, tile=tile)] = mm(v_t[head, cols(b, 3, tile)], p).astype(BF16)


def score_grad(i, b, first, count, tile, hdim, v_nat, probs, attn_t, da):
    lanes, own = cols(i, tile=2 * hdim), cols(b, tile=tile)
    prod = da.astype(F32) * attn_t[lanes, own].astype(F32)
    total = jnp.concatenate(
        [
            jnp.sum(prod[:hdim], axis=0, keepdims=True),
            jnp.sum(prod[hdim:], axis=0, keepdims=True),
        ],
        axis=1,
    )
    dp = mm(v_nat[cols(b + first, count, tile), lanes], halves(da, hdim))
    return (probs[i, b, cols(first, count, tile), :].astype(F32) * (dp - total)).astype(BF16)


def norm_grad(dn, xn, rstd):
    xhat = xn.astype(F32)
    first = jnp.mean(dn, axis=0, keepdims=True)
    second = jnp.mean(dn * xhat, axis=0, keepdims=True)
    return rstd * (dn - first - xhat * second)


def rim_grad(b, t, tile, hdim, q_t, probs, da, ds, w_qkv, xn_t, inv, d_rim):
    width = q_t.shape[0]
    own, near, here = cols(b, tile=tile), cols(t - b, tile=tile), cols(t, tile=tile)
    for i in range(HEADS // 2):
        lanes = cols(i, tile=2 * hdim)
        after = slice(width + i * 2 * hdim, width + (i + 1) * 2 * hdim)
        d_rim[lanes, :] = mm(halves(q_t[lanes, own], hdim), ds(i), NT).astype(BF16)
        d_rim[after, :] = mm(halves(da(lanes), hdim), probs[i, b, near, :], NT).astype(BF16)
    dn = mm(w_qkv[:, width:], d_rim[...])
    return norm_grad(dn, xn_t[:, here], inv[0:1, here]).astype(BF16)


def add(a, b):
    return (a[...].astype(F32) + b[...].astype(F32)).astype(BF16)


def stage_rest_kernel(blk, tile, moved, rim, *refs):
    if moved:
        g_prev, arrived, *refs = refs
    else:
        g, *refs = refs
    w_out, v_nat, probs, attn_t, *refs = refs
    if rim:
        w_qkv, xn_t, inv, q_t, *refs = refs
        *refs, d_rim = refs
        *refs, c_on = refs
    if moved:
        g, *refs = refs
        g[...] = add(g_prev, arrived)
    da, ds = refs
    hdim = g.shape[0] // HEADS
    da[...] = mm(w_out[...], g[...]).astype(BF16)
    for b in range(blk - 1):
        for i in range(HEADS // 2):
            part = da[cols(i, tile=2 * hdim), cols(b, tile=tile)]
            ds[i, b] = score_grad(i, b, 0, 3, tile, hdim, v_nat, probs, attn_t, part)
    if rim:
        c_on[...] = rim_grad(
            0, 0, tile, hdim, q_t, probs, lambda lanes: da[lanes, :tile],
            lambda i: ds[i, 0, :tile, :], w_qkv, xn_t, inv, d_rim,
        )


def stage_one_kernel(blk, tile, moved, *refs):
    if moved:
        g_prev, arrived, *refs = refs
    else:
        g, *refs = refs
    w_out, v_nat, probs, attn_t, w_qkv, xn_t, inv, q_t, *refs = refs
    if moved:
        g, *refs = refs
        g[...] = add(g_prev, arrived)
    da, c_off, d_rim = refs
    hdim = g.shape[0] // HEADS
    da[...] = mm(w_out[...], g[...]).astype(BF16)
    b = blk - 1
    ds = [
        score_grad(i, b, 2, 1, tile, hdim, v_nat, probs, attn_t, da[cols(i, tile=2 * hdim), :])
        for i in range(HEADS // 2)
    ]
    c_off[...] = rim_grad(
        b, blk + 1, tile, hdim, q_t, probs, lambda lanes: da[lanes, :], lambda i: ds[i],
        w_qkv, xn_t, inv, d_rim,
    )


def own_terms(blk, tile, hdim, first, last, q_t, k_t, probs, da, ds, d_qkv):
    width = q_t.shape[0]
    for i in range(HEADS // 2):
        lanes = cols(i, tile=2 * hdim)
        for n, left, right in (
            (1, lambda b: q_t[lanes, cols(b, tile=tile)], lambda b, near: ds(i, b, near, slice(None))),
            (2, lambda b: da(lanes, b), lambda b, near: probs[i, b, near, :]),
        ):
            total = [None] * (blk + 2)
            for b in range(blk):
                low, high = max(b, first), min(b + 3, last + 1)
                near = slice((low - b) * tile, (high - b) * tile)
                part = mm(halves(left(b), hdim), right(b, near), NT)
                for t in range(low, high):
                    more = part[:, cols(t - low, tile=tile)]
                    total[t] = more if total[t] is None else total[t] + more
            start = n * width + i * 2 * hdim
            for t in range(first, last + 1):
                d_qkv[start : start + 2 * hdim, cols(t - first, tile=tile)] = total[t].astype(BF16)
        for b in range(blk):
            for h in (2 * i, 2 * i + 1):
                head = cols(h, tile=hdim)
                d_qkv[head, cols(b + 1 - first, tile=tile)] = mm(
                    k_t[head, cols(b, 3, tile)],
                    ds(i, b, slice(None), cols(h % 2, tile=tile)),
                ).astype(BF16)


def joined(blk, tile, da_rest, da_one, ds_rest, ds_one):
    def da(lanes, b):
        return da_rest[lanes, cols(b, tile=tile)] if b < blk - 1 else da_one[lanes, :]

    def ds(i, b, near, across):
        return ds_rest[i, b, near, across] if b < blk - 1 else ds_one[i, near, across]

    return da, ds


def stage_main_kernel(
    blk, tile, g_rest, g_one, da_rest, da_one, ds_rest, w_qkv, xn_t, inv, v_nat, k_t, q_t, probs,
    attn_t, rest, one, ds_one, d_qkv,
):
    hdim = g_rest.shape[0] // HEADS
    for i in range(HEADS // 2):
        part = da_one[cols(i, tile=2 * hdim), :]
        ds_one[i] = score_grad(i, blk - 1, 0, 3, tile, hdim, v_nat, probs, attn_t, part)
    da, ds = joined(blk, tile, da_rest, da_one, ds_rest, ds_one)
    own_terms(blk, tile, hdim, 1, blk, q_t, k_t, probs, da, ds, d_qkv)
    dn = mm(w_qkv[...], d_qkv[...])
    for b in range(blk):
        own, here = cols(b, tile=tile), cols(b + 1, tile=tile)
        out = norm_grad(dn[:, own], xn_t[:, here], inv[0:1, here])
        if b < blk - 1:
            rest[:, own] = (g_rest[:, own].astype(F32) + out).astype(BF16)
        else:
            one[...] = (g_one[...].astype(F32) + out).astype(BF16)


def add_on_kernel(tile, rest, on, out):
    out[...] = rest[...]
    out[:, :tile] = (rest[:, :tile].astype(F32) + on[...].astype(F32)).astype(BF16)


def add_off_kernel(one, off, out):
    out[...] = add(one, off)


def last_terms_kernel(
    blk, tile, chips, g_prev, arrived, g_rest, da_rest, ds_rest, w_out, v_nat, k_t, q_t, probs, attn_t,
    xn_t, g_one, d_qkv, *refs
):
    *give, da_one, ds_one = refs
    width = g_prev.shape[0]
    hdim = width // HEADS
    g_one[...] = add(g_prev, arrived)
    da_one[...] = mm(w_out[...], g_one[...]).astype(BF16)
    for i in range(HEADS // 2):
        part = da_one[cols(i, tile=2 * hdim), :]
        ds_one[i] = score_grad(i, blk - 1, 0, 3, tile, hdim, v_nat, probs, attn_t, part)
    for t in (0, blk + 1):
        d_qkv[:width, cols(t, tile=tile)] = jnp.zeros((width, tile), BF16)
    da, ds = joined(blk, tile, da_rest, da_one, ds_rest, ds_one)
    own_terms(blk, tile, hdim, 0, blk + 1, q_t, k_t, probs, da, ds, d_qkv)
    if give:
        core = 1 - lax.rem(lax.axis_index("dom"), 2)
        part = weight_rows(core, chips, xn_t, d_qkv, attn_t, g_rest, g_one)
        rows = width // (2 * chips)
        for z in range(chips):
            here = slice(z * rows, (z + 1) * rows)
            for across, term in part:
                give[0][z, :, across] = term[here].astype(BF16)


def last_input_kernel(
    blk, tile, after, g_rest, g_one, d_qkv, w_qkv, xn_t, inv, y, c_on, c_off
):
    dn = mm(w_qkv[...], d_qkv[...])
    outs = [
        norm_grad(dn[:, cols(t, tile=tile)], xn_t[:, cols(t, tile=tile)], inv[0:1, cols(t, tile=tile)])
        for t in range(blk + 2)
    ]
    c_on[...] = outs[0].astype(BF16)
    c_off[...] = outs[-1].astype(BF16)
    for b in range(blk):
        own = cols(b, tile=tile)
        g = g_rest[:, own] if b < blk - 1 else g_one[...]
        y[:, own] = (g.astype(F32) + outs[b + 1]).astype(BF16)


def finish_input_kernel(blk, tile, y_t, on, off, out):
    for b in range(blk):
        part = y_t[:, cols(b, tile=tile)].astype(F32)
        if b == 0:
            part = part + on[...].astype(F32)
        if b == blk - 1:
            part = part + off[...].astype(F32)
        out[rows_of(b, blk, tile), :] = part.T.astype(BF16)


def weight_rows(core, chips, xn_t, d_qkv, attn_t, g_rest, g_one):
    def picked(ref):
        rows = ref.shape[0] // (2 * chips)
        starts = [pl.multiple_of((2 * z + core) * rows, rows) for z in range(chips)]
        return jnp.concatenate([ref[pl.ds(s, rows), :] for s in starts], axis=0)

    wide, split = d_qkv.shape[0], g_rest.shape[1]
    attn = picked(attn_t)
    out = mm(attn[:, :split], g_rest[...], NT) + mm(attn[:, split:], g_one[...], NT)
    return (
        (slice(0, wide), mm(picked(xn_t), d_qkv[...], NT)),
        (slice(wide, wide + out.shape[1]), out),
    )


def keep_kernel(chips, steps, got, xn_t, d_qkv, attn_t, g_rest, g_one, *refs):
    *outs, both = refs
    me = lax.axis_index("dom")
    chip = me // 2
    rows = got.shape[1]
    for across, term in weight_rows(lax.rem(me, 2), chips, xn_t, d_qkv, attn_t, g_rest, g_one):
        for z in range(chips):
            both[z, :, across] = term[z * rows : (z + 1) * rows] + got[z, :, across].astype(F32)
    half = got.shape[2] // 2
    for n, (first, second) in enumerate(steps):
        give, own = outs[2 * n : 2 * n + 2]
        across = slice(n * half, (n + 1) * half)
        give[0] = both[lax.bitwise_xor(chip, first), :, across].astype(BF16)
        give[1] = both[lax.bitwise_xor(chip, first ^ second), :, across].astype(BF16)
        own[0] = both[chip, :, across]
        own[1] = both[lax.bitwise_xor(chip, second), :, across]


def middle_kernel(own_a, got_a, own_b, got_b, *refs):
    give_a, rest_a, give_b, rest_b = refs[-4:]
    for own, got, give, rest in ((own_b, got_b, give_b, rest_b), (own_a, got_a, give_a, rest_a)):
        rest[...] = own[0] + got[0].astype(F32)
        give[...] = (own[1] + got[1].astype(F32)).astype(BF16)


def total_kernel(rest_a, got_a, rest_b, got_b, qkv_grad, out_grad):
    width = out_grad.shape[1]
    qkv_grad[:, : 2 * width] = rest_a[...] + got_a[...].astype(F32)
    total = rest_b[...] + got_b[...].astype(F32)
    qkv_grad[:, 2 * width :] = total[:, :width]
    out_grad[...] = total[:, width:]


def other_core(parts):
    return [(i, i ^ 1) for i in range(parts)]


def next_chip(parts):
    return [(i, (i + 1 if i % 2 else i - 1) % parts) for i in range(parts)]


def chips_apart(parts, step):
    return [(i, i ^ (2 * step)) for i in range(parts)]


def local(layer_inputs, top_grad, w_qkv, w_out, neighbours):
    sections = lax.axis_size("section")
    parts = lax.axis_size("dom")
    blk = neighbours.shape[0]
    rows, width = top_grad.shape[1:]
    tile = rows // blk
    ext = rows + 2 * tile
    hdim = width // HEADS
    scale = 1.0 / hdim**0.5
    x = layer_inputs[0, 0]
    w_in, w_back = w_qkv[0], w_out[0]
    whole, most, single = ((width, n) for n in (rows, rows - tile, tile))
    pairs = HEADS // 2
    pair_shape = (3 * tile, 2 * tile)
    x_on, x_off = call(
        functools.partial(pick_kernel, blk, tile), "pick", [((tile, width), BF16)] * 2, [x]
    )
    x_on = lax.ppermute(x_on, "dom", other_core(parts))
    x_off = lax.ppermute(x_off, "dom", next_chip(parts))
    *kept, q_t = call(
        functools.partial(prelude_own_kernel, blk, tile, scale), "prelude_own",
        [
            (whole, BF16), ((8, rows), F32), ((rows, width), BF16), ((rows, width), BF16),
            (whole, BF16), (whole, BF16), (whole, BF16),
        ],
        [x, w_in],
    )
    xn_t, inv, v_nat, k_t, probs, attn_t, g_rest, g_one = call(
        functools.partial(prelude_kernel, blk, tile, scale), "prelude",
        [
            ((width, ext), BF16), ((8, ext), F32), ((ext, width), BF16), ((width, ext), BF16),
            ((pairs, blk, *pair_shape), BF16), (whole, BF16), (most, BF16), (single, BF16),
        ],
        [neighbours, x_on, x_off, w_in, *kept, q_t, top_grad[0]],
        scratch=[
            ((ext, width), BF16), ((width, ext), BF16), ((pairs, blk, *pair_shape), F32),
        ],
        smem=1,
    )
    common = [w_back, v_nat, probs, attn_t]
    for_rim = [w_in, xn_t, inv, q_t]
    rim_scratch = [((2 * width, tile), BF16)]
    rest_shape = [(most, BF16), ((pairs, blk - 1, *pair_shape), BF16)]
    rest = one = None
    for k in range(sections - 1):
        here = sections - 1 - k
        moved = k > 0
        *new, da_rest, ds_rest, c_on = call(
            functools.partial(stage_rest_kernel, blk, tile, moved, True), "stage_rest",
            [(most, BF16)] * moved + rest_shape + [(single, BF16)],
            [g_rest, *[rest] * moved, *common, *for_rim], scratch=rim_scratch,
        )
        g_rest = new[0] if moved else g_rest
        on = lax.ppermute(c_on, "dom", other_core(parts))
        *new, da_one, c_off = call(
            functools.partial(stage_one_kernel, blk, tile, moved), "stage_one",
            [(single, BF16)] * (moved + 2),
            [g_one, *[one] * moved, *common, *for_rim], scratch=rim_scratch,
        )
        g_one = new[0] if moved else g_one
        off = lax.ppermute(c_off, "dom", next_chip(parts))
        rest, one = call(
            functools.partial(stage_main_kernel, blk, tile), "stage_main",
            [(most, BF16), (single, BF16)],
            [
                g_rest, g_one, da_rest, da_one, ds_rest, w_in, xn_t, inv, v_nat, k_t, q_t, probs, attn_t
            ],
            scratch=[((pairs, *pair_shape), BF16), ((3 * width, rows), BF16)],
        )
        rest = call(functools.partial(add_on_kernel, tile), "add_on", [(most, BF16)], [rest, on])[0]
        one = call(add_off_kernel, "add_off", [(single, BF16)], [one, off])[0]
        rest, one = (lax.ppermute(part, "section", [(here, here - 1)]) for part in (rest, one))
    direct = parts == 8
    chips = parts // 2
    every = 4 * width
    row = width // parts
    g_rest, da_rest, ds_rest = call(
        functools.partial(stage_rest_kernel, blk, tile, True, False), "last_rest",
        [(most, BF16)] + rest_shape, [g_rest, rest, *common],
    )
    g_one, d_qkv, *give = call(
        functools.partial(last_terms_kernel, blk, tile, chips), "last_terms",
        [(single, BF16), ((3 * width, ext), BF16)] + [((chips, row, every), BF16)] * direct,
        [g_one, one, g_rest, da_rest, ds_rest, w_back, v_nat, k_t, q_t, probs, attn_t, xn_t],
        scratch=[(single, BF16), ((pairs, *pair_shape), BF16)],
    )
    after = d_qkv
    if direct:
        got = lax.ppermute(give[0], "dom", other_core(parts))
        steps = ((1, 2), (2, 1))
        give_a, own_a, give_b, own_b = call(
            functools.partial(keep_kernel, chips, steps), "keep",
            [((2, row, every // 2), BF16), ((2, row, every // 2), F32)] * 2,
            [got, xn_t, d_qkv, attn_t, g_rest, g_one], scratch=[((chips, row, every), F32)],
        )
        got_b = lax.ppermute(give_b, "dom", chips_apart(parts, steps[1][0]))
        got_a = lax.ppermute(give_a, "dom", chips_apart(parts, steps[0][0]))
        after = own_a
    y, c_on, c_off = call(
        functools.partial(last_input_kernel, blk, tile), "last_input",
        [(whole, BF16), (single, BF16), (single, BF16)],
        [after, g_rest, g_one, d_qkv, w_in, xn_t, inv],
    )
    off = lax.ppermute(c_off, "dom", next_chip(parts))
    on = lax.ppermute(c_on, "dom", other_core(parts))
    if direct:
        give_a, rest_a, give_b, rest_b = call(
            middle_kernel, "middle", [((row, every // 2), BF16), ((row, every // 2), F32)] * 2,
            [own_a, got_a, own_b, got_b, on],
        )
        got_b = lax.ppermute(give_b, "dom", chips_apart(parts, steps[1][1]))
        got_a = lax.ppermute(give_a, "dom", chips_apart(parts, steps[0][1]))
    y = call(
        functools.partial(finish_input_kernel, blk, tile), "finish_input", [((rows, width), BF16)],
        [y, on, off],
    )[0]
    if direct:
        qkv_grad, out_grad = call(
            total_kernel, "total", [((row, 3 * width), F32), ((row, width), F32)],
            [rest_a, got_a, rest_b, got_b],
        )
    else:
        g_t = jnp.concatenate([g_rest, g_one], axis=1)
        term = jnp.concatenate([mm(xn_t, d_qkv, NT), mm(attn_t, g_t, NT)], axis=1)
        total = lax.psum_scatter(term, "dom", scatter_dimension=0, tiled=True)
        qkv_grad, out_grad = total[:, : 3 * width], total[:, 3 * width :]
    return (y[None, None], qkv_grad[None], out_grad[None])


def solution(mesh):
    placed = (
        P("section", None, "dom", None),
        P(None, "dom", None),
        P("section", None, None),
        P("section", None, None),
        P("dom", None),
    )
    return jax.shard_map(
        local,
        mesh=mesh,
        in_specs=placed,
        out_specs=(
            P("section", None, "dom", None),
            P("section", "dom", None),
            P("section", "dom", None),
        ),
        check_vma=False,
    )
```

time: 107 us -> 99.9 us (0.934)
  waiting for transfers between devices: 46.9 us -> 38.1 us
  Pallas kernels: 30.9 us -> 32.7 us
    ppermute x6, waiting for transfers between devices: 27.8 us -> 12 us  [local(): lax.ppermute(part, 'section', [(here, here - 1)])]
    ppermute x1, waiting for transfers between devices: 0.01 us -> 7.1 us  [local(): got_a = lax.ppermute(give_a, 'dom', chips_apart(parts, steps[0][0]))]
    ppermute x1, starting transfers between devices: 1.13 us -> 3.73 us  [local(): got_b = lax.ppermute(give_b, 'dom', chips_apart(parts, steps[1][1]))]
    ppermute x1, starting transfers between devices: 2.62 us -> 0.07 us  [local(): got_a = lax.ppermute(give_a, 'dom', chips_apart(parts, steps[0][1]))]
    ppermute x1, waiting for transfers between devices: 0.01 us -> 2.47 us  [local(): got_b = lax.ppermute(give_b, 'dom', chips_apart(parts, steps[1][0]))]
    pallas_call x21 -> x25, Pallas kernels: 30.9 us -> 32.7 us  [call(): pl.pallas_call(kernel, in_specs=[scalars] * smem + [vmem] * (len(args) -...]
    ppermute x4, waiting for transfers between devices: 11.6 us -> 10.1 us  [local(): off = lax.ppermute(c_off, 'dom', next_chip(parts))]
    ppermute x1, waiting for transfers between devices: 4.1 us -> 2.77 us  [local(): got_a = lax.ppermute(give_a, 'dom', chips_apart(parts, steps[0][1]))]
  transfers between devices with their start and end apart: 21 -> 21, of which waited for: 8 -> 11; matrix products, arithmetic and copies ran while one was open for 0% -> 0% of each run, Pallas kernels for 14% -> 22%
where the time goes in v4:
time: 99.9 us; the launch traced here: 99.7 us
  waiting for transfers between devices  38.1 us (38%)
  Pallas kernels  32.7 us (33%)
  starting transfers between devices  25.5 us (26%)
  local copies, waits for them, and re-layouts  2.41 us (2%)
    pallas_call x25, Pallas kernels, call(): pl.pallas_call(kernel, in_specs=[scalars] * smem + [vmem] * (len(args) -...  32.7 us
    ppermute x6, waiting for transfers between devices, local(): lax.ppermute(part, 'section', [(here, here - 1)])  12 us
    ppermute x4, waiting for transfers between devices, local(): off = lax.ppermute(c_off, 'dom', next_chip(parts))  10.1 us
    ppermute x4, starting transfers between devices, local(): off = lax.ppermute(c_off, 'dom', next_chip(parts))  7.82 us
    ppermute x1, waiting for transfers between devices, local(): got_a = lax.ppermute(give_a, 'dom', chips_apart(parts, steps[0][0]))  7.1 us
    ppermute x6, starting transfers between devices, local(): lax.ppermute(part, 'section', [(here, here - 1)])  5.68 us
    ppermute x1, starting transfers between devices, local(): x_off = lax.ppermute(x_off, 'dom', next_chip(parts))  4.71 us
    ppermute x1, starting transfers between devices, local(): got_b = lax.ppermute(give_b, 'dom', chips_apart(parts, steps[1][1]))  3.73 us
  transfers between devices with their start and end apart: 21, of which 11 were waited for; matrix products, arithmetic and copies ran while one was open for 0% of the time, Pallas kernels for 22%

profile of v4, /device:TPU:0, one launch (start us, length us, event | category | flops | bytes accessed | tf_op | source)
XLA Modules:
  0.0 99.7 jit_solution(14333996369183294926)
XLA Ops:
  0.6 1.0 copy-done.3
  1.7 0.5 collective-permute-start
  2.2 4.7 %collective-permute-start.1 = (bf16[128,512]{1,0:T(8,128)(2,1)S(1)}, bf16[128,512]{1,0:T(8,128)(2,1)S(1)}, u32[]{:S(2)}, u32[]{:S(2)}) collective-permute-start(bf16[128,512]{1,0:T(8,128)(2,1)S(1)} %get-tuple-element.65), channel_id=1, source_target_pairs={{0,7},{1,2},{2,1},{3,4},{4,3},{5,6},{6,5},{7,0},{8,15},{9,10},{10,... | collective-permute-start | bytes 393224 | tf_op jit(solution)/shard_map/ppermute | solution.py:443
  6.9 1.4 %copy-done = bf16[1,512,1536]{2,1,0:T(8,128)(2,1)S(1)} copy-done((bf16[1,512,1536]{2,1,0:T(8,128)(2,1)S(1)}, bf16[1,512,1536]{2,1,0:T(8,128)(2,1)}, u32[]{:S(2)}) %copy-start) | copy-done | bytes 1572888
  8.3 1.2 %prelude_own.1 = (bf16[512,384]{1,0:T(8,128)(2,1)S(1)}, f32[8,384]{1,0:T(8,128)S(1)}, bf16[384,512]{1,0:T(8,128)(2,1)S(1)}, bf16[384,512]{1,0:T(8,128)(2,1)S(1)}...) custom-call(bf16[384,512]{1,0:T(8,128)(2,1)S(1)} %bitcast.28, ...), custom_call_target="tpu_custom_call" | custom-call | flops 1 | bytes 1 | tf_op jit(solution)/shard_map/prelude_own/pallas_call | solution.py:30
  9.5 0.0 collective-permute-done.x_on
  9.6 0.7 collective-permute-done.1.x_off
  10.2 0.0 copy-start.2
  10.3 3.5 %prelude.1 = (bf16[512,640]{1,0:T(8,128)(2,1)S(1)}, f32[8,640]{1,0:T(8,128)S(1)}, bf16[640,512]{1,0:T(8,128)(2,1)S(1)}, bf16[512,640]{1,0:T(8,128)(2,1)S(1)}, bf...) custom-call(s32[3,3]{1,0:T(4,128)S(1)} %copy-done.5, ...), custom_call_target="tpu_custom_call" | custom-call | flops 1 | bytes 1 | tf_op jit(solution)/shard_map/prelude/pallas_call | solution.py:30
  13.7 1.7 %stage_rest.3 = (bf16[512,256]{1,0:T(8,128)(2,1)S(1)}, bf16[4,2,384,256]{3,2,1,0:T(8,128)(2,1)S(1)}, bf16[512,128]{1,0:T(8,128)(2,1)S(1)}) custom-call(bf16[512,256]{1,0:T(8,128)(2,1)S(1)} %get-tuple-element.74.refs_0_.g_rest, bf16[512,512]{1,0:T(8,128)(2,1)S(1)} %bitcast.19, bf16[640,512]{1,0:T(8,128)(2,1)S(1)} %get-tuple-element.75.refs_2_.v_nat.refs_3_, ...), custom_call_target="tpu_custom_call" | custom-call | flops 1 | bytes 1 | tf_op jit(solution)/shard_map/stage_rest/pallas_call | solution.py:30
  15.5 0.1 collective-permute-start.4
  15.5 1.4 %stage_one.3 = (bf16[512,128]{1,0:T(8,128)(2,1)S(1)}, bf16[512,128]{1,0:T(8,128)(2,1)S(1)}) custom-call(bf16[512,128]{1,0:T(8,128)(2,1)S(1)} %get-tuple-element.73.refs_0_.g_one, bf16[512,512]{1,0:T(8,128)(2,1)S(1)} %bitcast.20, bf16[640,512]{1,0:T(8,128)(2,1)S(1)} %get-tuple-element.75.refs_2_.v_nat.refs_3_, ...), custom_call_target="tpu_custom_call" | custom-call | flops 1 | bytes 1 | tf_op jit(solution)/shard_map/stage_one/pallas_call | solution.py:30
  16.9 3.1 %stage_main.3 = (bf16[512,256]{1,0:T(8,128)(2,1)S(1)}, bf16[512,128]{1,0:T(8,128)(2,1)S(1)}) custom-call(bf16[512,256]{1,0:T(8,128)(2,1)S(1)} %get-tuple-element.74.refs_0_.g_rest, bf16[512,128]{1,0:T(8,128)(2,1)S(1)} %get-tuple-element.73.refs_0_.g_one, bf16[512,256]{1,0:T(8,128)(2,1)S(1)} %get-tuple-element.80.da_rest, ...), custom_call_target="tpu_custom_call" | custom-call | flops 1 | bytes 1 | tf_op jit(solution)/shard_map/stage_main/pallas_call | solution.py:30
  20.0 0.0 collective-permute-done.4.on
  20.0 0.1 add_on.3
  20.1 0.7 collective-permute-start.5
  20.8 2.9 %collective-permute-start.2 = (bf16[512,128]{1,0:T(8,128)(2,1)S(1)}, bf16[512,128]{1,0:T(8,128)(2,1)S(1)}, u32[]{:S(2)}, u32[]{:S(2)}) collective-permute-start(bf16[512,128]{1,0:T(8,128)(2,1)S(1)} %get-tuple-element.85), channel_id=1, source_target_pairs={{0,7},{1,2},{2,1},{3,4},{4,3},{5,6},{6,5},{7,0},{8,15},{9,10},{10,... | collective-permute-start | bytes 393224 | tf_op jit(solution)/shard_map/ppermute | solution.py:485
  23.7 4.7 %collective-permute-done.2.off = bf16[512,128]{1,0:T(8,128)(2,1)S(1)} collective-permute-done((bf16[512,128]{1,0:T(8,128)(2,1)S(1)}, bf16[512,128]{1,0:T(8,128)(2,1)S(1)}, u32[]{:S(2)}, u32[]{:S(2)}) %collective-permute-start.2) | collective-permute-done | bytes 131104 | tf_op jit(solution)/shard_map/ppermute | solution.py:485
  28.4 0.8 collective-permute-start.3
  29.3 0.0 collective-permute-done.5.refs_1_
  29.3 1.7 %stage_rest.4 = (bf16[512,256]{1,0:T(8,128)(2,1)S(1)}, bf16[512,256]{1,0:T(8,128)(2,1)S(1)}, bf16[4,2,384,256]{3,2,1,0:T(8,128)(2,1)S(1)}, bf16[512,128]{1,0:T(8,128)(2,1)S(1)}) custom-call(bf16[512,256]{1,0:T(8,128)(2,1)S(1)} %get-tuple-element.74.refs_0_.g_rest, bf16[512,256]{1,0:T(8,128)(2,1)S(1)} %collective-permute-done.5.refs_1_, ...), custom_call_target="tpu_custom_call" | custom-call | flops 1 | bytes 1 | tf_op jit(solution)/shard_map/stage_rest/pallas_call | solution.py:30
  31.1 0.1 collective-permute-start.8
  31.1 0.0 collective-permute-done.3.refs_1_
  31.1 1.4 %stage_one.4 = (bf16[512,128]{1,0:T(8,128)(2,1)S(1)}, bf16[512,128]{1,0:T(8,128)(2,1)S(1)}, bf16[512,128]{1,0:T(8,128)(2,1)S(1)}) custom-call(bf16[512,128]{1,0:T(8,128)(2,1)S(1)} %get-tuple-element.73.refs_0_.g_one, bf16[512,128]{1,0:T(8,128)(2,1)S(1)} %collective-permute-done.3.refs_1_, bf16[512,512]{1,0:T(8,128)(2,1)S(1)} %bitcast.22, ...), custom_call_target="tpu_custom_call" | custom-call | flops 1 | bytes 1 | tf_op jit(solution)/shard_map/stage_one/pallas_call | solution.py:30
  32.6 3.1 %stage_main.4 = (bf16[512,256]{1,0:T(8,128)(2,1)S(1)}, bf16[512,128]{1,0:T(8,128)(2,1)S(1)}) custom-call(bf16[512,256]{1,0:T(8,128)(2,1)S(1)} %get-tuple-element.89.g_rest.refs_0_, bf16[512,128]{1,0:T(8,128)(2,1)S(1)} %get-tuple-element.86.g_one.refs_0_, bf16[512,256]{1,0:T(8,128)(2,1)S(1)} %get-tuple-element.90.da_rest, ...), custom_call_target="tpu_custom_call" | custom-call | flops 1 | bytes 1 | tf_op jit(solution)/shard_map/stage_main/pallas_call | solution.py:30
  35.6 0.0 collective-permute-done.8.on
  35.6 0.1 add_on.4
  35.7 0.7 collective-permute-start.9
  36.4 1.5 %collective-permute-start.6 = (bf16[512,128]{1,0:T(8,128)(2,1)S(1)}, bf16[512,128]{1,0:T(8,128)(2,1)S(1)}, u32[]{:S(2)}, u32[]{:S(2)}) collective-permute-start(bf16[512,128]{1,0:T(8,128)(2,1)S(1)} %get-tuple-element.94), channel_id=1, source_target_pairs={{0,7},{1,2},{2,1},{3,4},{4,3},{5,6},{6,5},{7,0},{8,15},{9,10},{10,... | collective-permute-start | bytes 393224 | tf_op jit(solution)/shard_map/ppermute | solution.py:485
  37.9 4.8 %collective-permute-done.6.off = bf16[512,128]{1,0:T(8,128)(2,1)S(1)} collective-permute-done((bf16[512,128]{1,0:T(8,128)(2,1)S(1)}, bf16[512,128]{1,0:T(8,128)(2,1)S(1)}, u32[]{:S(2)}, u32[]{:S(2)}) %collective-permute-start.6) | collective-permute-done | bytes 131104 | tf_op jit(solution)/shard_map/ppermute | solution.py:485
  42.8 0.7 collective-permute-start.7
  43.5 0.0 collective-permute-done.9.refs_1_
  43.5 1.7 %stage_rest.5 = (bf16[512,256]{1,0:T(8,128)(2,1)S(1)}, bf16[512,256]{1,0:T(8,128)(2,1)S(1)}, bf16[4,2,384,256]{3,2,1,0:T(8,128)(2,1)S(1)}, bf16[512,128]{1,0:T(8,128)(2,1)S(1)}) custom-call(bf16[512,256]{1,0:T(8,128)(2,1)S(1)} %get-tuple-element.89.g_rest.refs_0_, bf16[512,256]{1,0:T(8,128)(2,1)S(1)} %collective-permute-done.9.refs_1_, ...), custom_call_target="tpu_custom_call" | custom-call | flops 1 | bytes 1 | tf_op jit(solution)/shard_map/stage_rest/pallas_call | solution.py:30
  45.2 0.1 collective-permute-start.12
  45.3 0.0 collective-permute-done.7.refs_1_
  45.3 1.4 %stage_one.5 = (bf16[512,128]{1,0:T(8,128)(2,1)S(1)}, bf16[512,128]{1,0:T(8,128)(2,1)S(1)}, bf16[512,128]{1,0:T(8,128)(2,1)S(1)}) custom-call(bf16[512,128]{1,0:T(8,128)(2,1)S(1)} %get-tuple-element.86.g_one.refs_0_, bf16[512,128]{1,0:T(8,128)(2,1)S(1)} %collective-permute-done.7.refs_1_, bf16[512,512]{1,0:T(8,128)(2,1)S(1)} %bitcast.24, ...), custom_call_target="tpu_custom_call" | custom-call | flops 1 | bytes 1 | tf_op jit(solution)/shard_map/stage_one/pallas_call | solution.py:30
  46.7 1.4 %collective-permute-start.10 = (bf16[512,128]{1,0:T(8,128)(2,1)S(1)}, bf16[512,128]{1,0:T(8,128)(2,1)S(1)}, u32[]{:S(2)}, u32[]{:S(2)}) collective-permute-start(bf16[512,128]{1,0:T(8,128)(2,1)S(1)} %get-tuple-element.103), channel_id=1, source_target_pairs={{0,7},{1,2},{2,1},{3,4},{4,3},{5,6},{6,5},{7,0},{8,15},{9,10},{10,... | collective-permute-start | bytes 393224 | tf_op jit(solution)/shard_map/ppermute | solution.py:485
  48.1 3.1 %stage_main.5 = (bf16[512,256]{1,0:T(8,128)(2,1)S(1)}, bf16[512,128]{1,0:T(8,128)(2,1)S(1)}) custom-call(bf16[512,256]{1,0:T(8,128)(2,1)S(1)} %get-tuple-element.98.g_rest.refs_0_, bf16[512,128]{1,0:T(8,128)(2,1)S(1)} %get-tuple-element.95.g_one.g_prev, bf16[512,256]{1,0:T(8,128)(2,1)S(1)} %get-tuple-element.99.da_rest, ...), custom_call_target="tpu_custom_call" | custom-call | flops 1 | bytes 1 | tf_op jit(solution)/shard_map/stage_main/pallas_call | solution.py:30
  51.2 0.1 add_on.5
  51.3 1.3 %collective-permute-start.13 = (bf16[512,256]{1,0:T(8,128)(2,1)S(1)}, bf16[512,256]{1,0:T(8,128)(2,1)S(1)}, u32[]{:S(2)}, u32[]{:S(2)}) collective-permute-start(bf16[512,256]{1,0:T(8,128)(2,1)S(1)} %add_on.5), channel_id=1, source_target_pairs={{8,0},{9,1},{10,2},{11,3},{12,4},{13,5},{14,6},{15,7}} | collective-permute-start | bytes 786440 | tf_op jit(solution)/shard_map/ppermute | solution.py:496
  52.6 0.5 collective-permute-done.10.off
  53.1 1.5 %collective-permute-start.11 = (bf16[512,128]{1,0:T(8,128)(2,1)S(1)}, bf16[512,128]{1,0:T(8,128)(2,1)S(1)}, u32[]{:S(2)}, u32[]{:S(2)}) collective-permute-start(bf16[512,128]{1,0:T(8,128)(2,1)S(1)} %add_off.5), channel_id=1, source_target_pairs={{8,0},{9,1},{10,2},{11,3},{12,4},{13,5},{14,6},{15,7}} | collective-permute-start | bytes 393224 | tf_op jit(solution)/shard_map/ppermute | solution.py:496
  54.6 11.6 %collective-permute-done.13.refs_1_ = bf16[512,256]{1,0:T(8,128)(2,1)S(1)} collective-permute-done((bf16[512,256]{1,0:T(8,128)(2,1)S(1)}, bf16[512,256]{1,0:T(8,128)(2,1)S(1)}, u32[]{:S(2)}, u32[]{:S(2)}) %collective-permute-start.13) | collective-permute-done | bytes 262176 | tf_op jit(solution)/shard_map/ppermute | solution.py:496
  66.3 1.1 %last_rest.1 = (bf16[512,256]{1,0:T(8,128)(2,1)S(1)}, bf16[512,256]{1,0:T(8,128)(2,1)S(1)}, bf16[4,2,384,256]{3,2,1,0:T(8,128)(2,1)S(1)}) custom-call(bf16[512,256]{1,0:T(8,128)(2,1)S(1)} %get-tuple-element.98.g_rest.refs_0_, bf16[512,256]{1,0:T(8,128)(2,1)S(1)} %collective-permute-done.13.refs_1_, bf16[512,512]{1,0:T(8,128)(2,1)S(1)} %bitcast.25, ...), custom_call_target="tpu_custom_call" | custom-call | flops 1 | bytes 1 | tf_op jit(solution)/shard_map/last_rest/pallas_call | solution.py:30
  67.4 0.3 collective-permute-done.11.arrived
  67.7 3.4 %last_terms.1 = (bf16[512,128]{1,0:T(8,128)(2,1)S(1)}, bf16[1536,640]{1,0:T(8,128)(2,1)S(1)}, bf16[4,64,2048]{2,1,0:T(8,128)(2,1)S(1)}) custom-call(bf16[512,128]{1,0:T(8,128)(2,1)S(1)} %get-tuple-element.95.g_one.g_prev, bf16[512,128]{1,0:T(8,128)(2,1)S(1)} %collective-permute-done.11.arrived, bf16[512,256]{1,0:T(8,128)(2,1)S(1)} %get-tuple-element.106.g_rest, ...), custom_call_target="tpu_custom_call" | custom-call | flops 1 | bytes 1 | tf_op jit(solution)/shard_map/last_terms/pallas_call | solution.py:30
  71.1 0.1 collective-permute-start.14
  71.2 2.6 %collective-permute-done.14.got = bf16[4,64,2048]{2,1,0:T(8,128)(2,1)S(1)} collective-permute-done((bf16[4,64,2048]{2,1,0:T(8,128)(2,1)S(1)}, bf16[4,64,2048]{2,1,0:T(8,128)(2,1)S(1)}, u32[]{:S(2)}, u32[]{:S(2)}) %collective-permute-start.14) | collective-permute-done | bytes 1048608 | tf_op jit(solution)/shard_map/ppermute | solution.py:513
  73.8 1.0 %keep.1 = (bf16[2,64,1024]{2,1,0:T(8,128)(2,1)S(1)}, f32[2,64,1024]{2,1,0:T(8,128)S(1)}, bf16[2,64,1024]{2,1,0:T(8,128)(2,1)S(1)}, f32[2,64,1024]{2,1,0:T(8,128)S(1)}) custom-call(bf16[4,64,2048]{2,1,0:T(8,128)(2,1)S(1)} %collective-permute-done.14.got, bf16[512,640]{1,0:T(8,128)(2,1)S(1)} %get-tuple-element.78.refs_6_.xn_t.refs_7_, ...), custom_call_target="tpu_custom_call" | custom-call | flops 1 | bytes 1 | tf_op jit(solution)/shard_map/keep/pallas_call | solution.py:30
  74.9 0.1 collective-permute-start.17
  74.9 2.5 %collective-permute-start.18 = (bf16[2,64,1024]{2,1,0:T(8,128)(2,1)S(1)}, bf16[2,64,1024]{2,1,0:T(8,128)(2,1)S(1)}, u32[]{:S(2)}, u32[]{:S(2)}) collective-permute-start(bf16[2,64,1024]{2,1,0:T(8,128)(2,1)S(1)} %get-tuple-element.118), channel_id=1, source_target_pairs={{0,4},{1,5},{2,6},{3,7},{4,0},{5,1},{6,2},{7,3},{8,12},{9,13},{10,... | collective-permute-start | bytes 786440 | tf_op jit(solution)/shard_map/ppermute | solution.py:520
  77.5 1.8 %last_input.1 = (bf16[512,384]{1,0:T(8,128)(2,1)S(1)}, bf16[512,128]{1,0:T(8,128)(2,1)S(1)}, bf16[512,128]{1,0:T(8,128)(2,1)S(1)}) custom-call(f32[2,64,1024]{2,1,0:T(8,128)S(1)} %get-tuple-element.112.after.own_a, bf16[512,256]{1,0:T(8,128)(2,1)S(1)} %get-tuple-element.106.g_rest, bf16[512,128]{1,0:T(8,128)(2,1)S(1)} %get-tuple-element.111.g_one, ...), custom_call_target="tpu_custom_call" | custom-call | flops 1 | bytes 1 | tf_op jit(solution)/shard_map/last_input/pallas_call | solution.py:30
  79.3 0.1 collective-permute-start.15
  79.4 1.9 %collective-permute-start.16 = (bf16[512,128]{1,0:T(8,128)(2,1)S(1)}, bf16[512,128]{1,0:T(8,128)(2,1)S(1)}, u32[]{:S(2)}, u32[]{:S(2)}) collective-permute-start(bf16[512,128]{1,0:T(8,128)(2,1)S(1)} %get-tuple-element.115), channel_id=1, source_target_pairs={{0,7},{1,2},{2,1},{3,4},{4,3},{5,6},{6,5},{7,0},{8,15},{9,10},{10,... | collective-permute-start | bytes 393224 | tf_op jit(solution)/shard_map/ppermute | solution.py:528
  81.3 7.1 %collective-permute-done.17.got_a = bf16[2,64,1024]{2,1,0:T(8,128)(2,1)S(1)} collective-permute-done((bf16[2,64,1024]{2,1,0:T(8,128)(2,1)S(1)}, bf16[2,64,1024]{2,1,0:T(8,128)(2,1)S(1)}, u32[]{:S(2)}, u32[]{:S(2)}) %collective-permute-start.17) | collective-permute-done | bytes 262176 | tf_op jit(solution)/shard_map/ppermute | solution.py:521
  88.4 2.5 %collective-permute-done.18.got_b = bf16[2,64,1024]{2,1,0:T(8,128)(2,1)S(1)} collective-permute-done((bf16[2,64,1024]{2,1,0:T(8,128)(2,1)S(1)}, bf16[2,64,1024]{2,1,0:T(8,128)(2,1)S(1)}, u32[]{:S(2)}, u32[]{:S(2)}) %collective-permute-start.18) | collective-permute-done | bytes 262176 | tf_op jit(solution)/shard_map/ppermute | solution.py:520
  90.9 0.1 middle.1
  91.0 0.1 collective-permute-start.19
  91.1 3.7 %collective-permute-start.20 = (bf16[64,1024]{1,0:T(8,128)(2,1)S(1)}, bf16[64,1024]{1,0:T(8,128)(2,1)S(1)}, u32[]{:S(2)}, u32[]{:S(2)}) collective-permute-start(bf16[64,1024]{1,0:T(8,128)(2,1)S(1)} %get-tuple-element.122), channel_id=1, source_target_pairs={{0,2},{1,3},{2,0},{3,1},{4,6},{5,7},{6,4},{7,5},{8,10},{9,11},{10,... | collective-permute-start | bytes 393224 | tf_op jit(solution)/shard_map/ppermute | solution.py:535
  94.8 0.0 collective-permute-done.16.off
  94.8 0.9 finish_input.1
  95.7 2.8 %collective-permute-done.19.got_a = bf16[64,1024]{1,0:T(8,128)(2,1)S(1)} collective-permute-done((bf16[64,1024]{1,0:T(8,128)(2,1)S(1)}, bf16[64,1024]{1,0:T(8,128)(2,1)S(1)}, u32[]{:S(2)}, u32[]{:S(2)}) %collective-permute-start.19) | collective-permute-done | bytes 131104 | tf_op jit(solution)/shard_map/ppermute | solution.py:536
  98.5 0.4 collective-permute-done.20.got_b
  98.8 0.8 total.1
  (15 shorter events, 0.1 us)
Async XLA Ops:
  0.6 1.0 %copy-start.3 = (bf16[1,1,384,512]{3,2,1,0:T(8,128)(2,1)S(1)}, bf16[1,1,384,512]{3,2,1,0:T(8,128)(2,1)}, u32[]{:S(2)}) copy-start(bf16[1,1,384,512]{3,2,1,0:T(8,128)(2,1)} %param.5) | copy-start | bytes 1179652
  1.6 8.6 %copy-start.4 = (bf16[1,384,512]{2,1,0:T(8,128)(2,1)S(1)}, bf16[1,384,512]{2,1,0:T(8,128)(2,1)}, u32[]{:S(2)}) copy-start(bf16[1,384,512]{2,1,0:T(8,128)(2,1)} %param.6) | copy-start | bytes 1179652
  1.6 8.6 %copy-start.5 = (s32[3,3]{1,0:T(4,128)S(1)}, s32[3,3]{1,0:T(4,128)}, u32[]{:S(2)}) copy-start(s32[3,3]{1,0:T(4,128)} %neighbours.1) | copy-start | bytes 112
  1.7 7.9 %collective-permute-start = (bf16[128,512]{1,0:T(8,128)(2,1)S(1)}, bf16[128,512]{1,0:T(8,128)(2,1)S(1)}, u32[]{:S(2)}, u32[]{:S(2)}) collective-permute-start(bf16[128,512]{1,0:T(8,128)(2,1)S(1)} %get-tuple-element.64), channel_id=1, source_target_pairs={{0,1},{1,0},{2,3},{3,2},{4,5},{5,4},{6,7},{7,6},{8,9},{9,8},{10,11... | collective-permute-start | bytes 393224 | tf_op jit(solution)/shard_map/ppermute | solution.py:442
  2.2 8.1 %collective-permute-start.1 = (bf16[128,512]{1,0:T(8,128)(2,1)S(1)}, bf16[128,512]{1,0:T(8,128)(2,1)S(1)}, u32[]{:S(2)}, u32[]{:S(2)}) collective-permute-start(bf16[128,512]{1,0:T(8,128)(2,1)S(1)} %get-tuple-element.65), channel_id=1, source_target_pairs={{0,7},{1,2},{2,1},{3,4},{4,3},{5,6},{6,5},{7,0},{8,15},{9,10},{10,... | collective-permute-start | bytes 393224 | tf_op jit(solution)/shard_map/ppermute | solution.py:443
  6.9 1.4 %copy-start = (bf16[1,512,1536]{2,1,0:T(8,128)(2,1)S(1)}, bf16[1,512,1536]{2,1,0:T(8,128)(2,1)}, u32[]{:S(2)}) copy-start(bf16[1,512,1536]{2,1,0:T(8,128)(2,1)} %param.7) | copy-start | bytes 4718596
  8.3 1.9 %copy-start.1 = (bf16[1,512,1536]{2,1,0:T(8,128)(2,1)S(1)}, bf16[1,512,1536]{2,1,0:T(8,128)(2,1)}, u32[]{:S(2)}) copy-start(bf16[1,512,1536]{2,1,0:T(8,128)(2,1)} %param.7) | copy-start | bytes 4718596
  10.2 3.5 %copy-start.2 = (bf16[1,512,512]{2,1,0:T(8,128)(2,1)S(1)}, bf16[1,512,512]{2,1,0:T(8,128)(2,1)}, u32[]{:S(2)}) copy-start(bf16[1,512,512]{2,1,0:T(8,128)(2,1)} %param.8) | copy-start | bytes 1572868
  15.5 4.5 %collective-permute-start.4 = (bf16[512,128]{1,0:T(8,128)(2,1)S(1)}, bf16[512,128]{1,0:T(8,128)(2,1)S(1)}, u32[]{:S(2)}, u32[]{:S(2)}) collective-permute-start(bf16[512,128]{1,0:T(8,128)(2,1)S(1)} %get-tuple-element.88), channel_id=1, source_target_pairs={{0,1},{1,0},{2,3},{3,2},{4,5},{5,4},{6,7},{7,6},{8,9},{9,8},{10,11... | collective-permute-start | bytes 393224 | tf_op jit(solution)/shard_map/ppermute | solution.py:478
  20.1 9.2 %collective-permute-start.5 = (bf16[512,256]{1,0:T(8,128)(2,1)S(1)}, bf16[512,256]{1,0:T(8,128)(2,1)S(1)}, u32[]{:S(2)}, u32[]{:S(2)}) collective-permute-start(bf16[512,256]{1,0:T(8,128)(2,1)S(1)} %add_on.3), channel_id=1, source_target_pairs={{24,16},{25,17},{26,18},{27,19},{28,20},{29,21},{30,22},{31,23}} | collective-permute-start | bytes 786440 | tf_op jit(solution)/shard_map/ppermute | solution.py:496
  20.8 7.6 %collective-permute-start.2 = (bf16[512,128]{1,0:T(8,128)(2,1)S(1)}, bf16[512,128]{1,0:T(8,128)(2,1)S(1)}, u32[]{:S(2)}, u32[]{:S(2)}) collective-permute-start(bf16[512,128]{1,0:T(8,128)(2,1)S(1)} %get-tuple-element.85), channel_id=1, source_target_pairs={{0,7},{1,2},{2,1},{3,4},{4,3},{5,6},{6,5},{7,0},{8,15},{9,10},{10,... | collective-permute-start | bytes 393224 | tf_op jit(solution)/shard_map/ppermute | solution.py:485
  28.4 2.7 %collective-permute-start.3 = (bf16[512,128]{1,0:T(8,128)(2,1)S(1)}, bf16[512,128]{1,0:T(8,128)(2,1)S(1)}, u32[]{:S(2)}, u32[]{:S(2)}) collective-permute-start(bf16[512,128]{1,0:T(8,128)(2,1)S(1)} %add_off.3), channel_id=1, source_target_pairs={{24,16},{25,17},{26,18},{27,19},{28,20},{29,21},{30,22},{31,23}} | collective-permute-start | bytes 393224 | tf_op jit(solution)/shard_map/ppermute | solution.py:496
  31.1 4.6 %collective-permute-start.8 = (bf16[512,128]{1,0:T(8,128)(2,1)S(1)}, bf16[512,128]{1,0:T(8,128)(2,1)S(1)}, u32[]{:S(2)}, u32[]{:S(2)}) collective-permute-start(bf16[512,128]{1,0:T(8,128)(2,1)S(1)} %get-tuple-element.97), channel_id=1, source_target_pairs={{0,1},{1,0},{2,3},{3,2},{4,5},{5,4},{6,7},{7,6},{8,9},{9,8},{10,11... | collective-permute-start | bytes 393224 | tf_op jit(solution)/shard_map/ppermute | solution.py:478
  35.7 7.8 %collective-permute-start.9 = (bf16[512,256]{1,0:T(8,128)(2,1)S(1)}, bf16[512,256]{1,0:T(8,128)(2,1)S(1)}, u32[]{:S(2)}, u32[]{:S(2)}) collective-permute-start(bf16[512,256]{1,0:T(8,128)(2,1)S(1)} %add_on.4), channel_id=1, source_target_pairs={{16,8},{17,9},{18,10},{19,11},{20,12},{21,13},{22,14},{23,15}} | collective-permute-start | bytes 786440 | tf_op jit(solution)/shard_map/ppermute | solution.py:496
  36.4 6.4 %collective-permute-start.6 = (bf16[512,128]{1,0:T(8,128)(2,1)S(1)}, bf16[512,128]{1,0:T(8,128)(2,1)S(1)}, u32[]{:S(2)}, u32[]{:S(2)}) collective-permute-start(bf16[512,128]{1,0:T(8,128)(2,1)S(1)} %get-tuple-element.94), channel_id=1, source_target_pairs={{0,7},{1,2},{2,1},{3,4},{4,3},{5,6},{6,5},{7,0},{8,15},{9,10},{10,... | collective-permute-start | bytes 393224 | tf_op jit(solution)/shard_map/ppermute | solution.py:485
  42.8 2.5 %collective-permute-start.7 = (bf16[512,128]{1,0:T(8,128)(2,1)S(1)}, bf16[512,128]{1,0:T(8,128)(2,1)S(1)}, u32[]{:S(2)}, u32[]{:S(2)}) collective-permute-start(bf16[512,128]{1,0:T(8,128)(2,1)S(1)} %add_off.4), channel_id=1, source_target_pairs={{16,8},{17,9},{18,10},{19,11},{20,12},{21,13},{22,14},{23,15}} | collective-permute-start | bytes 393224 | tf_op jit(solution)/shard_map/ppermute | solution.py:496
  45.2 6.0 %collective-permute-start.12 = (bf16[512,128]{1,0:T(8,128)(2,1)S(1)}, bf16[512,128]{1,0:T(8,128)(2,1)S(1)}, u32[]{:S(2)}, u32[]{:S(2)}) collective-permute-start(bf16[512,128]{1,0:T(8,128)(2,1)S(1)} %get-tuple-element.105), channel_id=1, source_target_pairs={{0,1},{1,0},{2,3},{3,2},{4,5},{5,4},{6,7},{7,6},{8,9},{9,8},{10,11... | collective-permute-start | bytes 393224 | tf_op jit(solution)/shard_map/ppermute | solution.py:478
  46.7 6.4 %collective-permute-start.10 = (bf16[512,128]{1,0:T(8,128)(2,1)S(1)}, bf16[512,128]{1,0:T(8,128)(2,1)S(1)}, u32[]{:S(2)}, u32[]{:S(2)}) collective-permute-start(bf16[512,128]{1,0:T(8,128)(2,1)S(1)} %get-tuple-element.103), channel_id=1, source_target_pairs={{0,7},{1,2},{2,1},{3,4},{4,3},{5,6},{6,5},{7,0},{8,15},{9,10},{10,... | collective-permute-start | bytes 393224 | tf_op jit(solution)/shard_map/ppermute | solution.py:485
  51.3 15.0 %collective-permute-start.13 = (bf16[512,256]{1,0:T(8,128)(2,1)S(1)}, bf16[512,256]{1,0:T(8,128)(2,1)S(1)}, u32[]{:S(2)}, u32[]{:S(2)}) collective-permute-start(bf16[512,256]{1,0:T(8,128)(2,1)S(1)} %add_on.5), channel_id=1, source_target_pairs={{8,0},{9,1},{10,2},{11,3},{12,4},{13,5},{14,6},{15,7}} | collective-permute-start | bytes 786440 | tf_op jit(solution)/shard_map/ppermute | solution.py:496
  53.1 14.6 %collective-permute-start.11 = (bf16[512,128]{1,0:T(8,128)(2,1)S(1)}, bf16[512,128]{1,0:T(8,128)(2,1)S(1)}, u32[]{:S(2)}, u32[]{:S(2)}) collective-permute-start(bf16[512,128]{1,0:T(8,128)(2,1)S(1)} %add_off.5), channel_id=1, source_target_pairs={{8,0},{9,1},{10,2},{11,3},{12,4},{13,5},{14,6},{15,7}} | collective-permute-start | bytes 393224 | tf_op jit(solution)/shard_map/ppermute | solution.py:496
  71.1 2.7 %collective-permute-start.14 = (bf16[4,64,2048]{2,1,0:T(8,128)(2,1)S(1)}, bf16[4,64,2048]{2,1,0:T(8,128)(2,1)S(1)}, u32[]{:S(2)}, u32[]{:S(2)}) collective-permute-start(bf16[4,64,2048]{2,1,0:T(8,128)(2,1)S(1)} %get-tuple-element.109), channel_id=1, source_target_pairs={{0,1},{1,0},{2,3},{3,2},{4,5},{5,4},{6,7},{7,6},{8,9},{9,8},{10,11... | collective-permute-start | bytes 3145736 | tf_op jit(solution)/shard_map/ppermute | solution.py:513
  74.9 13.6 %collective-permute-start.17 = (bf16[2,64,1024]{2,1,0:T(8,128)(2,1)S(1)}, bf16[2,64,1024]{2,1,0:T(8,128)(2,1)S(1)}, u32[]{:S(2)}, u32[]{:S(2)}) collective-permute-start(bf16[2,64,1024]{2,1,0:T(8,128)(2,1)S(1)} %get-tuple-element.116), channel_id=1, source_target_pairs={{0,2},{1,3},{2,0},{3,1},{4,6},{5,7},{6,4},{7,5},{8,10},{9,11},{10,... | collective-permute-start | bytes 786440 | tf_op jit(solution)/shard_map/ppermute | solution.py:521
  74.9 16.0 %collective-permute-start.18 = (bf16[2,64,1024]{2,1,0:T(8,128)(2,1)S(1)}, bf16[2,64,1024]{2,1,0:T(8,128)(2,1)S(1)}, u32[]{:S(2)}, u32[]{:S(2)}) collective-permute-start(bf16[2,64,1024]{2,1,0:T(8,128)(2,1)S(1)} %get-tuple-element.118), channel_id=1, source_target_pairs={{0,4},{1,5},{2,6},{3,7},{4,0},{5,1},{6,2},{7,3},{8,12},{9,13},{10,... | collective-permute-start | bytes 786440 | tf_op jit(solution)/shard_map/ppermute | solution.py:520
  79.3 2.0 %collective-permute-start.15 = (bf16[512,128]{1,0:T(8,128)(2,1)S(1)}, bf16[512,128]{1,0:T(8,128)(2,1)S(1)}, u32[]{:S(2)}, u32[]{:S(2)}) collective-permute-start(bf16[512,128]{1,0:T(8,128)(2,1)S(1)} %get-tuple-element.114), channel_id=1, source_target_pairs={{0,1},{1,0},{2,3},{3,2},{4,5},{5,4},{6,7},{7,6},{8,9},{9,8},{10,11... | collective-permute-start | bytes 393224 | tf_op jit(solution)/shard_map/ppermute | solution.py:529
  79.4 15.4 %collective-permute-start.16 = (bf16[512,128]{1,0:T(8,128)(2,1)S(1)}, bf16[512,128]{1,0:T(8,128)(2,1)S(1)}, u32[]{:S(2)}, u32[]{:S(2)}) collective-permute-start(bf16[512,128]{1,0:T(8,128)(2,1)S(1)} %get-tuple-element.115), channel_id=1, source_target_pairs={{0,7},{1,2},{2,1},{3,4},{4,3},{5,6},{6,5},{7,0},{8,15},{9,10},{10,... | collective-permute-start | bytes 393224 | tf_op jit(solution)/shard_map/ppermute | solution.py:528
  91.0 7.5 %collective-permute-start.19 = (bf16[64,1024]{1,0:T(8,128)(2,1)S(1)}, bf16[64,1024]{1,0:T(8,128)(2,1)S(1)}, u32[]{:S(2)}, u32[]{:S(2)}) collective-permute-start(bf16[64,1024]{1,0:T(8,128)(2,1)S(1)} %get-tuple-element.120), channel_id=1, source_target_pairs={{0,4},{1,5},{2,6},{3,7},{4,0},{5,1},{6,2},{7,3},{8,12},{9,13},{10,... | collective-permute-start | bytes 393224 | tf_op jit(solution)/shard_map/ppermute | solution.py:536
  91.1 7.8 %collective-permute-start.20 = (bf16[64,1024]{1,0:T(8,128)(2,1)S(1)}, bf16[64,1024]{1,0:T(8,128)(2,1)S(1)}, u32[]{:S(2)}, u32[]{:S(2)}) collective-permute-start(bf16[64,1024]{1,0:T(8,128)(2,1)S(1)} %get-tuple-element.122), channel_id=1, source_target_pairs={{0,2},{1,3},{2,0},{3,1},{4,6},{5,7},{6,4},{7,5},{8,10},{9,11},{10,... | collective-permute-start | bytes 393224 | tf_op jit(solution)/shard_map/ppermute | solution.py:535

commit v5 on v4

--- a/solution.py
+++ b/solution.py
@@ -101,7 +101,7 @@
 def prelude_kernel(
     blk, tile, scale, neighbours, x_on, x_off, w_qkv,
     xn_own, inv_own, k_own, v_own, kt_own, vt_own, q_t, top,
-    xn_t, inv, v_nat, k_t, probs, attn_t, g_rest, g_one, k_nat, v_t, scores,
+    xn_t, inv, v_nat, k_t, probs, attn_t, g_zero, g_mid, g_one, k_nat, v_t, scores,
 ):
     width = x_on.shape[1]
     hdim = width // HEADS
@@ -115,8 +115,10 @@
     is_last = lax.axis_index("section") == lax.axis_size("section") - 1
     for b in range(blk):
         g = jnp.where(is_last, top[rows_of(b, blk, tile), :].astype(F32).T, 0.0).astype(BF16)
-        if b < blk - 1:
-            g_rest[:, cols(b, tile=tile)] = g
+        if b == 0:
+            g_zero[...] = g
+        elif b < blk - 1:
+            g_mid[:, cols(b - 1, tile=tile)] = g
         else:
             g_one[...] = g
     for t, rows in ((0, x_on), (blk + 1, x_off)):
@@ -193,31 +195,110 @@
     return (a[...].astype(F32) + b[...].astype(F32)).astype(BF16)
 
 
-def stage_rest_kernel(blk, tile, moved, rim, *refs):
+def joined(blk, tile, das, dss):
+    def da(lanes, b):
+        if b == 0:
+            return das[0][lanes, :]
+        return das[1][lanes, cols(b - 1, tile=tile)] if b < blk - 1 else das[2][lanes, :]
+
+    def ds(i, b, near, across):
+        if b == 0:
+            return dss[0][i, near, across]
+        return dss[1][i, b - 1, near, across] if b < blk - 1 else dss[2][i, near, across]
+
+    return da, ds
+
+
+def end_grads(b, tile, hdim, g, w_out, v_nat, probs, attn_t, da, ds):
+    da[...] = mm(w_out[...], g[...]).astype(BF16)
+    for i in range(HEADS // 2):
+        part = da[cols(i, tile=2 * hdim), :]
+        ds[i] = score_grad(i, b, 0, 3, tile, hdim, v_nat, probs, attn_t, part)
+
+
+def mid_grads(blk, tile, hdim, g, w_out, v_nat, probs, attn_t, da, ds):
+    da[...] = mm(w_out[...], g[...]).astype(BF16)
+    for b in range(1, blk - 1):
+        for i in range(HEADS // 2):
+            part = da[cols(i, tile=2 * hdim), cols(b - 1, tile=tile)]
+            ds[i, b - 1] = score_grad(i, b, 0, 3, tile, hdim, v_nat, probs, attn_t, part)
+
+
+def own_terms(blk, tile, hdim, first, last, q_t, k_t, probs, da, ds, d_qkv):
+    width = q_t.shape[0]
+    for i in range(HEADS // 2):
+        lanes = cols(i, tile=2 * hdim)
+        for n, left, right in (
+            (1, lambda b: q_t[lanes, cols(b, tile=tile)], lambda b, near: ds(i, b, near, slice(None))),
+            (2, lambda b: da(lanes, b), lambda b, near: probs[i, b, near, :]),
+        ):
+            total = [None] * (blk + 2)
+            for b in range(max(first - 2, 0), min(last + 1, blk)):
+                low, high = max(b, first), min(b + 3, last + 1)
+                near = slice((low - b) * tile, (high - b) * tile)
+                part = mm(halves(left(b), hdim), right(b, near), NT)
+                for t in range(low, high):
+                    more = part[:, cols(t - low, tile=tile)]
+                    total[t] = more if total[t] is None else total[t] + more
+            start = n * width + i * 2 * hdim
+            for t in range(first, last + 1):
+                d_qkv[start : start + 2 * hdim, cols(t - first, tile=tile)] = total[t].astype(BF16)
+        for b in range(max(first - 1, 0), min(last, blk)):
+            for h in (2 * i, 2 * i + 1):
+                head = cols(h, tile=hdim)
+                d_qkv[head, cols(b + 1 - first, tile=tile)] = mm(
+                    k_t[head, cols(b, 3, tile)],
+                    ds(i, b, slice(None), cols(h % 2, tile=tile)),
+                ).astype(BF16)
+
+
+def stage_zero_kernel(blk, tile, moved, *refs):
     if moved:
         g_prev, arrived, *refs = refs
     else:
         g, *refs = refs
-    w_out, v_nat, probs, attn_t, *refs = refs
-    if rim:
-        w_qkv, xn_t, inv, q_t, *refs = refs
-        *refs, d_rim = refs
-        *refs, c_on = refs
+    w_out, v_nat, probs, attn_t, w_qkv, xn_t, inv, q_t, *refs = refs
     if moved:
         g, *refs = refs
         g[...] = add(g_prev, arrived)
-    da, ds = refs
+    da, ds, c_on, d_rim = refs
     hdim = g.shape[0] // HEADS
-    da[...] = mm(w_out[...], g[...]).astype(BF16)
-    for b in range(blk - 1):
-        for i in range(HEADS // 2):
-            part = da[cols(i, tile=2 * hdim), cols(b, tile=tile)]
-            ds[i, b] = score_grad(i, b, 0, 3, tile, hdim, v_nat, probs, attn_t, part)
-    if rim:
-        c_on[...] = rim_grad(
-            0, 0, tile, hdim, q_t, probs, lambda lanes: da[lanes, :tile],
-            lambda i: ds[i, 0, :tile, :], w_qkv, xn_t, inv, d_rim,
-        )
+    end_grads(0, tile, hdim, g, w_out, v_nat, probs, attn_t, da, ds)
+    c_on[...] = rim_grad(
+        0, 0, tile, hdim, q_t, probs, lambda lanes: da[lanes, :], lambda i: ds[i, :tile, :],
+        w_qkv, xn_t, inv, d_rim,
+    )
+
+
+def stage_mid_kernel(blk, tile, moved, *refs):
+    if moved:
+        g_prev, arrived, *refs = refs
+    else:
+        g, *refs = refs
+    g_zero, da_zero, ds_zero, w_out, v_nat, probs, attn_t, w_qkv, xn_t, inv, q_t, k_t, *refs = refs
+    if moved:
+        g, *refs = refs
+        g[...] = add(g_prev, arrived)
+    da, ds, y, d_first = refs
+    hdim = g.shape[0] // HEADS
+    mid_grads(blk, tile, hdim, g, w_out, v_nat, probs, attn_t, da, ds)
+    by_block = joined(blk, tile, (da_zero, da), (ds_zero, ds))
+    own_terms(blk, tile, hdim, 1, 1, q_t, k_t, probs, *by_block, d_first)
+    dn = mm(w_qkv[...], d_first[...])
+    here = cols(1, tile=tile)
+    y[...] = (g_zero[...].astype(F32) + norm_grad(dn, xn_t[:, here], inv[0:1, here])).astype(BF16)
+
+
+def last_mid_kernel(
+    blk, tile, g_prev, arrived, da_zero, ds_zero, w_out, v_nat, probs, attn_t, q_t, k_t, g, da, ds, d_low
+):
+    g[...] = add(g_prev, arrived)
+    width = g.shape[0]
+    hdim = width // HEADS
+    mid_grads(blk, tile, hdim, g, w_out, v_nat, probs, attn_t, da, ds)
+    d_low[:width, :tile] = jnp.zeros((width, tile), BF16)
+    by_block = joined(blk, tile, (da_zero, da), (ds_zero, ds))
+    own_terms(blk, tile, hdim, 0, 1, q_t, k_t, probs, *by_block, d_low)
 
 
 def stage_one_kernel(blk, tile, moved, *refs):
@@ -243,92 +324,45 @@
     )
 
 
-def own_terms(blk, tile, hdim, first, last, q_t, k_t, probs, da, ds, d_qkv):
-    width = q_t.shape[0]
-    for i in range(HEADS // 2):
-        lanes = cols(i, tile=2 * hdim)
-        for n, left, right in (
-            (1, lambda b: q_t[lanes, cols(b, tile=tile)], lambda b, near: ds(i, b, near, slice(None))),
-            (2, lambda b: da(lanes, b), lambda b, near: probs[i, b, near, :]),
-        ):
-            total = [None] * (blk + 2)
-            for b in range(blk):
-                low, high = max(b, first), min(b + 3, last + 1)
-                near = slice((low - b) * tile, (high - b) * tile)
-                part = mm(halves(left(b), hdim), right(b, near), NT)
-                for t in range(low, high):
-                    more = part[:, cols(t - low, tile=tile)]
-                    total[t] = more if total[t] is None else total[t] + more
-            start = n * width + i * 2 * hdim
-            for t in range(first, last + 1):
-                d_qkv[start : start + 2 * hdim, cols(t - first, tile=tile)] = total[t].astype(BF16)
-        for b in range(blk):
-            for h in (2 * i, 2 * i + 1):
-                head = cols(h, tile=hdim)
-                d_qkv[head, cols(b + 1 - first, tile=tile)] = mm(
-                    k_t[head, cols(b, 3, tile)],
-                    ds(i, b, slice(None), cols(h % 2, tile=tile)),
-                ).astype(BF16)
-
-
-def joined(blk, tile, da_rest, da_one, ds_rest, ds_one):
-    def da(lanes, b):
-        return da_rest[lanes, cols(b, tile=tile)] if b < blk - 1 else da_one[lanes, :]
-
-    def ds(i, b, near, across):
-        return ds_rest[i, b, near, across] if b < blk - 1 else ds_one[i, near, across]
-
-    return da, ds
-
-
 def stage_main_kernel(
-    blk, tile, g_rest, g_one, da_rest, da_one, ds_rest, w_qkv, xn_t, inv, v_nat, k_t, q_t, probs,
-    attn_t, rest, one, ds_one, d_qkv,
+    blk, tile, g_mid, g_one, da_zero, da_mid, da_one, ds_zero, ds_mid, w_qkv, xn_t, inv, v_nat, k_t, q_t,
+    probs, attn_t, mid, one, ds_one, d_qkv,
 ):
-    hdim = g_rest.shape[0] // HEADS
+    hdim = g_mid.shape[0] // HEADS
     for i in range(HEADS // 2):
         part = da_one[cols(i, tile=2 * hdim), :]
         ds_one[i] = score_grad(i, blk - 1, 0, 3, tile, hdim, v_nat, probs, attn_t, part)
-    da, ds = joined(blk, tile, da_rest, da_one, ds_rest, ds_one)
-    own_terms(blk, tile, hdim, 1, blk, q_t, k_t, probs, da, ds, d_qkv)
+    by_block = joined(blk, tile, (da_zero, da_mid, da_one), (ds_zero, ds_mid, ds_one))
+    own_terms(blk, tile, hdim, 2, blk, q_t, k_t, probs, *by_block, d_qkv)
     dn = mm(w_qkv[...], d_qkv[...])
-    for b in range(blk):
-        own, here = cols(b, tile=tile), cols(b + 1, tile=tile)
-        out = norm_grad(dn[:, own], xn_t[:, here], inv[0:1, here])
+    for b in range(1, blk):
+        here, place = cols(b + 1, tile=tile), cols(b - 1, tile=tile)
+        out = norm_grad(dn[:, place], xn_t[:, here], inv[0:1, here])
         if b < blk - 1:
-            rest[:, own] = (g_rest[:, own].astype(F32) + out).astype(BF16)
+            mid[:, place] = (g_mid[:, place].astype(F32) + out).astype(BF16)
         else:
             one[...] = (g_one[...].astype(F32) + out).astype(BF16)
 
 
-def add_on_kernel(tile, rest, on, out):
-    out[...] = rest[...]
-    out[:, :tile] = (rest[:, :tile].astype(F32) + on[...].astype(F32)).astype(BF16)
-
-
-def add_off_kernel(one, off, out):
-    out[...] = add(one, off)
+def add_rim_kernel(one, rim, out):
+    out[...] = add(one, rim)
 
 
 def last_terms_kernel(
-    blk, tile, chips, g_prev, arrived, g_rest, da_rest, ds_rest, w_out, v_nat, k_t, q_t, probs, attn_t,
-    xn_t, g_one, d_qkv, *refs
+    blk, tile, chips, g_prev, arrived, g_zero, g_mid, da_zero, da_mid, ds_zero, ds_mid, w_out, v_nat, k_t,
+    q_t, probs, attn_t, xn_t, d_low, g_one, d_high, *refs
 ):
     *give, da_one, ds_one = refs
     width = g_prev.shape[0]
     hdim = width // HEADS
     g_one[...] = add(g_prev, arrived)
-    da_one[...] = mm(w_out[...], g_one[...]).astype(BF16)
-    for i in range(HEADS // 2):
-        part = da_one[cols(i, tile=2 * hdim), :]
-        ds_one[i] = score_grad(i, blk - 1, 0, 3, tile, hdim, v_nat, probs, attn_t, part)
-    for t in (0, blk + 1):
-        d_qkv[:width, cols(t, tile=tile)] = jnp.zeros((width, tile), BF16)
-    da, ds = joined(blk, tile, da_rest, da_one, ds_rest, ds_one)
-    own_terms(blk, tile, hdim, 0, blk + 1, q_t, k_t, probs, da, ds, d_qkv)
+    end_grads(blk - 1, tile, hdim, g_one, w_out, v_nat, probs, attn_t, da_one, ds_one)
+    d_high[:width, cols(blk - 1, tile=tile)] = jnp.zeros((width, tile), BF16)
+    by_block = joined(blk, tile, (da_zero, da_mid, da_one), (ds_zero, ds_mid, ds_one))
+    own_terms(blk, tile, hdim, 2, blk + 1, q_t, k_t, probs, *by_block, d_high)
     if give:
         core = 1 - lax.rem(lax.axis_index("dom"), 2)
-        part = weight_rows(core, chips, xn_t, d_qkv, attn_t, g_rest, g_one)
+        part = weight_rows(core, chips, xn_t, (d_low, d_high), attn_t, (g_zero, g_mid, g_one))
         rows = width // (2 * chips)
         for z in range(chips):
             here = slice(z * rows, (z + 1) * rows)
@@ -337,18 +371,19 @@
 
 
 def last_input_kernel(
-    blk, tile, after, g_rest, g_one, d_qkv, w_qkv, xn_t, inv, y, c_on, c_off
+    blk, tile, after, g_zero, g_mid, g_one, d_low, d_high, w_qkv, xn_t, inv, y, c_on, c_off
 ):
-    dn = mm(w_qkv[...], d_qkv[...])
-    outs = [
-        norm_grad(dn[:, cols(t, tile=tile)], xn_t[:, cols(t, tile=tile)], inv[0:1, cols(t, tile=tile)])
-        for t in range(blk + 2)
-    ]
+    outs = []
+    for part in (d_low, d_high):
+        dn = mm(w_qkv[...], part[...])
+        for n in range(part.shape[1] // tile):
+            here = cols(len(outs), tile=tile)
+            outs.append(norm_grad(dn[:, cols(n, tile=tile)], xn_t[:, here], inv[0:1, here]))
     c_on[...] = outs[0].astype(BF16)
     c_off[...] = outs[-1].astype(BF16)
     for b in range(blk):
         own = cols(b, tile=tile)
-        g = g_rest[:, own] if b < blk - 1 else g_one[...]
+        g = g_zero[...] if b == 0 else g_mid[:, cols(b - 1, tile=tile)] if b < blk - 1 else g_one[...]
         y[:, own] = (g.astype(F32) + outs[b + 1]).astype(BF16)
 
 
@@ -362,27 +397,36 @@
         out[rows_of(b, blk, tile), :] = part.T.astype(BF16)
 
 
-def weight_rows(core, chips, xn_t, d_qkv, attn_t, g_rest, g_one):
+def weight_rows(core, chips, xn_t, d_qkv, attn_t, g):
     def picked(ref):
         rows = ref.shape[0] // (2 * chips)
         starts = [pl.multiple_of((2 * z + core) * rows, rows) for z in range(chips)]
         return jnp.concatenate([ref[pl.ds(s, rows), :] for s in starts], axis=0)
 
-    wide, split = d_qkv.shape[0], g_rest.shape[1]
-    attn = picked(attn_t)
-    out = mm(attn[:, :split], g_rest[...], NT) + mm(attn[:, split:], g_one[...], NT)
+    def product(ref, parts):
+        left, start, total = picked(ref), 0, None
+        for part in parts:
+            more = mm(left[:, start : start + part.shape[1]], part[...], NT)
+            total = more if total is None else total + more
+            start += part.shape[1]
+        return total
+
+    wide, width = d_qkv[0].shape[0], g[0].shape[0]
     return (
-        (slice(0, wide), mm(picked(xn_t), d_qkv[...], NT)),
-        (slice(wide, wide + out.shape[1]), out),
-    )
-
-
-def keep_kernel(chips, steps, got, xn_t, d_qkv, attn_t, g_rest, g_one, *refs):
+        (slice(0, wide), product(xn_t, d_qkv)),
+        (slice(wide, wide + width), product(attn_t, g)),
+    )
+
+
+def keep_kernel(chips, steps, got, xn_t, d_low, d_high, attn_t, g_zero, g_mid, g_one, *refs):
     *outs, both = refs
     me = lax.axis_index("dom")
     chip = me // 2
     rows = got.shape[1]
-    for across, term in weight_rows(lax.rem(me, 2), chips, xn_t, d_qkv, attn_t, g_rest, g_one):
+    terms = weight_rows(
+        lax.rem(me, 2), chips, xn_t, (d_low, d_high), attn_t, (g_zero, g_mid, g_one)
+    )
+    for across, term in terms:
         for z in range(chips):
             both[z, :, across] = term[z * rows : (z + 1) * rows] + got[z, :, across].astype(F32)
     half = got.shape[2] // 2
@@ -433,7 +477,7 @@
     scale = 1.0 / hdim**0.5
     x = layer_inputs[0, 0]
     w_in, w_back = w_qkv[0], w_out[0]
-    whole, most, single = ((width, n) for n in (rows, rows - tile, tile))
+    whole, middle, single = ((width, n) for n in (rows, rows - 2 * tile, tile))
     pairs = HEADS // 2
     pair_shape = (3 * tile, 2 * tile)
     x_on, x_off = call(
@@ -449,11 +493,12 @@
         ],
         [x, w_in],
     )
-    xn_t, inv, v_nat, k_t, probs, attn_t, g_rest, g_one = call(
+    xn_t, inv, v_nat, k_t, probs, attn_t, g_zero, g_mid, g_one = call(
         functools.partial(prelude_kernel, blk, tile, scale), "prelude",
         [
             ((width, ext), BF16), ((8, ext), F32), ((ext, width), BF16), ((width, ext), BF16),
-            ((pairs, blk, *pair_shape), BF16), (whole, BF16), (most, BF16), (single, BF16),
+            ((pairs, blk, *pair_shape), BF16), (whole, BF16), (single, BF16), (middle, BF16),
+            (single, BF16),
         ],
         [neighbours, x_on, x_off, w_in, *kept, q_t, top_grad[0]],
         scratch=[
@@ -463,59 +508,78 @@
     )
     common = [w_back, v_nat, probs, attn_t]
     for_rim = [w_in, xn_t, inv, q_t]
+    others = (width, rows - 2 * tile)
     rim_scratch = [((2 * width, tile), BF16)]
-    rest_shape = [(most, BF16), ((pairs, blk - 1, *pair_shape), BF16)]
-    rest = one = None
+    zero_shape = [(single, BF16), ((pairs, *pair_shape), BF16)]
+    mid_shape = [(middle, BF16), ((pairs, blk - 2, *pair_shape), BF16)]
+    received = []
     for k in range(sections - 1):
         here = sections - 1 - k
         moved = k > 0
-        *new, da_rest, ds_rest, c_on = call(
-            functools.partial(stage_rest_kernel, blk, tile, moved, True), "stage_rest",
-            [(most, BF16)] * moved + rest_shape + [(single, BF16)],
-            [g_rest, *[rest] * moved, *common, *for_rim], scratch=rim_scratch,
-        )
-        g_rest = new[0] if moved else g_rest
+        *new, da_zero, ds_zero, c_on = call(
+            functools.partial(stage_zero_kernel, blk, tile, moved), "stage_zero",
+            [(single, BF16)] * moved + zero_shape + [(single, BF16)],
+            [g_zero, *received[:1], *common, *for_rim], scratch=rim_scratch,
+        )
+        g_zero = new[0] if moved else g_zero
         on = lax.ppermute(c_on, "dom", other_core(parts))
+        *new, da_mid, ds_mid, zero = call(
+            functools.partial(stage_mid_kernel, blk, tile, moved), "stage_mid",
+            [(middle, BF16)] * moved + mid_shape + [(single, BF16)],
+            [g_mid, *received[1:2], g_zero, da_zero, ds_zero, *common, *for_rim, k_t],
+            scratch=[((3 * width, tile), BF16)],
+        )
+        g_mid = new[0] if moved else g_mid
+        zero = call(add_rim_kernel, "add_on", [(single, BF16)], [zero, on])[0]
         *new, da_one, c_off = call(
             functools.partial(stage_one_kernel, blk, tile, moved), "stage_one",
             [(single, BF16)] * (moved + 2),
-            [g_one, *[one] * moved, *common, *for_rim], scratch=rim_scratch,
+            [g_one, *received[2:], *common, *for_rim], scratch=rim_scratch,
         )
         g_one = new[0] if moved else g_one
         off = lax.ppermute(c_off, "dom", next_chip(parts))
-        rest, one = call(
+        mid, one = call(
             functools.partial(stage_main_kernel, blk, tile), "stage_main",
-            [(most, BF16), (single, BF16)],
+            [(middle, BF16), (single, BF16)],
             [
-                g_rest, g_one, da_rest, da_one, ds_rest, w_in, xn_t, inv, v_nat, k_t, q_t, probs, attn_t
+                g_mid, g_one, da_zero, da_mid, da_one, ds_zero, ds_mid, w_in, xn_t, inv, v_nat, k_t, q_t,
+                probs, attn_t,
             ],
-            scratch=[((pairs, *pair_shape), BF16), ((3 * width, rows), BF16)],
-        )
-        rest = call(functools.partial(add_on_kernel, tile), "add_on", [(most, BF16)], [rest, on])[0]
-        one = call(add_off_kernel, "add_off", [(single, BF16)], [one, off])[0]
-        rest, one = (lax.ppermute(part, "section", [(here, here - 1)]) for part in (rest, one))
+            scratch=[((pairs, *pair_shape), BF16), ((3 * width, rows - tile), BF16)],
+        )
+        one = call(add_rim_kernel, "add_off", [(single, BF16)], [one, off])[0]
+        received = [lax.ppermute(part, "section", [(here, here - 1)]) for part in (zero, mid, one)]
     direct = parts == 8
     chips = parts // 2
     every = 4 * width
     row = width // parts
-    g_rest, da_rest, ds_rest = call(
-        functools.partial(stage_rest_kernel, blk, tile, True, False), "last_rest",
-        [(most, BF16)] + rest_shape, [g_rest, rest, *common],
-    )
-    g_one, d_qkv, *give = call(
+    g_zero, da_zero, ds_zero, _ = call(
+        functools.partial(stage_zero_kernel, blk, tile, True), "last_zero",
+        [(single, BF16)] + zero_shape + [(single, BF16)],
+        [g_zero, received[0], *common, *for_rim], scratch=rim_scratch,
+    )
+    g_mid, da_mid, ds_mid, d_low = call(
+        functools.partial(last_mid_kernel, blk, tile), "last_mid",
+        [(middle, BF16)] + mid_shape + [((3 * width, 2 * tile), BF16)],
+        [g_mid, received[1], da_zero, ds_zero, *common, q_t, k_t],
+    )
+    g_one, d_high, *give = call(
         functools.partial(last_terms_kernel, blk, tile, chips), "last_terms",
-        [(single, BF16), ((3 * width, ext), BF16)] + [((chips, row, every), BF16)] * direct,
-        [g_one, one, g_rest, da_rest, ds_rest, w_back, v_nat, k_t, q_t, probs, attn_t, xn_t],
+        [(single, BF16), ((3 * width, rows), BF16)] + [((chips, row, every), BF16)] * direct,
+        [
+            g_one, received[2], g_zero, g_mid, da_zero, da_mid, ds_zero, ds_mid, w_back, v_nat, k_t, q_t,
+            probs, attn_t, xn_t, d_low,
+        ],
         scratch=[(single, BF16), ((pairs, *pair_shape), BF16)],
     )
-    after = d_qkv
+    after = d_high
     if direct:
         got = lax.ppermute(give[0], "dom", other_core(parts))
         steps = ((1, 2), (2, 1))
         give_a, own_a, give_b, own_b = call(
             functools.partial(keep_kernel, chips, steps), "keep",
             [((2, row, every // 2), BF16), ((2, row, every // 2), F32)] * 2,
-            [got, xn_t, d_qkv, attn_t, g_rest, g_one], scratch=[((chips, row, every), F32)],
+            [got, xn_t, d_low, d_high, attn_t, g_zero, g_mid, g_one], scratch=[((chips, row, every), F32)],
         )
         got_b = lax.ppermute(give_b, "dom", chips_apart(parts, steps[1][0]))
         got_a = lax.ppermute(give_a, "dom", chips_apart(parts, steps[0][0]))
@@ -523,7 +587,7 @@
     y, c_on, c_off = call(
         functools.partial(last_input_kernel, blk, tile), "last_input",
         [(whole, BF16), (single, BF16), (single, BF16)],
-        [after, g_rest, g_one, d_qkv, w_in, xn_t, inv],
+        [after, g_zero, g_mid, g_one, d_low, d_high, w_in, xn_t, inv],
     )
     off = lax.ppermute(c_off, "dom", next_chip(parts))
     on = lax.ppermute(c_on, "dom", other_core(parts))
@@ -544,7 +608,8 @@
             [rest_a, got_a, rest_b, got_b],
         )
     else:
-        g_t = jnp.concatenate([g_rest, g_one], axis=1)
+        g_t = jnp.concatenate([g_zero, g_mid, g_one], axis=1)
+        d_qkv = jnp.concatenate([d_low, d_high], axis=1)
         term = jnp.concatenate([mm(xn_t, d_qkv, NT), mm(attn_t, g_t, NT)], axis=1)
         total = lax.psum_scatter(term, "dom", scatter_dimension=0, tiled=True)
         qkv_grad, out_grad = total[:, : 3 * width], total[:, 3 * width :]

time: 99.9 us -> 98 us (0.981)
  waiting for transfers between devices: 38.1 us -> 29.2 us
  Pallas kernels: 32.7 us -> 38.1 us
  starting transfers between devices: 25.5 us -> 27 us
    ppermute x4, waiting for transfers between devices: 10.1 us -> 0.27 us  [local(): off = lax.ppermute(c_off, 'dom', next_chip(parts))]
    pallas_call x25 -> x29, Pallas kernels: 32.7 us -> 38.1 us  [call(): pl.pallas_call(kernel, in_specs=[scalars] * smem + [vmem] * (len(args) -...]
    ppermute x6 -> x9, starting transfers between devices: 5.68 us -> 8.29 us  [local(): lax.ppermute(part, 'section', [(here, here - 1)])]
    ppermute x1, starting transfers between devices: 3.73 us -> 2.18 us  [local(): got_b = lax.ppermute(give_b, 'dom', chips_apart(parts, steps[1][1]))]
    ppermute x1, waiting for transfers between devices: 2.77 us -> 3.84 us  [local(): got_a = lax.ppermute(give_a, 'dom', chips_apart(parts, steps[0][1]))]
    ppermute x6 -> x9, waiting for transfers between devices: 12 us -> 11.5 us  [local(): lax.ppermute(part, 'section', [(here, here - 1)])]
  transfers between devices with their start and end apart: 21 -> 24, of which waited for: 11 -> 8; matrix products, arithmetic and copies ran while one was open for 0% -> 0% of each run, Pallas kernels for 22% -> 29%
where the time goes in v5:
time: 98 us; the launch traced here: 97.7 us
  Pallas kernels  38.1 us (39%)
  waiting for transfers between devices  29.2 us (30%)
  starting transfers between devices  27 us (28%)
  local copies, waits for them, and re-layouts  2.41 us (2%)
  between operations  1.06 us (1%)
    pallas_call x29, Pallas kernels, call(): pl.pallas_call(kernel, in_specs=[scalars] * smem + [vmem] * (len(args) -...  38.1 us
    ppermute x9, waiting for transfers between devices, local(): lax.ppermute(part, 'section', [(here, here - 1)])  11.5 us
    ppermute x4, starting transfers between devices, local(): off = lax.ppermute(c_off, 'dom', next_chip(parts))  8.71 us
    ppermute x9, starting transfers between devices, local(): lax.ppermute(part, 'section', [(here, here - 1)])  8.29 us
    ppermute x1, waiting for transfers between devices, local(): got_a = lax.ppermute(give_a, 'dom', chips_apart(parts, steps[0][0]))  6.66 us
    ppermute x1, starting transfers between devices, local(): x_off = lax.ppermute(x_off, 'dom', next_chip(parts))  4.71 us
    ppermute x1, waiting for transfers between devices, local(): got_a = lax.ppermute(give_a, 'dom', chips_apart(parts, steps[0][1]))  3.84 us
    ppermute x1, waiting for transfers between devices, local(): got_b = lax.ppermute(give_b, 'dom', chips_apart(parts, steps[1][0]))  3.34 us
  transfers between devices with their start and end apart: 24, of which 8 were waited for; matrix products, arithmetic and copies ran while one was open for 0% of the time, Pallas kernels for 29%

profile of v5, /device:TPU:0, one launch (start us, length us, event | category | flops | bytes accessed | tf_op | source)
XLA Modules:
  0.0 97.7 jit_solution(8252180500625913619)
XLA Ops:
  0.6 1.0 %copy-done.3 = bf16[1,1,384,512]{3,2,1,0:T(8,128)(2,1)S(1)} copy-done((bf16[1,1,384,512]{3,2,1,0:T(8,128)(2,1)S(1)}, bf16[1,1,384,512]{3,2,1,0:T(8,128)(2,1)}, u32[]{:S(2)}) %copy-start.3) | copy-done | bytes 393240
  1.7 0.5 collective-permute-start
  2.2 4.7 %collective-permute-start.1 = (bf16[128,512]{1,0:T(8,128)(2,1)S(1)}, bf16[128,512]{1,0:T(8,128)(2,1)S(1)}, u32[]{:S(2)}, u32[]{:S(2)}) collective-permute-start(bf16[128,512]{1,0:T(8,128)(2,1)S(1)} %get-tuple-element.81), channel_id=1, source_target_pairs={{0,7},{1,2},{2,1},{3,4},{4,3},{5,6},{6,5},{7,0},{8,15},{9,10},{10,... | collective-permute-start | bytes 393224 | tf_op jit(solution)/shard_map/ppermute | solution.py:487
  6.9 1.4 %copy-done = bf16[1,512,1536]{2,1,0:T(8,128)(2,1)S(1)} copy-done((bf16[1,512,1536]{2,1,0:T(8,128)(2,1)S(1)}, bf16[1,512,1536]{2,1,0:T(8,128)(2,1)}, u32[]{:S(2)}) %copy-start) | copy-done | bytes 1572888
  8.3 1.2 %prelude_own.1 = (bf16[512,384]{1,0:T(8,128)(2,1)S(1)}, f32[8,384]{1,0:T(8,128)S(1)}, bf16[384,512]{1,0:T(8,128)(2,1)S(1)}, bf16[384,512]{1,0:T(8,128)(2,1)S(1)}...) custom-call(bf16[384,512]{1,0:T(8,128)(2,1)S(1)} %bitcast.36, ...), custom_call_target="tpu_custom_call" | custom-call | flops 1 | bytes 1 | tf_op jit(solution)/shard_map/prelude_own/pallas_call | solution.py:30
  9.5 0.0 collective-permute-done.x_on
  9.6 0.7 collective-permute-done.1.x_off
  10.2 0.0 copy-start.2
  10.3 3.4 %prelude.1 = (bf16[512,640]{1,0:T(8,128)(2,1)S(1)}, f32[8,640]{1,0:T(8,128)S(1)}, bf16[640,512]{1,0:T(8,128)(2,1)S(1)}, bf16[512,640]{1,0:T(8,128)(2,1)S(1)}, bf...) custom-call(s32[3,3]{1,0:T(4,128)S(1)} %copy-done.5, ...), custom_call_target="tpu_custom_call" | custom-call | flops 1 | bytes 1 | tf_op jit(solution)/shard_map/prelude/pallas_call | solution.py:30
  13.7 1.5 %stage_zero.3 = (bf16[512,128]{1,0:T(8,128)(2,1)S(1)}, bf16[4,384,256]{2,1,0:T(8,128)(2,1)S(1)}, bf16[512,128]{1,0:T(8,128)(2,1)S(1)}) custom-call(bf16[512,128]{1,0:T(8,128)(2,1)S(1)} %get-tuple-element.91.refs_0_.refs_1_, bf16[512,512]{1,0:T(8,128)(2,1)S(1)} %bitcast.23, bf16[640,512]{1,0:T(8,128)(2,1)S(1)} %get-tuple-element.92.refs_2_.refs_5_.v_nat.refs_3_.refs_6_, ...), custom_call_target="tpu_custom_call" | custom-call | flops 1 | bytes 1 | tf_op jit(solution)/shard_map/stage_zero/pallas_call | solution.py:30
  15.2 0.1 collective-permute-start.5
  15.3 1.4 %stage_one.3 = (bf16[512,128]{1,0:T(8,128)(2,1)S(1)}, bf16[512,128]{1,0:T(8,128)(2,1)S(1)}) custom-call(bf16[512,128]{1,0:T(8,128)(2,1)S(1)} %get-tuple-element.89.refs_0_.g_one, bf16[512,512]{1,0:T(8,128)(2,1)S(1)} %bitcast.24, bf16[640,512]{1,0:T(8,128)(2,1)S(1)} %get-tuple-element.92.refs_2_.refs_5_.v_nat.refs_3_.refs_6_, ...), custom_call_target="tpu_custom_call" | custom-call | flops 1 | bytes 1 | tf_op jit(solution)/shard_map/stage_one/pallas_call | solution.py:30
  16.7 2.9 %collective-permute-start.2 = (bf16[512,128]{1,0:T(8,128)(2,1)S(1)}, bf16[512,128]{1,0:T(8,128)(2,1)S(1)}, u32[]{:S(2)}, u32[]{:S(2)}) collective-permute-start(bf16[512,128]{1,0:T(8,128)(2,1)S(1)} %get-tuple-element.104), channel_id=1, source_target_pairs={{0,7},{1,2},{2,1},{3,4},{4,3},{5,6},{6,5},{7,0},{8,15},{9,10},{10,... | collective-permute-start | bytes 393224 | tf_op jit(solution)/shard_map/ppermute | solution.py:540
  19.6 2.2 %stage_mid.3 = (bf16[512,128]{1,0:T(8,128)(2,1)S(1)}, bf16[4,1,384,256]{3,2,1,0:T(8,128)(2,1)S(1)}, bf16[512,128]{1,0:T(8,128)(2,1)S(1)}) custom-call(bf16[512,128]{1,0:T(8,128)(2,1)S(1)} %get-tuple-element.90.refs_0_.g_mid, bf16[512,128]{1,0:T(8,128)(2,1)S(1)} %get-tuple-element.91.refs_0_.refs_1_, bf16[512,128]{1,0:T(8,128)(2,1)S(1)} %get-tuple-element.97.refs_2_.da_zero, ...), custom_call_target="tpu_custom_call" | custom-call | flops 1 | bytes 1 | tf_op jit(solution)/shard_map/stage_mid/pallas_call | solution.py:30
  21.8 0.0 collective-permute-done.5.rim
  21.9 0.7 collective-permute-start.6
  22.5 2.1 %stage_main.3 = (bf16[512,128]{1,0:T(8,128)(2,1)S(1)}, bf16[512,128]{1,0:T(8,128)(2,1)S(1)}) custom-call(bf16[512,128]{1,0:T(8,128)(2,1)S(1)} %get-tuple-element.90.refs_0_.g_mid, bf16[512,128]{1,0:T(8,128)(2,1)S(1)} %get-tuple-element.89.refs_0_.g_one, bf16[512,128]{1,0:T(8,128)(2,1)S(1)} %get-tuple-element.97.refs_2_.da_zero, ...), custom_call_target="tpu_custom_call" | custom-call | flops 1 | bytes 1 | tf_op jit(solution)/shard_map/stage_main/pallas_call | solution.py:30
  24.7 0.7 collective-permute-start.3
  25.4 0.8 collective-permute-start.4
  26.2 0.0 collective-permute-done.6.refs_1_
  26.2 1.6 %stage_zero.4 = (bf16[512,128]{1,0:T(8,128)(2,1)S(1)}, bf16[512,128]{1,0:T(8,128)(2,1)S(1)}, bf16[4,384,256]{2,1,0:T(8,128)(2,1)S(1)}, bf16[512,128]{1,0:T(8,128)(2,1)S(1)}) custom-call(bf16[512,128]{1,0:T(8,128)(2,1)S(1)} %get-tuple-element.91.refs_0_.refs_1_, bf16[512,128]{1,0:T(8,128)(2,1)S(1)} %collective-permute-done.6.refs_1_, ...), custom_call_target="tpu_custom_call" | custom-call | flops 1 | bytes 1 | tf_op jit(solution)/shard_map/stage_zero/pallas_call | solution.py:30
  27.8 0.1 collective-permute-start.10
  27.9 1.4 %stage_one.4 = (bf16[512,128]{1,0:T(8,128)(2,1)S(1)}, bf16[512,128]{1,0:T(8,128)(2,1)S(1)}, bf16[512,128]{1,0:T(8,128)(2,1)S(1)}) custom-call(bf16[512,128]{1,0:T(8,128)(2,1)S(1)} %get-tuple-element.89.refs_0_.g_one, bf16[512,128]{1,0:T(8,128)(2,1)S(1)} %collective-permute-done.3.refs_1_, bf16[512,512]{1,0:T(8,128)(2,1)S(1)} %bitcast.27, ...), custom_call_target="tpu_custom_call" | custom-call | flops 1 | bytes 1 | tf_op jit(solution)/shard_map/stage_one/pallas_call | solution.py:30
  29.3 1.2 %collective-permute-start.7 = (bf16[512,128]{1,0:T(8,128)(2,1)S(1)}, bf16[512,128]{1,0:T(8,128)(2,1)S(1)}, u32[]{:S(2)}, u32[]{:S(2)}) collective-permute-start(bf16[512,128]{1,0:T(8,128)(2,1)S(1)} %get-tuple-element.117), channel_id=1, source_target_pairs={{0,7},{1,2},{2,1},{3,4},{4,3},{5,6},{6,5},{7,0},{8,15},{9,10},{10,... | collective-permute-start | bytes 393224 | tf_op jit(solution)/shard_map/ppermute | solution.py:540
  30.5 2.2 %stage_mid.4 = (bf16[512,128]{1,0:T(8,128)(2,1)S(1)}, bf16[512,128]{1,0:T(8,128)(2,1)S(1)}, bf16[4,1,384,256]{3,2,1,0:T(8,128)(2,1)S(1)}, bf16[512,128]{1,0:T(8,128)(2,1)S(1)}) custom-call(bf16[512,128]{1,0:T(8,128)(2,1)S(1)} %get-tuple-element.90.refs_0_.g_mid, bf16[512,128]{1,0:T(8,128)(2,1)S(1)} %collective-permute-done.4.refs_1_, ...), custom_call_target="tpu_custom_call" | custom-call | flops 1 | bytes 1 | tf_op jit(solution)/shard_map/stage_mid/pallas_call | solution.py:30
  32.8 0.7 collective-permute-start.11
  33.5 2.1 %stage_main.4 = (bf16[512,128]{1,0:T(8,128)(2,1)S(1)}, bf16[512,128]{1,0:T(8,128)(2,1)S(1)}) custom-call(bf16[512,128]{1,0:T(8,128)(2,1)S(1)} %get-tuple-element.112.g_mid.refs_0_, bf16[512,128]{1,0:T(8,128)(2,1)S(1)} %get-tuple-element.105.g_one.refs_0_, bf16[512,128]{1,0:T(8,128)(2,1)S(1)} %get-tuple-element.110.refs_3_.da_zero, ...), custom_call_target="tpu_custom_call" | custom-call | flops 1 | bytes 1 | tf_op jit(solution)/shard_map/stage_main/pallas_call | solution.py:30
  35.6 0.3 collective-permute-done.7.rim
  35.9 0.7 collective-permute-start.8
  36.5 0.7 collective-permute-start.9
  37.2 0.0 collective-permute-done.11.refs_1_
  37.2 1.5 %stage_zero.5 = (bf16[512,128]{1,0:T(8,128)(2,1)S(1)}, bf16[512,128]{1,0:T(8,128)(2,1)S(1)}, bf16[4,384,256]{2,1,0:T(8,128)(2,1)S(1)}, bf16[512,128]{1,0:T(8,128)(2,1)S(1)}) custom-call(bf16[512,128]{1,0:T(8,128)(2,1)S(1)} %get-tuple-element.109.refs_2_.refs_0_, bf16[512,128]{1,0:T(8,128)(2,1)S(1)} %collective-permute-done.11.refs_1_, ...), custom_call_target="tpu_custom_call" | custom-call | flops 1 | bytes 1 | tf_op jit(solution)/shard_map/stage_zero/pallas_call | solution.py:30
  38.8 0.1 collective-permute-start.14
  38.9 0.0 collective-permute-done.8.refs_1_
  38.9 1.4 %stage_one.5 = (bf16[512,128]{1,0:T(8,128)(2,1)S(1)}, bf16[512,128]{1,0:T(8,128)(2,1)S(1)}, bf16[512,128]{1,0:T(8,128)(2,1)S(1)}) custom-call(bf16[512,128]{1,0:T(8,128)(2,1)S(1)} %get-tuple-element.105.g_one.refs_0_, bf16[512,128]{1,0:T(8,128)(2,1)S(1)} %collective-permute-done.8.refs_1_, bf16[512,512]{1,0:T(8,128)(2,1)S(1)} %bitcast.30, ...), custom_call_target="tpu_custom_call" | custom-call | flops 1 | bytes 1 | tf_op jit(solution)/shard_map/stage_one/pallas_call | solution.py:30
  40.3 2.2 %collective-permute-start.12 = (bf16[512,128]{1,0:T(8,128)(2,1)S(1)}, bf16[512,128]{1,0:T(8,128)(2,1)S(1)}, u32[]{:S(2)}, u32[]{:S(2)}) collective-permute-start(bf16[512,128]{1,0:T(8,128)(2,1)S(1)} %get-tuple-element.130), channel_id=1, source_target_pairs={{0,7},{1,2},{2,1},{3,4},{4,3},{5,6},{6,5},{7,0},{8,15},{9,10},{10,... | collective-permute-start | bytes 393224 | tf_op jit(solution)/shard_map/ppermute | solution.py:540
  42.5 0.0 collective-permute-done.9.refs_1_
  42.5 2.2 %stage_mid.5 = (bf16[512,128]{1,0:T(8,128)(2,1)S(1)}, bf16[512,128]{1,0:T(8,128)(2,1)S(1)}, bf16[4,1,384,256]{3,2,1,0:T(8,128)(2,1)S(1)}, bf16[512,128]{1,0:T(8,128)(2,1)S(1)}) custom-call(bf16[512,128]{1,0:T(8,128)(2,1)S(1)} %get-tuple-element.112.g_mid.refs_0_, bf16[512,128]{1,0:T(8,128)(2,1)S(1)} %collective-permute-done.9.refs_1_, ...), custom_call_target="tpu_custom_call" | custom-call | flops 1 | bytes 1 | tf_op jit(solution)/shard_map/stage_mid/pallas_call | solution.py:30
  44.7 2.1 %stage_main.5 = (bf16[512,128]{1,0:T(8,128)(2,1)S(1)}, bf16[512,128]{1,0:T(8,128)(2,1)S(1)}) custom-call(bf16[512,128]{1,0:T(8,128)(2,1)S(1)} %get-tuple-element.125.g_mid.g_prev, bf16[512,128]{1,0:T(8,128)(2,1)S(1)} %get-tuple-element.118.g_one.g_prev, bf16[512,128]{1,0:T(8,128)(2,1)S(1)} %get-tuple-element.123.refs_3_.da_zero, ...), custom_call_target="tpu_custom_call" | custom-call | flops 1 | bytes 1 | tf_op jit(solution)/shard_map/stage_main/pallas_call | solution.py:30
  46.8 0.0 collective-permute-done.14.rim
  46.9 1.3 %collective-permute-start.15 = (bf16[512,128]{1,0:T(8,128)(2,1)S(1)}, bf16[512,128]{1,0:T(8,128)(2,1)S(1)}, u32[]{:S(2)}, u32[]{:S(2)}) collective-permute-start(bf16[512,128]{1,0:T(8,128)(2,1)S(1)} %add_on.5), channel_id=1, source_target_pairs={{8,0},{9,1},{10,2},{11,3},{12,4},{13,5},{14,6},{15,7}} | collective-permute-start | bytes 393224 | tf_op jit(solution)/shard_map/ppermute | solution.py:551
  48.2 1.3 %collective-permute-start.16 = (bf16[512,128]{1,0:T(8,128)(2,1)S(1)}, bf16[512,128]{1,0:T(8,128)(2,1)S(1)}, u32[]{:S(2)}, u32[]{:S(2)}) collective-permute-start(bf16[512,128]{1,0:T(8,128)(2,1)S(1)} %get-tuple-element.134), channel_id=1, source_target_pairs={{8,0},{9,1},{10,2},{11,3},{12,4},{13,5},{14,6},{15,7}} | collective-permute-start | bytes 393224 | tf_op jit(solution)/shard_map/ppermute | solution.py:551
  49.5 1.5 %collective-permute-start.13 = (bf16[512,128]{1,0:T(8,128)(2,1)S(1)}, bf16[512,128]{1,0:T(8,128)(2,1)S(1)}, u32[]{:S(2)}, u32[]{:S(2)}) collective-permute-start(bf16[512,128]{1,0:T(8,128)(2,1)S(1)} %add_off.5), channel_id=1, source_target_pairs={{8,0},{9,1},{10,2},{11,3},{12,4},{13,5},{14,6},{15,7}} | collective-permute-start | bytes 393224 | tf_op jit(solution)/shard_map/ppermute | solution.py:551
  51.1 11.5 %collective-permute-done.15.refs_1_ = bf16[512,128]{1,0:T(8,128)(2,1)S(1)} collective-permute-done((bf16[512,128]{1,0:T(8,128)(2,1)S(1)}, bf16[512,128]{1,0:T(8,128)(2,1)S(1)}, u32[]{:S(2)}, u32[]{:S(2)}) %collective-permute-start.15) | collective-permute-done | bytes 131104 | tf_op jit(solution)/shard_map/ppermute | solution.py:551
  62.5 2.2 %last_zero.1 = (bf16[512,128]{1,0:T(8,128)(2,1)S(1)}, bf16[512,128]{1,0:T(8,128)(2,1)S(1)}, bf16[4,384,256]{2,1,0:T(8,128)(2,1)S(1)}, bf16[512,128]{1,0:T(8,128)(2,1)}) custom-call(bf16[512,128]{1,0:T(8,128)(2,1)S(1)} %get-tuple-element.122.refs_2_.refs_0_, bf16[512,128]{1,0:T(8,128)(2,1)S(1)} %collective-permute-done.15.refs_1_, ...), custom_call_target="tpu_custom_call" | custom-call | flops 1 | bytes 1 | tf_op jit(solution)/shard_map/last_zero/pallas_call | solution.py:30
  64.7 1.5 %last_mid.1 = (bf16[512,128]{1,0:T(8,128)(2,1)S(1)}, bf16[512,128]{1,0:T(8,128)(2,1)S(1)}, bf16[4,1,384,256]{3,2,1,0:T(8,128)(2,1)S(1)}, bf16[1536,256]{1,0:T(8,128)(2,1)S(1)}) custom-call(bf16[512,128]{1,0:T(8,128)(2,1)S(1)} %get-tuple-element.125.g_mid.g_prev, bf16[512,128]{1,0:T(8,128)(2,1)S(1)} %collective-permute-done.16.arrived, ...), custom_call_target="tpu_custom_call" | custom-call | flops 1 | bytes 1 | tf_op jit(solution)/shard_map/last_mid/pallas_call | solution.py:30
  66.2 3.0 %last_terms.1 = (bf16[512,128]{1,0:T(8,128)(2,1)S(1)}, bf16[1536,384]{1,0:T(8,128)(2,1)S(1)}, bf16[4,64,2048]{2,1,0:T(8,128)(2,1)S(1)}) custom-call(bf16[512,128]{1,0:T(8,128)(2,1)S(1)} %get-tuple-element.118.g_one.g_prev, bf16[512,128]{1,0:T(8,128)(2,1)S(1)} %collective-permute-done.13.arrived, bf16[512,128]{1,0:T(8,128)(2,1)S(1)} %get-tuple-element.133.g_zero, ...), custom_call_target="tpu_custom_call" | custom-call | flops 1 | bytes 1 | tf_op jit(solution)/shard_map/last_terms/pallas_call | solution.py:30
  69.2 0.1 collective-permute-start.17
  69.3 2.6 %collective-permute-done.17.got = bf16[4,64,2048]{2,1,0:T(8,128)(2,1)S(1)} collective-permute-done((bf16[4,64,2048]{2,1,0:T(8,128)(2,1)S(1)}, bf16[4,64,2048]{2,1,0:T(8,128)(2,1)S(1)}, u32[]{:S(2)}, u32[]{:S(2)}) %collective-permute-start.17) | collective-permute-done | bytes 1048608 | tf_op jit(solution)/shard_map/ppermute | solution.py:577
  71.9 1.1 %keep.1 = (bf16[2,64,1024]{2,1,0:T(8,128)(2,1)S(1)}, f32[2,64,1024]{2,1,0:T(8,128)S(1)}, bf16[2,64,1024]{2,1,0:T(8,128)(2,1)S(1)}, f32[2,64,1024]{2,1,0:T(8,128)S(1)}) custom-call(bf16[4,64,2048]{2,1,0:T(8,128)(2,1)S(1)} %collective-permute-done.17.got, bf16[512,640]{1,0:T(8,128)(2,1)S(1)} %get-tuple-element.95.refs_6_.refs_9_.xn_t.refs_7_.refs_10_, ...), custom_call_target="tpu_custom_call" | custom-call | flops 1 | bytes 1 | tf_op jit(solution)/shard_map/keep/pallas_call | solution.py:30
  73.1 0.1 collective-permute-start.20
  73.2 2.1 %collective-permute-start.21 = (bf16[2,64,1024]{2,1,0:T(8,128)(2,1)S(1)}, bf16[2,64,1024]{2,1,0:T(8,128)(2,1)S(1)}, u32[]{:S(2)}, u32[]{:S(2)}) collective-permute-start(bf16[2,64,1024]{2,1,0:T(8,128)(2,1)S(1)} %get-tuple-element.150), channel_id=1, source_target_pairs={{0,4},{1,5},{2,6},{3,7},{4,0},{5,1},{6,2},{7,3},{8,12},{9,13},{10,... | collective-permute-start | bytes 786440 | tf_op jit(solution)/shard_map/ppermute | solution.py:584
  75.3 1.8 %last_input.1 = (bf16[512,384]{1,0:T(8,128)(2,1)S(1)}, bf16[512,128]{1,0:T(8,128)(2,1)S(1)}, bf16[512,128]{1,0:T(8,128)(2,1)S(1)}) custom-call(f32[2,64,1024]{2,1,0:T(8,128)S(1)} %get-tuple-element.144.after.own_a, bf16[512,128]{1,0:T(8,128)(2,1)S(1)} %get-tuple-element.133.g_zero, bf16[512,128]{1,0:T(8,128)(2,1)S(1)} %get-tuple-element.137.g_mid, ...), custom_call_target="tpu_custom_call" | custom-call | flops 1 | bytes 1 | tf_op jit(solution)/shard_map/last_input/pallas_call | solution.py:30
  77.1 0.1 collective-permute-start.18
  77.2 2.4 %collective-permute-start.19 = (bf16[512,128]{1,0:T(8,128)(2,1)S(1)}, bf16[512,128]{1,0:T(8,128)(2,1)S(1)}, u32[]{:S(2)}, u32[]{:S(2)}) collective-permute-start(bf16[512,128]{1,0:T(8,128)(2,1)S(1)} %get-tuple-element.147), channel_id=1, source_target_pairs={{0,7},{1,2},{2,1},{3,4},{4,3},{5,6},{6,5},{7,0},{8,15},{9,10},{10,... | collective-permute-start | bytes 393224 | tf_op jit(solution)/shard_map/ppermute | solution.py:592
  79.6 6.7 %collective-permute-done.20.got_a = bf16[2,64,1024]{2,1,0:T(8,128)(2,1)S(1)} collective-permute-done((bf16[2,64,1024]{2,1,0:T(8,128)(2,1)S(1)}, bf16[2,64,1024]{2,1,0:T(8,128)(2,1)S(1)}, u32[]{:S(2)}, u32[]{:S(2)}) %collective-permute-start.20) | collective-permute-done | bytes 262176 | tf_op jit(solution)/shard_map/ppermute | solution.py:585
  86.2 3.3 %collective-permute-done.21.got_b = bf16[2,64,1024]{2,1,0:T(8,128)(2,1)S(1)} collective-permute-done((bf16[2,64,1024]{2,1,0:T(8,128)(2,1)S(1)}, bf16[2,64,1024]{2,1,0:T(8,128)(2,1)S(1)}, u32[]{:S(2)}, u32[]{:S(2)}) %collective-permute-start.21) | collective-permute-done | bytes 262176 | tf_op jit(solution)/shard_map/ppermute | solution.py:584
  89.6 0.1 middle.1
  89.6 0.1 collective-permute-start.22
  89.7 2.2 %collective-permute-start.23 = (bf16[64,1024]{1,0:T(8,128)(2,1)S(1)}, bf16[64,1024]{1,0:T(8,128)(2,1)S(1)}, u32[]{:S(2)}, u32[]{:S(2)}) collective-permute-start(bf16[64,1024]{1,0:T(8,128)(2,1)S(1)} %get-tuple-element.154), channel_id=1, source_target_pairs={{0,2},{1,3},{2,0},{3,1},{4,6},{5,7},{6,4},{7,5},{8,10},{9,11},{10,... | collective-permute-start | bytes 393224 | tf_op jit(solution)/shard_map/ppermute | solution.py:599
  91.9 0.9 finish_input.1
  92.8 3.8 %collective-permute-done.22.got_a = bf16[64,1024]{1,0:T(8,128)(2,1)S(1)} collective-permute-done((bf16[64,1024]{1,0:T(8,128)(2,1)S(1)}, bf16[64,1024]{1,0:T(8,128)(2,1)S(1)}, u32[]{:S(2)}, u32[]{:S(2)}) %collective-permute-start.22) | collective-permute-done | bytes 131104 | tf_op jit(solution)/shard_map/ppermute | solution.py:600
  96.7 0.2 collective-permute-done.23.got_b
  96.9 0.8 total.1
  (25 shorter events, 0.3 us)
Async XLA Ops:
  0.6 1.0 %copy-start.3 = (bf16[1,1,384,512]{3,2,1,0:T(8,128)(2,1)S(1)}, bf16[1,1,384,512]{3,2,1,0:T(8,128)(2,1)}, u32[]{:S(2)}) copy-start(bf16[1,1,384,512]{3,2,1,0:T(8,128)(2,1)} %param.5) | copy-start | bytes 1179652
  1.6 8.6 %copy-start.4 = (bf16[1,384,512]{2,1,0:T(8,128)(2,1)S(1)}, bf16[1,384,512]{2,1,0:T(8,128)(2,1)}, u32[]{:S(2)}) copy-start(bf16[1,384,512]{2,1,0:T(8,128)(2,1)} %param.6) | copy-start | bytes 1179652
  1.6 8.6 %copy-start.5 = (s32[3,3]{1,0:T(4,128)S(1)}, s32[3,3]{1,0:T(4,128)}, u32[]{:S(2)}) copy-start(s32[3,3]{1,0:T(4,128)} %neighbours.1) | copy-start | bytes 112
  1.7 7.9 %collective-permute-start = (bf16[128,512]{1,0:T(8,128)(2,1)S(1)}, bf16[128,512]{1,0:T(8,128)(2,1)S(1)}, u32[]{:S(2)}, u32[]{:S(2)}) collective-permute-start(bf16[128,512]{1,0:T(8,128)(2,1)S(1)} %get-tuple-element.80), channel_id=1, source_target_pairs={{0,1},{1,0},{2,3},{3,2},{4,5},{5,4},{6,7},{7,6},{8,9},{9,8},{10,11... | collective-permute-start | bytes 393224 | tf_op jit(solution)/shard_map/ppermute | solution.py:486
  2.2 8.1 %collective-permute-start.1 = (bf16[128,512]{1,0:T(8,128)(2,1)S(1)}, bf16[128,512]{1,0:T(8,128)(2,1)S(1)}, u32[]{:S(2)}, u32[]{:S(2)}) collective-permute-start(bf16[128,512]{1,0:T(8,128)(2,1)S(1)} %get-tuple-element.81), channel_id=1, source_target_pairs={{0,7},{1,2},{2,1},{3,4},{4,3},{5,6},{6,5},{7,0},{8,15},{9,10},{10,... | collective-permute-start | bytes 393224 | tf_op jit(solution)/shard_map/ppermute | solution.py:487
  6.9 1.4 %copy-start = (bf16[1,512,1536]{2,1,0:T(8,128)(2,1)S(1)}, bf16[1,512,1536]{2,1,0:T(8,128)(2,1)}, u32[]{:S(2)}) copy-start(bf16[1,512,1536]{2,1,0:T(8,128)(2,1)} %param.7) | copy-start | bytes 4718596
  8.3 1.9 %copy-start.1 = (bf16[1,512,1536]{2,1,0:T(8,128)(2,1)S(1)}, bf16[1,512,1536]{2,1,0:T(8,128)(2,1)}, u32[]{:S(2)}) copy-start(bf16[1,512,1536]{2,1,0:T(8,128)(2,1)} %param.7) | copy-start | bytes 4718596
  10.2 3.4 %copy-start.2 = (bf16[1,512,512]{2,1,0:T(8,128)(2,1)S(1)}, bf16[1,512,512]{2,1,0:T(8,128)(2,1)}, u32[]{:S(2)}) copy-start(bf16[1,512,512]{2,1,0:T(8,128)(2,1)} %param.8) | copy-start | bytes 1572868
  15.2 6.6 %collective-permute-start.5 = (bf16[512,128]{1,0:T(8,128)(2,1)S(1)}, bf16[512,128]{1,0:T(8,128)(2,1)S(1)}, u32[]{:S(2)}, u32[]{:S(2)}) collective-permute-start(bf16[512,128]{1,0:T(8,128)(2,1)S(1)} %get-tuple-element.108), channel_id=1, source_target_pairs={{0,1},{1,0},{2,3},{3,2},{4,5},{5,4},{6,7},{7,6},{8,9},{9,8},{10,11... | collective-permute-start | bytes 393224 | tf_op jit(solution)/shard_map/ppermute | solution.py:525
  16.7 7.9 %collective-permute-start.2 = (bf16[512,128]{1,0:T(8,128)(2,1)S(1)}, bf16[512,128]{1,0:T(8,128)(2,1)S(1)}, u32[]{:S(2)}, u32[]{:S(2)}) collective-permute-start(bf16[512,128]{1,0:T(8,128)(2,1)S(1)} %get-tuple-element.104), channel_id=1, source_target_pairs={{0,7},{1,2},{2,1},{3,4},{4,3},{5,6},{6,5},{7,0},{8,15},{9,10},{10,... | collective-permute-start | bytes 393224 | tf_op jit(solution)/shard_map/ppermute | solution.py:540
  21.9 4.4 %collective-permute-start.6 = (bf16[512,128]{1,0:T(8,128)(2,1)S(1)}, bf16[512,128]{1,0:T(8,128)(2,1)S(1)}, u32[]{:S(2)}, u32[]{:S(2)}) collective-permute-start(bf16[512,128]{1,0:T(8,128)(2,1)S(1)} %add_on.3), channel_id=1, source_target_pairs={{24,16},{25,17},{26,18},{27,19},{28,20},{29,21},{30,22},{31,23}} | collective-permute-start | bytes 393224 | tf_op jit(solution)/shard_map/ppermute | solution.py:551
  24.7 3.2 %collective-permute-start.3 = (bf16[512,128]{1,0:T(8,128)(2,1)S(1)}, bf16[512,128]{1,0:T(8,128)(2,1)S(1)}, u32[]{:S(2)}, u32[]{:S(2)}) collective-permute-start(bf16[512,128]{1,0:T(8,128)(2,1)S(1)} %add_off.3), channel_id=1, source_target_pairs={{24,16},{25,17},{26,18},{27,19},{28,20},{29,21},{30,22},{31,23}} | collective-permute-start | bytes 393224 | tf_op jit(solution)/shard_map/ppermute | solution.py:551
  25.4 5.1 %collective-permute-start.4 = (bf16[512,128]{1,0:T(8,128)(2,1)S(1)}, bf16[512,128]{1,0:T(8,128)(2,1)S(1)}, u32[]{:S(2)}, u32[]{:S(2)}) collective-permute-start(bf16[512,128]{1,0:T(8,128)(2,1)S(1)} %get-tuple-element.106), channel_id=1, source_target_pairs={{24,16},{25,17},{26,18},{27,19},{28,20},{29,21},{30,22},{31,23}} | collective-permute-start | bytes 393224 | tf_op jit(solution)/shard_map/ppermute | solution.py:551
  27.8 4.9 %collective-permute-start.10 = (bf16[512,128]{1,0:T(8,128)(2,1)S(1)}, bf16[512,128]{1,0:T(8,128)(2,1)S(1)}, u32[]{:S(2)}, u32[]{:S(2)}) collective-permute-start(bf16[512,128]{1,0:T(8,128)(2,1)S(1)} %get-tuple-element.121), channel_id=1, source_target_pairs={{0,1},{1,0},{2,3},{3,2},{4,5},{5,4},{6,7},{7,6},{8,9},{9,8},{10,11... | collective-permute-start | bytes 393224 | tf_op jit(solution)/shard_map/ppermute | solution.py:525
  29.3 6.5 %collective-permute-start.7 = (bf16[512,128]{1,0:T(8,128)(2,1)S(1)}, bf16[512,128]{1,0:T(8,128)(2,1)S(1)}, u32[]{:S(2)}, u32[]{:S(2)}) collective-permute-start(bf16[512,128]{1,0:T(8,128)(2,1)S(1)} %get-tuple-element.117), channel_id=1, source_target_pairs={{0,7},{1,2},{2,1},{3,4},{4,3},{5,6},{6,5},{7,0},{8,15},{9,10},{10,... | collective-permute-start | bytes 393224 | tf_op jit(solution)/shard_map/ppermute | solution.py:540
  32.8 4.4 %collective-permute-start.11 = (bf16[512,128]{1,0:T(8,128)(2,1)S(1)}, bf16[512,128]{1,0:T(8,128)(2,1)S(1)}, u32[]{:S(2)}, u32[]{:S(2)}) collective-permute-start(bf16[512,128]{1,0:T(8,128)(2,1)S(1)} %add_on.4), channel_id=1, source_target_pairs={{16,8},{17,9},{18,10},{19,11},{20,12},{21,13},{22,14},{23,15}} | collective-permute-start | bytes 393224 | tf_op jit(solution)/shard_map/ppermute | solution.py:551
  35.9 3.0 %collective-permute-start.8 = (bf16[512,128]{1,0:T(8,128)(2,1)S(1)}, bf16[512,128]{1,0:T(8,128)(2,1)S(1)}, u32[]{:S(2)}, u32[]{:S(2)}) collective-permute-start(bf16[512,128]{1,0:T(8,128)(2,1)S(1)} %add_off.4), channel_id=1, source_target_pairs={{16,8},{17,9},{18,10},{19,11},{20,12},{21,13},{22,14},{23,15}} | collective-permute-start | bytes 393224 | tf_op jit(solution)/shard_map/ppermute | solution.py:551
  36.5 6.0 %collective-permute-start.9 = (bf16[512,128]{1,0:T(8,128)(2,1)S(1)}, bf16[512,128]{1,0:T(8,128)(2,1)S(1)}, u32[]{:S(2)}, u32[]{:S(2)}) collective-permute-start(bf16[512,128]{1,0:T(8,128)(2,1)S(1)} %get-tuple-element.119), channel_id=1, source_target_pairs={{16,8},{17,9},{18,10},{19,11},{20,12},{21,13},{22,14},{23,15}} | collective-permute-start | bytes 393224 | tf_op jit(solution)/shard_map/ppermute | solution.py:551
  38.8 8.1 %collective-permute-start.14 = (bf16[512,128]{1,0:T(8,128)(2,1)S(1)}, bf16[512,128]{1,0:T(8,128)(2,1)S(1)}, u32[]{:S(2)}, u32[]{:S(2)}) collective-permute-start(bf16[512,128]{1,0:T(8,128)(2,1)S(1)} %get-tuple-element.132), channel_id=1, source_target_pairs={{0,1},{1,0},{2,3},{3,2},{4,5},{5,4},{6,7},{7,6},{8,9},{9,8},{10,11... | collective-permute-start | bytes 393224 | tf_op jit(solution)/shard_map/ppermute | solution.py:525
  40.3 9.2 %collective-permute-start.12 = (bf16[512,128]{1,0:T(8,128)(2,1)S(1)}, bf16[512,128]{1,0:T(8,128)(2,1)S(1)}, u32[]{:S(2)}, u32[]{:S(2)}) collective-permute-start(bf16[512,128]{1,0:T(8,128)(2,1)S(1)} %get-tuple-element.130), channel_id=1, source_target_pairs={{0,7},{1,2},{2,1},{3,4},{4,3},{5,6},{6,5},{7,0},{8,15},{9,10},{10,... | collective-permute-start | bytes 393224 | tf_op jit(solution)/shard_map/ppermute | solution.py:540
  46.9 15.6 %collective-permute-start.15 = (bf16[512,128]{1,0:T(8,128)(2,1)S(1)}, bf16[512,128]{1,0:T(8,128)(2,1)S(1)}, u32[]{:S(2)}, u32[]{:S(2)}) collective-permute-start(bf16[512,128]{1,0:T(8,128)(2,1)S(1)} %add_on.5), channel_id=1, source_target_pairs={{8,0},{9,1},{10,2},{11,3},{12,4},{13,5},{14,6},{15,7}} | collective-permute-start | bytes 393224 | tf_op jit(solution)/shard_map/ppermute | solution.py:551
  48.2 16.5 %collective-permute-start.16 = (bf16[512,128]{1,0:T(8,128)(2,1)S(1)}, bf16[512,128]{1,0:T(8,128)(2,1)S(1)}, u32[]{:S(2)}, u32[]{:S(2)}) collective-permute-start(bf16[512,128]{1,0:T(8,128)(2,1)S(1)} %get-tuple-element.134), channel_id=1, source_target_pairs={{8,0},{9,1},{10,2},{11,3},{12,4},{13,5},{14,6},{15,7}} | collective-permute-start | bytes 393224 | tf_op jit(solution)/shard_map/ppermute | solution.py:551
  49.5 16.7 %collective-permute-start.13 = (bf16[512,128]{1,0:T(8,128)(2,1)S(1)}, bf16[512,128]{1,0:T(8,128)(2,1)S(1)}, u32[]{:S(2)}, u32[]{:S(2)}) collective-permute-start(bf16[512,128]{1,0:T(8,128)(2,1)S(1)} %add_off.5), channel_id=1, source_target_pairs={{8,0},{9,1},{10,2},{11,3},{12,4},{13,5},{14,6},{15,7}} | collective-permute-start | bytes 393224 | tf_op jit(solution)/shard_map/ppermute | solution.py:551
  69.2 2.7 %collective-permute-start.17 = (bf16[4,64,2048]{2,1,0:T(8,128)(2,1)S(1)}, bf16[4,64,2048]{2,1,0:T(8,128)(2,1)S(1)}, u32[]{:S(2)}, u32[]{:S(2)}) collective-permute-start(bf16[4,64,2048]{2,1,0:T(8,128)(2,1)S(1)} %get-tuple-element.141), channel_id=1, source_target_pairs={{0,1},{1,0},{2,3},{3,2},{4,5},{5,4},{6,7},{7,6},{8,9},{9,8},{10,11... | collective-permute-start | bytes 3145736 | tf_op jit(solution)/shard_map/ppermute | solution.py:577
  73.1 13.1 %collective-permute-start.20 = (bf16[2,64,1024]{2,1,0:T(8,128)(2,1)S(1)}, bf16[2,64,1024]{2,1,0:T(8,128)(2,1)S(1)}, u32[]{:S(2)}, u32[]{:S(2)}) collective-permute-start(bf16[2,64,1024]{2,1,0:T(8,128)(2,1)S(1)} %get-tuple-element.148), channel_id=1, source_target_pairs={{0,2},{1,3},{2,0},{3,1},{4,6},{5,7},{6,4},{7,5},{8,10},{9,11},{10,... | collective-permute-start | bytes 786440 | tf_op jit(solution)/shard_map/ppermute | solution.py:585
  73.2 16.4 %collective-permute-start.21 = (bf16[2,64,1024]{2,1,0:T(8,128)(2,1)S(1)}, bf16[2,64,1024]{2,1,0:T(8,128)(2,1)S(1)}, u32[]{:S(2)}, u32[]{:S(2)}) collective-permute-start(bf16[2,64,1024]{2,1,0:T(8,128)(2,1)S(1)} %get-tuple-element.150), channel_id=1, source_target_pairs={{0,4},{1,5},{2,6},{3,7},{4,0},{5,1},{6,2},{7,3},{8,12},{9,13},{10,... | collective-permute-start | bytes 786440 | tf_op jit(solution)/shard_map/ppermute | solution.py:584
  77.1 2.5 %collective-permute-start.18 = (bf16[512,128]{1,0:T(8,128)(2,1)S(1)}, bf16[512,128]{1,0:T(8,128)(2,1)S(1)}, u32[]{:S(2)}, u32[]{:S(2)}) collective-permute-start(bf16[512,128]{1,0:T(8,128)(2,1)S(1)} %get-tuple-element.146), channel_id=1, source_target_pairs={{0,1},{1,0},{2,3},{3,2},{4,5},{5,4},{6,7},{7,6},{8,9},{9,8},{10,11... | collective-permute-start | bytes 393224 | tf_op jit(solution)/shard_map/ppermute | solution.py:593
  77.2 14.7 %collective-permute-start.19 = (bf16[512,128]{1,0:T(8,128)(2,1)S(1)}, bf16[512,128]{1,0:T(8,128)(2,1)S(1)}, u32[]{:S(2)}, u32[]{:S(2)}) collective-permute-start(bf16[512,128]{1,0:T(8,128)(2,1)S(1)} %get-tuple-element.147), channel_id=1, source_target_pairs={{0,7},{1,2},{2,1},{3,4},{4,3},{5,6},{6,5},{7,0},{8,15},{9,10},{10,... | collective-permute-start | bytes 393224 | tf_op jit(solution)/shard_map/ppermute | solution.py:592
  89.6 7.0 %collective-permute-start.22 = (bf16[64,1024]{1,0:T(8,128)(2,1)S(1)}, bf16[64,1024]{1,0:T(8,128)(2,1)S(1)}, u32[]{:S(2)}, u32[]{:S(2)}) collective-permute-start(bf16[64,1024]{1,0:T(8,128)(2,1)S(1)} %get-tuple-element.152), channel_id=1, source_target_pairs={{0,4},{1,5},{2,6},{3,7},{4,0},{5,1},{6,2},{7,3},{8,12},{9,13},{10,... | collective-permute-start | bytes 393224 | tf_op jit(solution)/shard_map/ppermute | solution.py:600
  89.7 7.2 %collective-permute-start.23 = (bf16[64,1024]{1,0:T(8,128)(2,1)S(1)}, bf16[64,1024]{1,0:T(8,128)(2,1)S(1)}, u32[]{:S(2)}, u32[]{:S(2)}) collective-permute-start(bf16[64,1024]{1,0:T(8,128)(2,1)S(1)} %get-tuple-element.154), channel_id=1, source_target_pairs={{0,2},{1,3},{2,0},{3,1},{4,6},{5,7},{6,4},{7,5},{8,10},{9,11},{10,... | collective-permute-start | bytes 393224 | tf_op jit(solution)/shard_map/ppermute | solution.py:599

commit v6 on v5

--- a/solution.py
+++ b/solution.py
@@ -418,25 +418,29 @@
     )
 
 
-def keep_kernel(chips, steps, got, xn_t, d_low, d_high, attn_t, g_zero, g_mid, g_one, *refs):
-    *outs, both = refs
-    me = lax.axis_index("dom")
-    chip = me // 2
-    rows = got.shape[1]
-    terms = weight_rows(
-        lax.rem(me, 2), chips, xn_t, (d_low, d_high), attn_t, (g_zero, g_mid, g_one)
-    )
-    for across, term in terms:
+def mine_kernel(chips, xn_t, d_low, d_high, attn_t, g_zero, g_mid, g_one, both):
+    core = lax.rem(lax.axis_index("dom"), 2)
+    rows = both.shape[1]
+    for across, term in weight_rows(core, chips, xn_t, (d_low, d_high), attn_t, (g_zero, g_mid, g_one)):
         for z in range(chips):
-            both[z, :, across] = term[z * rows : (z + 1) * rows] + got[z, :, across].astype(F32)
+            both[z, :, across] = term[z * rows : (z + 1) * rows]
+
+
+def keep_kernel(chips, steps, got, both, *outs):
+    chip = lax.axis_index("dom") // 2
     half = got.shape[2] // 2
     for n, (first, second) in enumerate(steps):
         give, own = outs[2 * n : 2 * n + 2]
         across = slice(n * half, (n + 1) * half)
-        give[0] = both[lax.bitwise_xor(chip, first), :, across].astype(BF16)
-        give[1] = both[lax.bitwise_xor(chip, first ^ second), :, across].astype(BF16)
-        own[0] = both[chip, :, across]
-        own[1] = both[lax.bitwise_xor(chip, second), :, across]
+
+        def total(distance):
+            z = lax.bitwise_xor(chip, distance)
+            return both[z, :, across] + got[z, :, across].astype(F32)
+
+        give[0] = total(first).astype(BF16)
+        give[1] = total(first ^ second).astype(BF16)
+        own[0] = total(0)
+        own[1] = total(second)
 
 
 def middle_kernel(own_a, got_a, own_b, got_b, *refs):
@@ -576,13 +580,17 @@
     if direct:
         got = lax.ppermute(give[0], "dom", other_core(parts))
         steps = ((1, 2), (2, 1))
+        mine = call(
+            functools.partial(mine_kernel, chips), "mine", [((chips, row, every), F32)],
+            [xn_t, d_low, d_high, attn_t, g_zero, g_mid, g_one],
+        )[0]
         give_a, own_a, give_b, own_b = call(
             functools.partial(keep_kernel, chips, steps), "keep",
             [((2, row, every // 2), BF16), ((2, row, every // 2), F32)] * 2,
-            [got, xn_t, d_low, d_high, attn_t, g_zero, g_mid, g_one], scratch=[((chips, row, every), F32)],
-        )
+            [got, mine],
+        )
+        got_a = lax.ppermute(give_a, "dom", chips_apart(parts, steps[0][0]))
         got_b = lax.ppermute(give_b, "dom", chips_apart(parts, steps[1][0]))
-        got_a = lax.ppermute(give_a, "dom", chips_apart(parts, steps[0][0]))
         after = own_a
     y, c_on, c_off = call(
         functools.partial(last_input_kernel, blk, tile), "last_input",

time: 98 us -> 97 us (0.990)
  waiting for transfers between devices: 29.2 us -> 28.1 us
    ppermute x1, waiting for transfers between devices: 2.65 us -> 1.63 us  [local(): got = lax.ppermute(give[0], 'dom', other_core(parts))]
    pallas_call x29 -> x30, Pallas kernels: 38.1 us -> 38.1 us  [call(): pl.pallas_call(kernel, in_specs=[scalars] * smem + [vmem] * (len(args) -...]
  transfers between devices with their start and end apart: 24 -> 24, of which waited for: 8 -> 8; matrix products, arithmetic and copies ran while one was open for 0% -> 0% of each run, Pallas kernels for 29% -> 30%
where the time goes in v6:
time: 97 us; the launch traced here: 96.7 us
  Pallas kernels  38.1 us (39%)
  waiting for transfers between devices  28.1 us (29%)
  starting transfers between devices  27 us (28%)
  local copies, waits for them, and re-layouts  2.41 us (2%)
  between operations  1.06 us (1%)
    pallas_call x30, Pallas kernels, call(): pl.pallas_call(kernel, in_specs=[scalars] * smem + [vmem] * (len(args) -...  38.1 us
    ppermute x9, waiting for transfers between devices, local(): lax.ppermute(part, 'section', [(here, here - 1)])  11.5 us
    ppermute x4, starting transfers between devices, local(): off = lax.ppermute(c_off, 'dom', next_chip(parts))  8.7 us
    ppermute x9, starting transfers between devices, local(): lax.ppermute(part, 'section', [(here, here - 1)])  8.29 us
    ppermute x1, waiting for transfers between devices, local(): got_a = lax.ppermute(give_a, 'dom', chips_apart(parts, steps[0][0]))  6.66 us
    ppermute x1, starting transfers between devices, local(): x_off = lax.ppermute(x_off, 'dom', next_chip(parts))  4.71 us
    ppermute x1, waiting for transfers between devices, local(): got_a = lax.ppermute(give_a, 'dom', chips_apart(parts, steps[0][1]))  3.82 us
    ppermute x1, waiting for transfers between devices, local(): got_b = lax.ppermute(give_b, 'dom', chips_apart(parts, steps[1][0]))  3.31 us
  transfers between devices with their start and end apart: 24, of which 8 were waited for; matrix products, arithmetic and copies ran while one was open for 0% of the time, Pallas kernels for 30%

profile of v6, /device:TPU:0, one launch (start us, length us, event | category | flops | bytes accessed | tf_op | source)
XLA Modules:
  0.0 96.7 jit_solution(3806627662390057936)
XLA Ops:
  0.6 1.0 %copy-done.3 = bf16[1,1,384,512]{3,2,1,0:T(8,128)(2,1)S(1)} copy-done((bf16[1,1,384,512]{3,2,1,0:T(8,128)(2,1)S(1)}, bf16[1,1,384,512]{3,2,1,0:T(8,128)(2,1)}, u32[]{:S(2)}) %copy-start.3) | copy-done | bytes 393240
  1.7 0.5 collective-permute-start
  2.2 4.7 %collective-permute-start.1 = (bf16[128,512]{1,0:T(8,128)(2,1)S(1)}, bf16[128,512]{1,0:T(8,128)(2,1)S(1)}, u32[]{:S(2)}, u32[]{:S(2)}) collective-permute-start(bf16[128,512]{1,0:T(8,128)(2,1)S(1)} %get-tuple-element.81), channel_id=1, source_target_pairs={{0,7},{1,2},{2,1},{3,4},{4,3},{5,6},{6,5},{7,0},{8,15},{9,10},{10,... | collective-permute-start | bytes 393224 | tf_op jit(solution)/shard_map/ppermute | solution.py:491
  6.9 1.4 %copy-done = bf16[1,512,1536]{2,1,0:T(8,128)(2,1)S(1)} copy-done((bf16[1,512,1536]{2,1,0:T(8,128)(2,1)S(1)}, bf16[1,512,1536]{2,1,0:T(8,128)(2,1)}, u32[]{:S(2)}) %copy-start) | copy-done | bytes 1572888
  8.3 1.2 %prelude_own.1 = (bf16[512,384]{1,0:T(8,128)(2,1)S(1)}, f32[8,384]{1,0:T(8,128)S(1)}, bf16[384,512]{1,0:T(8,128)(2,1)S(1)}, bf16[384,512]{1,0:T(8,128)(2,1)S(1)}...) custom-call(bf16[384,512]{1,0:T(8,128)(2,1)S(1)} %bitcast.36, ...), custom_call_target="tpu_custom_call" | custom-call | flops 1 | bytes 1 | tf_op jit(solution)/shard_map/prelude_own/pallas_call | solution.py:30
  9.5 0.0 collective-permute-done.x_on
  9.6 0.7 collective-permute-done.1.x_off
  10.2 0.0 copy-start.2
  10.3 3.4 %prelude.1 = (bf16[512,640]{1,0:T(8,128)(2,1)S(1)}, f32[8,640]{1,0:T(8,128)S(1)}, bf16[640,512]{1,0:T(8,128)(2,1)S(1)}, bf16[512,640]{1,0:T(8,128)(2,1)S(1)}, bf...) custom-call(s32[3,3]{1,0:T(4,128)S(1)} %copy-done.5, ...), custom_call_target="tpu_custom_call" | custom-call | flops 1 | bytes 1 | tf_op jit(solution)/shard_map/prelude/pallas_call | solution.py:30
  13.7 1.5 %stage_zero.3 = (bf16[512,128]{1,0:T(8,128)(2,1)S(1)}, bf16[4,384,256]{2,1,0:T(8,128)(2,1)S(1)}, bf16[512,128]{1,0:T(8,128)(2,1)S(1)}) custom-call(bf16[512,128]{1,0:T(8,128)(2,1)S(1)} %get-tuple-element.91.refs_0_.refs_1_, bf16[512,512]{1,0:T(8,128)(2,1)S(1)} %bitcast.23, bf16[640,512]{1,0:T(8,128)(2,1)S(1)} %get-tuple-element.92.refs_2_.refs_5_.v_nat.refs_3_.refs_6_, ...), custom_call_target="tpu_custom_call" | custom-call | flops 1 | bytes 1 | tf_op jit(solution)/shard_map/stage_zero/pallas_call | solution.py:30
  15.2 0.1 collective-permute-start.5
  15.3 1.4 %stage_one.3 = (bf16[512,128]{1,0:T(8,128)(2,1)S(1)}, bf16[512,128]{1,0:T(8,128)(2,1)S(1)}) custom-call(bf16[512,128]{1,0:T(8,128)(2,1)S(1)} %get-tuple-element.89.refs_0_.g_one, bf16[512,512]{1,0:T(8,128)(2,1)S(1)} %bitcast.24, bf16[640,512]{1,0:T(8,128)(2,1)S(1)} %get-tuple-element.92.refs_2_.refs_5_.v_nat.refs_3_.refs_6_, ...), custom_call_target="tpu_custom_call" | custom-call | flops 1 | bytes 1 | tf_op jit(solution)/shard_map/stage_one/pallas_call | solution.py:30
  16.7 2.9 %collective-permute-start.2 = (bf16[512,128]{1,0:T(8,128)(2,1)S(1)}, bf16[512,128]{1,0:T(8,128)(2,1)S(1)}, u32[]{:S(2)}, u32[]{:S(2)}) collective-permute-start(bf16[512,128]{1,0:T(8,128)(2,1)S(1)} %get-tuple-element.104), channel_id=1, source_target_pairs={{0,7},{1,2},{2,1},{3,4},{4,3},{5,6},{6,5},{7,0},{8,15},{9,10},{10,... | collective-permute-start | bytes 393224 | tf_op jit(solution)/shard_map/ppermute | solution.py:544
  19.6 2.2 %stage_mid.3 = (bf16[512,128]{1,0:T(8,128)(2,1)S(1)}, bf16[4,1,384,256]{3,2,1,0:T(8,128)(2,1)S(1)}, bf16[512,128]{1,0:T(8,128)(2,1)S(1)}) custom-call(bf16[512,128]{1,0:T(8,128)(2,1)S(1)} %get-tuple-element.90.refs_0_.g_mid, bf16[512,128]{1,0:T(8,128)(2,1)S(1)} %get-tuple-element.91.refs_0_.refs_1_, bf16[512,128]{1,0:T(8,128)(2,1)S(1)} %get-tuple-element.97.refs_2_.da_zero, ...), custom_call_target="tpu_custom_call" | custom-call | flops 1 | bytes 1 | tf_op jit(solution)/shard_map/stage_mid/pallas_call | solution.py:30
  21.8 0.0 collective-permute-done.5.rim
  21.9 0.7 collective-permute-start.6
  22.5 2.1 %stage_main.3 = (bf16[512,128]{1,0:T(8,128)(2,1)S(1)}, bf16[512,128]{1,0:T(8,128)(2,1)S(1)}) custom-call(bf16[512,128]{1,0:T(8,128)(2,1)S(1)} %get-tuple-element.90.refs_0_.g_mid, bf16[512,128]{1,0:T(8,128)(2,1)S(1)} %get-tuple-element.89.refs_0_.g_one, bf16[512,128]{1,0:T(8,128)(2,1)S(1)} %get-tuple-element.97.refs_2_.da_zero, ...), custom_call_target="tpu_custom_call" | custom-call | flops 1 | bytes 1 | tf_op jit(solution)/shard_map/stage_main/pallas_call | solution.py:30
  24.7 0.7 collective-permute-start.3
  25.4 0.8 collective-permute-start.4
  26.2 0.0 collective-permute-done.6.refs_1_
  26.2 1.6 %stage_zero.4 = (bf16[512,128]{1,0:T(8,128)(2,1)S(1)}, bf16[512,128]{1,0:T(8,128)(2,1)S(1)}, bf16[4,384,256]{2,1,0:T(8,128)(2,1)S(1)}, bf16[512,128]{1,0:T(8,128)(2,1)S(1)}) custom-call(bf16[512,128]{1,0:T(8,128)(2,1)S(1)} %get-tuple-element.91.refs_0_.refs_1_, bf16[512,128]{1,0:T(8,128)(2,1)S(1)} %collective-permute-done.6.refs_1_, ...), custom_call_target="tpu_custom_call" | custom-call | flops 1 | bytes 1 | tf_op jit(solution)/shard_map/stage_zero/pallas_call | solution.py:30
  27.8 0.1 collective-permute-start.10
  27.9 1.4 %stage_one.4 = (bf16[512,128]{1,0:T(8,128)(2,1)S(1)}, bf16[512,128]{1,0:T(8,128)(2,1)S(1)}, bf16[512,128]{1,0:T(8,128)(2,1)S(1)}) custom-call(bf16[512,128]{1,0:T(8,128)(2,1)S(1)} %get-tuple-element.89.refs_0_.g_one, bf16[512,128]{1,0:T(8,128)(2,1)S(1)} %collective-permute-done.3.refs_1_, bf16[512,512]{1,0:T(8,128)(2,1)S(1)} %bitcast.27, ...), custom_call_target="tpu_custom_call" | custom-call | flops 1 | bytes 1 | tf_op jit(solution)/shard_map/stage_one/pallas_call | solution.py:30
  29.3 1.2 %collective-permute-start.7 = (bf16[512,128]{1,0:T(8,128)(2,1)S(1)}, bf16[512,128]{1,0:T(8,128)(2,1)S(1)}, u32[]{:S(2)}, u32[]{:S(2)}) collective-permute-start(bf16[512,128]{1,0:T(8,128)(2,1)S(1)} %get-tuple-element.117), channel_id=1, source_target_pairs={{0,7},{1,2},{2,1},{3,4},{4,3},{5,6},{6,5},{7,0},{8,15},{9,10},{10,... | collective-permute-start | bytes 393224 | tf_op jit(solution)/shard_map/ppermute | solution.py:544
  30.5 2.2 %stage_mid.4 = (bf16[512,128]{1,0:T(8,128)(2,1)S(1)}, bf16[512,128]{1,0:T(8,128)(2,1)S(1)}, bf16[4,1,384,256]{3,2,1,0:T(8,128)(2,1)S(1)}, bf16[512,128]{1,0:T(8,128)(2,1)S(1)}) custom-call(bf16[512,128]{1,0:T(8,128)(2,1)S(1)} %get-tuple-element.90.refs_0_.g_mid, bf16[512,128]{1,0:T(8,128)(2,1)S(1)} %collective-permute-done.4.refs_1_, ...), custom_call_target="tpu_custom_call" | custom-call | flops 1 | bytes 1 | tf_op jit(solution)/shard_map/stage_mid/pallas_call | solution.py:30
  32.8 0.7 collective-permute-start.11
  33.5 2.1 %stage_main.4 = (bf16[512,128]{1,0:T(8,128)(2,1)S(1)}, bf16[512,128]{1,0:T(8,128)(2,1)S(1)}) custom-call(bf16[512,128]{1,0:T(8,128)(2,1)S(1)} %get-tuple-element.112.g_mid.refs_0_, bf16[512,128]{1,0:T(8,128)(2,1)S(1)} %get-tuple-element.105.g_one.refs_0_, bf16[512,128]{1,0:T(8,128)(2,1)S(1)} %get-tuple-element.110.refs_3_.da_zero, ...), custom_call_target="tpu_custom_call" | custom-call | flops 1 | bytes 1 | tf_op jit(solution)/shard_map/stage_main/pallas_call | solution.py:30
  35.6 0.3 collective-permute-done.7.rim
  35.9 0.7 collective-permute-start.8
  36.5 0.7 collective-permute-start.9
  37.2 0.0 collective-permute-done.11.refs_1_
  37.2 1.5 %stage_zero.5 = (bf16[512,128]{1,0:T(8,128)(2,1)S(1)}, bf16[512,128]{1,0:T(8,128)(2,1)S(1)}, bf16[4,384,256]{2,1,0:T(8,128)(2,1)S(1)}, bf16[512,128]{1,0:T(8,128)(2,1)S(1)}) custom-call(bf16[512,128]{1,0:T(8,128)(2,1)S(1)} %get-tuple-element.109.refs_2_.refs_0_, bf16[512,128]{1,0:T(8,128)(2,1)S(1)} %collective-permute-done.11.refs_1_, ...), custom_call_target="tpu_custom_call" | custom-call | flops 1 | bytes 1 | tf_op jit(solution)/shard_map/stage_zero/pallas_call | solution.py:30
  38.8 0.1 collective-permute-start.14
  38.9 0.0 collective-permute-done.8.refs_1_
  38.9 1.4 %stage_one.5 = (bf16[512,128]{1,0:T(8,128)(2,1)S(1)}, bf16[512,128]{1,0:T(8,128)(2,1)S(1)}, bf16[512,128]{1,0:T(8,128)(2,1)S(1)}) custom-call(bf16[512,128]{1,0:T(8,128)(2,1)S(1)} %get-tuple-element.105.g_one.refs_0_, bf16[512,128]{1,0:T(8,128)(2,1)S(1)} %collective-permute-done.8.refs_1_, bf16[512,512]{1,0:T(8,128)(2,1)S(1)} %bitcast.30, ...), custom_call_target="tpu_custom_call" | custom-call | flops 1 | bytes 1 | tf_op jit(solution)/shard_map/stage_one/pallas_call | solution.py:30
  40.3 2.2 %collective-permute-start.12 = (bf16[512,128]{1,0:T(8,128)(2,1)S(1)}, bf16[512,128]{1,0:T(8,128)(2,1)S(1)}, u32[]{:S(2)}, u32[]{:S(2)}) collective-permute-start(bf16[512,128]{1,0:T(8,128)(2,1)S(1)} %get-tuple-element.130), channel_id=1, source_target_pairs={{0,7},{1,2},{2,1},{3,4},{4,3},{5,6},{6,5},{7,0},{8,15},{9,10},{10,... | collective-permute-start | bytes 393224 | tf_op jit(solution)/shard_map/ppermute | solution.py:544
  42.5 0.0 collective-permute-done.9.refs_1_
  42.5 2.2 %stage_mid.5 = (bf16[512,128]{1,0:T(8,128)(2,1)S(1)}, bf16[512,128]{1,0:T(8,128)(2,1)S(1)}, bf16[4,1,384,256]{3,2,1,0:T(8,128)(2,1)S(1)}, bf16[512,128]{1,0:T(8,128)(2,1)S(1)}) custom-call(bf16[512,128]{1,0:T(8,128)(2,1)S(1)} %get-tuple-element.112.g_mid.refs_0_, bf16[512,128]{1,0:T(8,128)(2,1)S(1)} %collective-permute-done.9.refs_1_, ...), custom_call_target="tpu_custom_call" | custom-call | flops 1 | bytes 1 | tf_op jit(solution)/shard_map/stage_mid/pallas_call | solution.py:30
  44.7 2.1 %stage_main.5 = (bf16[512,128]{1,0:T(8,128)(2,1)S(1)}, bf16[512,128]{1,0:T(8,128)(2,1)S(1)}) custom-call(bf16[512,128]{1,0:T(8,128)(2,1)S(1)} %get-tuple-element.125.g_mid.g_prev, bf16[512,128]{1,0:T(8,128)(2,1)S(1)} %get-tuple-element.118.g_one.g_prev, bf16[512,128]{1,0:T(8,128)(2,1)S(1)} %get-tuple-element.123.refs_3_.da_zero, ...), custom_call_target="tpu_custom_call" | custom-call | flops 1 | bytes 1 | tf_op jit(solution)/shard_map/stage_main/pallas_call | solution.py:30
  46.9 1.3 %collective-permute-start.15 = (bf16[512,128]{1,0:T(8,128)(2,1)S(1)}, bf16[512,128]{1,0:T(8,128)(2,1)S(1)}, u32[]{:S(2)}, u32[]{:S(2)}) collective-permute-start(bf16[512,128]{1,0:T(8,128)(2,1)S(1)} %add_on.5), channel_id=1, source_target_pairs={{8,0},{9,1},{10,2},{11,3},{12,4},{13,5},{14,6},{15,7}} | collective-permute-start | bytes 393224 | tf_op jit(solution)/shard_map/ppermute | solution.py:555
  48.2 1.3 %collective-permute-start.16 = (bf16[512,128]{1,0:T(8,128)(2,1)S(1)}, bf16[512,128]{1,0:T(8,128)(2,1)S(1)}, u32[]{:S(2)}, u32[]{:S(2)}) collective-permute-start(bf16[512,128]{1,0:T(8,128)(2,1)S(1)} %get-tuple-element.134), channel_id=1, source_target_pairs={{8,0},{9,1},{10,2},{11,3},{12,4},{13,5},{14,6},{15,7}} | collective-permute-start | bytes 393224 | tf_op jit(solution)/shard_map/ppermute | solution.py:555
  49.5 1.5 %collective-permute-start.13 = (bf16[512,128]{1,0:T(8,128)(2,1)S(1)}, bf16[512,128]{1,0:T(8,128)(2,1)S(1)}, u32[]{:S(2)}, u32[]{:S(2)}) collective-permute-start(bf16[512,128]{1,0:T(8,128)(2,1)S(1)} %add_off.5), channel_id=1, source_target_pairs={{8,0},{9,1},{10,2},{11,3},{12,4},{13,5},{14,6},{15,7}} | collective-permute-start | bytes 393224 | tf_op jit(solution)/shard_map/ppermute | solution.py:555
  51.1 11.5 %collective-permute-done.15.refs_1_ = bf16[512,128]{1,0:T(8,128)(2,1)S(1)} collective-permute-done((bf16[512,128]{1,0:T(8,128)(2,1)S(1)}, bf16[512,128]{1,0:T(8,128)(2,1)S(1)}, u32[]{:S(2)}, u32[]{:S(2)}) %collective-permute-start.15) | collective-permute-done | bytes 131104 | tf_op jit(solution)/shard_map/ppermute | solution.py:555
  62.5 2.2 %last_zero.1 = (bf16[512,128]{1,0:T(8,128)(2,1)S(1)}, bf16[512,128]{1,0:T(8,128)(2,1)S(1)}, bf16[4,384,256]{2,1,0:T(8,128)(2,1)S(1)}, bf16[512,128]{1,0:T(8,128)(2,1)}) custom-call(bf16[512,128]{1,0:T(8,128)(2,1)S(1)} %get-tuple-element.122.refs_2_.refs_0_, bf16[512,128]{1,0:T(8,128)(2,1)S(1)} %collective-permute-done.15.refs_1_, ...), custom_call_target="tpu_custom_call" | custom-call | flops 1 | bytes 1 | tf_op jit(solution)/shard_map/last_zero/pallas_call | solution.py:30
  64.7 1.5 %last_mid.1 = (bf16[512,128]{1,0:T(8,128)(2,1)S(1)}, bf16[512,128]{1,0:T(8,128)(2,1)S(1)}, bf16[4,1,384,256]{3,2,1,0:T(8,128)(2,1)S(1)}, bf16[1536,256]{1,0:T(8,128)(2,1)S(1)}) custom-call(bf16[512,128]{1,0:T(8,128)(2,1)S(1)} %get-tuple-element.125.g_mid.g_prev, bf16[512,128]{1,0:T(8,128)(2,1)S(1)} %collective-permute-done.16.arrived, ...), custom_call_target="tpu_custom_call" | custom-call | flops 1 | bytes 1 | tf_op jit(solution)/shard_map/last_mid/pallas_call | solution.py:30
  66.2 3.0 %last_terms.1 = (bf16[512,128]{1,0:T(8,128)(2,1)S(1)}, bf16[1536,384]{1,0:T(8,128)(2,1)S(1)}, bf16[4,64,2048]{2,1,0:T(8,128)(2,1)S(1)}) custom-call(bf16[512,128]{1,0:T(8,128)(2,1)S(1)} %get-tuple-element.118.g_one.g_prev, bf16[512,128]{1,0:T(8,128)(2,1)S(1)} %collective-permute-done.13.arrived, bf16[512,128]{1,0:T(8,128)(2,1)S(1)} %get-tuple-element.133.g_zero, ...), custom_call_target="tpu_custom_call" | custom-call | flops 1 | bytes 1 | tf_op jit(solution)/shard_map/last_terms/pallas_call | solution.py:30
  69.2 0.1 collective-permute-start.17
  69.3 1.0 %mine.1.both = f32[4,64,2048]{2,1,0:T(8,128)S(1)} custom-call(bf16[512,640]{1,0:T(8,128)(2,1)S(1)} %get-tuple-element.95.refs_6_.refs_9_.xn_t.refs_7_.refs_10_, bf16[1536,256]{1,0:T(8,128)(2,1)S(1)} %get-tuple-element.140.d_low, bf16[1536,384]{1,0:T(8,128)(2,1)S(1)} %get-tuple-element.142.d_high, ...), custom_call_target="tpu_custom_call" | custom-call | flops 1 | bytes 1 | tf_op jit(solution)/shard_map/mine/pallas_call | solution.py:30
  70.3 1.6 %collective-permute-done.17.got = bf16[4,64,2048]{2,1,0:T(8,128)(2,1)S(1)} collective-permute-done((bf16[4,64,2048]{2,1,0:T(8,128)(2,1)S(1)}, bf16[4,64,2048]{2,1,0:T(8,128)(2,1)S(1)}, u32[]{:S(2)}, u32[]{:S(2)}) %collective-permute-start.17) | collective-permute-done | bytes 1048608 | tf_op jit(solution)/shard_map/ppermute | solution.py:581
  71.9 0.2 keep.1
  72.1 0.1 collective-permute-start.20
  72.2 2.1 %collective-permute-start.21 = (bf16[2,64,1024]{2,1,0:T(8,128)(2,1)S(1)}, bf16[2,64,1024]{2,1,0:T(8,128)(2,1)S(1)}, u32[]{:S(2)}, u32[]{:S(2)}) collective-permute-start(bf16[2,64,1024]{2,1,0:T(8,128)(2,1)S(1)} %get-tuple-element.150), channel_id=1, source_target_pairs={{0,4},{1,5},{2,6},{3,7},{4,0},{5,1},{6,2},{7,3},{8,12},{9,13},{10,... | collective-permute-start | bytes 786440 | tf_op jit(solution)/shard_map/ppermute | solution.py:593
  74.3 1.8 %last_input.1 = (bf16[512,384]{1,0:T(8,128)(2,1)S(1)}, bf16[512,128]{1,0:T(8,128)(2,1)S(1)}, bf16[512,128]{1,0:T(8,128)(2,1)S(1)}) custom-call(f32[2,64,1024]{2,1,0:T(8,128)S(1)} %get-tuple-element.144.after.own_a, bf16[512,128]{1,0:T(8,128)(2,1)S(1)} %get-tuple-element.133.g_zero, bf16[512,128]{1,0:T(8,128)(2,1)S(1)} %get-tuple-element.137.g_mid, ...), custom_call_target="tpu_custom_call" | custom-call | flops 1 | bytes 1 | tf_op jit(solution)/shard_map/last_input/pallas_call | solution.py:30
  76.1 0.1 collective-permute-start.18
  76.2 2.4 %collective-permute-start.19 = (bf16[512,128]{1,0:T(8,128)(2,1)S(1)}, bf16[512,128]{1,0:T(8,128)(2,1)S(1)}, u32[]{:S(2)}, u32[]{:S(2)}) collective-permute-start(bf16[512,128]{1,0:T(8,128)(2,1)S(1)} %get-tuple-element.147), channel_id=1, source_target_pairs={{0,7},{1,2},{2,1},{3,4},{4,3},{5,6},{6,5},{7,0},{8,15},{9,10},{10,... | collective-permute-start | bytes 393224 | tf_op jit(solution)/shard_map/ppermute | solution.py:600
  78.6 6.7 %collective-permute-done.20.got_a = bf16[2,64,1024]{2,1,0:T(8,128)(2,1)S(1)} collective-permute-done((bf16[2,64,1024]{2,1,0:T(8,128)(2,1)S(1)}, bf16[2,64,1024]{2,1,0:T(8,128)(2,1)S(1)}, u32[]{:S(2)}, u32[]{:S(2)}) %collective-permute-start.20) | collective-permute-done | bytes 262176 | tf_op jit(solution)/shard_map/ppermute | solution.py:592
  85.2 3.3 %collective-permute-done.21.got_b = bf16[2,64,1024]{2,1,0:T(8,128)(2,1)S(1)} collective-permute-done((bf16[2,64,1024]{2,1,0:T(8,128)(2,1)S(1)}, bf16[2,64,1024]{2,1,0:T(8,128)(2,1)S(1)}, u32[]{:S(2)}, u32[]{:S(2)}) %collective-permute-start.21) | collective-permute-done | bytes 262176 | tf_op jit(solution)/shard_map/ppermute | solution.py:593
  88.6 0.1 middle.1
  88.6 0.1 collective-permute-start.22
  88.7 2.2 %collective-permute-start.23 = (bf16[64,1024]{1,0:T(8,128)(2,1)S(1)}, bf16[64,1024]{1,0:T(8,128)(2,1)S(1)}, u32[]{:S(2)}, u32[]{:S(2)}) collective-permute-start(bf16[64,1024]{1,0:T(8,128)(2,1)S(1)} %get-tuple-element.154), channel_id=1, source_target_pairs={{0,2},{1,3},{2,0},{3,1},{4,6},{5,7},{6,4},{7,5},{8,10},{9,11},{10,... | collective-permute-start | bytes 393224 | tf_op jit(solution)/shard_map/ppermute | solution.py:607
  90.9 0.9 finish_input.1
  91.9 3.8 %collective-permute-done.22.got_a = bf16[64,1024]{1,0:T(8,128)(2,1)S(1)} collective-permute-done((bf16[64,1024]{1,0:T(8,128)(2,1)S(1)}, bf16[64,1024]{1,0:T(8,128)(2,1)S(1)}, u32[]{:S(2)}, u32[]{:S(2)}) %collective-permute-start.22) | collective-permute-done | bytes 131104 | tf_op jit(solution)/shard_map/ppermute | solution.py:608
  95.7 0.2 collective-permute-done.23.got_b
  95.9 0.8 total.1
  (26 shorter events, 0.3 us)
Async XLA Ops:
  0.6 1.0 %copy-start.3 = (bf16[1,1,384,512]{3,2,1,0:T(8,128)(2,1)S(1)}, bf16[1,1,384,512]{3,2,1,0:T(8,128)(2,1)}, u32[]{:S(2)}) copy-start(bf16[1,1,384,512]{3,2,1,0:T(8,128)(2,1)} %param.5) | copy-start | bytes 1179652
  1.6 8.6 %copy-start.4 = (bf16[1,384,512]{2,1,0:T(8,128)(2,1)S(1)}, bf16[1,384,512]{2,1,0:T(8,128)(2,1)}, u32[]{:S(2)}) copy-start(bf16[1,384,512]{2,1,0:T(8,128)(2,1)} %param.6) | copy-start | bytes 1179652
  1.6 8.6 %copy-start.5 = (s32[3,3]{1,0:T(4,128)S(1)}, s32[3,3]{1,0:T(4,128)}, u32[]{:S(2)}) copy-start(s32[3,3]{1,0:T(4,128)} %neighbours.1) | copy-start | bytes 112
  1.7 7.9 %collective-permute-start = (bf16[128,512]{1,0:T(8,128)(2,1)S(1)}, bf16[128,512]{1,0:T(8,128)(2,1)S(1)}, u32[]{:S(2)}, u32[]{:S(2)}) collective-permute-start(bf16[128,512]{1,0:T(8,128)(2,1)S(1)} %get-tuple-element.80), channel_id=1, source_target_pairs={{0,1},{1,0},{2,3},{3,2},{4,5},{5,4},{6,7},{7,6},{8,9},{9,8},{10,11... | collective-permute-start | bytes 393224 | tf_op jit(solution)/shard_map/ppermute | solution.py:490
  2.2 8.1 %collective-permute-start.1 = (bf16[128,512]{1,0:T(8,128)(2,1)S(1)}, bf16[128,512]{1,0:T(8,128)(2,1)S(1)}, u32[]{:S(2)}, u32[]{:S(2)}) collective-permute-start(bf16[128,512]{1,0:T(8,128)(2,1)S(1)} %get-tuple-element.81), channel_id=1, source_target_pairs={{0,7},{1,2},{2,1},{3,4},{4,3},{5,6},{6,5},{7,0},{8,15},{9,10},{10,... | collective-permute-start | bytes 393224 | tf_op jit(solution)/shard_map/ppermute | solution.py:491
  6.9 1.4 %copy-start = (bf16[1,512,1536]{2,1,0:T(8,128)(2,1)S(1)}, bf16[1,512,1536]{2,1,0:T(8,128)(2,1)}, u32[]{:S(2)}) copy-start(bf16[1,512,1536]{2,1,0:T(8,128)(2,1)} %param.7) | copy-start | bytes 4718596
  8.3 1.9 %copy-start.1 = (bf16[1,512,1536]{2,1,0:T(8,128)(2,1)S(1)}, bf16[1,512,1536]{2,1,0:T(8,128)(2,1)}, u32[]{:S(2)}) copy-start(bf16[1,512,1536]{2,1,0:T(8,128)(2,1)} %param.7) | copy-start | bytes 4718596
  10.2 3.4 %copy-start.2 = (bf16[1,512,512]{2,1,0:T(8,128)(2,1)S(1)}, bf16[1,512,512]{2,1,0:T(8,128)(2,1)}, u32[]{:S(2)}) copy-start(bf16[1,512,512]{2,1,0:T(8,128)(2,1)} %param.8) | copy-start | bytes 1572868
  15.2 6.6 %collective-permute-start.5 = (bf16[512,128]{1,0:T(8,128)(2,1)S(1)}, bf16[512,128]{1,0:T(8,128)(2,1)S(1)}, u32[]{:S(2)}, u32[]{:S(2)}) collective-permute-start(bf16[512,128]{1,0:T(8,128)(2,1)S(1)} %get-tuple-element.108), channel_id=1, source_target_pairs={{0,1},{1,0},{2,3},{3,2},{4,5},{5,4},{6,7},{7,6},{8,9},{9,8},{10,11... | collective-permute-start | bytes 393224 | tf_op jit(solution)/shard_map/ppermute | solution.py:529
  16.7 7.9 %collective-permute-start.2 = (bf16[512,128]{1,0:T(8,128)(2,1)S(1)}, bf16[512,128]{1,0:T(8,128)(2,1)S(1)}, u32[]{:S(2)}, u32[]{:S(2)}) collective-permute-start(bf16[512,128]{1,0:T(8,128)(2,1)S(1)} %get-tuple-element.104), channel_id=1, source_target_pairs={{0,7},{1,2},{2,1},{3,4},{4,3},{5,6},{6,5},{7,0},{8,15},{9,10},{10,... | collective-permute-start | bytes 393224 | tf_op jit(solution)/shard_map/ppermute | solution.py:544
  21.9 4.4 %collective-permute-start.6 = (bf16[512,128]{1,0:T(8,128)(2,1)S(1)}, bf16[512,128]{1,0:T(8,128)(2,1)S(1)}, u32[]{:S(2)}, u32[]{:S(2)}) collective-permute-start(bf16[512,128]{1,0:T(8,128)(2,1)S(1)} %add_on.3), channel_id=1, source_target_pairs={{24,16},{25,17},{26,18},{27,19},{28,20},{29,21},{30,22},{31,23}} | collective-permute-start | bytes 393224 | tf_op jit(solution)/shard_map/ppermute | solution.py:555
  24.7 3.2 %collective-permute-start.3 = (bf16[512,128]{1,0:T(8,128)(2,1)S(1)}, bf16[512,128]{1,0:T(8,128)(2,1)S(1)}, u32[]{:S(2)}, u32[]{:S(2)}) collective-permute-start(bf16[512,128]{1,0:T(8,128)(2,1)S(1)} %add_off.3), channel_id=1, source_target_pairs={{24,16},{25,17},{26,18},{27,19},{28,20},{29,21},{30,22},{31,23}} | collective-permute-start | bytes 393224 | tf_op jit(solution)/shard_map/ppermute | solution.py:555
  25.4 5.1 %collective-permute-start.4 = (bf16[512,128]{1,0:T(8,128)(2,1)S(1)}, bf16[512,128]{1,0:T(8,128)(2,1)S(1)}, u32[]{:S(2)}, u32[]{:S(2)}) collective-permute-start(bf16[512,128]{1,0:T(8,128)(2,1)S(1)} %get-tuple-element.106), channel_id=1, source_target_pairs={{24,16},{25,17},{26,18},{27,19},{28,20},{29,21},{30,22},{31,23}} | collective-permute-start | bytes 393224 | tf_op jit(solution)/shard_map/ppermute | solution.py:555
  27.8 4.9 %collective-permute-start.10 = (bf16[512,128]{1,0:T(8,128)(2,1)S(1)}, bf16[512,128]{1,0:T(8,128)(2,1)S(1)}, u32[]{:S(2)}, u32[]{:S(2)}) collective-permute-start(bf16[512,128]{1,0:T(8,128)(2,1)S(1)} %get-tuple-element.121), channel_id=1, source_target_pairs={{0,1},{1,0},{2,3},{3,2},{4,5},{5,4},{6,7},{7,6},{8,9},{9,8},{10,11... | collective-permute-start | bytes 393224 | tf_op jit(solution)/shard_map/ppermute | solution.py:529
  29.3 6.5 %collective-permute-start.7 = (bf16[512,128]{1,0:T(8,128)(2,1)S(1)}, bf16[512,128]{1,0:T(8,128)(2,1)S(1)}, u32[]{:S(2)}, u32[]{:S(2)}) collective-permute-start(bf16[512,128]{1,0:T(8,128)(2,1)S(1)} %get-tuple-element.117), channel_id=1, source_target_pairs={{0,7},{1,2},{2,1},{3,4},{4,3},{5,6},{6,5},{7,0},{8,15},{9,10},{10,... | collective-permute-start | bytes 393224 | tf_op jit(solution)/shard_map/ppermute | solution.py:544
  32.8 4.4 %collective-permute-start.11 = (bf16[512,128]{1,0:T(8,128)(2,1)S(1)}, bf16[512,128]{1,0:T(8,128)(2,1)S(1)}, u32[]{:S(2)}, u32[]{:S(2)}) collective-permute-start(bf16[512,128]{1,0:T(8,128)(2,1)S(1)} %add_on.4), channel_id=1, source_target_pairs={{16,8},{17,9},{18,10},{19,11},{20,12},{21,13},{22,14},{23,15}} | collective-permute-start | bytes 393224 | tf_op jit(solution)/shard_map/ppermute | solution.py:555
  35.9 3.0 %collective-permute-start.8 = (bf16[512,128]{1,0:T(8,128)(2,1)S(1)}, bf16[512,128]{1,0:T(8,128)(2,1)S(1)}, u32[]{:S(2)}, u32[]{:S(2)}) collective-permute-start(bf16[512,128]{1,0:T(8,128)(2,1)S(1)} %add_off.4), channel_id=1, source_target_pairs={{16,8},{17,9},{18,10},{19,11},{20,12},{21,13},{22,14},{23,15}} | collective-permute-start | bytes 393224 | tf_op jit(solution)/shard_map/ppermute | solution.py:555
  36.5 6.0 %collective-permute-start.9 = (bf16[512,128]{1,0:T(8,128)(2,1)S(1)}, bf16[512,128]{1,0:T(8,128)(2,1)S(1)}, u32[]{:S(2)}, u32[]{:S(2)}) collective-permute-start(bf16[512,128]{1,0:T(8,128)(2,1)S(1)} %get-tuple-element.119), channel_id=1, source_target_pairs={{16,8},{17,9},{18,10},{19,11},{20,12},{21,13},{22,14},{23,15}} | collective-permute-start | bytes 393224 | tf_op jit(solution)/shard_map/ppermute | solution.py:555
  38.8 8.1 %collective-permute-start.14 = (bf16[512,128]{1,0:T(8,128)(2,1)S(1)}, bf16[512,128]{1,0:T(8,128)(2,1)S(1)}, u32[]{:S(2)}, u32[]{:S(2)}) collective-permute-start(bf16[512,128]{1,0:T(8,128)(2,1)S(1)} %get-tuple-element.132), channel_id=1, source_target_pairs={{0,1},{1,0},{2,3},{3,2},{4,5},{5,4},{6,7},{7,6},{8,9},{9,8},{10,11... | collective-permute-start | bytes 393224 | tf_op jit(solution)/shard_map/ppermute | solution.py:529
  40.3 9.2 %collective-permute-start.12 = (bf16[512,128]{1,0:T(8,128)(2,1)S(1)}, bf16[512,128]{1,0:T(8,128)(2,1)S(1)}, u32[]{:S(2)}, u32[]{:S(2)}) collective-permute-start(bf16[512,128]{1,0:T(8,128)(2,1)S(1)} %get-tuple-element.130), channel_id=1, source_target_pairs={{0,7},{1,2},{2,1},{3,4},{4,3},{5,6},{6,5},{7,0},{8,15},{9,10},{10,... | collective-permute-start | bytes 393224 | tf_op jit(solution)/shard_map/ppermute | solution.py:544
  46.9 15.6 %collective-permute-start.15 = (bf16[512,128]{1,0:T(8,128)(2,1)S(1)}, bf16[512,128]{1,0:T(8,128)(2,1)S(1)}, u32[]{:S(2)}, u32[]{:S(2)}) collective-permute-start(bf16[512,128]{1,0:T(8,128)(2,1)S(1)} %add_on.5), channel_id=1, source_target_pairs={{8,0},{9,1},{10,2},{11,3},{12,4},{13,5},{14,6},{15,7}} | collective-permute-start | bytes 393224 | tf_op jit(solution)/shard_map/ppermute | solution.py:555
  48.2 16.5 %collective-permute-start.16 = (bf16[512,128]{1,0:T(8,128)(2,1)S(1)}, bf16[512,128]{1,0:T(8,128)(2,1)S(1)}, u32[]{:S(2)}, u32[]{:S(2)}) collective-permute-start(bf16[512,128]{1,0:T(8,128)(2,1)S(1)} %get-tuple-element.134), channel_id=1, source_target_pairs={{8,0},{9,1},{10,2},{11,3},{12,4},{13,5},{14,6},{15,7}} | collective-permute-start | bytes 393224 | tf_op jit(solution)/shard_map/ppermute | solution.py:555
  49.5 16.7 %collective-permute-start.13 = (bf16[512,128]{1,0:T(8,128)(2,1)S(1)}, bf16[512,128]{1,0:T(8,128)(2,1)S(1)}, u32[]{:S(2)}, u32[]{:S(2)}) collective-permute-start(bf16[512,128]{1,0:T(8,128)(2,1)S(1)} %add_off.5), channel_id=1, source_target_pairs={{8,0},{9,1},{10,2},{11,3},{12,4},{13,5},{14,6},{15,7}} | collective-permute-start | bytes 393224 | tf_op jit(solution)/shard_map/ppermute | solution.py:555
  69.2 2.7 %collective-permute-start.17 = (bf16[4,64,2048]{2,1,0:T(8,128)(2,1)S(1)}, bf16[4,64,2048]{2,1,0:T(8,128)(2,1)S(1)}, u32[]{:S(2)}, u32[]{:S(2)}) collective-permute-start(bf16[4,64,2048]{2,1,0:T(8,128)(2,1)S(1)} %get-tuple-element.141), channel_id=1, source_target_pairs={{0,1},{1,0},{2,3},{3,2},{4,5},{5,4},{6,7},{7,6},{8,9},{9,8},{10,11... | collective-permute-start | bytes 3145736 | tf_op jit(solution)/shard_map/ppermute | solution.py:581
  72.1 13.1 %collective-permute-start.20 = (bf16[2,64,1024]{2,1,0:T(8,128)(2,1)S(1)}, bf16[2,64,1024]{2,1,0:T(8,128)(2,1)S(1)}, u32[]{:S(2)}, u32[]{:S(2)}) collective-permute-start(bf16[2,64,1024]{2,1,0:T(8,128)(2,1)S(1)} %get-tuple-element.148), channel_id=1, source_target_pairs={{0,2},{1,3},{2,0},{3,1},{4,6},{5,7},{6,4},{7,5},{8,10},{9,11},{10,... | collective-permute-start | bytes 786440 | tf_op jit(solution)/shard_map/ppermute | solution.py:592
  72.2 16.4 %collective-permute-start.21 = (bf16[2,64,1024]{2,1,0:T(8,128)(2,1)S(1)}, bf16[2,64,1024]{2,1,0:T(8,128)(2,1)S(1)}, u32[]{:S(2)}, u32[]{:S(2)}) collective-permute-start(bf16[2,64,1024]{2,1,0:T(8,128)(2,1)S(1)} %get-tuple-element.150), channel_id=1, source_target_pairs={{0,4},{1,5},{2,6},{3,7},{4,0},{5,1},{6,2},{7,3},{8,12},{9,13},{10,... | collective-permute-start | bytes 786440 | tf_op jit(solution)/shard_map/ppermute | solution.py:593
  76.1 2.5 %collective-permute-start.18 = (bf16[512,128]{1,0:T(8,128)(2,1)S(1)}, bf16[512,128]{1,0:T(8,128)(2,1)S(1)}, u32[]{:S(2)}, u32[]{:S(2)}) collective-permute-start(bf16[512,128]{1,0:T(8,128)(2,1)S(1)} %get-tuple-element.146), channel_id=1, source_target_pairs={{0,1},{1,0},{2,3},{3,2},{4,5},{5,4},{6,7},{7,6},{8,9},{9,8},{10,11... | collective-permute-start | bytes 393224 | tf_op jit(solution)/shard_map/ppermute | solution.py:601
  76.2 14.7 %collective-permute-start.19 = (bf16[512,128]{1,0:T(8,128)(2,1)S(1)}, bf16[512,128]{1,0:T(8,128)(2,1)S(1)}, u32[]{:S(2)}, u32[]{:S(2)}) collective-permute-start(bf16[512,128]{1,0:T(8,128)(2,1)S(1)} %get-tuple-element.147), channel_id=1, source_target_pairs={{0,7},{1,2},{2,1},{3,4},{4,3},{5,6},{6,5},{7,0},{8,15},{9,10},{10,... | collective-permute-start | bytes 393224 | tf_op jit(solution)/shard_map/ppermute | solution.py:600
  88.6 7.0 %collective-permute-start.22 = (bf16[64,1024]{1,0:T(8,128)(2,1)S(1)}, bf16[64,1024]{1,0:T(8,128)(2,1)S(1)}, u32[]{:S(2)}, u32[]{:S(2)}) collective-permute-start(bf16[64,1024]{1,0:T(8,128)(2,1)S(1)} %get-tuple-element.152), channel_id=1, source_target_pairs={{0,4},{1,5},{2,6},{3,7},{4,0},{5,1},{6,2},{7,3},{8,12},{9,13},{10,... | collective-permute-start | bytes 393224 | tf_op jit(solution)/shard_map/ppermute | solution.py:608
  88.7 7.2 %collective-permute-start.23 = (bf16[64,1024]{1,0:T(8,128)(2,1)S(1)}, bf16[64,1024]{1,0:T(8,128)(2,1)S(1)}, u32[]{:S(2)}, u32[]{:S(2)}) collective-permute-start(bf16[64,1024]{1,0:T(8,128)(2,1)S(1)} %get-tuple-element.154), channel_id=1, source_target_pairs={{0,2},{1,3},{2,0},{3,1},{4,6},{5,7},{6,4},{7,5},{8,10},{9,11},{10,... | collective-permute-start | bytes 393224 | tf_op jit(solution)/shard_map/ppermute | solution.py:607

commit v7 on v6

--- a/solution.py
+++ b/solution.py
@@ -349,7 +349,7 @@
 
 
 def last_terms_kernel(
-    blk, tile, chips, g_prev, arrived, g_zero, g_mid, da_zero, da_mid, ds_zero, ds_mid, w_out, v_nat, k_t,
+    blk, tile, chips, after, g_prev, arrived, g_zero, g_mid, da_zero, da_mid, ds_zero, ds_mid, w_out, v_nat, k_t,
     q_t, probs, attn_t, xn_t, d_low, g_one, d_high, *refs
 ):
     *give, da_one, ds_one = refs
@@ -371,20 +371,19 @@
 
 
 def last_input_kernel(
-    blk, tile, after, g_zero, g_mid, g_one, d_low, d_high, w_qkv, xn_t, inv, y, c_on, c_off
+    blk, tile, after, g_zero, g_mid, g_one, d_low, d_high, w_qkv, xn_t, inv, y, c_off
 ):
     outs = []
-    for part in (d_low, d_high):
-        dn = mm(w_qkv[...], part[...])
+    for part in (d_low[:, tile:], d_high[...]):
+        dn = mm(w_qkv[...], part)
         for n in range(part.shape[1] // tile):
-            here = cols(len(outs), tile=tile)
+            here = cols(len(outs) + 1, tile=tile)
             outs.append(norm_grad(dn[:, cols(n, tile=tile)], xn_t[:, here], inv[0:1, here]))
-    c_on[...] = outs[0].astype(BF16)
     c_off[...] = outs[-1].astype(BF16)
     for b in range(blk):
         own = cols(b, tile=tile)
         g = g_zero[...] if b == 0 else g_mid[:, cols(b - 1, tile=tile)] if b < blk - 1 else g_one[...]
-        y[:, own] = (g.astype(F32) + outs[b + 1]).astype(BF16)
+        y[:, own] = (g.astype(F32) + outs[b]).astype(BF16)
 
 
 def finish_input_kernel(blk, tile, y_t, on, off, out):
@@ -557,11 +556,12 @@
     chips = parts // 2
     every = 4 * width
     row = width // parts
-    g_zero, da_zero, ds_zero, _ = call(
+    g_zero, da_zero, ds_zero, c_on = call(
         functools.partial(stage_zero_kernel, blk, tile, True), "last_zero",
         [(single, BF16)] + zero_shape + [(single, BF16)],
         [g_zero, received[0], *common, *for_rim], scratch=rim_scratch,
     )
+    on = lax.ppermute(c_on, "dom", other_core(parts))
     g_mid, da_mid, ds_mid, d_low = call(
         functools.partial(last_mid_kernel, blk, tile), "last_mid",
         [(middle, BF16)] + mid_shape + [((3 * width, 2 * tile), BF16)],
@@ -571,7 +571,7 @@
         functools.partial(last_terms_kernel, blk, tile, chips), "last_terms",
         [(single, BF16), ((3 * width, rows), BF16)] + [((chips, row, every), BF16)] * direct,
         [
-            g_one, received[2], g_zero, g_mid, da_zero, da_mid, ds_zero, ds_mid, w_back, v_nat, k_t, q_t,
+            on, g_one, received[2], g_zero, g_mid, da_zero, da_mid, ds_zero, ds_mid, w_back, v_nat, k_t, q_t,
             probs, attn_t, xn_t, d_low,
         ],
         scratch=[(single, BF16), ((pairs, *pair_shape), BF16)],
@@ -592,17 +592,16 @@
         got_a = lax.ppermute(give_a, "dom", chips_apart(parts, steps[0][0]))
         got_b = lax.ppermute(give_b, "dom", chips_apart(parts, steps[1][0]))
         after = own_a
-    y, c_on, c_off = call(
+    y, c_off = call(
         functools.partial(last_input_kernel, blk, tile), "last_input",
-        [(whole, BF16), (single, BF16), (single, BF16)],
+        [(whole, BF16), (single, BF16)],
         [after, g_zero, g_mid, g_one, d_low, d_high, w_in, xn_t, inv],
     )
     off = lax.ppermute(c_off, "dom", next_chip(parts))
-    on = lax.ppermute(c_on, "dom", other_core(parts))
     if direct:
         give_a, rest_a, give_b, rest_b = call(
             middle_kernel, "middle", [((row, every // 2), BF16), ((row, every // 2), F32)] * 2,
-            [own_a, got_a, own_b, got_b, on],
+            [own_a, got_a, own_b, got_b, c_off],
         )
         got_b = lax.ppermute(give_b, "dom", chips_apart(parts, steps[1][1]))
         got_a = lax.ppermute(give_a, "dom", chips_apart(parts, steps[0][1]))

time: 97 us -> 96.6 us (level)
  waiting for transfers between devices: 28.1 us -> 29.6 us
  starting transfers between devices: 27 us -> 25.8 us
  transfers between devices with their start and end apart: 24 -> 24, of which waited for: 8 -> 9; matrix products, arithmetic and copies ran while one was open for 0% -> 0% of each run, Pallas kernels for 30% -> 30%
where the time goes in v7:
time: 96.6 us; the launch traced here: 96.3 us
  Pallas kernels  37.4 us (39%)
  waiting for transfers between devices  29.6 us (31%)
  starting transfers between devices  25.8 us (27%)
  local copies, waits for them, and re-layouts  2.41 us (2%)
  between operations  1.07 us (1%)
    pallas_call x30, Pallas kernels, call(): pl.pallas_call(kernel, in_specs=[scalars] * smem + [vmem] * (len(args) -...  37.4 us
    ppermute x9, waiting for transfers between devices, local(): lax.ppermute(part, 'section', [(here, here - 1)])  11.2 us
    ppermute x4, starting transfers between devices, local(): off = lax.ppermute(c_off, 'dom', next_chip(parts))  8.46 us
    ppermute x9, starting transfers between devices, local(): lax.ppermute(part, 'section', [(here, here - 1)])  8.29 us
    ppermute x1, waiting for transfers between devices, local(): got_a = lax.ppermute(give_a, 'dom', chips_apart(parts, steps[0][0]))  7.06 us
    ppermute x1, starting transfers between devices, local(): x_off = lax.ppermute(x_off, 'dom', next_chip(parts))  4.71 us
    ppermute x1, waiting for transfers between devices, local(): got_a = lax.ppermute(give_a, 'dom', chips_apart(parts, steps[0][1]))  4.15 us
    ppermute x1, waiting for transfers between devices, local(): got_b = lax.ppermute(give_b, 'dom', chips_apart(parts, steps[1][0]))  4.04 us
  transfers between devices with their start and end apart: 24, of which 9 were waited for; matrix products, arithmetic and copies ran while one was open for 0% of the time, Pallas kernels for 30%

profile of v7, /device:TPU:0, one launch (start us, length us, event | category | flops | bytes accessed | tf_op | source)
XLA Modules:
  0.0 96.3 jit_solution(4281967515612901265)
XLA Ops:
  0.6 1.0 %copy-done.3 = bf16[1,1,384,512]{3,2,1,0:T(8,128)(2,1)S(1)} copy-done((bf16[1,1,384,512]{3,2,1,0:T(8,128)(2,1)S(1)}, bf16[1,1,384,512]{3,2,1,0:T(8,128)(2,1)}, u32[]{:S(2)}) %copy-start.3) | copy-done | bytes 393240
  1.7 0.5 collective-permute-start
  2.2 4.7 %collective-permute-start.1 = (bf16[128,512]{1,0:T(8,128)(2,1)S(1)}, bf16[128,512]{1,0:T(8,128)(2,1)S(1)}, u32[]{:S(2)}, u32[]{:S(2)}) collective-permute-start(bf16[128,512]{1,0:T(8,128)(2,1)S(1)} %get-tuple-element.81), channel_id=1, source_target_pairs={{0,7},{1,2},{2,1},{3,4},{4,3},{5,6},{6,5},{7,0},{8,15},{9,10},{10,... | collective-permute-start | bytes 393224 | tf_op jit(solution)/shard_map/ppermute | solution.py:490
  6.9 1.4 %copy-done = bf16[1,512,1536]{2,1,0:T(8,128)(2,1)S(1)} copy-done((bf16[1,512,1536]{2,1,0:T(8,128)(2,1)S(1)}, bf16[1,512,1536]{2,1,0:T(8,128)(2,1)}, u32[]{:S(2)}) %copy-start) | copy-done | bytes 1572888
  8.3 1.2 %prelude_own.1 = (bf16[512,384]{1,0:T(8,128)(2,1)S(1)}, f32[8,384]{1,0:T(8,128)S(1)}, bf16[384,512]{1,0:T(8,128)(2,1)S(1)}, bf16[384,512]{1,0:T(8,128)(2,1)S(1)}...) custom-call(bf16[384,512]{1,0:T(8,128)(2,1)S(1)} %bitcast.36, ...), custom_call_target="tpu_custom_call" | custom-call | flops 1 | bytes 1 | tf_op jit(solution)/shard_map/prelude_own/pallas_call | solution.py:30
  9.5 0.0 collective-permute-done.x_on
  9.6 0.7 collective-permute-done.1.x_off
  10.2 0.0 copy-start.2
  10.3 3.4 %prelude.1 = (bf16[512,640]{1,0:T(8,128)(2,1)S(1)}, f32[8,640]{1,0:T(8,128)S(1)}, bf16[640,512]{1,0:T(8,128)(2,1)S(1)}, bf16[512,640]{1,0:T(8,128)(2,1)S(1)}, bf...) custom-call(s32[3,3]{1,0:T(4,128)S(1)} %copy-done.5, ...), custom_call_target="tpu_custom_call" | custom-call | flops 1 | bytes 1 | tf_op jit(solution)/shard_map/prelude/pallas_call | solution.py:30
  13.7 1.5 %stage_zero.3 = (bf16[512,128]{1,0:T(8,128)(2,1)S(1)}, bf16[4,384,256]{2,1,0:T(8,128)(2,1)S(1)}, bf16[512,128]{1,0:T(8,128)(2,1)S(1)}) custom-call(bf16[512,128]{1,0:T(8,128)(2,1)S(1)} %get-tuple-element.89.refs_0_.refs_1_, bf16[512,512]{1,0:T(8,128)(2,1)S(1)} %bitcast.23, bf16[640,512]{1,0:T(8,128)(2,1)S(1)} %get-tuple-element.91.refs_2_.refs_5_.refs_3_.v_nat.refs_6_, ...), custom_call_target="tpu_custom_call" | custom-call | flops 1 | bytes 1 | tf_op jit(solution)/shard_map/stage_zero/pallas_call | solution.py:30
  15.2 0.1 collective-permute-start.2
  15.3 1.4 %stage_one.3 = (bf16[512,128]{1,0:T(8,128)(2,1)S(1)}, bf16[512,128]{1,0:T(8,128)(2,1)S(1)}) custom-call(bf16[512,128]{1,0:T(8,128)(2,1)S(1)} %get-tuple-element.102.refs_0_.g_one, bf16[512,512]{1,0:T(8,128)(2,1)S(1)} %bitcast.24, bf16[640,512]{1,0:T(8,128)(2,1)S(1)} %get-tuple-element.91.refs_2_.refs_5_.refs_3_.v_nat.refs_6_, ...), custom_call_target="tpu_custom_call" | custom-call | flops 1 | bytes 1 | tf_op jit(solution)/shard_map/stage_one/pallas_call | solution.py:30
  16.7 2.9 %collective-permute-start.7 = (bf16[512,128]{1,0:T(8,128)(2,1)S(1)}, bf16[512,128]{1,0:T(8,128)(2,1)S(1)}, u32[]{:S(2)}, u32[]{:S(2)}) collective-permute-start(bf16[512,128]{1,0:T(8,128)(2,1)S(1)} %get-tuple-element.114), channel_id=1, source_target_pairs={{0,7},{1,2},{2,1},{3,4},{4,3},{5,6},{6,5},{7,0},{8,15},{9,10},{10,... | collective-permute-start | bytes 393224 | tf_op jit(solution)/shard_map/ppermute | solution.py:543
  19.6 2.2 %stage_mid.3 = (bf16[512,128]{1,0:T(8,128)(2,1)S(1)}, bf16[4,1,384,256]{3,2,1,0:T(8,128)(2,1)S(1)}, bf16[512,128]{1,0:T(8,128)(2,1)S(1)}) custom-call(bf16[512,128]{1,0:T(8,128)(2,1)S(1)} %get-tuple-element.90.refs_0_.g_mid, bf16[512,128]{1,0:T(8,128)(2,1)S(1)} %get-tuple-element.89.refs_0_.refs_1_, bf16[512,128]{1,0:T(8,128)(2,1)S(1)} %get-tuple-element.96.refs_2_.da_zero, ...), custom_call_target="tpu_custom_call" | custom-call | flops 1 | bytes 1 | tf_op jit(solution)/shard_map/stage_mid/pallas_call | solution.py:30
  21.8 0.0 collective-permute-done.2.rim
  21.9 0.7 collective-permute-start.3
  22.5 2.1 %stage_main.3 = (bf16[512,128]{1,0:T(8,128)(2,1)S(1)}, bf16[512,128]{1,0:T(8,128)(2,1)S(1)}) custom-call(bf16[512,128]{1,0:T(8,128)(2,1)S(1)} %get-tuple-element.90.refs_0_.g_mid, bf16[512,128]{1,0:T(8,128)(2,1)S(1)} %get-tuple-element.102.refs_0_.g_one, bf16[512,128]{1,0:T(8,128)(2,1)S(1)} %get-tuple-element.96.refs_2_.da_zero, ...), custom_call_target="tpu_custom_call" | custom-call | flops 1 | bytes 1 | tf_op jit(solution)/shard_map/stage_main/pallas_call | solution.py:30
  24.7 0.7 collective-permute-start.8
  25.4 0.8 collective-permute-start.4
  26.2 0.0 collective-permute-done.3.refs_1_
  26.2 1.6 %stage_zero.4 = (bf16[512,128]{1,0:T(8,128)(2,1)S(1)}, bf16[512,128]{1,0:T(8,128)(2,1)S(1)}, bf16[4,384,256]{2,1,0:T(8,128)(2,1)S(1)}, bf16[512,128]{1,0:T(8,128)(2,1)S(1)}) custom-call(bf16[512,128]{1,0:T(8,128)(2,1)S(1)} %get-tuple-element.89.refs_0_.refs_1_, bf16[512,128]{1,0:T(8,128)(2,1)S(1)} %collective-permute-done.3.refs_1_, ...), custom_call_target="tpu_custom_call" | custom-call | flops 1 | bytes 1 | tf_op jit(solution)/shard_map/stage_zero/pallas_call | solution.py:30
  27.8 0.1 collective-permute-start.5
  27.9 1.4 %stage_one.4 = (bf16[512,128]{1,0:T(8,128)(2,1)S(1)}, bf16[512,128]{1,0:T(8,128)(2,1)S(1)}, bf16[512,128]{1,0:T(8,128)(2,1)S(1)}) custom-call(bf16[512,128]{1,0:T(8,128)(2,1)S(1)} %get-tuple-element.102.refs_0_.g_one, bf16[512,128]{1,0:T(8,128)(2,1)S(1)} %collective-permute-done.8.refs_1_, bf16[512,512]{1,0:T(8,128)(2,1)S(1)} %bitcast.27, ...), custom_call_target="tpu_custom_call" | custom-call | flops 1 | bytes 1 | tf_op jit(solution)/shard_map/stage_one/pallas_call | solution.py:30
  29.3 1.2 %collective-permute-start.13 = (bf16[512,128]{1,0:T(8,128)(2,1)S(1)}, bf16[512,128]{1,0:T(8,128)(2,1)S(1)}, u32[]{:S(2)}, u32[]{:S(2)}) collective-permute-start(bf16[512,128]{1,0:T(8,128)(2,1)S(1)} %get-tuple-element.126), channel_id=1, source_target_pairs={{0,7},{1,2},{2,1},{3,4},{4,3},{5,6},{6,5},{7,0},{8,15},{9,10},{10,... | collective-permute-start | bytes 393224 | tf_op jit(solution)/shard_map/ppermute | solution.py:543
  30.5 2.2 %stage_mid.4 = (bf16[512,128]{1,0:T(8,128)(2,1)S(1)}, bf16[512,128]{1,0:T(8,128)(2,1)S(1)}, bf16[4,1,384,256]{3,2,1,0:T(8,128)(2,1)S(1)}, bf16[512,128]{1,0:T(8,128)(2,1)S(1)}) custom-call(bf16[512,128]{1,0:T(8,128)(2,1)S(1)} %get-tuple-element.90.refs_0_.g_mid, bf16[512,128]{1,0:T(8,128)(2,1)S(1)} %collective-permute-done.4.refs_1_, ...), custom_call_target="tpu_custom_call" | custom-call | flops 1 | bytes 1 | tf_op jit(solution)/shard_map/stage_mid/pallas_call | solution.py:30
  32.8 0.7 collective-permute-start.6
  33.5 2.1 %stage_main.4 = (bf16[512,128]{1,0:T(8,128)(2,1)S(1)}, bf16[512,128]{1,0:T(8,128)(2,1)S(1)}) custom-call(bf16[512,128]{1,0:T(8,128)(2,1)S(1)} %get-tuple-element.112.g_mid.refs_0_, bf16[512,128]{1,0:T(8,128)(2,1)S(1)} %get-tuple-element.115.g_one.refs_0_, bf16[512,128]{1,0:T(8,128)(2,1)S(1)} %get-tuple-element.107.refs_3_.da_zero, ...), custom_call_target="tpu_custom_call" | custom-call | flops 1 | bytes 1 | tf_op jit(solution)/shard_map/stage_main/pallas_call | solution.py:30
  35.6 0.3 collective-permute-done.13.rim
  35.9 0.7 collective-permute-start.14
  36.5 0.7 collective-permute-start.9
  37.2 0.0 collective-permute-done.6.refs_1_
  37.2 1.5 %stage_zero.5 = (bf16[512,128]{1,0:T(8,128)(2,1)S(1)}, bf16[512,128]{1,0:T(8,128)(2,1)S(1)}, bf16[4,384,256]{2,1,0:T(8,128)(2,1)S(1)}, bf16[512,128]{1,0:T(8,128)(2,1)S(1)}) custom-call(bf16[512,128]{1,0:T(8,128)(2,1)S(1)} %get-tuple-element.101.refs_2_.refs_0_, bf16[512,128]{1,0:T(8,128)(2,1)S(1)} %collective-permute-done.6.refs_1_, ...), custom_call_target="tpu_custom_call" | custom-call | flops 1 | bytes 1 | tf_op jit(solution)/shard_map/stage_zero/pallas_call | solution.py:30
  38.8 0.1 collective-permute-start.10
  38.9 0.0 collective-permute-done.14.refs_1_
  38.9 1.4 %stage_one.5 = (bf16[512,128]{1,0:T(8,128)(2,1)S(1)}, bf16[512,128]{1,0:T(8,128)(2,1)S(1)}, bf16[512,128]{1,0:T(8,128)(2,1)S(1)}) custom-call(bf16[512,128]{1,0:T(8,128)(2,1)S(1)} %get-tuple-element.115.g_one.refs_0_, bf16[512,128]{1,0:T(8,128)(2,1)S(1)} %collective-permute-done.14.refs_1_, bf16[512,512]{1,0:T(8,128)(2,1)S(1)} %bitcast.30, ...), custom_call_target="tpu_custom_call" | custom-call | flops 1 | bytes 1 | tf_op jit(solution)/shard_map/stage_one/pallas_call | solution.py:30
  40.3 2.2 %collective-permute-start.15 = (bf16[512,128]{1,0:T(8,128)(2,1)S(1)}, bf16[512,128]{1,0:T(8,128)(2,1)S(1)}, u32[]{:S(2)}, u32[]{:S(2)}) collective-permute-start(bf16[512,128]{1,0:T(8,128)(2,1)S(1)} %get-tuple-element.133), channel_id=1, source_target_pairs={{0,7},{1,2},{2,1},{3,4},{4,3},{5,6},{6,5},{7,0},{8,15},{9,10},{10,... | collective-permute-start | bytes 393224 | tf_op jit(solution)/shard_map/ppermute | solution.py:543
  42.5 2.2 %stage_mid.5 = (bf16[512,128]{1,0:T(8,128)(2,1)S(1)}, bf16[512,128]{1,0:T(8,128)(2,1)S(1)}, bf16[4,1,384,256]{3,2,1,0:T(8,128)(2,1)S(1)}, bf16[512,128]{1,0:T(8,128)(2,1)S(1)}) custom-call(bf16[512,128]{1,0:T(8,128)(2,1)S(1)} %get-tuple-element.112.g_mid.refs_0_, bf16[512,128]{1,0:T(8,128)(2,1)S(1)} %collective-permute-done.9.refs_1_, ...), custom_call_target="tpu_custom_call" | custom-call | flops 1 | bytes 1 | tf_op jit(solution)/shard_map/stage_mid/pallas_call | solution.py:30
  44.8 1.3 %collective-permute-start.11 = (bf16[512,128]{1,0:T(8,128)(2,1)S(1)}, bf16[512,128]{1,0:T(8,128)(2,1)S(1)}, u32[]{:S(2)}, u32[]{:S(2)}) collective-permute-start(bf16[512,128]{1,0:T(8,128)(2,1)S(1)} %add_on.5), channel_id=1, source_target_pairs={{8,0},{9,1},{10,2},{11,3},{12,4},{13,5},{14,6},{15,7}} | collective-permute-start | bytes 393224 | tf_op jit(solution)/shard_map/ppermute | solution.py:554
  46.1 2.1 %stage_main.5 = (bf16[512,128]{1,0:T(8,128)(2,1)S(1)}, bf16[512,128]{1,0:T(8,128)(2,1)S(1)}) custom-call(bf16[512,128]{1,0:T(8,128)(2,1)S(1)} %get-tuple-element.128.g_mid.g_prev, bf16[512,128]{1,0:T(8,128)(2,1)S(1)} %get-tuple-element.127.g_one.g_prev, bf16[512,128]{1,0:T(8,128)(2,1)S(1)} %get-tuple-element.120.refs_3_.da_zero, ...), custom_call_target="tpu_custom_call" | custom-call | flops 1 | bytes 1 | tf_op jit(solution)/shard_map/stage_main/pallas_call | solution.py:30
  48.2 1.3 %collective-permute-start.17 = (bf16[512,128]{1,0:T(8,128)(2,1)S(1)}, bf16[512,128]{1,0:T(8,128)(2,1)S(1)}, u32[]{:S(2)}, u32[]{:S(2)}) collective-permute-start(bf16[512,128]{1,0:T(8,128)(2,1)S(1)} %get-tuple-element.135), channel_id=1, source_target_pairs={{8,0},{9,1},{10,2},{11,3},{12,4},{13,5},{14,6},{15,7}} | collective-permute-start | bytes 393224 | tf_op jit(solution)/shard_map/ppermute | solution.py:554
  49.5 1.5 %collective-permute-start.16 = (bf16[512,128]{1,0:T(8,128)(2,1)S(1)}, bf16[512,128]{1,0:T(8,128)(2,1)S(1)}, u32[]{:S(2)}, u32[]{:S(2)}) collective-permute-start(bf16[512,128]{1,0:T(8,128)(2,1)S(1)} %add_off.5), channel_id=1, source_target_pairs={{8,0},{9,1},{10,2},{11,3},{12,4},{13,5},{14,6},{15,7}} | collective-permute-start | bytes 393224 | tf_op jit(solution)/shard_map/ppermute | solution.py:554
  51.1 10.1 %collective-permute-done.11.refs_1_ = bf16[512,128]{1,0:T(8,128)(2,1)S(1)} collective-permute-done((bf16[512,128]{1,0:T(8,128)(2,1)S(1)}, bf16[512,128]{1,0:T(8,128)(2,1)S(1)}, u32[]{:S(2)}, u32[]{:S(2)}) %collective-permute-start.11) | collective-permute-done | bytes 131104 | tf_op jit(solution)/shard_map/ppermute | solution.py:554
  61.1 1.5 %last_zero.1 = (bf16[512,128]{1,0:T(8,128)(2,1)S(1)}, bf16[512,128]{1,0:T(8,128)(2,1)S(1)}, bf16[4,384,256]{2,1,0:T(8,128)(2,1)S(1)}, bf16[512,128]{1,0:T(8,128)(2,1)S(1)}) custom-call(bf16[512,128]{1,0:T(8,128)(2,1)S(1)} %get-tuple-element.111.refs_2_.refs_0_, bf16[512,128]{1,0:T(8,128)(2,1)S(1)} %collective-permute-done.11.refs_1_, ...), custom_call_target="tpu_custom_call" | custom-call | flops 1 | bytes 1 | tf_op jit(solution)/shard_map/last_zero/pallas_call | solution.py:30
  62.7 0.1 collective-permute-start.12
  62.7 1.1 %collective-permute-done.17.arrived = bf16[512,128]{1,0:T(8,128)(2,1)S(1)} collective-permute-done((bf16[512,128]{1,0:T(8,128)(2,1)S(1)}, bf16[512,128]{1,0:T(8,128)(2,1)S(1)}, u32[]{:S(2)}, u32[]{:S(2)}) %collective-permute-start.17) | collective-permute-done | bytes 131104 | tf_op jit(solution)/shard_map/ppermute | solution.py:554
  63.8 1.5 %last_mid.1 = (bf16[512,128]{1,0:T(8,128)(2,1)S(1)}, bf16[512,128]{1,0:T(8,128)(2,1)S(1)}, bf16[4,1,384,256]{3,2,1,0:T(8,128)(2,1)S(1)}, bf16[1536,256]{1,0:T(8,128)(2,1)S(1)}) custom-call(bf16[512,128]{1,0:T(8,128)(2,1)S(1)} %get-tuple-element.128.g_mid.g_prev, bf16[512,128]{1,0:T(8,128)(2,1)S(1)} %collective-permute-done.17.arrived, ...), custom_call_target="tpu_custom_call" | custom-call | flops 1 | bytes 1 | tf_op jit(solution)/shard_map/last_mid/pallas_call | solution.py:30
  65.3 3.0 %last_terms.1 = (bf16[512,128]{1,0:T(8,128)(2,1)S(1)}, bf16[1536,384]{1,0:T(8,128)(2,1)S(1)}, bf16[4,64,2048]{2,1,0:T(8,128)(2,1)S(1)}) custom-call(bf16[512,128]{1,0:T(8,128)(2,1)S(1)} %collective-permute-done.12.after.on, bf16[512,128]{1,0:T(8,128)(2,1)S(1)} %get-tuple-element.127.g_one.g_prev, bf16[512,128]{1,0:T(8,128)(2,1)S(1)} %collective-permute-done.16.arrived, ...), custom_call_target="tpu_custom_call" | custom-call | flops 1 | bytes 1 | tf_op jit(solution)/shard_map/last_terms/pallas_call | solution.py:30
  68.3 0.1 collective-permute-start.18
  68.4 1.0 %mine.1.both = f32[4,64,2048]{2,1,0:T(8,128)S(1)} custom-call(bf16[512,640]{1,0:T(8,128)(2,1)S(1)} %get-tuple-element.94.refs_6_.refs_9_.refs_7_.xn_t.refs_10_, bf16[1536,256]{1,0:T(8,128)(2,1)S(1)} %get-tuple-element.141.d_low, bf16[1536,384]{1,0:T(8,128)(2,1)S(1)} %get-tuple-element.143.d_high, ...), custom_call_target="tpu_custom_call" | custom-call | flops 1 | bytes 1 | tf_op jit(solution)/shard_map/mine/pallas_call | solution.py:30
  69.4 1.6 %collective-permute-done.18.got = bf16[4,64,2048]{2,1,0:T(8,128)(2,1)S(1)} collective-permute-done((bf16[4,64,2048]{2,1,0:T(8,128)(2,1)S(1)}, bf16[4,64,2048]{2,1,0:T(8,128)(2,1)S(1)}, u32[]{:S(2)}, u32[]{:S(2)}) %collective-permute-start.18) | collective-permute-done | bytes 1048608 | tf_op jit(solution)/shard_map/ppermute | solution.py:581
  71.1 0.2 keep.1
  71.2 0.1 collective-permute-start.20
  71.3 1.5 %collective-permute-start.21 = (bf16[2,64,1024]{2,1,0:T(8,128)(2,1)S(1)}, bf16[2,64,1024]{2,1,0:T(8,128)(2,1)S(1)}, u32[]{:S(2)}, u32[]{:S(2)}) collective-permute-start(bf16[2,64,1024]{2,1,0:T(8,128)(2,1)S(1)} %get-tuple-element.150), channel_id=1, source_target_pairs={{0,4},{1,5},{2,6},{3,7},{4,0},{5,1},{6,2},{7,3},{8,12},{9,13},{10,... | collective-permute-start | bytes 786440 | tf_op jit(solution)/shard_map/ppermute | solution.py:593
  72.8 1.8 %last_input.1 = (bf16[512,384]{1,0:T(8,128)(2,1)S(1)}, bf16[512,128]{1,0:T(8,128)(2,1)S(1)}) custom-call(f32[2,64,1024]{2,1,0:T(8,128)S(1)} %get-tuple-element.145.after.own_a, bf16[512,128]{1,0:T(8,128)(2,1)S(1)} %get-tuple-element.134.g_zero, bf16[512,128]{1,0:T(8,128)(2,1)S(1)} %get-tuple-element.138.g_mid, ...), custom_call_target="tpu_custom_call" | custom-call | flops 1 | bytes 1 | tf_op jit(solution)/shard_map/last_input/pallas_call | solution.py:30
  74.5 2.1 %collective-permute-start.19 = (bf16[512,128]{1,0:T(8,128)(2,1)S(1)}, bf16[512,128]{1,0:T(8,128)(2,1)S(1)}, u32[]{:S(2)}, u32[]{:S(2)}) collective-permute-start(bf16[512,128]{1,0:T(8,128)(2,1)S(1)} %get-tuple-element.147.refs_0_), channel_id=1, source_target_pairs={{0,7},{1,2},{2,1},{3,4},{4,3},{5,6},{6,5},{7,0},{8,15},{9,10},{10,... | collective-permute-start | bytes 393224 | tf_op jit(solution)/shard_map/ppermute | solution.py:600
  76.7 7.1 %collective-permute-done.20.got_a = bf16[2,64,1024]{2,1,0:T(8,128)(2,1)S(1)} collective-permute-done((bf16[2,64,1024]{2,1,0:T(8,128)(2,1)S(1)}, bf16[2,64,1024]{2,1,0:T(8,128)(2,1)S(1)}, u32[]{:S(2)}, u32[]{:S(2)}) %collective-permute-start.20) | collective-permute-done | bytes 262176 | tf_op jit(solution)/shard_map/ppermute | solution.py:592
  83.7 4.0 %collective-permute-done.21.got_b = bf16[2,64,1024]{2,1,0:T(8,128)(2,1)S(1)} collective-permute-done((bf16[2,64,1024]{2,1,0:T(8,128)(2,1)S(1)}, bf16[2,64,1024]{2,1,0:T(8,128)(2,1)S(1)}, u32[]{:S(2)}, u32[]{:S(2)}) %collective-permute-start.21) | collective-permute-done | bytes 262176 | tf_op jit(solution)/shard_map/ppermute | solution.py:593
  87.8 0.1 middle.1
  87.9 0.1 collective-permute-start.22
  88.0 1.8 %collective-permute-start.23 = (bf16[64,1024]{1,0:T(8,128)(2,1)S(1)}, bf16[64,1024]{1,0:T(8,128)(2,1)S(1)}, u32[]{:S(2)}, u32[]{:S(2)}) collective-permute-start(bf16[64,1024]{1,0:T(8,128)(2,1)S(1)} %get-tuple-element.154), channel_id=1, source_target_pairs={{0,2},{1,3},{2,0},{3,1},{4,6},{5,7},{6,4},{7,5},{8,10},{9,11},{10,... | collective-permute-start | bytes 393224 | tf_op jit(solution)/shard_map/ppermute | solution.py:606
  89.8 0.9 finish_input.1
  90.7 4.2 %collective-permute-done.22.got_a = bf16[64,1024]{1,0:T(8,128)(2,1)S(1)} collective-permute-done((bf16[64,1024]{1,0:T(8,128)(2,1)S(1)}, bf16[64,1024]{1,0:T(8,128)(2,1)S(1)}, u32[]{:S(2)}, u32[]{:S(2)}) %collective-permute-start.22) | collective-permute-done | bytes 131104 | tf_op jit(solution)/shard_map/ppermute | solution.py:607
  94.9 0.6 collective-permute-done.23.got_b
  95.5 0.8 total.1
  (26 shorter events, 0.3 us)
Async XLA Ops:
  0.6 1.0 %copy-start.3 = (bf16[1,1,384,512]{3,2,1,0:T(8,128)(2,1)S(1)}, bf16[1,1,384,512]{3,2,1,0:T(8,128)(2,1)}, u32[]{:S(2)}) copy-start(bf16[1,1,384,512]{3,2,1,0:T(8,128)(2,1)} %param.5) | copy-start | bytes 1179652
  1.6 8.6 %copy-start.4 = (bf16[1,384,512]{2,1,0:T(8,128)(2,1)S(1)}, bf16[1,384,512]{2,1,0:T(8,128)(2,1)}, u32[]{:S(2)}) copy-start(bf16[1,384,512]{2,1,0:T(8,128)(2,1)} %param.6) | copy-start | bytes 1179652
  1.6 8.6 %copy-start.5 = (s32[3,3]{1,0:T(4,128)S(1)}, s32[3,3]{1,0:T(4,128)}, u32[]{:S(2)}) copy-start(s32[3,3]{1,0:T(4,128)} %neighbours.1) | copy-start | bytes 112
  1.7 7.9 %collective-permute-start = (bf16[128,512]{1,0:T(8,128)(2,1)S(1)}, bf16[128,512]{1,0:T(8,128)(2,1)S(1)}, u32[]{:S(2)}, u32[]{:S(2)}) collective-permute-start(bf16[128,512]{1,0:T(8,128)(2,1)S(1)} %get-tuple-element.80), channel_id=1, source_target_pairs={{0,1},{1,0},{2,3},{3,2},{4,5},{5,4},{6,7},{7,6},{8,9},{9,8},{10,11... | collective-permute-start | bytes 393224 | tf_op jit(solution)/shard_map/ppermute | solution.py:489
  2.2 8.1 %collective-permute-start.1 = (bf16[128,512]{1,0:T(8,128)(2,1)S(1)}, bf16[128,512]{1,0:T(8,128)(2,1)S(1)}, u32[]{:S(2)}, u32[]{:S(2)}) collective-permute-start(bf16[128,512]{1,0:T(8,128)(2,1)S(1)} %get-tuple-element.81), channel_id=1, source_target_pairs={{0,7},{1,2},{2,1},{3,4},{4,3},{5,6},{6,5},{7,0},{8,15},{9,10},{10,... | collective-permute-start | bytes 393224 | tf_op jit(solution)/shard_map/ppermute | solution.py:490
  6.9 1.4 %copy-start = (bf16[1,512,1536]{2,1,0:T(8,128)(2,1)S(1)}, bf16[1,512,1536]{2,1,0:T(8,128)(2,1)}, u32[]{:S(2)}) copy-start(bf16[1,512,1536]{2,1,0:T(8,128)(2,1)} %param.7) | copy-start | bytes 4718596
  8.3 1.9 %copy-start.1 = (bf16[1,512,1536]{2,1,0:T(8,128)(2,1)S(1)}, bf16[1,512,1536]{2,1,0:T(8,128)(2,1)}, u32[]{:S(2)}) copy-start(bf16[1,512,1536]{2,1,0:T(8,128)(2,1)} %param.7) | copy-start | bytes 4718596
  10.2 3.4 %copy-start.2 = (bf16[1,512,512]{2,1,0:T(8,128)(2,1)S(1)}, bf16[1,512,512]{2,1,0:T(8,128)(2,1)}, u32[]{:S(2)}) copy-start(bf16[1,512,512]{2,1,0:T(8,128)(2,1)} %param.8) | copy-start | bytes 1572868
  15.2 6.6 %collective-permute-start.2 = (bf16[512,128]{1,0:T(8,128)(2,1)S(1)}, bf16[512,128]{1,0:T(8,128)(2,1)S(1)}, u32[]{:S(2)}, u32[]{:S(2)}) collective-permute-start(bf16[512,128]{1,0:T(8,128)(2,1)S(1)} %get-tuple-element.100), channel_id=1, source_target_pairs={{0,1},{1,0},{2,3},{3,2},{4,5},{5,4},{6,7},{7,6},{8,9},{9,8},{10,11... | collective-permute-start | bytes 393224 | tf_op jit(solution)/shard_map/ppermute | solution.py:528
  16.7 7.9 %collective-permute-start.7 = (bf16[512,128]{1,0:T(8,128)(2,1)S(1)}, bf16[512,128]{1,0:T(8,128)(2,1)S(1)}, u32[]{:S(2)}, u32[]{:S(2)}) collective-permute-start(bf16[512,128]{1,0:T(8,128)(2,1)S(1)} %get-tuple-element.114), channel_id=1, source_target_pairs={{0,7},{1,2},{2,1},{3,4},{4,3},{5,6},{6,5},{7,0},{8,15},{9,10},{10,... | collective-permute-start | bytes 393224 | tf_op jit(solution)/shard_map/ppermute | solution.py:543
  21.9 4.4 %collective-permute-start.3 = (bf16[512,128]{1,0:T(8,128)(2,1)S(1)}, bf16[512,128]{1,0:T(8,128)(2,1)S(1)}, u32[]{:S(2)}, u32[]{:S(2)}) collective-permute-start(bf16[512,128]{1,0:T(8,128)(2,1)S(1)} %add_on.3), channel_id=1, source_target_pairs={{24,16},{25,17},{26,18},{27,19},{28,20},{29,21},{30,22},{31,23}} | collective-permute-start | bytes 393224 | tf_op jit(solution)/shard_map/ppermute | solution.py:554
  24.7 3.2 %collective-permute-start.8 = (bf16[512,128]{1,0:T(8,128)(2,1)S(1)}, bf16[512,128]{1,0:T(8,128)(2,1)S(1)}, u32[]{:S(2)}, u32[]{:S(2)}) collective-permute-start(bf16[512,128]{1,0:T(8,128)(2,1)S(1)} %add_off.3), channel_id=1, source_target_pairs={{24,16},{25,17},{26,18},{27,19},{28,20},{29,21},{30,22},{31,23}} | collective-permute-start | bytes 393224 | tf_op jit(solution)/shard_map/ppermute | solution.py:554
  25.4 5.1 %collective-permute-start.4 = (bf16[512,128]{1,0:T(8,128)(2,1)S(1)}, bf16[512,128]{1,0:T(8,128)(2,1)S(1)}, u32[]{:S(2)}, u32[]{:S(2)}) collective-permute-start(bf16[512,128]{1,0:T(8,128)(2,1)S(1)} %get-tuple-element.106), channel_id=1, source_target_pairs={{24,16},{25,17},{26,18},{27,19},{28,20},{29,21},{30,22},{31,23}} | collective-permute-start | bytes 393224 | tf_op jit(solution)/shard_map/ppermute | solution.py:554
  27.8 4.9 %collective-permute-start.5 = (bf16[512,128]{1,0:T(8,128)(2,1)S(1)}, bf16[512,128]{1,0:T(8,128)(2,1)S(1)}, u32[]{:S(2)}, u32[]{:S(2)}) collective-permute-start(bf16[512,128]{1,0:T(8,128)(2,1)S(1)} %get-tuple-element.110), channel_id=1, source_target_pairs={{0,1},{1,0},{2,3},{3,2},{4,5},{5,4},{6,7},{7,6},{8,9},{9,8},{10,11... | collective-permute-start | bytes 393224 | tf_op jit(solution)/shard_map/ppermute | solution.py:528
  29.3 6.5 %collective-permute-start.13 = (bf16[512,128]{1,0:T(8,128)(2,1)S(1)}, bf16[512,128]{1,0:T(8,128)(2,1)S(1)}, u32[]{:S(2)}, u32[]{:S(2)}) collective-permute-start(bf16[512,128]{1,0:T(8,128)(2,1)S(1)} %get-tuple-element.126), channel_id=1, source_target_pairs={{0,7},{1,2},{2,1},{3,4},{4,3},{5,6},{6,5},{7,0},{8,15},{9,10},{10,... | collective-permute-start | bytes 393224 | tf_op jit(solution)/shard_map/ppermute | solution.py:543
  32.8 4.4 %collective-permute-start.6 = (bf16[512,128]{1,0:T(8,128)(2,1)S(1)}, bf16[512,128]{1,0:T(8,128)(2,1)S(1)}, u32[]{:S(2)}, u32[]{:S(2)}) collective-permute-start(bf16[512,128]{1,0:T(8,128)(2,1)S(1)} %add_on.4), channel_id=1, source_target_pairs={{16,8},{17,9},{18,10},{19,11},{20,12},{21,13},{22,14},{23,15}} | collective-permute-start | bytes 393224 | tf_op jit(solution)/shard_map/ppermute | solution.py:554
  35.9 3.0 %collective-permute-start.14 = (bf16[512,128]{1,0:T(8,128)(2,1)S(1)}, bf16[512,128]{1,0:T(8,128)(2,1)S(1)}, u32[]{:S(2)}, u32[]{:S(2)}) collective-permute-start(bf16[512,128]{1,0:T(8,128)(2,1)S(1)} %add_off.4), channel_id=1, source_target_pairs={{16,8},{17,9},{18,10},{19,11},{20,12},{21,13},{22,14},{23,15}} | collective-permute-start | bytes 393224 | tf_op jit(solution)/shard_map/ppermute | solution.py:554
  36.5 6.0 %collective-permute-start.9 = (bf16[512,128]{1,0:T(8,128)(2,1)S(1)}, bf16[512,128]{1,0:T(8,128)(2,1)S(1)}, u32[]{:S(2)}, u32[]{:S(2)}) collective-permute-start(bf16[512,128]{1,0:T(8,128)(2,1)S(1)} %get-tuple-element.119), channel_id=1, source_target_pairs={{16,8},{17,9},{18,10},{19,11},{20,12},{21,13},{22,14},{23,15}} | collective-permute-start | bytes 393224 | tf_op jit(solution)/shard_map/ppermute | solution.py:554
  38.8 5.9 %collective-permute-start.10 = (bf16[512,128]{1,0:T(8,128)(2,1)S(1)}, bf16[512,128]{1,0:T(8,128)(2,1)S(1)}, u32[]{:S(2)}, u32[]{:S(2)}) collective-permute-start(bf16[512,128]{1,0:T(8,128)(2,1)S(1)} %get-tuple-element.123), channel_id=1, source_target_pairs={{0,1},{1,0},{2,3},{3,2},{4,5},{5,4},{6,7},{7,6},{8,9},{9,8},{10,11... | collective-permute-start | bytes 393224 | tf_op jit(solution)/shard_map/ppermute | solution.py:528
  40.3 9.2 %collective-permute-start.15 = (bf16[512,128]{1,0:T(8,128)(2,1)S(1)}, bf16[512,128]{1,0:T(8,128)(2,1)S(1)}, u32[]{:S(2)}, u32[]{:S(2)}) collective-permute-start(bf16[512,128]{1,0:T(8,128)(2,1)S(1)} %get-tuple-element.133), channel_id=1, source_target_pairs={{0,7},{1,2},{2,1},{3,4},{4,3},{5,6},{6,5},{7,0},{8,15},{9,10},{10,... | collective-permute-start | bytes 393224 | tf_op jit(solution)/shard_map/ppermute | solution.py:543
  44.8 16.3 %collective-permute-start.11 = (bf16[512,128]{1,0:T(8,128)(2,1)S(1)}, bf16[512,128]{1,0:T(8,128)(2,1)S(1)}, u32[]{:S(2)}, u32[]{:S(2)}) collective-permute-start(bf16[512,128]{1,0:T(8,128)(2,1)S(1)} %add_on.5), channel_id=1, source_target_pairs={{8,0},{9,1},{10,2},{11,3},{12,4},{13,5},{14,6},{15,7}} | collective-permute-start | bytes 393224 | tf_op jit(solution)/shard_map/ppermute | solution.py:554
  48.2 15.6 %collective-permute-start.17 = (bf16[512,128]{1,0:T(8,128)(2,1)S(1)}, bf16[512,128]{1,0:T(8,128)(2,1)S(1)}, u32[]{:S(2)}, u32[]{:S(2)}) collective-permute-start(bf16[512,128]{1,0:T(8,128)(2,1)S(1)} %get-tuple-element.135), channel_id=1, source_target_pairs={{8,0},{9,1},{10,2},{11,3},{12,4},{13,5},{14,6},{15,7}} | collective-permute-start | bytes 393224 | tf_op jit(solution)/shard_map/ppermute | solution.py:554
  49.5 15.8 %collective-permute-start.16 = (bf16[512,128]{1,0:T(8,128)(2,1)S(1)}, bf16[512,128]{1,0:T(8,128)(2,1)S(1)}, u32[]{:S(2)}, u32[]{:S(2)}) collective-permute-start(bf16[512,128]{1,0:T(8,128)(2,1)S(1)} %add_off.5), channel_id=1, source_target_pairs={{8,0},{9,1},{10,2},{11,3},{12,4},{13,5},{14,6},{15,7}} | collective-permute-start | bytes 393224 | tf_op jit(solution)/shard_map/ppermute | solution.py:554
  62.7 2.7 %collective-permute-start.12 = (bf16[512,128]{1,0:T(8,128)(2,1)S(1)}, bf16[512,128]{1,0:T(8,128)(2,1)S(1)}, u32[]{:S(2)}, u32[]{:S(2)}) collective-permute-start(bf16[512,128]{1,0:T(8,128)(2,1)S(1)} %get-tuple-element.124), channel_id=1, source_target_pairs={{0,1},{1,0},{2,3},{3,2},{4,5},{5,4},{6,7},{7,6},{8,9},{9,8},{10,11... | collective-permute-start | bytes 393224 | tf_op jit(solution)/shard_map/ppermute | solution.py:564
  68.3 2.7 %collective-permute-start.18 = (bf16[4,64,2048]{2,1,0:T(8,128)(2,1)S(1)}, bf16[4,64,2048]{2,1,0:T(8,128)(2,1)S(1)}, u32[]{:S(2)}, u32[]{:S(2)}) collective-permute-start(bf16[4,64,2048]{2,1,0:T(8,128)(2,1)S(1)} %get-tuple-element.142), channel_id=1, source_target_pairs={{0,1},{1,0},{2,3},{3,2},{4,5},{5,4},{6,7},{7,6},{8,9},{9,8},{10,11... | collective-permute-start | bytes 3145736 | tf_op jit(solution)/shard_map/ppermute | solution.py:581
  71.2 12.5 %collective-permute-start.20 = (bf16[2,64,1024]{2,1,0:T(8,128)(2,1)S(1)}, bf16[2,64,1024]{2,1,0:T(8,128)(2,1)S(1)}, u32[]{:S(2)}, u32[]{:S(2)}) collective-permute-start(bf16[2,64,1024]{2,1,0:T(8,128)(2,1)S(1)} %get-tuple-element.148), channel_id=1, source_target_pairs={{0,2},{1,3},{2,0},{3,1},{4,6},{5,7},{6,4},{7,5},{8,10},{9,11},{10,... | collective-permute-start | bytes 786440 | tf_op jit(solution)/shard_map/ppermute | solution.py:592
  71.3 16.5 %collective-permute-start.21 = (bf16[2,64,1024]{2,1,0:T(8,128)(2,1)S(1)}, bf16[2,64,1024]{2,1,0:T(8,128)(2,1)S(1)}, u32[]{:S(2)}, u32[]{:S(2)}) collective-permute-start(bf16[2,64,1024]{2,1,0:T(8,128)(2,1)S(1)} %get-tuple-element.150), channel_id=1, source_target_pairs={{0,4},{1,5},{2,6},{3,7},{4,0},{5,1},{6,2},{7,3},{8,12},{9,13},{10,... | collective-permute-start | bytes 786440 | tf_op jit(solution)/shard_map/ppermute | solution.py:593
  74.5 15.2 %collective-permute-start.19 = (bf16[512,128]{1,0:T(8,128)(2,1)S(1)}, bf16[512,128]{1,0:T(8,128)(2,1)S(1)}, u32[]{:S(2)}, u32[]{:S(2)}) collective-permute-start(bf16[512,128]{1,0:T(8,128)(2,1)S(1)} %get-tuple-element.147.refs_0_), channel_id=1, source_target_pairs={{0,7},{1,2},{2,1},{3,4},{4,3},{5,6},{6,5},{7,0},{8,15},{9,10},{10,... | collective-permute-start | bytes 393224 | tf_op jit(solution)/shard_map/ppermute | solution.py:600
  87.9 7.0 %collective-permute-start.22 = (bf16[64,1024]{1,0:T(8,128)(2,1)S(1)}, bf16[64,1024]{1,0:T(8,128)(2,1)S(1)}, u32[]{:S(2)}, u32[]{:S(2)}) collective-permute-start(bf16[64,1024]{1,0:T(8,128)(2,1)S(1)} %get-tuple-element.152), channel_id=1, source_target_pairs={{0,4},{1,5},{2,6},{3,7},{4,0},{5,1},{6,2},{7,3},{8,12},{9,13},{10,... | collective-permute-start | bytes 393224 | tf_op jit(solution)/shard_map/ppermute | solution.py:607
  88.0 7.5 %collective-permute-start.23 = (bf16[64,1024]{1,0:T(8,128)(2,1)S(1)}, bf16[64,1024]{1,0:T(8,128)(2,1)S(1)}, u32[]{:S(2)}, u32[]{:S(2)}) collective-permute-start(bf16[64,1024]{1,0:T(8,128)(2,1)S(1)} %get-tuple-element.154), channel_id=1, source_target_pairs={{0,2},{1,3},{2,0},{3,1},{4,6},{5,7},{6,4},{7,5},{8,10},{9,11},{10,... | collective-permute-start | bytes 393224 | tf_op jit(solution)/shard_map/ppermute | solution.py:606

commit v8 on v7

--- a/solution.py
+++ b/solution.py
@@ -324,6 +324,18 @@
     )
 
 
+def stage_start_kernel(
+    blk, tile, g_zero, g_mid, g_one, w_out, v_nat, probs, attn_t, w_qkv, xn_t, inv, q_t, k_t,
+    da_zero, ds_zero, c_on, da_one, c_off, da_mid, ds_mid, zero, d_rim, d_rim_too, d_first,
+):
+    common = (w_out, v_nat, probs, attn_t, w_qkv, xn_t, inv, q_t)
+    stage_zero_kernel(blk, tile, False, g_zero, *common, da_zero, ds_zero, c_on, d_rim)
+    stage_one_kernel(blk, tile, False, g_one, *common, da_one, c_off, d_rim_too)
+    stage_mid_kernel(
+        blk, tile, False, g_mid, g_zero, da_zero, ds_zero, *common, k_t, da_mid, ds_mid, zero, d_first
+    )
+
+
 def stage_main_kernel(
     blk, tile, g_mid, g_one, da_zero, da_mid, da_one, ds_zero, ds_mid, w_qkv, xn_t, inv, v_nat, k_t, q_t,
     probs, attn_t, mid, one, ds_one, d_qkv,
@@ -518,28 +530,33 @@
     received = []
     for k in range(sections - 1):
         here = sections - 1 - k
-        moved = k > 0
-        *new, da_zero, ds_zero, c_on = call(
-            functools.partial(stage_zero_kernel, blk, tile, moved), "stage_zero",
-            [(single, BF16)] * moved + zero_shape + [(single, BF16)],
-            [g_zero, *received[:1], *common, *for_rim], scratch=rim_scratch,
-        )
-        g_zero = new[0] if moved else g_zero
-        on = lax.ppermute(c_on, "dom", other_core(parts))
-        *new, da_mid, ds_mid, zero = call(
-            functools.partial(stage_mid_kernel, blk, tile, moved), "stage_mid",
-            [(middle, BF16)] * moved + mid_shape + [(single, BF16)],
-            [g_mid, *received[1:2], g_zero, da_zero, ds_zero, *common, *for_rim, k_t],
-            scratch=[((3 * width, tile), BF16)],
-        )
-        g_mid = new[0] if moved else g_mid
+        if k == 0:
+            da_zero, ds_zero, c_on, da_one, c_off, da_mid, ds_mid, zero = call(
+                functools.partial(stage_start_kernel, blk, tile), "stage_start",
+                zero_shape + [(single, BF16)] * 3 + mid_shape + [(single, BF16)],
+                [g_zero, g_mid, g_one, *common, *for_rim, k_t],
+                scratch=rim_scratch * 2 + [((3 * width, tile), BF16)],
+            )
+            on = lax.ppermute(c_on, "dom", other_core(parts))
+        else:
+            g_zero, da_zero, ds_zero, c_on = call(
+                functools.partial(stage_zero_kernel, blk, tile, True), "stage_zero",
+                [(single, BF16)]  + zero_shape + [(single, BF16)],
+                [g_zero, received[0], *common, *for_rim], scratch=rim_scratch,
+            )
+            on = lax.ppermute(c_on, "dom", other_core(parts))
+            g_mid, da_mid, ds_mid, zero = call(
+                functools.partial(stage_mid_kernel, blk, tile, True), "stage_mid",
+                [(middle, BF16)]  + mid_shape + [(single, BF16)],
+                [g_mid, received[1], g_zero, da_zero, ds_zero, *common, *for_rim, k_t],
+                scratch=[((3 * width, tile), BF16)],
+            )
+            g_one, da_one, c_off = call(
+                functools.partial(stage_one_kernel, blk, tile, True), "stage_one",
+                [(single, BF16)] * 3,
+                [g_one, received[2], *common, *for_rim], scratch=rim_scratch,
+            )
         zero = call(add_rim_kernel, "add_on", [(single, BF16)], [zero, on])[0]
-        *new, da_one, c_off = call(
-            functools.partial(stage_one_kernel, blk, tile, moved), "stage_one",
-            [(single, BF16)] * (moved + 2),
-            [g_one, *received[2:], *common, *for_rim], scratch=rim_scratch,
-        )
-        g_one = new[0] if moved else g_one
         off = lax.ppermute(c_off, "dom", next_chip(parts))
         mid, one = call(
             functools.partial(stage_main_kernel, blk, tile), "stage_main",

time: 96.6 us -> 96.4 us (level)
    ppermute x4, waiting for transfers between devices: 0.27 us -> 1.86 us  [local(): off = lax.ppermute(c_off, 'dom', next_chip(parts))]
    ppermute x9, waiting for transfers between devices: 11.2 us -> 9.89 us  [local(): lax.ppermute(part, 'section', [(here, here - 1)])]
    pallas_call x30 -> x28, Pallas kernels: 37.4 us -> 36.7 us  [call(): pl.pallas_call(kernel, in_specs=[scalars] * smem + [vmem] * (len(args) -...]
  transfers between devices with their start and end apart: 24 -> 24, of which waited for: 9 -> 9; matrix products, arithmetic and copies ran while one was open for 0% -> 0% of each run, Pallas kernels for 30% -> 26%
where the time goes in v8:
time: 96.4 us; the launch traced here: 96.1 us
  Pallas kernels  36.7 us (38%)
  waiting for transfers between devices  29.9 us (31%)
  starting transfers between devices  26 us (27%)
  local copies, waits for them, and re-layouts  2.41 us (2%)
  between operations  1.05 us (1%)
    pallas_call x28, Pallas kernels, call(): pl.pallas_call(kernel, in_specs=[scalars] * smem + [vmem] * (len(args) -...  36.7 us
    ppermute x9, waiting for transfers between devices, local(): lax.ppermute(part, 'section', [(here, here - 1)])  9.89 us
    ppermute x4, starting transfers between devices, local(): off = lax.ppermute(c_off, 'dom', next_chip(parts))  8.55 us
    ppermute x9, starting transfers between devices, local(): lax.ppermute(part, 'section', [(here, here - 1)])  8.29 us
    ppermute x1, waiting for transfers between devices, local(): got_a = lax.ppermute(give_a, 'dom', chips_apart(parts, steps[0][0]))  7.25 us
    ppermute x1, starting transfers between devices, local(): x_off = lax.ppermute(x_off, 'dom', next_chip(parts))  4.71 us
    ppermute x1, waiting for transfers between devices, local(): got_a = lax.ppermute(give_a, 'dom', chips_apart(parts, steps[0][1]))  4.15 us
    ppermute x1, waiting for transfers between devices, local(): got_b = lax.ppermute(give_b, 'dom', chips_apart(parts, steps[1][0]))  3.86 us
  transfers between devices with their start and end apart: 24, of which 9 were waited for; matrix products, arithmetic and copies ran while one was open for 0% of the time, Pallas kernels for 26%

profile of v8, /device:TPU:0, one launch (start us, length us, event | category | flops | bytes accessed | tf_op | source)
XLA Modules:
  0.0 96.1 jit_solution(13783932851131738665)
XLA Ops:
  0.6 1.0 %copy-done.3 = bf16[1,1,384,512]{3,2,1,0:T(8,128)(2,1)S(1)} copy-done((bf16[1,1,384,512]{3,2,1,0:T(8,128)(2,1)S(1)}, bf16[1,1,384,512]{3,2,1,0:T(8,128)(2,1)}, u32[]{:S(2)}) %copy-start.3) | copy-done | bytes 393240
  1.7 0.5 collective-permute-start
  2.2 4.7 %collective-permute-start.1 = (bf16[128,512]{1,0:T(8,128)(2,1)S(1)}, bf16[128,512]{1,0:T(8,128)(2,1)S(1)}, u32[]{:S(2)}, u32[]{:S(2)}) collective-permute-start(bf16[128,512]{1,0:T(8,128)(2,1)S(1)} %get-tuple-element.81), channel_id=1, source_target_pairs={{0,7},{1,2},{2,1},{3,4},{4,3},{5,6},{6,5},{7,0},{8,15},{9,10},{10,... | collective-permute-start | bytes 393224 | tf_op jit(solution)/shard_map/ppermute | solution.py:502
  6.9 1.4 %copy-done = bf16[1,512,1536]{2,1,0:T(8,128)(2,1)S(1)} copy-done((bf16[1,512,1536]{2,1,0:T(8,128)(2,1)S(1)}, bf16[1,512,1536]{2,1,0:T(8,128)(2,1)}, u32[]{:S(2)}) %copy-start) | copy-done | bytes 1572888
  8.3 1.2 %prelude_own.1 = (bf16[512,384]{1,0:T(8,128)(2,1)S(1)}, f32[8,384]{1,0:T(8,128)S(1)}, bf16[384,512]{1,0:T(8,128)(2,1)S(1)}, bf16[384,512]{1,0:T(8,128)(2,1)S(1)}...) custom-call(bf16[384,512]{1,0:T(8,128)(2,1)S(1)} %bitcast.32, ...), custom_call_target="tpu_custom_call" | custom-call | flops 1 | bytes 1 | tf_op jit(solution)/shard_map/prelude_own/pallas_call | solution.py:30
  9.5 0.0 collective-permute-done.x_on
  9.6 0.7 collective-permute-done.1.x_off
  10.2 0.0 copy-start.2
  10.3 3.4 %prelude.1 = (bf16[512,640]{1,0:T(8,128)(2,1)S(1)}, f32[8,640]{1,0:T(8,128)S(1)}, bf16[640,512]{1,0:T(8,128)(2,1)S(1)}, bf16[512,640]{1,0:T(8,128)(2,1)S(1)}, bf...) custom-call(s32[3,3]{1,0:T(4,128)S(1)} %copy-done.5, ...), custom_call_target="tpu_custom_call" | custom-call | flops 1 | bytes 1 | tf_op jit(solution)/shard_map/prelude/pallas_call | solution.py:30
  13.7 4.4 %stage_start.1 = (bf16[512,128]{1,0:T(8,128)(2,1)S(1)}, bf16[4,384,256]{2,1,0:T(8,128)(2,1)S(1)}, bf16[512,128]{1,0:T(8,128)(2,1)S(1)}, bf16[512,128]{1,0:T(8,12...) custom-call(bf16[512,128]{1,0:T(8,128)(2,1)S(1)} %get-tuple-element., ...), custom_call_target="tpu_custom_call" | custom-call | flops 1 | bytes 1 | tf_op jit(solution)/shard_map/stage_start/pallas_call | solution.py:30
  18.1 0.1 collective-permute-start.2
  18.2 2.9 %collective-permute-start.7 = (bf16[512,128]{1,0:T(8,128)(2,1)S(1)}, bf16[512,128]{1,0:T(8,128)(2,1)S(1)}, u32[]{:S(2)}, u32[]{:S(2)}) collective-permute-start(bf16[512,128]{1,0:T(8,128)(2,1)S(1)} %get-tuple-element.114), channel_id=1, source_target_pairs={{0,7},{1,2},{2,1},{3,4},{4,3},{5,6},{6,5},{7,0},{8,15},{9,10},{10,... | collective-permute-start | bytes 393224 | tf_op jit(solution)/shard_map/ppermute | solution.py:560
  21.2 0.7 collective-permute-start.3
  21.9 2.1 %stage_main.3 = (bf16[512,128]{1,0:T(8,128)(2,1)S(1)}, bf16[512,128]{1,0:T(8,128)(2,1)S(1)}) custom-call(bf16[512,128]{1,0:T(8,128)(2,1)S(1)} %get-tuple-element.90.g_mid.refs_0_, bf16[512,128]{1,0:T(8,128)(2,1)S(1)} %get-tuple-element.91.g_one.refs_0_, bf16[512,128]{1,0:T(8,128)(2,1)S(1)} %get-tuple-element.101.da_zero, ...), custom_call_target="tpu_custom_call" | custom-call | flops 1 | bytes 1 | tf_op jit(solution)/shard_map/stage_main/pallas_call | solution.py:30
  24.0 1.8 %collective-permute-done.7.rim = bf16[512,128]{1,0:T(8,128)(2,1)S(1)} collective-permute-done((bf16[512,128]{1,0:T(8,128)(2,1)S(1)}, bf16[512,128]{1,0:T(8,128)(2,1)S(1)}, u32[]{:S(2)}, u32[]{:S(2)}) %collective-permute-start.7) | collective-permute-done | bytes 131104 | tf_op jit(solution)/shard_map/ppermute | solution.py:560
  25.9 0.7 collective-permute-start.8
  26.5 0.8 collective-permute-start.4
  27.4 0.0 collective-permute-done.3.refs_1_
  27.4 1.5 %stage_zero.2 = (bf16[512,128]{1,0:T(8,128)(2,1)S(1)}, bf16[512,128]{1,0:T(8,128)(2,1)S(1)}, bf16[4,384,256]{2,1,0:T(8,128)(2,1)S(1)}, bf16[512,128]{1,0:T(8,128)(2,1)S(1)}) custom-call(bf16[512,128]{1,0:T(8,128)(2,1)S(1)} %get-tuple-element.89.g_zero.refs_0_, bf16[512,128]{1,0:T(8,128)(2,1)S(1)} %collective-permute-done.3.refs_1_, ...), custom_call_target="tpu_custom_call" | custom-call | flops 1 | bytes 1 | tf_op jit(solution)/shard_map/stage_zero/pallas_call | solution.py:30
  29.0 0.1 collective-permute-start.5
  29.0 0.0 collective-permute-done.8.refs_1_
  29.0 1.4 %stage_one.2 = (bf16[512,128]{1,0:T(8,128)(2,1)S(1)}, bf16[512,128]{1,0:T(8,128)(2,1)S(1)}, bf16[512,128]{1,0:T(8,128)(2,1)S(1)}) custom-call(bf16[512,128]{1,0:T(8,128)(2,1)S(1)} %get-tuple-element.91.g_one.refs_0_, bf16[512,128]{1,0:T(8,128)(2,1)S(1)} %collective-permute-done.8.refs_1_, bf16[512,512]{1,0:T(8,128)(2,1)S(1)} %bitcast.23, ...), custom_call_target="tpu_custom_call" | custom-call | flops 1 | bytes 1 | tf_op jit(solution)/shard_map/stage_one/pallas_call | solution.py:30
  30.5 1.6 %collective-permute-start.13 = (bf16[512,128]{1,0:T(8,128)(2,1)S(1)}, bf16[512,128]{1,0:T(8,128)(2,1)S(1)}, u32[]{:S(2)}, u32[]{:S(2)}) collective-permute-start(bf16[512,128]{1,0:T(8,128)(2,1)S(1)} %get-tuple-element.126), channel_id=1, source_target_pairs={{0,7},{1,2},{2,1},{3,4},{4,3},{5,6},{6,5},{7,0},{8,15},{9,10},{10,... | collective-permute-start | bytes 393224 | tf_op jit(solution)/shard_map/ppermute | solution.py:560
  32.1 0.0 collective-permute-done.4.refs_1_
  32.1 2.2 %stage_mid.2 = (bf16[512,128]{1,0:T(8,128)(2,1)S(1)}, bf16[512,128]{1,0:T(8,128)(2,1)S(1)}, bf16[4,1,384,256]{3,2,1,0:T(8,128)(2,1)S(1)}, bf16[512,128]{1,0:T(8,128)(2,1)S(1)}) custom-call(bf16[512,128]{1,0:T(8,128)(2,1)S(1)} %get-tuple-element.90.g_mid.refs_0_, bf16[512,128]{1,0:T(8,128)(2,1)S(1)} %collective-permute-done.4.refs_1_, ...), custom_call_target="tpu_custom_call" | custom-call | flops 1 | bytes 1 | tf_op jit(solution)/shard_map/stage_mid/pallas_call | solution.py:30
  34.3 0.0 collective-permute-done.5.rim
  34.3 0.7 collective-permute-start.6
  35.0 2.1 %stage_main.4 = (bf16[512,128]{1,0:T(8,128)(2,1)S(1)}, bf16[512,128]{1,0:T(8,128)(2,1)S(1)}) custom-call(bf16[512,128]{1,0:T(8,128)(2,1)S(1)} %get-tuple-element.112.g_mid.refs_0_, bf16[512,128]{1,0:T(8,128)(2,1)S(1)} %get-tuple-element.115.g_one.refs_0_, bf16[512,128]{1,0:T(8,128)(2,1)S(1)} %get-tuple-element.107.refs_3_.da_zero, ...), custom_call_target="tpu_custom_call" | custom-call | flops 1 | bytes 1 | tf_op jit(solution)/shard_map/stage_main/pallas_call | solution.py:30
  37.1 0.0 collective-permute-done.13.rim
  37.2 0.7 collective-permute-start.14
  37.8 0.7 collective-permute-start.9
  38.5 1.6 %stage_zero.3 = (bf16[512,128]{1,0:T(8,128)(2,1)S(1)}, bf16[512,128]{1,0:T(8,128)(2,1)S(1)}, bf16[4,384,256]{2,1,0:T(8,128)(2,1)S(1)}, bf16[512,128]{1,0:T(8,128)(2,1)S(1)}) custom-call(bf16[512,128]{1,0:T(8,128)(2,1)S(1)} %get-tuple-element.100.refs_2_.refs_0_, bf16[512,128]{1,0:T(8,128)(2,1)S(1)} %collective-permute-done.6.refs_1_, ...), custom_call_target="tpu_custom_call" | custom-call | flops 1 | bytes 1 | tf_op jit(solution)/shard_map/stage_zero/pallas_call | solution.py:30
  40.1 0.1 collective-permute-start.10
  40.2 0.0 collective-permute-done.14.refs_1_
  40.2 1.4 %stage_one.3 = (bf16[512,128]{1,0:T(8,128)(2,1)S(1)}, bf16[512,128]{1,0:T(8,128)(2,1)S(1)}, bf16[512,128]{1,0:T(8,128)(2,1)S(1)}) custom-call(bf16[512,128]{1,0:T(8,128)(2,1)S(1)} %get-tuple-element.115.g_one.refs_0_, bf16[512,128]{1,0:T(8,128)(2,1)S(1)} %collective-permute-done.14.refs_1_, bf16[512,512]{1,0:T(8,128)(2,1)S(1)} %bitcast.26, ...), custom_call_target="tpu_custom_call" | custom-call | flops 1 | bytes 1 | tf_op jit(solution)/shard_map/stage_one/pallas_call | solution.py:30
  41.6 2.1 %collective-permute-start.15 = (bf16[512,128]{1,0:T(8,128)(2,1)S(1)}, bf16[512,128]{1,0:T(8,128)(2,1)S(1)}, u32[]{:S(2)}, u32[]{:S(2)}) collective-permute-start(bf16[512,128]{1,0:T(8,128)(2,1)S(1)} %get-tuple-element.133), channel_id=1, source_target_pairs={{0,7},{1,2},{2,1},{3,4},{4,3},{5,6},{6,5},{7,0},{8,15},{9,10},{10,... | collective-permute-start | bytes 393224 | tf_op jit(solution)/shard_map/ppermute | solution.py:560
  43.7 2.2 %stage_mid.3 = (bf16[512,128]{1,0:T(8,128)(2,1)S(1)}, bf16[512,128]{1,0:T(8,128)(2,1)S(1)}, bf16[4,1,384,256]{3,2,1,0:T(8,128)(2,1)S(1)}, bf16[512,128]{1,0:T(8,128)(2,1)S(1)}) custom-call(bf16[512,128]{1,0:T(8,128)(2,1)S(1)} %get-tuple-element.112.g_mid.refs_0_, bf16[512,128]{1,0:T(8,128)(2,1)S(1)} %collective-permute-done.9.refs_1_, ...), custom_call_target="tpu_custom_call" | custom-call | flops 1 | bytes 1 | tf_op jit(solution)/shard_map/stage_mid/pallas_call | solution.py:30
  45.9 1.3 %collective-permute-start.11 = (bf16[512,128]{1,0:T(8,128)(2,1)S(1)}, bf16[512,128]{1,0:T(8,128)(2,1)S(1)}, u32[]{:S(2)}, u32[]{:S(2)}) collective-permute-start(bf16[512,128]{1,0:T(8,128)(2,1)S(1)} %add_on.5), channel_id=1, source_target_pairs={{8,0},{9,1},{10,2},{11,3},{12,4},{13,5},{14,6},{15,7}} | collective-permute-start | bytes 393224 | tf_op jit(solution)/shard_map/ppermute | solution.py:571
  47.2 2.1 %stage_main.5 = (bf16[512,128]{1,0:T(8,128)(2,1)S(1)}, bf16[512,128]{1,0:T(8,128)(2,1)S(1)}) custom-call(bf16[512,128]{1,0:T(8,128)(2,1)S(1)} %get-tuple-element.128.g_mid.g_prev, bf16[512,128]{1,0:T(8,128)(2,1)S(1)} %get-tuple-element.127.g_one.g_prev, bf16[512,128]{1,0:T(8,128)(2,1)S(1)} %get-tuple-element.120.refs_3_.da_zero, ...), custom_call_target="tpu_custom_call" | custom-call | flops 1 | bytes 1 | tf_op jit(solution)/shard_map/stage_main/pallas_call | solution.py:30
  49.3 1.3 %collective-permute-start.17 = (bf16[512,128]{1,0:T(8,128)(2,1)S(1)}, bf16[512,128]{1,0:T(8,128)(2,1)S(1)}, u32[]{:S(2)}, u32[]{:S(2)}) collective-permute-start(bf16[512,128]{1,0:T(8,128)(2,1)S(1)} %get-tuple-element.135), channel_id=1, source_target_pairs={{8,0},{9,1},{10,2},{11,3},{12,4},{13,5},{14,6},{15,7}} | collective-permute-start | bytes 393224 | tf_op jit(solution)/shard_map/ppermute | solution.py:571
  50.7 1.5 %collective-permute-start.16 = (bf16[512,128]{1,0:T(8,128)(2,1)S(1)}, bf16[512,128]{1,0:T(8,128)(2,1)S(1)}, u32[]{:S(2)}, u32[]{:S(2)}) collective-permute-start(bf16[512,128]{1,0:T(8,128)(2,1)S(1)} %add_off.5), channel_id=1, source_target_pairs={{8,0},{9,1},{10,2},{11,3},{12,4},{13,5},{14,6},{15,7}} | collective-permute-start | bytes 393224 | tf_op jit(solution)/shard_map/ppermute | solution.py:571
  52.2 8.5 %collective-permute-done.11.refs_1_ = bf16[512,128]{1,0:T(8,128)(2,1)S(1)} collective-permute-done((bf16[512,128]{1,0:T(8,128)(2,1)S(1)}, bf16[512,128]{1,0:T(8,128)(2,1)S(1)}, u32[]{:S(2)}, u32[]{:S(2)}) %collective-permute-start.11) | collective-permute-done | bytes 131104 | tf_op jit(solution)/shard_map/ppermute | solution.py:571
  60.7 1.5 %last_zero.1 = (bf16[512,128]{1,0:T(8,128)(2,1)S(1)}, bf16[512,128]{1,0:T(8,128)(2,1)S(1)}, bf16[4,384,256]{2,1,0:T(8,128)(2,1)S(1)}, bf16[512,128]{1,0:T(8,128)(2,1)S(1)}) custom-call(bf16[512,128]{1,0:T(8,128)(2,1)S(1)} %get-tuple-element.111.refs_2_.refs_0_, bf16[512,128]{1,0:T(8,128)(2,1)S(1)} %collective-permute-done.11.refs_1_, ...), custom_call_target="tpu_custom_call" | custom-call | flops 1 | bytes 1 | tf_op jit(solution)/shard_map/last_zero/pallas_call | solution.py:30
  62.2 0.1 collective-permute-start.12
  62.3 1.4 %collective-permute-done.17.arrived = bf16[512,128]{1,0:T(8,128)(2,1)S(1)} collective-permute-done((bf16[512,128]{1,0:T(8,128)(2,1)S(1)}, bf16[512,128]{1,0:T(8,128)(2,1)S(1)}, u32[]{:S(2)}, u32[]{:S(2)}) %collective-permute-start.17) | collective-permute-done | bytes 131104 | tf_op jit(solution)/shard_map/ppermute | solution.py:571
  63.7 1.5 %last_mid.1 = (bf16[512,128]{1,0:T(8,128)(2,1)S(1)}, bf16[512,128]{1,0:T(8,128)(2,1)S(1)}, bf16[4,1,384,256]{3,2,1,0:T(8,128)(2,1)S(1)}, bf16[1536,256]{1,0:T(8,128)(2,1)S(1)}) custom-call(bf16[512,128]{1,0:T(8,128)(2,1)S(1)} %get-tuple-element.128.g_mid.g_prev, bf16[512,128]{1,0:T(8,128)(2,1)S(1)} %collective-permute-done.17.arrived, ...), custom_call_target="tpu_custom_call" | custom-call | flops 1 | bytes 1 | tf_op jit(solution)/shard_map/last_mid/pallas_call | solution.py:30
  65.2 3.0 %last_terms.1 = (bf16[512,128]{1,0:T(8,128)(2,1)S(1)}, bf16[1536,384]{1,0:T(8,128)(2,1)S(1)}, bf16[4,64,2048]{2,1,0:T(8,128)(2,1)S(1)}) custom-call(bf16[512,128]{1,0:T(8,128)(2,1)S(1)} %collective-permute-done.12.after.on, bf16[512,128]{1,0:T(8,128)(2,1)S(1)} %get-tuple-element.127.g_one.g_prev, bf16[512,128]{1,0:T(8,128)(2,1)S(1)} %collective-permute-done.16.arrived, ...), custom_call_target="tpu_custom_call" | custom-call | flops 1 | bytes 1 | tf_op jit(solution)/shard_map/last_terms/pallas_call | solution.py:30
  68.2 0.1 collective-permute-start.18
  68.3 1.0 %mine.1.both = f32[4,64,2048]{2,1,0:T(8,128)S(1)} custom-call(bf16[512,640]{1,0:T(8,128)(2,1)S(1)} %get-tuple-element.95.xn_t.refs_7_.refs_10_, bf16[1536,256]{1,0:T(8,128)(2,1)S(1)} %get-tuple-element.141.d_low, bf16[1536,384]{1,0:T(8,128)(2,1)S(1)} %get-tuple-element.143.d_high, bf16[512,384]{1,0:T(8,128)(2,1)S(1)} %get-tuple-element.94.attn_t.refs_5_.refs_8_, ...), custom_call_target="tpu_custom_call" | custom-call | flops 1 | bytes 1 | tf_op jit(solution)/shard_map/mine/pallas_call | solution.py:30
  69.3 1.6 %collective-permute-done.18.got = bf16[4,64,2048]{2,1,0:T(8,128)(2,1)S(1)} collective-permute-done((bf16[4,64,2048]{2,1,0:T(8,128)(2,1)S(1)}, bf16[4,64,2048]{2,1,0:T(8,128)(2,1)S(1)}, u32[]{:S(2)}, u32[]{:S(2)}) %collective-permute-start.18) | collective-permute-done | bytes 1048608 | tf_op jit(solution)/shard_map/ppermute | solution.py:598
  70.9 0.2 keep.1
  71.1 0.1 collective-permute-start.20
  71.2 1.7 %collective-permute-start.21 = (bf16[2,64,1024]{2,1,0:T(8,128)(2,1)S(1)}, bf16[2,64,1024]{2,1,0:T(8,128)(2,1)S(1)}, u32[]{:S(2)}, u32[]{:S(2)}) collective-permute-start(bf16[2,64,1024]{2,1,0:T(8,128)(2,1)S(1)} %get-tuple-element.150), channel_id=1, source_target_pairs={{0,4},{1,5},{2,6},{3,7},{4,0},{5,1},{6,2},{7,3},{8,12},{9,13},{10,... | collective-permute-start | bytes 786440 | tf_op jit(solution)/shard_map/ppermute | solution.py:610
  72.8 1.8 %last_input.1 = (bf16[512,384]{1,0:T(8,128)(2,1)S(1)}, bf16[512,128]{1,0:T(8,128)(2,1)S(1)}) custom-call(f32[2,64,1024]{2,1,0:T(8,128)S(1)} %get-tuple-element.145.after.own_a, bf16[512,128]{1,0:T(8,128)(2,1)S(1)} %get-tuple-element.134.g_zero, bf16[512,128]{1,0:T(8,128)(2,1)S(1)} %get-tuple-element.138.g_mid, ...), custom_call_target="tpu_custom_call" | custom-call | flops 1 | bytes 1 | tf_op jit(solution)/shard_map/last_input/pallas_call | solution.py:30
  74.6 2.0 %collective-permute-start.19 = (bf16[512,128]{1,0:T(8,128)(2,1)S(1)}, bf16[512,128]{1,0:T(8,128)(2,1)S(1)}, u32[]{:S(2)}, u32[]{:S(2)}) collective-permute-start(bf16[512,128]{1,0:T(8,128)(2,1)S(1)} %get-tuple-element.147.refs_0_), channel_id=1, source_target_pairs={{0,7},{1,2},{2,1},{3,4},{4,3},{5,6},{6,5},{7,0},{8,15},{9,10},{10,... | collective-permute-start | bytes 393224 | tf_op jit(solution)/shard_map/ppermute | solution.py:617
  76.5 7.2 %collective-permute-done.20.got_a = bf16[2,64,1024]{2,1,0:T(8,128)(2,1)S(1)} collective-permute-done((bf16[2,64,1024]{2,1,0:T(8,128)(2,1)S(1)}, bf16[2,64,1024]{2,1,0:T(8,128)(2,1)S(1)}, u32[]{:S(2)}, u32[]{:S(2)}) %collective-permute-start.20) | collective-permute-done | bytes 262176 | tf_op jit(solution)/shard_map/ppermute | solution.py:609
  83.8 3.9 %collective-permute-done.21.got_b = bf16[2,64,1024]{2,1,0:T(8,128)(2,1)S(1)} collective-permute-done((bf16[2,64,1024]{2,1,0:T(8,128)(2,1)S(1)}, bf16[2,64,1024]{2,1,0:T(8,128)(2,1)S(1)}, u32[]{:S(2)}, u32[]{:S(2)}) %collective-permute-start.21) | collective-permute-done | bytes 262176 | tf_op jit(solution)/shard_map/ppermute | solution.py:610
  87.6 0.1 middle.1
  87.7 0.1 collective-permute-start.22
  87.8 1.8 %collective-permute-start.23 = (bf16[64,1024]{1,0:T(8,128)(2,1)S(1)}, bf16[64,1024]{1,0:T(8,128)(2,1)S(1)}, u32[]{:S(2)}, u32[]{:S(2)}) collective-permute-start(bf16[64,1024]{1,0:T(8,128)(2,1)S(1)} %get-tuple-element.154), channel_id=1, source_target_pairs={{0,2},{1,3},{2,0},{3,1},{4,6},{5,7},{6,4},{7,5},{8,10},{9,11},{10,... | collective-permute-start | bytes 393224 | tf_op jit(solution)/shard_map/ppermute | solution.py:623
  89.6 0.9 finish_input.1
  90.6 4.1 %collective-permute-done.22.got_a = bf16[64,1024]{1,0:T(8,128)(2,1)S(1)} collective-permute-done((bf16[64,1024]{1,0:T(8,128)(2,1)S(1)}, bf16[64,1024]{1,0:T(8,128)(2,1)S(1)}, u32[]{:S(2)}, u32[]{:S(2)}) %collective-permute-start.22) | collective-permute-done | bytes 131104 | tf_op jit(solution)/shard_map/ppermute | solution.py:624
  94.7 0.6 collective-permute-done.23.got_b
  95.3 0.8 total.1
  (24 shorter events, 0.3 us)
Async XLA Ops:
  0.6 1.0 %copy-start.3 = (bf16[1,1,384,512]{3,2,1,0:T(8,128)(2,1)S(1)}, bf16[1,1,384,512]{3,2,1,0:T(8,128)(2,1)}, u32[]{:S(2)}) copy-start(bf16[1,1,384,512]{3,2,1,0:T(8,128)(2,1)} %param.5) | copy-start | bytes 1179652
  1.6 8.6 %copy-start.4 = (bf16[1,384,512]{2,1,0:T(8,128)(2,1)S(1)}, bf16[1,384,512]{2,1,0:T(8,128)(2,1)}, u32[]{:S(2)}) copy-start(bf16[1,384,512]{2,1,0:T(8,128)(2,1)} %param.6) | copy-start | bytes 1179652
  1.6 8.6 %copy-start.5 = (s32[3,3]{1,0:T(4,128)S(1)}, s32[3,3]{1,0:T(4,128)}, u32[]{:S(2)}) copy-start(s32[3,3]{1,0:T(4,128)} %neighbours.1) | copy-start | bytes 112
  1.7 7.9 %collective-permute-start = (bf16[128,512]{1,0:T(8,128)(2,1)S(1)}, bf16[128,512]{1,0:T(8,128)(2,1)S(1)}, u32[]{:S(2)}, u32[]{:S(2)}) collective-permute-start(bf16[128,512]{1,0:T(8,128)(2,1)S(1)} %get-tuple-element.80), channel_id=1, source_target_pairs={{0,1},{1,0},{2,3},{3,2},{4,5},{5,4},{6,7},{7,6},{8,9},{9,8},{10,11... | collective-permute-start | bytes 393224 | tf_op jit(solution)/shard_map/ppermute | solution.py:501
  2.2 8.1 %collective-permute-start.1 = (bf16[128,512]{1,0:T(8,128)(2,1)S(1)}, bf16[128,512]{1,0:T(8,128)(2,1)S(1)}, u32[]{:S(2)}, u32[]{:S(2)}) collective-permute-start(bf16[128,512]{1,0:T(8,128)(2,1)S(1)} %get-tuple-element.81), channel_id=1, source_target_pairs={{0,7},{1,2},{2,1},{3,4},{4,3},{5,6},{6,5},{7,0},{8,15},{9,10},{10,... | collective-permute-start | bytes 393224 | tf_op jit(solution)/shard_map/ppermute | solution.py:502
  6.9 1.4 %copy-start = (bf16[1,512,1536]{2,1,0:T(8,128)(2,1)S(1)}, bf16[1,512,1536]{2,1,0:T(8,128)(2,1)}, u32[]{:S(2)}) copy-start(bf16[1,512,1536]{2,1,0:T(8,128)(2,1)} %param.7) | copy-start | bytes 4718596
  8.3 1.9 %copy-start.1 = (bf16[1,512,1536]{2,1,0:T(8,128)(2,1)S(1)}, bf16[1,512,1536]{2,1,0:T(8,128)(2,1)}, u32[]{:S(2)}) copy-start(bf16[1,512,1536]{2,1,0:T(8,128)(2,1)} %param.7) | copy-start | bytes 4718596
  10.2 3.4 %copy-start.2 = (bf16[1,512,512]{2,1,0:T(8,128)(2,1)S(1)}, bf16[1,512,512]{2,1,0:T(8,128)(2,1)}, u32[]{:S(2)}) copy-start(bf16[1,512,512]{2,1,0:T(8,128)(2,1)} %param.8) | copy-start | bytes 1572868
  18.1 3.0 %collective-permute-start.2 = (bf16[512,128]{1,0:T(8,128)(2,1)S(1)}, bf16[512,128]{1,0:T(8,128)(2,1)S(1)}, u32[]{:S(2)}, u32[]{:S(2)}) collective-permute-start(bf16[512,128]{1,0:T(8,128)(2,1)S(1)} %get-tuple-element.99), channel_id=1, source_target_pairs={{0,1},{1,0},{2,3},{3,2},{4,5},{5,4},{6,7},{7,6},{8,9},{9,8},{10,11... | collective-permute-start | bytes 393224 | tf_op jit(solution)/shard_map/ppermute | solution.py:540
  18.2 7.6 %collective-permute-start.7 = (bf16[512,128]{1,0:T(8,128)(2,1)S(1)}, bf16[512,128]{1,0:T(8,128)(2,1)S(1)}, u32[]{:S(2)}, u32[]{:S(2)}) collective-permute-start(bf16[512,128]{1,0:T(8,128)(2,1)S(1)} %get-tuple-element.114), channel_id=1, source_target_pairs={{0,7},{1,2},{2,1},{3,4},{4,3},{5,6},{6,5},{7,0},{8,15},{9,10},{10,... | collective-permute-start | bytes 393224 | tf_op jit(solution)/shard_map/ppermute | solution.py:560
  21.2 6.2 %collective-permute-start.3 = (bf16[512,128]{1,0:T(8,128)(2,1)S(1)}, bf16[512,128]{1,0:T(8,128)(2,1)S(1)}, u32[]{:S(2)}, u32[]{:S(2)}) collective-permute-start(bf16[512,128]{1,0:T(8,128)(2,1)S(1)} %add_on.3), channel_id=1, source_target_pairs={{24,16},{25,17},{26,18},{27,19},{28,20},{29,21},{30,22},{31,23}} | collective-permute-start | bytes 393224 | tf_op jit(solution)/shard_map/ppermute | solution.py:571
  25.9 3.2 %collective-permute-start.8 = (bf16[512,128]{1,0:T(8,128)(2,1)S(1)}, bf16[512,128]{1,0:T(8,128)(2,1)S(1)}, u32[]{:S(2)}, u32[]{:S(2)}) collective-permute-start(bf16[512,128]{1,0:T(8,128)(2,1)S(1)} %add_off.3), channel_id=1, source_target_pairs={{24,16},{25,17},{26,18},{27,19},{28,20},{29,21},{30,22},{31,23}} | collective-permute-start | bytes 393224 | tf_op jit(solution)/shard_map/ppermute | solution.py:571
  26.5 5.5 %collective-permute-start.4 = (bf16[512,128]{1,0:T(8,128)(2,1)S(1)}, bf16[512,128]{1,0:T(8,128)(2,1)S(1)}, u32[]{:S(2)}, u32[]{:S(2)}) collective-permute-start(bf16[512,128]{1,0:T(8,128)(2,1)S(1)} %get-tuple-element.106), channel_id=1, source_target_pairs={{24,16},{25,17},{26,18},{27,19},{28,20},{29,21},{30,22},{31,23}} | collective-permute-start | bytes 393224 | tf_op jit(solution)/shard_map/ppermute | solution.py:571
  29.0 5.3 %collective-permute-start.5 = (bf16[512,128]{1,0:T(8,128)(2,1)S(1)}, bf16[512,128]{1,0:T(8,128)(2,1)S(1)}, u32[]{:S(2)}, u32[]{:S(2)}) collective-permute-start(bf16[512,128]{1,0:T(8,128)(2,1)S(1)} %get-tuple-element.110), channel_id=1, source_target_pairs={{0,1},{1,0},{2,3},{3,2},{4,5},{5,4},{6,7},{7,6},{8,9},{9,8},{10,11... | collective-permute-start | bytes 393224 | tf_op jit(solution)/shard_map/ppermute | solution.py:547
  30.5 6.7 %collective-permute-start.13 = (bf16[512,128]{1,0:T(8,128)(2,1)S(1)}, bf16[512,128]{1,0:T(8,128)(2,1)S(1)}, u32[]{:S(2)}, u32[]{:S(2)}) collective-permute-start(bf16[512,128]{1,0:T(8,128)(2,1)S(1)} %get-tuple-element.126), channel_id=1, source_target_pairs={{0,7},{1,2},{2,1},{3,4},{4,3},{5,6},{6,5},{7,0},{8,15},{9,10},{10,... | collective-permute-start | bytes 393224 | tf_op jit(solution)/shard_map/ppermute | solution.py:560
  34.3 4.2 %collective-permute-start.6 = (bf16[512,128]{1,0:T(8,128)(2,1)S(1)}, bf16[512,128]{1,0:T(8,128)(2,1)S(1)}, u32[]{:S(2)}, u32[]{:S(2)}) collective-permute-start(bf16[512,128]{1,0:T(8,128)(2,1)S(1)} %add_on.4), channel_id=1, source_target_pairs={{16,8},{17,9},{18,10},{19,11},{20,12},{21,13},{22,14},{23,15}} | collective-permute-start | bytes 393224 | tf_op jit(solution)/shard_map/ppermute | solution.py:571
  37.2 3.0 %collective-permute-start.14 = (bf16[512,128]{1,0:T(8,128)(2,1)S(1)}, bf16[512,128]{1,0:T(8,128)(2,1)S(1)}, u32[]{:S(2)}, u32[]{:S(2)}) collective-permute-start(bf16[512,128]{1,0:T(8,128)(2,1)S(1)} %add_off.4), channel_id=1, source_target_pairs={{16,8},{17,9},{18,10},{19,11},{20,12},{21,13},{22,14},{23,15}} | collective-permute-start | bytes 393224 | tf_op jit(solution)/shard_map/ppermute | solution.py:571
  37.8 5.8 %collective-permute-start.9 = (bf16[512,128]{1,0:T(8,128)(2,1)S(1)}, bf16[512,128]{1,0:T(8,128)(2,1)S(1)}, u32[]{:S(2)}, u32[]{:S(2)}) collective-permute-start(bf16[512,128]{1,0:T(8,128)(2,1)S(1)} %get-tuple-element.119), channel_id=1, source_target_pairs={{16,8},{17,9},{18,10},{19,11},{20,12},{21,13},{22,14},{23,15}} | collective-permute-start | bytes 393224 | tf_op jit(solution)/shard_map/ppermute | solution.py:571
  40.1 5.8 %collective-permute-start.10 = (bf16[512,128]{1,0:T(8,128)(2,1)S(1)}, bf16[512,128]{1,0:T(8,128)(2,1)S(1)}, u32[]{:S(2)}, u32[]{:S(2)}) collective-permute-start(bf16[512,128]{1,0:T(8,128)(2,1)S(1)} %get-tuple-element.123), channel_id=1, source_target_pairs={{0,1},{1,0},{2,3},{3,2},{4,5},{5,4},{6,7},{7,6},{8,9},{9,8},{10,11... | collective-permute-start | bytes 393224 | tf_op jit(solution)/shard_map/ppermute | solution.py:547
  41.6 9.0 %collective-permute-start.15 = (bf16[512,128]{1,0:T(8,128)(2,1)S(1)}, bf16[512,128]{1,0:T(8,128)(2,1)S(1)}, u32[]{:S(2)}, u32[]{:S(2)}) collective-permute-start(bf16[512,128]{1,0:T(8,128)(2,1)S(1)} %get-tuple-element.133), channel_id=1, source_target_pairs={{0,7},{1,2},{2,1},{3,4},{4,3},{5,6},{6,5},{7,0},{8,15},{9,10},{10,... | collective-permute-start | bytes 393224 | tf_op jit(solution)/shard_map/ppermute | solution.py:560
  45.9 14.7 %collective-permute-start.11 = (bf16[512,128]{1,0:T(8,128)(2,1)S(1)}, bf16[512,128]{1,0:T(8,128)(2,1)S(1)}, u32[]{:S(2)}, u32[]{:S(2)}) collective-permute-start(bf16[512,128]{1,0:T(8,128)(2,1)S(1)} %add_on.5), channel_id=1, source_target_pairs={{8,0},{9,1},{10,2},{11,3},{12,4},{13,5},{14,6},{15,7}} | collective-permute-start | bytes 393224 | tf_op jit(solution)/shard_map/ppermute | solution.py:571
  49.3 14.4 %collective-permute-start.17 = (bf16[512,128]{1,0:T(8,128)(2,1)S(1)}, bf16[512,128]{1,0:T(8,128)(2,1)S(1)}, u32[]{:S(2)}, u32[]{:S(2)}) collective-permute-start(bf16[512,128]{1,0:T(8,128)(2,1)S(1)} %get-tuple-element.135), channel_id=1, source_target_pairs={{8,0},{9,1},{10,2},{11,3},{12,4},{13,5},{14,6},{15,7}} | collective-permute-start | bytes 393224 | tf_op jit(solution)/shard_map/ppermute | solution.py:571
  50.7 14.5 %collective-permute-start.16 = (bf16[512,128]{1,0:T(8,128)(2,1)S(1)}, bf16[512,128]{1,0:T(8,128)(2,1)S(1)}, u32[]{:S(2)}, u32[]{:S(2)}) collective-permute-start(bf16[512,128]{1,0:T(8,128)(2,1)S(1)} %add_off.5), channel_id=1, source_target_pairs={{8,0},{9,1},{10,2},{11,3},{12,4},{13,5},{14,6},{15,7}} | collective-permute-start | bytes 393224 | tf_op jit(solution)/shard_map/ppermute | solution.py:571
  62.2 3.0 %collective-permute-start.12 = (bf16[512,128]{1,0:T(8,128)(2,1)S(1)}, bf16[512,128]{1,0:T(8,128)(2,1)S(1)}, u32[]{:S(2)}, u32[]{:S(2)}) collective-permute-start(bf16[512,128]{1,0:T(8,128)(2,1)S(1)} %get-tuple-element.124), channel_id=1, source_target_pairs={{0,1},{1,0},{2,3},{3,2},{4,5},{5,4},{6,7},{7,6},{8,9},{9,8},{10,11... | collective-permute-start | bytes 393224 | tf_op jit(solution)/shard_map/ppermute | solution.py:581
  68.2 2.7 %collective-permute-start.18 = (bf16[4,64,2048]{2,1,0:T(8,128)(2,1)S(1)}, bf16[4,64,2048]{2,1,0:T(8,128)(2,1)S(1)}, u32[]{:S(2)}, u32[]{:S(2)}) collective-permute-start(bf16[4,64,2048]{2,1,0:T(8,128)(2,1)S(1)} %get-tuple-element.142), channel_id=1, source_target_pairs={{0,1},{1,0},{2,3},{3,2},{4,5},{5,4},{6,7},{7,6},{8,9},{9,8},{10,11... | collective-permute-start | bytes 3145736 | tf_op jit(solution)/shard_map/ppermute | solution.py:598
  71.1 12.7 %collective-permute-start.20 = (bf16[2,64,1024]{2,1,0:T(8,128)(2,1)S(1)}, bf16[2,64,1024]{2,1,0:T(8,128)(2,1)S(1)}, u32[]{:S(2)}, u32[]{:S(2)}) collective-permute-start(bf16[2,64,1024]{2,1,0:T(8,128)(2,1)S(1)} %get-tuple-element.148), channel_id=1, source_target_pairs={{0,2},{1,3},{2,0},{3,1},{4,6},{5,7},{6,4},{7,5},{8,10},{9,11},{10,... | collective-permute-start | bytes 786440 | tf_op jit(solution)/shard_map/ppermute | solution.py:609
  71.2 16.5 %collective-permute-start.21 = (bf16[2,64,1024]{2,1,0:T(8,128)(2,1)S(1)}, bf16[2,64,1024]{2,1,0:T(8,128)(2,1)S(1)}, u32[]{:S(2)}, u32[]{:S(2)}) collective-permute-start(bf16[2,64,1024]{2,1,0:T(8,128)(2,1)S(1)} %get-tuple-element.150), channel_id=1, source_target_pairs={{0,4},{1,5},{2,6},{3,7},{4,0},{5,1},{6,2},{7,3},{8,12},{9,13},{10,... | collective-permute-start | bytes 786440 | tf_op jit(solution)/shard_map/ppermute | solution.py:610
  74.6 15.1 %collective-permute-start.19 = (bf16[512,128]{1,0:T(8,128)(2,1)S(1)}, bf16[512,128]{1,0:T(8,128)(2,1)S(1)}, u32[]{:S(2)}, u32[]{:S(2)}) collective-permute-start(bf16[512,128]{1,0:T(8,128)(2,1)S(1)} %get-tuple-element.147.refs_0_), channel_id=1, source_target_pairs={{0,7},{1,2},{2,1},{3,4},{4,3},{5,6},{6,5},{7,0},{8,15},{9,10},{10,... | collective-permute-start | bytes 393224 | tf_op jit(solution)/shard_map/ppermute | solution.py:617
  87.7 7.0 %collective-permute-start.22 = (bf16[64,1024]{1,0:T(8,128)(2,1)S(1)}, bf16[64,1024]{1,0:T(8,128)(2,1)S(1)}, u32[]{:S(2)}, u32[]{:S(2)}) collective-permute-start(bf16[64,1024]{1,0:T(8,128)(2,1)S(1)} %get-tuple-element.152), channel_id=1, source_target_pairs={{0,4},{1,5},{2,6},{3,7},{4,0},{5,1},{6,2},{7,3},{8,12},{9,13},{10,... | collective-permute-start | bytes 393224 | tf_op jit(solution)/shard_map/ppermute | solution.py:624
  87.8 7.5 %collective-permute-start.23 = (bf16[64,1024]{1,0:T(8,128)(2,1)S(1)}, bf16[64,1024]{1,0:T(8,128)(2,1)S(1)}, u32[]{:S(2)}, u32[]{:S(2)}) collective-permute-start(bf16[64,1024]{1,0:T(8,128)(2,1)S(1)} %get-tuple-element.154), channel_id=1, source_target_pairs={{0,2},{1,3},{2,0},{3,1},{4,6},{5,7},{6,4},{7,5},{8,10},{9,11},{10,... | collective-permute-start | bytes 393224 | tf_op jit(solution)/shard_map/ppermute | solution.py:623

commit v9 on v8

--- a/solution.py
+++ b/solution.py
@@ -439,10 +439,11 @@
 
 def keep_kernel(chips, steps, got, both, *outs):
     chip = lax.axis_index("dom") // 2
-    half = got.shape[2] // 2
+    start = 0
     for n, (first, second) in enumerate(steps):
         give, own = outs[2 * n : 2 * n + 2]
-        across = slice(n * half, (n + 1) * half)
+        across = slice(start, start + own.shape[2])
+        start += own.shape[2]
 
         def total(distance):
             z = lax.bitwise_xor(chip, distance)
@@ -463,10 +464,11 @@
 
 def total_kernel(rest_a, got_a, rest_b, got_b, qkv_grad, out_grad):
     width = out_grad.shape[1]
-    qkv_grad[:, : 2 * width] = rest_a[...] + got_a[...].astype(F32)
+    split = rest_a.shape[1]
+    qkv_grad[:, :split] = rest_a[...] + got_a[...].astype(F32)
     total = rest_b[...] + got_b[...].astype(F32)
-    qkv_grad[:, 2 * width :] = total[:, :width]
-    out_grad[...] = total[:, width:]
+    qkv_grad[:, split:] = total[:, : total.shape[1] - width]
+    out_grad[...] = total[:, total.shape[1] - width :]
 
 
 def other_core(parts):
@@ -597,13 +599,14 @@
     if direct:
         got = lax.ppermute(give[0], "dom", other_core(parts))
         steps = ((1, 2), (2, 1))
+        shares = (every // 2 + width // 4, every // 2 - width // 4)
         mine = call(
             functools.partial(mine_kernel, chips), "mine", [((chips, row, every), F32)],
             [xn_t, d_low, d_high, attn_t, g_zero, g_mid, g_one],
         )[0]
         give_a, own_a, give_b, own_b = call(
             functools.partial(keep_kernel, chips, steps), "keep",
-            [((2, row, every // 2), BF16), ((2, row, every // 2), F32)] * 2,
+            [((2, row, n), dtype) for n in shares for dtype in (BF16, F32)],
             [got, mine],
         )
         got_a = lax.ppermute(give_a, "dom", chips_apart(parts, steps[0][0]))
@@ -617,7 +620,7 @@
     off = lax.ppermute(c_off, "dom", next_chip(parts))
     if direct:
         give_a, rest_a, give_b, rest_b = call(
-            middle_kernel, "middle", [((row, every // 2), BF16), ((row, every // 2), F32)] * 2,
+            middle_kernel, "middle", [((row, n), dtype) for n in shares for dtype in (BF16, F32)],
             [own_a, got_a, own_b, got_b, c_off],
         )
         got_b = lax.ppermute(give_b, "dom", chips_apart(parts, steps[1][1]))

time: 96.4 us -> 98.3 us (1.020)
  waiting for transfers between devices: 29.9 us -> 33.5 us
  starting transfers between devices: 26 us -> 24.4 us
    ppermute x4, waiting for transfers between devices: 1.86 us -> 8.59 us  [local(): off = lax.ppermute(c_off, 'dom', next_chip(parts))]
    ppermute x1, waiting for transfers between devices: 7.25 us -> 2.19 us  [local(): got_a = lax.ppermute(give_a, 'dom', chips_apart(parts, steps[0][0]))]
    ppermute x1, waiting for transfers between devices: 3.86 us -> 8.34 us  [local(): got_b = lax.ppermute(give_b, 'dom', chips_apart(parts, steps[1][0]))]
    ppermute x1, waiting for transfers between devices: 4.15 us -> 0.01 us  [local(): got_a = lax.ppermute(give_a, 'dom', chips_apart(parts, steps[0][1]))]
    ppermute x1, waiting for transfers between devices: 0.6 us -> 2.12 us  [local(): got_b = lax.ppermute(give_b, 'dom', chips_apart(parts, steps[1][1]))]
    ppermute x4, starting transfers between devices: 8.55 us -> 7.05 us  [local(): off = lax.ppermute(c_off, 'dom', next_chip(parts))]
    ppermute x1, starting transfers between devices: 1.82 us -> 0.52 us  [local(): got_b = lax.ppermute(give_b, 'dom', chips_apart(parts, steps[1][1]))]
    ppermute x1, starting transfers between devices: 0.07 us -> 1.25 us  [local(): got_a = lax.ppermute(give_a, 'dom', chips_apart(parts, steps[0][1]))]
  transfers between devices with their start and end apart: 24 -> 24, of which waited for: 9 -> 9; matrix products, arithmetic and copies ran while one was open for 0% -> 0% of each run, Pallas kernels for 26% -> 25%
where the time goes in v9:
time: 98.3 us; the launch traced here: 98.1 us
  Pallas kernels  36.7 us (37%)
  waiting for transfers between devices  33.5 us (34%)
  starting transfers between devices  24.4 us (25%)
  local copies, waits for them, and re-layouts  2.41 us (2%)
  between operations  1.04 us (1%)
    pallas_call x28, Pallas kernels, call(): pl.pallas_call(kernel, in_specs=[scalars] * smem + [vmem] * (len(args) -...  36.7 us
    ppermute x9, waiting for transfers between devices, local(): lax.ppermute(part, 'section', [(here, here - 1)])  9.89 us
    ppermute x4, waiting for transfers between devices, local(): off = lax.ppermute(c_off, 'dom', next_chip(parts))  8.59 us
    ppermute x1, waiting for transfers between devices, local(): got_b = lax.ppermute(give_b, 'dom', chips_apart(parts, steps[1][0]))  8.34 us
    ppermute x9, starting transfers between devices, local(): lax.ppermute(part, 'section', [(here, here - 1)])  8.29 us
    ppermute x4, starting transfers between devices, local(): off = lax.ppermute(c_off, 'dom', next_chip(parts))  7.05 us
    ppermute x1, starting transfers between devices, local(): x_off = lax.ppermute(x_off, 'dom', next_chip(parts))  4.71 us
    unnamed x12, local copies, waits for them, and re-layouts  2.41 us
  transfers between devices with their start and end apart: 24, of which 9 were waited for; matrix products, arithmetic and copies ran while one was open for 0% of the time, Pallas kernels for 25%

profile of v9, /device:TPU:0, one launch (start us, length us, event | category | flops | bytes accessed | tf_op | source)
XLA Modules:
  0.0 98.1 jit_solution(1634230481676231741)
XLA Ops:
  0.6 1.0 %copy-done.3 = bf16[1,1,384,512]{3,2,1,0:T(8,128)(2,1)S(1)} copy-done((bf16[1,1,384,512]{3,2,1,0:T(8,128)(2,1)S(1)}, bf16[1,1,384,512]{3,2,1,0:T(8,128)(2,1)}, u32[]{:S(2)}) %copy-start.3) | copy-done | bytes 393240
  1.7 0.5 collective-permute-start
  2.2 4.7 %collective-permute-start.1 = (bf16[128,512]{1,0:T(8,128)(2,1)S(1)}, bf16[128,512]{1,0:T(8,128)(2,1)S(1)}, u32[]{:S(2)}, u32[]{:S(2)}) collective-permute-start(bf16[128,512]{1,0:T(8,128)(2,1)S(1)} %get-tuple-element.81), channel_id=1, source_target_pairs={{0,7},{1,2},{2,1},{3,4},{4,3},{5,6},{6,5},{7,0},{8,15},{9,10},{10,... | collective-permute-start | bytes 393224 | tf_op jit(solution)/shard_map/ppermute | solution.py:504
  6.9 1.4 %copy-done = bf16[1,512,1536]{2,1,0:T(8,128)(2,1)S(1)} copy-done((bf16[1,512,1536]{2,1,0:T(8,128)(2,1)S(1)}, bf16[1,512,1536]{2,1,0:T(8,128)(2,1)}, u32[]{:S(2)}) %copy-start) | copy-done | bytes 1572888
  8.3 1.2 %prelude_own.1 = (bf16[512,384]{1,0:T(8,128)(2,1)S(1)}, f32[8,384]{1,0:T(8,128)S(1)}, bf16[384,512]{1,0:T(8,128)(2,1)S(1)}, bf16[384,512]{1,0:T(8,128)(2,1)S(1)}...) custom-call(bf16[384,512]{1,0:T(8,128)(2,1)S(1)} %bitcast.32, ...), custom_call_target="tpu_custom_call" | custom-call | flops 1 | bytes 1 | tf_op jit(solution)/shard_map/prelude_own/pallas_call | solution.py:30
  9.5 0.0 collective-permute-done.x_on
  9.6 0.7 collective-permute-done.1.x_off
  10.2 0.0 copy-start.2
  10.3 3.4 %prelude.1 = (bf16[512,640]{1,0:T(8,128)(2,1)S(1)}, f32[8,640]{1,0:T(8,128)S(1)}, bf16[640,512]{1,0:T(8,128)(2,1)S(1)}, bf16[512,640]{1,0:T(8,128)(2,1)S(1)}, bf...) custom-call(s32[3,3]{1,0:T(4,128)S(1)} %copy-done.5, ...), custom_call_target="tpu_custom_call" | custom-call | flops 1 | bytes 1 | tf_op jit(solution)/shard_map/prelude/pallas_call | solution.py:30
  13.7 4.4 %stage_start.1 = (bf16[512,128]{1,0:T(8,128)(2,1)S(1)}, bf16[4,384,256]{2,1,0:T(8,128)(2,1)S(1)}, bf16[512,128]{1,0:T(8,128)(2,1)S(1)}, bf16[512,128]{1,0:T(8,12...) custom-call(bf16[512,128]{1,0:T(8,128)(2,1)S(1)} %get-tuple-element., ...), custom_call_target="tpu_custom_call" | custom-call | flops 1 | bytes 1 | tf_op jit(solution)/shard_map/stage_start/pallas_call | solution.py:30
  18.1 0.1 collective-permute-start.2
  18.2 2.9 %collective-permute-start.7 = (bf16[512,128]{1,0:T(8,128)(2,1)S(1)}, bf16[512,128]{1,0:T(8,128)(2,1)S(1)}, u32[]{:S(2)}, u32[]{:S(2)}) collective-permute-start(bf16[512,128]{1,0:T(8,128)(2,1)S(1)} %get-tuple-element.114), channel_id=1, source_target_pairs={{0,7},{1,2},{2,1},{3,4},{4,3},{5,6},{6,5},{7,0},{8,15},{9,10},{10,... | collective-permute-start | bytes 393224 | tf_op jit(solution)/shard_map/ppermute | solution.py:562
  21.2 0.0 collective-permute-done.2.rim
  21.2 0.7 collective-permute-start.3
  21.9 2.1 %stage_main.3 = (bf16[512,128]{1,0:T(8,128)(2,1)S(1)}, bf16[512,128]{1,0:T(8,128)(2,1)S(1)}) custom-call(bf16[512,128]{1,0:T(8,128)(2,1)S(1)} %get-tuple-element.90.g_mid.refs_0_, bf16[512,128]{1,0:T(8,128)(2,1)S(1)} %get-tuple-element.91.g_one.refs_0_, bf16[512,128]{1,0:T(8,128)(2,1)S(1)} %get-tuple-element.101.da_zero, ...), custom_call_target="tpu_custom_call" | custom-call | flops 1 | bytes 1 | tf_op jit(solution)/shard_map/stage_main/pallas_call | solution.py:30
  24.0 1.8 %collective-permute-done.7.rim = bf16[512,128]{1,0:T(8,128)(2,1)S(1)} collective-permute-done((bf16[512,128]{1,0:T(8,128)(2,1)S(1)}, bf16[512,128]{1,0:T(8,128)(2,1)S(1)}, u32[]{:S(2)}, u32[]{:S(2)}) %collective-permute-start.7) | collective-permute-done | bytes 131104 | tf_op jit(solution)/shard_map/ppermute | solution.py:562
  25.9 0.7 collective-permute-start.8
  26.5 0.8 collective-permute-start.4
  27.4 1.5 %stage_zero.2 = (bf16[512,128]{1,0:T(8,128)(2,1)S(1)}, bf16[512,128]{1,0:T(8,128)(2,1)S(1)}, bf16[4,384,256]{2,1,0:T(8,128)(2,1)S(1)}, bf16[512,128]{1,0:T(8,128)(2,1)S(1)}) custom-call(bf16[512,128]{1,0:T(8,128)(2,1)S(1)} %get-tuple-element.89.g_zero.refs_0_, bf16[512,128]{1,0:T(8,128)(2,1)S(1)} %collective-permute-done.3.refs_1_, ...), custom_call_target="tpu_custom_call" | custom-call | flops 1 | bytes 1 | tf_op jit(solution)/shard_map/stage_zero/pallas_call | solution.py:30
  29.0 0.1 collective-permute-start.5
  29.0 0.0 collective-permute-done.8.refs_1_
  29.0 1.4 %stage_one.2 = (bf16[512,128]{1,0:T(8,128)(2,1)S(1)}, bf16[512,128]{1,0:T(8,128)(2,1)S(1)}, bf16[512,128]{1,0:T(8,128)(2,1)S(1)}) custom-call(bf16[512,128]{1,0:T(8,128)(2,1)S(1)} %get-tuple-element.91.g_one.refs_0_, bf16[512,128]{1,0:T(8,128)(2,1)S(1)} %collective-permute-done.8.refs_1_, bf16[512,512]{1,0:T(8,128)(2,1)S(1)} %bitcast.23, ...), custom_call_target="tpu_custom_call" | custom-call | flops 1 | bytes 1 | tf_op jit(solution)/shard_map/stage_one/pallas_call | solution.py:30
  30.5 1.6 %collective-permute-start.13 = (bf16[512,128]{1,0:T(8,128)(2,1)S(1)}, bf16[512,128]{1,0:T(8,128)(2,1)S(1)}, u32[]{:S(2)}, u32[]{:S(2)}) collective-permute-start(bf16[512,128]{1,0:T(8,128)(2,1)S(1)} %get-tuple-element.126), channel_id=1, source_target_pairs={{0,7},{1,2},{2,1},{3,4},{4,3},{5,6},{6,5},{7,0},{8,15},{9,10},{10,... | collective-permute-start | bytes 393224 | tf_op jit(solution)/shard_map/ppermute | solution.py:562
  32.1 2.2 %stage_mid.2 = (bf16[512,128]{1,0:T(8,128)(2,1)S(1)}, bf16[512,128]{1,0:T(8,128)(2,1)S(1)}, bf16[4,1,384,256]{3,2,1,0:T(8,128)(2,1)S(1)}, bf16[512,128]{1,0:T(8,128)(2,1)S(1)}) custom-call(bf16[512,128]{1,0:T(8,128)(2,1)S(1)} %get-tuple-element.90.g_mid.refs_0_, bf16[512,128]{1,0:T(8,128)(2,1)S(1)} %collective-permute-done.4.refs_1_, ...), custom_call_target="tpu_custom_call" | custom-call | flops 1 | bytes 1 | tf_op jit(solution)/shard_map/stage_mid/pallas_call | solution.py:30
  34.3 0.7 collective-permute-start.6
  35.0 2.1 %stage_main.4 = (bf16[512,128]{1,0:T(8,128)(2,1)S(1)}, bf16[512,128]{1,0:T(8,128)(2,1)S(1)}) custom-call(bf16[512,128]{1,0:T(8,128)(2,1)S(1)} %get-tuple-element.112.g_mid.refs_0_, bf16[512,128]{1,0:T(8,128)(2,1)S(1)} %get-tuple-element.115.g_one.refs_0_, bf16[512,128]{1,0:T(8,128)(2,1)S(1)} %get-tuple-element.107.refs_3_.da_zero, ...), custom_call_target="tpu_custom_call" | custom-call | flops 1 | bytes 1 | tf_op jit(solution)/shard_map/stage_main/pallas_call | solution.py:30
  37.1 0.0 collective-permute-done.13.rim
  37.2 0.7 collective-permute-start.14
  37.8 0.7 collective-permute-start.9
  38.5 1.6 %stage_zero.3 = (bf16[512,128]{1,0:T(8,128)(2,1)S(1)}, bf16[512,128]{1,0:T(8,128)(2,1)S(1)}, bf16[4,384,256]{2,1,0:T(8,128)(2,1)S(1)}, bf16[512,128]{1,0:T(8,128)(2,1)S(1)}) custom-call(bf16[512,128]{1,0:T(8,128)(2,1)S(1)} %get-tuple-element.100.refs_2_.refs_0_, bf16[512,128]{1,0:T(8,128)(2,1)S(1)} %collective-permute-done.6.refs_1_, ...), custom_call_target="tpu_custom_call" | custom-call | flops 1 | bytes 1 | tf_op jit(solution)/shard_map/stage_zero/pallas_call | solution.py:30
  40.1 0.1 collective-permute-start.10
  40.2 1.4 %stage_one.3 = (bf16[512,128]{1,0:T(8,128)(2,1)S(1)}, bf16[512,128]{1,0:T(8,128)(2,1)S(1)}, bf16[512,128]{1,0:T(8,128)(2,1)S(1)}) custom-call(bf16[512,128]{1,0:T(8,128)(2,1)S(1)} %get-tuple-element.115.g_one.refs_0_, bf16[512,128]{1,0:T(8,128)(2,1)S(1)} %collective-permute-done.14.refs_1_, bf16[512,512]{1,0:T(8,128)(2,1)S(1)} %bitcast.26, ...), custom_call_target="tpu_custom_call" | custom-call | flops 1 | bytes 1 | tf_op jit(solution)/shard_map/stage_one/pallas_call | solution.py:30
  41.6 2.1 %collective-permute-start.15 = (bf16[512,128]{1,0:T(8,128)(2,1)S(1)}, bf16[512,128]{1,0:T(8,128)(2,1)S(1)}, u32[]{:S(2)}, u32[]{:S(2)}) collective-permute-start(bf16[512,128]{1,0:T(8,128)(2,1)S(1)} %get-tuple-element.133), channel_id=1, source_target_pairs={{0,7},{1,2},{2,1},{3,4},{4,3},{5,6},{6,5},{7,0},{8,15},{9,10},{10,... | collective-permute-start | bytes 393224 | tf_op jit(solution)/shard_map/ppermute | solution.py:562
  43.7 2.2 %stage_mid.3 = (bf16[512,128]{1,0:T(8,128)(2,1)S(1)}, bf16[512,128]{1,0:T(8,128)(2,1)S(1)}, bf16[4,1,384,256]{3,2,1,0:T(8,128)(2,1)S(1)}, bf16[512,128]{1,0:T(8,128)(2,1)S(1)}) custom-call(bf16[512,128]{1,0:T(8,128)(2,1)S(1)} %get-tuple-element.112.g_mid.refs_0_, bf16[512,128]{1,0:T(8,128)(2,1)S(1)} %collective-permute-done.9.refs_1_, ...), custom_call_target="tpu_custom_call" | custom-call | flops 1 | bytes 1 | tf_op jit(solution)/shard_map/stage_mid/pallas_call | solution.py:30
  45.9 0.0 collective-permute-done.10.rim
  45.9 1.3 %collective-permute-start.11 = (bf16[512,128]{1,0:T(8,128)(2,1)S(1)}, bf16[512,128]{1,0:T(8,128)(2,1)S(1)}, u32[]{:S(2)}, u32[]{:S(2)}) collective-permute-start(bf16[512,128]{1,0:T(8,128)(2,1)S(1)} %add_on.5), channel_id=1, source_target_pairs={{8,0},{9,1},{10,2},{11,3},{12,4},{13,5},{14,6},{15,7}} | collective-permute-start | bytes 393224 | tf_op jit(solution)/shard_map/ppermute | solution.py:573
  47.2 2.1 %stage_main.5 = (bf16[512,128]{1,0:T(8,128)(2,1)S(1)}, bf16[512,128]{1,0:T(8,128)(2,1)S(1)}) custom-call(bf16[512,128]{1,0:T(8,128)(2,1)S(1)} %get-tuple-element.128.g_mid.g_prev, bf16[512,128]{1,0:T(8,128)(2,1)S(1)} %get-tuple-element.127.g_one.g_prev, bf16[512,128]{1,0:T(8,128)(2,1)S(1)} %get-tuple-element.120.refs_3_.da_zero, ...), custom_call_target="tpu_custom_call" | custom-call | flops 1 | bytes 1 | tf_op jit(solution)/shard_map/stage_main/pallas_call | solution.py:30
  49.3 1.3 %collective-permute-start.17 = (bf16[512,128]{1,0:T(8,128)(2,1)S(1)}, bf16[512,128]{1,0:T(8,128)(2,1)S(1)}, u32[]{:S(2)}, u32[]{:S(2)}) collective-permute-start(bf16[512,128]{1,0:T(8,128)(2,1)S(1)} %get-tuple-element.135), channel_id=1, source_target_pairs={{8,0},{9,1},{10,2},{11,3},{12,4},{13,5},{14,6},{15,7}} | collective-permute-start | bytes 393224 | tf_op jit(solution)/shard_map/ppermute | solution.py:573
  50.6 0.0 collective-permute-done.15.rim
  50.7 1.5 %collective-permute-start.16 = (bf16[512,128]{1,0:T(8,128)(2,1)S(1)}, bf16[512,128]{1,0:T(8,128)(2,1)S(1)}, u32[]{:S(2)}, u32[]{:S(2)}) collective-permute-start(bf16[512,128]{1,0:T(8,128)(2,1)S(1)} %add_off.5), channel_id=1, source_target_pairs={{8,0},{9,1},{10,2},{11,3},{12,4},{13,5},{14,6},{15,7}} | collective-permute-start | bytes 393224 | tf_op jit(solution)/shard_map/ppermute | solution.py:573
  52.2 8.5 %collective-permute-done.11.refs_1_ = bf16[512,128]{1,0:T(8,128)(2,1)S(1)} collective-permute-done((bf16[512,128]{1,0:T(8,128)(2,1)S(1)}, bf16[512,128]{1,0:T(8,128)(2,1)S(1)}, u32[]{:S(2)}, u32[]{:S(2)}) %collective-permute-start.11) | collective-permute-done | bytes 131104 | tf_op jit(solution)/shard_map/ppermute | solution.py:573
  60.7 1.5 %last_zero.1 = (bf16[512,128]{1,0:T(8,128)(2,1)S(1)}, bf16[512,128]{1,0:T(8,128)(2,1)S(1)}, bf16[4,384,256]{2,1,0:T(8,128)(2,1)S(1)}, bf16[512,128]{1,0:T(8,128)(2,1)S(1)}) custom-call(bf16[512,128]{1,0:T(8,128)(2,1)S(1)} %get-tuple-element.111.refs_2_.refs_0_, bf16[512,128]{1,0:T(8,128)(2,1)S(1)} %collective-permute-done.11.refs_1_, ...), custom_call_target="tpu_custom_call" | custom-call | flops 1 | bytes 1 | tf_op jit(solution)/shard_map/last_zero/pallas_call | solution.py:30
  62.2 0.1 collective-permute-start.12
  62.3 1.4 %collective-permute-done.17.arrived = bf16[512,128]{1,0:T(8,128)(2,1)S(1)} collective-permute-done((bf16[512,128]{1,0:T(8,128)(2,1)S(1)}, bf16[512,128]{1,0:T(8,128)(2,1)S(1)}, u32[]{:S(2)}, u32[]{:S(2)}) %collective-permute-start.17) | collective-permute-done | bytes 131104 | tf_op jit(solution)/shard_map/ppermute | solution.py:573
  63.7 1.5 %last_mid.1 = (bf16[512,128]{1,0:T(8,128)(2,1)S(1)}, bf16[512,128]{1,0:T(8,128)(2,1)S(1)}, bf16[4,1,384,256]{3,2,1,0:T(8,128)(2,1)S(1)}, bf16[1536,256]{1,0:T(8,128)(2,1)S(1)}) custom-call(bf16[512,128]{1,0:T(8,128)(2,1)S(1)} %get-tuple-element.128.g_mid.g_prev, bf16[512,128]{1,0:T(8,128)(2,1)S(1)} %collective-permute-done.17.arrived, ...), custom_call_target="tpu_custom_call" | custom-call | flops 1 | bytes 1 | tf_op jit(solution)/shard_map/last_mid/pallas_call | solution.py:30
  65.2 3.0 %last_terms.1 = (bf16[512,128]{1,0:T(8,128)(2,1)S(1)}, bf16[1536,384]{1,0:T(8,128)(2,1)S(1)}, bf16[4,64,2048]{2,1,0:T(8,128)(2,1)S(1)}) custom-call(bf16[512,128]{1,0:T(8,128)(2,1)S(1)} %collective-permute-done.12.after.on, bf16[512,128]{1,0:T(8,128)(2,1)S(1)} %get-tuple-element.127.g_one.g_prev, bf16[512,128]{1,0:T(8,128)(2,1)S(1)} %collective-permute-done.16.arrived, ...), custom_call_target="tpu_custom_call" | custom-call | flops 1 | bytes 1 | tf_op jit(solution)/shard_map/last_terms/pallas_call | solution.py:30
  68.2 0.1 collective-permute-start.18
  68.3 1.0 %mine.1.both = f32[4,64,2048]{2,1,0:T(8,128)S(1)} custom-call(bf16[512,640]{1,0:T(8,128)(2,1)S(1)} %get-tuple-element.95.xn_t.refs_7_.refs_10_, bf16[1536,256]{1,0:T(8,128)(2,1)S(1)} %get-tuple-element.141.d_low, bf16[1536,384]{1,0:T(8,128)(2,1)S(1)} %get-tuple-element.143.d_high, bf16[512,384]{1,0:T(8,128)(2,1)S(1)} %get-tuple-element.94.attn_t.refs_5_.refs_8_, ...), custom_call_target="tpu_custom_call" | custom-call | flops 1 | bytes 1 | tf_op jit(solution)/shard_map/mine/pallas_call | solution.py:30
  69.3 1.6 %collective-permute-done.18.got = bf16[4,64,2048]{2,1,0:T(8,128)(2,1)S(1)} collective-permute-done((bf16[4,64,2048]{2,1,0:T(8,128)(2,1)S(1)}, bf16[4,64,2048]{2,1,0:T(8,128)(2,1)S(1)}, u32[]{:S(2)}, u32[]{:S(2)}) %collective-permute-start.18) | collective-permute-done | bytes 1048608 | tf_op jit(solution)/shard_map/ppermute | solution.py:600
  70.9 0.2 keep.1
  71.1 0.1 collective-permute-start.20
  71.2 1.7 %collective-permute-start.21 = (bf16[2,64,896]{2,1,0:T(8,128)(2,1)S(1)}, bf16[2,64,896]{2,1,0:T(8,128)(2,1)S(1)}, u32[]{:S(2)}, u32[]{:S(2)}) collective-permute-start(bf16[2,64,896]{2,1,0:T(8,128)(2,1)S(1)} %get-tuple-element.150), channel_id=1, source_target_pairs={{0,4},{1,5},{2,6},{3,7},{4,0},{5,1},{6,2},{7,3},{8,12},{9,13},{10,... | collective-permute-start | bytes 688136 | tf_op jit(solution)/shard_map/ppermute | solution.py:613
  72.8 1.7 %last_input.1 = (bf16[512,384]{1,0:T(8,128)(2,1)S(1)}, bf16[512,128]{1,0:T(8,128)(2,1)S(1)}) custom-call(f32[2,64,1152]{2,1,0:T(8,128)S(1)} %get-tuple-element.145.after.own_a, bf16[512,128]{1,0:T(8,128)(2,1)S(1)} %get-tuple-element.134.g_zero, bf16[512,128]{1,0:T(8,128)(2,1)S(1)} %get-tuple-element.138.g_mid, ...), custom_call_target="tpu_custom_call" | custom-call | flops 1 | bytes 1 | tf_op jit(solution)/shard_map/last_input/pallas_call | solution.py:30
  74.6 8.3 %collective-permute-done.21.got_b = bf16[2,64,896]{2,1,0:T(8,128)(2,1)S(1)} collective-permute-done((bf16[2,64,896]{2,1,0:T(8,128)(2,1)S(1)}, bf16[2,64,896]{2,1,0:T(8,128)(2,1)S(1)}, u32[]{:S(2)}, u32[]{:S(2)}) %collective-permute-start.21) | collective-permute-done | bytes 229408 | tf_op jit(solution)/shard_map/ppermute | solution.py:613
  82.9 2.2 %collective-permute-done.20.got_a = bf16[2,64,1152]{2,1,0:T(8,128)(2,1)S(1)} collective-permute-done((bf16[2,64,1152]{2,1,0:T(8,128)(2,1)S(1)}, bf16[2,64,1152]{2,1,0:T(8,128)(2,1)S(1)}, u32[]{:S(2)}, u32[]{:S(2)}) %collective-permute-start.20) | collective-permute-done | bytes 294944 | tf_op jit(solution)/shard_map/ppermute | solution.py:612
  85.1 0.1 middle.1
  85.2 1.3 %collective-permute-start.22 = (bf16[64,1152]{1,0:T(8,128)(2,1)S(1)}, bf16[64,1152]{1,0:T(8,128)(2,1)S(1)}, u32[]{:S(2)}, u32[]{:S(2)}) collective-permute-start(bf16[64,1152]{1,0:T(8,128)(2,1)S(1)} %get-tuple-element.152), channel_id=1, source_target_pairs={{0,4},{1,5},{2,6},{3,7},{4,0},{5,1},{6,2},{7,3},{8,12},{9,13},{10,... | collective-permute-start | bytes 442376 | tf_op jit(solution)/shard_map/ppermute | solution.py:627
  86.5 0.5 collective-permute-start.19
  86.9 0.5 collective-permute-start.23
  87.4 6.7 %collective-permute-done.19.off = bf16[512,128]{1,0:T(8,128)(2,1)S(1)} collective-permute-done((bf16[512,128]{1,0:T(8,128)(2,1)S(1)}, bf16[512,128]{1,0:T(8,128)(2,1)S(1)}, u32[]{:S(2)}, u32[]{:S(2)}) %collective-permute-start.19) | collective-permute-done | bytes 131104 | tf_op jit(solution)/shard_map/ppermute | solution.py:620
  94.2 0.9 finish_input.1
  95.1 2.1 %collective-permute-done.23.got_b = bf16[64,896]{1,0:T(8,128)(2,1)S(1)} collective-permute-done((bf16[64,896]{1,0:T(8,128)(2,1)S(1)}, bf16[64,896]{1,0:T(8,128)(2,1)S(1)}, u32[]{:S(2)}, u32[]{:S(2)}) %collective-permute-start.23) | collective-permute-done | bytes 114720 | tf_op jit(solution)/shard_map/ppermute | solution.py:626
  97.2 0.0 collective-permute-done.22.got_a
  97.2 0.8 total.1
  (24 shorter events, 0.3 us)
Async XLA Ops:
  0.6 1.0 %copy-start.3 = (bf16[1,1,384,512]{3,2,1,0:T(8,128)(2,1)S(1)}, bf16[1,1,384,512]{3,2,1,0:T(8,128)(2,1)}, u32[]{:S(2)}) copy-start(bf16[1,1,384,512]{3,2,1,0:T(8,128)(2,1)} %param.5) | copy-start | bytes 1179652
  1.6 8.6 %copy-start.4 = (bf16[1,384,512]{2,1,0:T(8,128)(2,1)S(1)}, bf16[1,384,512]{2,1,0:T(8,128)(2,1)}, u32[]{:S(2)}) copy-start(bf16[1,384,512]{2,1,0:T(8,128)(2,1)} %param.6) | copy-start | bytes 1179652
  1.6 8.6 %copy-start.5 = (s32[3,3]{1,0:T(4,128)S(1)}, s32[3,3]{1,0:T(4,128)}, u32[]{:S(2)}) copy-start(s32[3,3]{1,0:T(4,128)} %neighbours.1) | copy-start | bytes 112
  1.7 7.9 %collective-permute-start = (bf16[128,512]{1,0:T(8,128)(2,1)S(1)}, bf16[128,512]{1,0:T(8,128)(2,1)S(1)}, u32[]{:S(2)}, u32[]{:S(2)}) collective-permute-start(bf16[128,512]{1,0:T(8,128)(2,1)S(1)} %get-tuple-element.80), channel_id=1, source_target_pairs={{0,1},{1,0},{2,3},{3,2},{4,5},{5,4},{6,7},{7,6},{8,9},{9,8},{10,11... | collective-permute-start | bytes 393224 | tf_op jit(solution)/shard_map/ppermute | solution.py:503
  2.2 8.1 %collective-permute-start.1 = (bf16[128,512]{1,0:T(8,128)(2,1)S(1)}, bf16[128,512]{1,0:T(8,128)(2,1)S(1)}, u32[]{:S(2)}, u32[]{:S(2)}) collective-permute-start(bf16[128,512]{1,0:T(8,128)(2,1)S(1)} %get-tuple-element.81), channel_id=1, source_target_pairs={{0,7},{1,2},{2,1},{3,4},{4,3},{5,6},{6,5},{7,0},{8,15},{9,10},{10,... | collective-permute-start | bytes 393224 | tf_op jit(solution)/shard_map/ppermute | solution.py:504
  6.9 1.4 %copy-start = (bf16[1,512,1536]{2,1,0:T(8,128)(2,1)S(1)}, bf16[1,512,1536]{2,1,0:T(8,128)(2,1)}, u32[]{:S(2)}) copy-start(bf16[1,512,1536]{2,1,0:T(8,128)(2,1)} %param.7) | copy-start | bytes 4718596
  8.3 1.9 %copy-start.1 = (bf16[1,512,1536]{2,1,0:T(8,128)(2,1)S(1)}, bf16[1,512,1536]{2,1,0:T(8,128)(2,1)}, u32[]{:S(2)}) copy-start(bf16[1,512,1536]{2,1,0:T(8,128)(2,1)} %param.7) | copy-start | bytes 4718596
  10.2 3.4 %copy-start.2 = (bf16[1,512,512]{2,1,0:T(8,128)(2,1)S(1)}, bf16[1,512,512]{2,1,0:T(8,128)(2,1)}, u32[]{:S(2)}) copy-start(bf16[1,512,512]{2,1,0:T(8,128)(2,1)} %param.8) | copy-start | bytes 1572868
  18.1 3.0 %collective-permute-start.2 = (bf16[512,128]{1,0:T(8,128)(2,1)S(1)}, bf16[512,128]{1,0:T(8,128)(2,1)S(1)}, u32[]{:S(2)}, u32[]{:S(2)}) collective-permute-start(bf16[512,128]{1,0:T(8,128)(2,1)S(1)} %get-tuple-element.99), channel_id=1, source_target_pairs={{0,1},{1,0},{2,3},{3,2},{4,5},{5,4},{6,7},{7,6},{8,9},{9,8},{10,11... | collective-permute-start | bytes 393224 | tf_op jit(solution)/shard_map/ppermute | solution.py:542
  18.2 7.6 %collective-permute-start.7 = (bf16[512,128]{1,0:T(8,128)(2,1)S(1)}, bf16[512,128]{1,0:T(8,128)(2,1)S(1)}, u32[]{:S(2)}, u32[]{:S(2)}) collective-permute-start(bf16[512,128]{1,0:T(8,128)(2,1)S(1)} %get-tuple-element.114), channel_id=1, source_target_pairs={{0,7},{1,2},{2,1},{3,4},{4,3},{5,6},{6,5},{7,0},{8,15},{9,10},{10,... | collective-permute-start | bytes 393224 | tf_op jit(solution)/shard_map/ppermute | solution.py:562
  21.2 6.2 %collective-permute-start.3 = (bf16[512,128]{1,0:T(8,128)(2,1)S(1)}, bf16[512,128]{1,0:T(8,128)(2,1)S(1)}, u32[]{:S(2)}, u32[]{:S(2)}) collective-permute-start(bf16[512,128]{1,0:T(8,128)(2,1)S(1)} %add_on.3), channel_id=1, source_target_pairs={{24,16},{25,17},{26,18},{27,19},{28,20},{29,21},{30,22},{31,23}} | collective-permute-start | bytes 393224 | tf_op jit(solution)/shard_map/ppermute | solution.py:573
  25.9 3.2 %collective-permute-start.8 = (bf16[512,128]{1,0:T(8,128)(2,1)S(1)}, bf16[512,128]{1,0:T(8,128)(2,1)S(1)}, u32[]{:S(2)}, u32[]{:S(2)}) collective-permute-start(bf16[512,128]{1,0:T(8,128)(2,1)S(1)} %add_off.3), channel_id=1, source_target_pairs={{24,16},{25,17},{26,18},{27,19},{28,20},{29,21},{30,22},{31,23}} | collective-permute-start | bytes 393224 | tf_op jit(solution)/shard_map/ppermute | solution.py:573
  26.5 5.5 %collective-permute-start.4 = (bf16[512,128]{1,0:T(8,128)(2,1)S(1)}, bf16[512,128]{1,0:T(8,128)(2,1)S(1)}, u32[]{:S(2)}, u32[]{:S(2)}) collective-permute-start(bf16[512,128]{1,0:T(8,128)(2,1)S(1)} %get-tuple-element.106), channel_id=1, source_target_pairs={{24,16},{25,17},{26,18},{27,19},{28,20},{29,21},{30,22},{31,23}} | collective-permute-start | bytes 393224 | tf_op jit(solution)/shard_map/ppermute | solution.py:573
  29.0 5.3 %collective-permute-start.5 = (bf16[512,128]{1,0:T(8,128)(2,1)S(1)}, bf16[512,128]{1,0:T(8,128)(2,1)S(1)}, u32[]{:S(2)}, u32[]{:S(2)}) collective-permute-start(bf16[512,128]{1,0:T(8,128)(2,1)S(1)} %get-tuple-element.110), channel_id=1, source_target_pairs={{0,1},{1,0},{2,3},{3,2},{4,5},{5,4},{6,7},{7,6},{8,9},{9,8},{10,11... | collective-permute-start | bytes 393224 | tf_op jit(solution)/shard_map/ppermute | solution.py:549
  30.5 6.7 %collective-permute-start.13 = (bf16[512,128]{1,0:T(8,128)(2,1)S(1)}, bf16[512,128]{1,0:T(8,128)(2,1)S(1)}, u32[]{:S(2)}, u32[]{:S(2)}) collective-permute-start(bf16[512,128]{1,0:T(8,128)(2,1)S(1)} %get-tuple-element.126), channel_id=1, source_target_pairs={{0,7},{1,2},{2,1},{3,4},{4,3},{5,6},{6,5},{7,0},{8,15},{9,10},{10,... | collective-permute-start | bytes 393224 | tf_op jit(solution)/shard_map/ppermute | solution.py:562
  34.3 4.2 %collective-permute-start.6 = (bf16[512,128]{1,0:T(8,128)(2,1)S(1)}, bf16[512,128]{1,0:T(8,128)(2,1)S(1)}, u32[]{:S(2)}, u32[]{:S(2)}) collective-permute-start(bf16[512,128]{1,0:T(8,128)(2,1)S(1)} %add_on.4), channel_id=1, source_target_pairs={{16,8},{17,9},{18,10},{19,11},{20,12},{21,13},{22,14},{23,15}} | collective-permute-start | bytes 393224 | tf_op jit(solution)/shard_map/ppermute | solution.py:573
  37.2 3.0 %collective-permute-start.14 = (bf16[512,128]{1,0:T(8,128)(2,1)S(1)}, bf16[512,128]{1,0:T(8,128)(2,1)S(1)}, u32[]{:S(2)}, u32[]{:S(2)}) collective-permute-start(bf16[512,128]{1,0:T(8,128)(2,1)S(1)} %add_off.4), channel_id=1, source_target_pairs={{16,8},{17,9},{18,10},{19,11},{20,12},{21,13},{22,14},{23,15}} | collective-permute-start | bytes 393224 | tf_op jit(solution)/shard_map/ppermute | solution.py:573
  37.8 5.8 %collective-permute-start.9 = (bf16[512,128]{1,0:T(8,128)(2,1)S(1)}, bf16[512,128]{1,0:T(8,128)(2,1)S(1)}, u32[]{:S(2)}, u32[]{:S(2)}) collective-permute-start(bf16[512,128]{1,0:T(8,128)(2,1)S(1)} %get-tuple-element.119), channel_id=1, source_target_pairs={{16,8},{17,9},{18,10},{19,11},{20,12},{21,13},{22,14},{23,15}} | collective-permute-start | bytes 393224 | tf_op jit(solution)/shard_map/ppermute | solution.py:573
  40.1 5.8 %collective-permute-start.10 = (bf16[512,128]{1,0:T(8,128)(2,1)S(1)}, bf16[512,128]{1,0:T(8,128)(2,1)S(1)}, u32[]{:S(2)}, u32[]{:S(2)}) collective-permute-start(bf16[512,128]{1,0:T(8,128)(2,1)S(1)} %get-tuple-element.123), channel_id=1, source_target_pairs={{0,1},{1,0},{2,3},{3,2},{4,5},{5,4},{6,7},{7,6},{8,9},{9,8},{10,11... | collective-permute-start | bytes 393224 | tf_op jit(solution)/shard_map/ppermute | solution.py:549
  41.6 9.0 %collective-permute-start.15 = (bf16[512,128]{1,0:T(8,128)(2,1)S(1)}, bf16[512,128]{1,0:T(8,128)(2,1)S(1)}, u32[]{:S(2)}, u32[]{:S(2)}) collective-permute-start(bf16[512,128]{1,0:T(8,128)(2,1)S(1)} %get-tuple-element.133), channel_id=1, source_target_pairs={{0,7},{1,2},{2,1},{3,4},{4,3},{5,6},{6,5},{7,0},{8,15},{9,10},{10,... | collective-permute-start | bytes 393224 | tf_op jit(solution)/shard_map/ppermute | solution.py:562
  45.9 14.7 %collective-permute-start.11 = (bf16[512,128]{1,0:T(8,128)(2,1)S(1)}, bf16[512,128]{1,0:T(8,128)(2,1)S(1)}, u32[]{:S(2)}, u32[]{:S(2)}) collective-permute-start(bf16[512,128]{1,0:T(8,128)(2,1)S(1)} %add_on.5), channel_id=1, source_target_pairs={{8,0},{9,1},{10,2},{11,3},{12,4},{13,5},{14,6},{15,7}} | collective-permute-start | bytes 393224 | tf_op jit(solution)/shard_map/ppermute | solution.py:573
  49.3 14.4 %collective-permute-start.17 = (bf16[512,128]{1,0:T(8,128)(2,1)S(1)}, bf16[512,128]{1,0:T(8,128)(2,1)S(1)}, u32[]{:S(2)}, u32[]{:S(2)}) collective-permute-start(bf16[512,128]{1,0:T(8,128)(2,1)S(1)} %get-tuple-element.135), channel_id=1, source_target_pairs={{8,0},{9,1},{10,2},{11,3},{12,4},{13,5},{14,6},{15,7}} | collective-permute-start | bytes 393224 | tf_op jit(solution)/shard_map/ppermute | solution.py:573
  50.7 14.5 %collective-permute-start.16 = (bf16[512,128]{1,0:T(8,128)(2,1)S(1)}, bf16[512,128]{1,0:T(8,128)(2,1)S(1)}, u32[]{:S(2)}, u32[]{:S(2)}) collective-permute-start(bf16[512,128]{1,0:T(8,128)(2,1)S(1)} %add_off.5), channel_id=1, source_target_pairs={{8,0},{9,1},{10,2},{11,3},{12,4},{13,5},{14,6},{15,7}} | collective-permute-start | bytes 393224 | tf_op jit(solution)/shard_map/ppermute | solution.py:573
  62.2 3.0 %collective-permute-start.12 = (bf16[512,128]{1,0:T(8,128)(2,1)S(1)}, bf16[512,128]{1,0:T(8,128)(2,1)S(1)}, u32[]{:S(2)}, u32[]{:S(2)}) collective-permute-start(bf16[512,128]{1,0:T(8,128)(2,1)S(1)} %get-tuple-element.124), channel_id=1, source_target_pairs={{0,1},{1,0},{2,3},{3,2},{4,5},{5,4},{6,7},{7,6},{8,9},{9,8},{10,11... | collective-permute-start | bytes 393224 | tf_op jit(solution)/shard_map/ppermute | solution.py:583
  68.2 2.7 %collective-permute-start.18 = (bf16[4,64,2048]{2,1,0:T(8,128)(2,1)S(1)}, bf16[4,64,2048]{2,1,0:T(8,128)(2,1)S(1)}, u32[]{:S(2)}, u32[]{:S(2)}) collective-permute-start(bf16[4,64,2048]{2,1,0:T(8,128)(2,1)S(1)} %get-tuple-element.142), channel_id=1, source_target_pairs={{0,1},{1,0},{2,3},{3,2},{4,5},{5,4},{6,7},{7,6},{8,9},{9,8},{10,11... | collective-permute-start | bytes 3145736 | tf_op jit(solution)/shard_map/ppermute | solution.py:600
  71.1 14.0 %collective-permute-start.20 = (bf16[2,64,1152]{2,1,0:T(8,128)(2,1)S(1)}, bf16[2,64,1152]{2,1,0:T(8,128)(2,1)S(1)}, u32[]{:S(2)}, u32[]{:S(2)}) collective-permute-start(bf16[2,64,1152]{2,1,0:T(8,128)(2,1)S(1)} %get-tuple-element.148), channel_id=1, source_target_pairs={{0,2},{1,3},{2,0},{3,1},{4,6},{5,7},{6,4},{7,5},{8,10},{9,11},{10,... | collective-permute-start | bytes 884744 | tf_op jit(solution)/shard_map/ppermute | solution.py:612
  71.2 11.8 %collective-permute-start.21 = (bf16[2,64,896]{2,1,0:T(8,128)(2,1)S(1)}, bf16[2,64,896]{2,1,0:T(8,128)(2,1)S(1)}, u32[]{:S(2)}, u32[]{:S(2)}) collective-permute-start(bf16[2,64,896]{2,1,0:T(8,128)(2,1)S(1)} %get-tuple-element.150), channel_id=1, source_target_pairs={{0,4},{1,5},{2,6},{3,7},{4,0},{5,1},{6,2},{7,3},{8,12},{9,13},{10,... | collective-permute-start | bytes 688136 | tf_op jit(solution)/shard_map/ppermute | solution.py:613
  85.2 12.0 %collective-permute-start.22 = (bf16[64,1152]{1,0:T(8,128)(2,1)S(1)}, bf16[64,1152]{1,0:T(8,128)(2,1)S(1)}, u32[]{:S(2)}, u32[]{:S(2)}) collective-permute-start(bf16[64,1152]{1,0:T(8,128)(2,1)S(1)} %get-tuple-element.152), channel_id=1, source_target_pairs={{0,4},{1,5},{2,6},{3,7},{4,0},{5,1},{6,2},{7,3},{8,12},{9,13},{10,... | collective-permute-start | bytes 442376 | tf_op jit(solution)/shard_map/ppermute | solution.py:627
  86.5 7.7 %collective-permute-start.19 = (bf16[512,128]{1,0:T(8,128)(2,1)S(1)}, bf16[512,128]{1,0:T(8,128)(2,1)S(1)}, u32[]{:S(2)}, u32[]{:S(2)}) collective-permute-start(bf16[512,128]{1,0:T(8,128)(2,1)S(1)} %get-tuple-element.147.refs_0_), channel_id=1, source_target_pairs={{0,7},{1,2},{2,1},{3,4},{4,3},{5,6},{6,5},{7,0},{8,15},{9,10},{10,... | collective-permute-start | bytes 393224 | tf_op jit(solution)/shard_map/ppermute | solution.py:620
  86.9 10.3 %collective-permute-start.23 = (bf16[64,896]{1,0:T(8,128)(2,1)S(1)}, bf16[64,896]{1,0:T(8,128)(2,1)S(1)}, u32[]{:S(2)}, u32[]{:S(2)}) collective-permute-start(bf16[64,896]{1,0:T(8,128)(2,1)S(1)} %get-tuple-element.154), channel_id=1, source_target_pairs={{0,2},{1,3},{2,0},{3,1},{4,6},{5,7},{6,4},{7,5},{8,10},{9,11},{10,... | collective-permute-start | bytes 344072 | tf_op jit(solution)/shard_map/ppermute | solution.py:626
